TPU v7x, 32 devices: a whole 2x2x4 slice. The times are simulated.
32 devices in a mesh: slab: 16 (over z, x, core), coil: 2 (over y).
Axes of the slice: x: 2, y: 2, z: 4, core: 2. Of those that a mesh axis runs over, the one named last changes fastest.
Arguments:
- current_image: bfloat16 [2, 5, 2, 2, 256, 384], P('coil', None, None, None, 'slab'), may hold values from -6 to 6
- coil_maps: bfloat16 [32, 2, 2, 256, 384], P(None, None, None, 'slab'), may hold values from -2.5 to 2.5
- measured: bfloat16 [2, 32, 5, 2, 2, 384, 256], P('coil', 'slab'), may hold values from -4 to 4
- sampling: int32 [2, 5, 384, 256], P('coil'), may hold values 0 or 1
- first_weight: bfloat16 [64, 10, 3, 3, 3], replicated, may hold values from -0.375 to 0.375
- first_bias: float32 [64], replicated, may hold values from -3 to 3
- second_weight: bfloat16 [10, 64, 3, 3, 3], replicated, may hold values from -0.15625 to 0.15625
- second_bias: float32 [10], replicated, may hold values from -3 to 3
Outputs:
- refined: bfloat16 [2, 5, 2, 2, 256, 384], P('coil', None, None, None, 'slab')
All inputs are finite; a program needn't handle non-finite values. No bound on the sum of `sampling` on one device may be relied on, other than what follows from the above.
Results may differ from a plain program's by a relative error of at most 0.014.
Values may be sent and summed in bfloat16 or wider, within the bound.
No kernel may reach another device: no remote copies, remote signals or barrier semaphores. Data moves between devices by JAX's collectives and lax.ppermute only.
A program may use at most 128 MiB of HBM per device.

v0:
```python
import math

import jax
import jax.numpy as jnp
import ml_dtypes
import numpy as np
from jax import lax
from jax.experimental import pallas as pl
from jax.experimental.pallas import tpu as pltpu
from jax.sharding import PartitionSpec as P

BF16 = jnp.bfloat16
F32 = jnp.float32
SLAB, COIL = "slab", "coil"


def dft_table(length, inverse):
    indices = np.arange(length, dtype=np.int64)
    wrapped = indices[:, None] * indices[None, :] % length
    angles = wrapped.astype(np.float32) * np.float32(2.0 * math.pi / length)
    factor = np.float32(1.0 / math.sqrt(length))
    cosine = np.cos(angles) * factor
    sine = np.sin(angles) * factor
    sign = np.float32(1.0 if inverse else -1.0)
    upper = np.stack([cosine, sign * sine], axis=1)
    lower = np.stack([-sign * sine, cosine], axis=1)
    return np.stack([upper, lower], axis=0).astype(ml_dtypes.bfloat16)


def as_right(table):
    length = table.shape[1]
    return jnp.asarray(table.reshape(2 * length, 2 * length))


def as_left(table):
    length = table.shape[1]
    return jnp.asarray(table.transpose(2, 3, 0, 1).reshape(2 * length, 2 * length))


class Ring:
    def __init__(self, devices):
        self.devices = devices
        self.chips = devices // 2
        self.half = self.chips // 2
        column = self.chips // 2
        self.order = [2 * i for i in range(column)] + [2 * i + 1 for i in reversed(range(column))]

    def perm(self, step):
        return [
            (2 * self.order[i] + core, 2 * self.order[(i + step) % self.chips] + core)
            for i in range(self.chips)
            for core in range(2)
        ]

    def siblings(self):
        return [(i, i ^ 1) for i in range(self.devices)]

    def offsets(self):
        out = [0]
        for step in range(1, self.half):
            out += [-step, step]
        return out + [self.half]

    def slabs(self):
        me = lax.axis_index(SLAB)
        chip, core = me // 2, me % 2
        column = self.chips // 2
        row = chip // 2
        place = jnp.where(chip % 2 == 0, row, self.chips - 1 - row)
        at = (place + jnp.array(self.offsets(), jnp.int32) + self.chips) % self.chips
        held = jnp.where(at < column, 2 * at, 2 * (self.chips - 1 - at) + 1)
        return jnp.concatenate([2 * held + core, 2 * held + 1 - core]).astype(jnp.int32)


def ring_gather(ring, own):
    up = down = own
    pieces = [own]
    for _ in range(1, ring.half):
        up = lax.ppermute(up, SLAB, ring.perm(1))
        down = lax.ppermute(down, SLAB, ring.perm(-1))
        pieces += [up, down]
    cut = own.shape[0] // 2
    up = lax.ppermute(up[:cut], SLAB, ring.perm(1))
    down = lax.ppermute(down[cut:], SLAB, ring.perm(-1))
    pieces.append(jnp.concatenate([up, down], axis=0))
    mine = jnp.stack(pieces)
    return mine, lax.ppermute(mine, SLAB, ring.siblings())


def plus(a, b):
    return (a.astype(F32) + b.astype(F32)).astype(BF16)


def ring_scatter(ring, sums):
    part = plus(sums[0], lax.ppermute(sums[1], SLAB, ring.siblings()))
    index = {offset: i for i, offset in enumerate(ring.offsets())}
    cut = part.shape[1] // 2
    far = part[index[ring.half]]
    up = lax.ppermute(far[:cut], SLAB, ring.perm(1))
    down = lax.ppermute(far[cut:], SLAB, ring.perm(-1))
    for step in range(ring.half - 1, 0, -1):
        above, below = part[index[step]], part[index[-step]]
        if step == ring.half - 1:
            above = jnp.concatenate([plus(above[:cut], up), above[cut:]], axis=0)
            below = jnp.concatenate([below[:cut], plus(below[cut:], down)], axis=0)
        else:
            above, below = plus(above, up), plus(below, down)
        up = lax.ppermute(above, SLAB, ring.perm(1))
        down = lax.ppermute(below, SLAB, ring.perm(-1))
    return part[0].astype(F32) + up.astype(F32) + down.astype(F32)


def nt_dot(a, b):
    return lax.dot_general(a, b, (((1,), (1,)), ((), ())), preferred_element_type=F32)


def nn_dot(a, b):
    return lax.dot_general(a, b, (((1,), (0,)), ((), ())), preferred_element_type=F32)


def gradient_kernel(
    slabs, mine, other, maps_a, maps_b, measured, sampling, ty_f, tz_f, tz_i, ty_i, out, products, backs
):
    pieces, _, rows, ny = mine.shape
    nz = 2 * pieces * rows
    first = slabs[2 * pieces]
    maps = (maps_a, maps_b)
    for k in range(2 * pieces):
        held = mine if k < pieces else other
        slab = slabs[k]
        at = pl.ds(pl.multiple_of(slab * rows, rows), rows)
        real = held[k % pieces, 0].astype(F32)
        imag = held[k % pieces, 1].astype(F32)
        for c in range(2):
            m_real = maps[c][slab, 0].astype(F32)
            m_imag = maps[c][slab, 1].astype(F32)
            products[c, at, :ny] = (m_real * real - m_imag * imag).astype(BF16)
            products[c, at, ny:] = (m_real * imag + m_imag * real).astype(BF16)
    mask = sampling[0, 0].astype(F32)
    lefts = []
    for c in range(2):
        spectra = nt_dot(ty_f[...], products[c]).astype(BF16)
        lefts.append(jnp.concatenate([spectra[:ny], spectra[ny:]], axis=1))
    spectrum = nn_dot(jnp.concatenate(lefts, axis=0), tz_f[...])
    residuals = []
    for c in range(2):
        coil = first if c == 0 else 1 - first
        spec = spectrum[c * ny : (c + 1) * ny]
        seen = measured[0, coil, 0, :, 0].astype(F32)
        residuals.append(
            jnp.concatenate(
                [(mask * (spec[:, :nz] - seen[0])).astype(BF16), (mask * (spec[:, nz:] - seen[1])).astype(BF16)],
                axis=1,
            )
        )
    depth = nt_dot(tz_i[...], jnp.concatenate(residuals, axis=0)).astype(BF16)
    for c in range(2):
        cols = slice(c * ny, (c + 1) * ny)
        line = jnp.concatenate([depth[:nz, cols], depth[nz:, cols]], axis=1)
        backs[c] = nn_dot(line, ty_i[...])
    for k in range(2 * pieces):
        slab = slabs[k]
        at = pl.ds(pl.multiple_of(slab * rows, rows), rows)
        real, imag = 0.0, 0.0
        for c in range(2):
            m_real = maps[c][slab, 0].astype(F32)
            m_imag = maps[c][slab, 1].astype(F32)
            b_real, b_imag = backs[c, at, :ny], backs[c, at, ny:]
            real += m_real * b_real + m_imag * b_imag
            imag += m_real * b_imag - m_imag * b_real
        out[k // pieces, k % pieces, 0] = real.astype(BF16)
        out[k // pieces, k % pieces, 1] = imag.astype(BF16)


def gradient(where, mine, other, maps_a, maps_b, measured, sampling, tables, x):
    pieces, channels, rows, ny = mine.shape
    encodings = channels // 2
    nz = 2 * pieces * rows
    coils = 2
    whole = lambda a: pl.BlockSpec(a.shape, lambda e, s: (0,) * a.ndim, pipeline_mode=pl.Buffered(1))
    held = pl.BlockSpec((pieces, 2, rows, ny), lambda e, s: (0, e, 0, 0))
    flops = 2 * encodings * coils * 2 * 4 * (nz * ny * ny + nz * nz * ny)
    return pl.pallas_call(
        gradient_kernel,
        grid_spec=pltpu.PrefetchScalarGridSpec(
            num_scalar_prefetch=1,
            grid=(encodings,),
            in_specs=[
                held,
                held,
                whole(maps_a),
                whole(maps_b),
                pl.BlockSpec((1, coils, 1, 2, 1, ny, nz), lambda e, s: (0, 0, e, 0, x, 0, 0)),
                pl.BlockSpec((1, 1, ny, nz), lambda e, s: (0, e, 0, 0)),
            ]
            + [whole(t) for t in tables],
            out_specs=pl.BlockSpec((2, pieces, 2, rows, ny), lambda e, s: (0, 0, e, 0, 0)),
            scratch_shapes=[
                pltpu.VMEM((coils, nz, 2 * ny), BF16),
                pltpu.VMEM((coils, nz, 2 * ny), F32),
            ],
        ),
        out_shape=jax.ShapeDtypeStruct((2, pieces, channels, rows, ny), BF16),
        compiler_params=pltpu.CompilerParams(vmem_limit_bytes=40 * 2**20),
        cost_estimate=pl.CostEstimate(flops=flops, bytes_accessed=8 * 2**20, transcendentals=0),
        name="gradient",
    )(where, mine, other, maps_a, maps_b, measured, sampling, *tables)


def shifted(value, step):
    rows = value.shape[:-1]
    edge = jnp.zeros(rows + (1,), value.dtype)
    if step > 0:
        return jnp.concatenate([value[..., 1:], edge], axis=-1)
    return jnp.concatenate([edge, value[..., :-1]], axis=-1)


def put_strided(ref, start, count, stride, value):
    for j in range(ref.shape[0]):
        ref[j, pl.ds(start, count, stride=stride), :] = value[:, j * 128 : (j + 1) * 128]


def get_lines(ref, start, count):
    return jnp.concatenate([ref[j, start : start + count, :] for j in range(ref.shape[0])], axis=1)


def convolution_kernel(ends, own, other, w_first, b_first, w_second, b_second, out, stacked, result):
    channels, depth, ny = own.shape
    rows = depth - 4
    group = stacked.shape[1] // depth
    lanes = result.shape[1] // rows
    stacked[...] = jnp.zeros_like(stacked)
    for t, source in enumerate((own, other)):
        for i in range(channels):
            value = source[i].astype(F32)
            for d in range(3):
                line = value if d == 1 else shifted(value, d - 1)
                put_strided(stacked, (d * 2 + t) * channels + i, depth, group, line)
    partial = []
    taps = w_second.shape[0] // 3
    for z in range(rows + 2):
        window = get_lines(stacked, z * group, 3 * group).astype(BF16)
        hidden = jnp.maximum(nn_dot(w_first[...], window) + b_first[...], 0.0)
        if z == 0:
            hidden = hidden * ends[0].astype(F32)
        if z == rows + 1:
            hidden = hidden * ends[1].astype(F32)
        partial.append(nn_dot(w_second[...], hidden.astype(BF16)))
        if z >= 2:
            total = partial[z - 2][:taps] + partial[z - 1][taps : 2 * taps] + partial[z][2 * taps :]
            line = (
                shifted(total[:lanes], -1) + total[lanes : 2 * lanes] + shifted(total[2 * lanes :], 1)
            )
            put_strided(result, z - 2, lanes, rows, line)
            partial[z - 2] = None
    for i in range(channels):
        value = own[i].astype(F32)[2 : 2 + rows]
        out[i] = (value + get_lines(result, i * rows, rows) + b_second[i]).astype(BF16)


def convolutions(ends, own, other, w_first, b_first, w_second, b_second):
    channels, depth, ny = own.shape
    rows = depth - 4
    group = w_first.shape[1] // 3
    lanes = w_second.shape[0] // 9
    vmem = pl.BlockSpec(memory_space=pltpu.VMEM)
    smem = pl.BlockSpec(memory_space=pltpu.SMEM)
    flops = 2 * (rows + 2) * ny * (w_first.size + w_second.size)
    return pl.pallas_call(
        convolution_kernel,
        in_specs=[smem, vmem, vmem, vmem, vmem, vmem, smem],
        out_specs=vmem,
        out_shape=jax.ShapeDtypeStruct((channels, rows, ny), BF16),
        scratch_shapes=[
            pltpu.VMEM((ny // 128, depth * group, 128), F32),
            pltpu.VMEM((ny // 128, lanes * rows, 128), F32),
        ],
        compiler_params=pltpu.CompilerParams(vmem_limit_bytes=24 * 2**20),
        cost_estimate=pl.CostEstimate(flops=flops, bytes_accessed=2**20, transcendentals=0),
        name="convolutions",
    )(ends, own, other, w_first, b_first, w_second, b_second)


def round_up(value, unit):
    return -(-value // unit) * unit


def convolution_weights(first_weight, first_bias, second_weight):
    q = lax.axis_index(COIL)
    ahead = 2 - 2 * q
    behind = 2 * q

    def tap(weight, index):
        return lax.dynamic_index_in_dim(weight, index, axis=2, keepdims=False)

    feat, channels = first_weight.shape[:2]
    same, of_other, of_own = (tap(first_weight, i) for i in (1, ahead, behind))
    first = jnp.stack([jnp.stack([same, of_other], 1), jnp.stack([of_own, same], 1)], 0)
    first = first.transpose(0, 1, 4, 5, 2, 3).reshape(2 * feat, 3, 6 * channels)
    group = round_up(6 * channels, 16)
    first = jnp.pad(first, ((0, 0), (0, 0), (0, group - 6 * channels))).reshape(2 * feat, 3 * group)
    bias = jnp.concatenate([first_bias, first_bias])[:, None]
    second = jnp.stack([tap(second_weight, 1), tap(second_weight, ahead)], 1)
    second = second.transpose(3, 4, 0, 1, 2).reshape(3, 3, channels, 2 * feat)
    lanes = round_up(channels, 8)
    second = jnp.pad(second, ((0, 0), (0, 0), (0, lanes - channels), (0, 0))).reshape(9 * lanes, 2 * feat)
    return first, bias, second


def paired(current_image, coil_maps, measured, sampling, first_weight, first_bias, second_weight, second_bias):
    devices = lax.axis_size(SLAB)
    ring = Ring(devices)
    me, q = lax.axis_index(SLAB), lax.axis_index(COIL)
    _, encodings, _, width, rows, ny = current_image.shape
    nz = rows * devices
    channels = 2 * encodings
    y_forward, y_inverse = dft_table(ny, False), dft_table(ny, True)
    z_forward, z_inverse = dft_table(nz, False), dft_table(nz, True)
    tables = (as_left(y_forward), as_right(z_forward), as_left(z_inverse), as_right(y_inverse))
    where = jnp.concatenate([ring.slabs(), q[None].astype(jnp.int32)])
    swap = [(0, 1), (1, 0)]
    pairs = coil_maps.reshape((devices, 2) + coil_maps.shape[1:])
    pairs = lax.dynamic_index_in_dim(pairs, q, axis=1, keepdims=False)
    weights = convolution_weights(first_weight, first_bias, second_weight)
    ends = jnp.stack([me > 0, me < devices - 1]).astype(jnp.int32)

    images = [current_image[0, :, :, x].reshape(channels, rows, ny) for x in range(width)]
    maps, gathered = [], []
    for x in range(width):
        kept = lax.all_to_all(pairs[:, :, x], SLAB, split_axis=0, concat_axis=0, tiled=True)
        maps.append((kept, lax.ppermute(kept, COIL, swap)))
        gathered.append(ring_gather(ring, images[x]))
    refined = []
    for x in range(width):
        sums = gradient(where, *gathered[x], *maps[x], measured, sampling, tables, x)
        updated = (images[x].astype(F32) - ring_scatter(ring, sums)).astype(BF16)
        up = [(i, i + 1) for i in range(devices - 1)]
        down = [(i + 1, i) for i in range(devices - 1)]
        bordered = jnp.concatenate(
            [
                lax.ppermute(updated[:, rows - 2 :], SLAB, up),
                updated,
                lax.ppermute(updated[:, :2], SLAB, down),
            ],
            axis=1,
        )
        other = lax.ppermute(bordered, COIL, swap)
        refined.append(convolutions(ends, bordered, other, *weights, second_bias))
    out = jnp.stack(refined, axis=1).reshape(encodings, 2, width, rows, ny)
    return out[None]


def with_halo(cells, sides, width):
    for axis, dim in sides:
        count = lax.axis_size(axis)
        ends = count - 1
        head = lax.slice_in_dim(cells, 0, width, axis=dim)
        tail = lax.slice_in_dim(cells, cells.shape[dim] - width, cells.shape[dim], axis=dim)
        cells = jnp.concatenate(
            [
                lax.ppermute(tail, axis, [(i, (i + 1) % count) for i in range(ends)]),
                cells,
                lax.ppermute(head, axis, [((i + 1) % count, i) for i in range(ends)]),
            ],
            axis=dim,
        )
    return cells


def plain_table(length, inverse):
    indices = jnp.arange(length, dtype=jnp.int32)
    wrapped = indices[:, None] * indices[None, :] % length
    angles = wrapped.astype(jnp.float32) * (2.0 * math.pi / length)
    factor = 1.0 / math.sqrt(length)
    cosine = jnp.cos(angles) * factor
    sine_part = jnp.sin(angles) * factor
    phase_sign = 1.0 if inverse else -1.0
    upper_rows = jnp.stack([cosine, phase_sign * sine_part], axis=1)
    lower_rows = jnp.stack([-phase_sign * sine_part, cosine], axis=1)
    return jnp.stack([upper_rows, lower_rows], axis=0).astype(jnp.bfloat16)


def coil_products(maps_part, image_part):
    maps_real = maps_part[:, 0][None, :, None].astype(jnp.float32)
    maps_imaginary = maps_part[:, 1][None, :, None].astype(jnp.float32)
    image_real = image_part[:, :, 0][:, None].astype(jnp.float32)
    image_imaginary = image_part[:, :, 1][:, None].astype(jnp.float32)
    real_part = maps_real * image_real - maps_imaginary * image_imaginary
    imaginary_part = maps_real * image_imaginary + maps_imaginary * image_real
    return jnp.stack([real_part, imaginary_part], axis=3).astype(jnp.bfloat16)


def transform(operand, matrix):
    return jnp.einsum("pcerxzy,ryqk->pceqxzk", operand, matrix, preferred_element_type=jnp.float32)


def combine_coils(maps_part, values):
    maps_real = maps_part[:, 0][None, :, None].astype(jnp.float32)
    maps_imaginary = maps_part[:, 1][None, :, None].astype(jnp.float32)
    real_sum = jnp.sum(maps_real * values[:, :, :, 0] + maps_imaginary * values[:, :, :, 1], axis=1)
    imaginary_sum = jnp.sum(
        maps_real * values[:, :, :, 1] - maps_imaginary * values[:, :, :, 0], axis=1
    )
    return jnp.stack([real_sum, imaginary_sum], axis=2)


def convolve(operand, weights):
    widened = jnp.pad(operand, ((0, 0), (0, 0), (0, 0), (0, 0), (1, 1)))
    return lax.conv_general_dilated(
        widened,
        weights,
        (1, 1, 1),
        "VALID",
        dimension_numbers=("DCNHW", "OIDHW", "DCNHW"),
        preferred_element_type=jnp.float32,
    )


def on_device(
    current_image,
    coil_maps,
    measured,
    sampling,
    first_weight,
    first_bias,
    second_weight,
    second_bias,
):
    depth = current_image.shape[4] * lax.axis_size("slab")
    forward_y = plain_table(current_image.shape[5], False)
    inverse_y = plain_table(current_image.shape[5], True)
    forward_z = plain_table(depth, False)
    inverse_z = plain_table(depth, True)
    sampled = sampling.astype(jnp.float32)[:, None, :, None, None]
    local_maps = lax.all_to_all(coil_maps, "slab", split_axis=0, concat_axis=3, tiled=True)
    row_spectra = transform(
        coil_products(local_maps, lax.all_gather(current_image, "slab", axis=4, tiled=True)),
        forward_y,
    ).astype(jnp.bfloat16)
    residual = (
        sampled
        * (
            jnp.einsum(
                "pcerxzk,rzqj->pceqxkj", row_spectra, forward_z, preferred_element_type=jnp.float32
            )
            - measured.astype(jnp.float32)
        )
    ).astype(jnp.bfloat16)
    depth_back = jnp.einsum(
        "pcerxkj,rjqz->pceqxzk", residual, inverse_z, preferred_element_type=jnp.float32
    ).astype(jnp.bfloat16)
    partial_sum = combine_coils(local_maps, transform(depth_back, inverse_y))
    gradient = lax.psum_scatter(
        partial_sum.astype(jnp.bfloat16), "slab", scatter_dimension=4, tiled=True
    ).astype(jnp.float32)
    updated = (current_image.astype(jnp.float32) - gradient).astype(jnp.bfloat16)
    stacked = updated.reshape((updated.shape[0], 2 * updated.shape[1]) + updated.shape[3:])
    bias_first = first_bias[None, :, None, None, None]
    bordered = with_halo(stacked, (("slab", 3), ("coil", 0)), 1)
    hidden = jax.nn.relu(convolve(bordered, first_weight) + bias_first).astype(jnp.bfloat16)
    bordered_hidden = with_halo(hidden, (("slab", 3), ("coil", 0)), 1)
    second = convolve(bordered_hidden, second_weight)
    refined = stacked.astype(jnp.float32) + second + second_bias[None, :, None, None, None]
    return refined.astype(jnp.bfloat16).reshape(updated.shape)


def solution(mesh):
    devices, phases = mesh.shape[SLAB], mesh.shape[COIL]

    def per_device(*args):
        coils, phase = args[2].shape[1], args[0].shape[0]
        if phases == 2 and coils == 2 and phase == 1 and devices % 4 == 0 and args[0].shape[4] % 16 == 0:
            return paired(*args)
        return on_device(*args)

    in_specs = (
        P("coil", None, None, None, "slab", None),
        P(None, None, None, "slab", None),
        P("coil", "slab", None, None, None, None, None),
        P("coil", None, None, None),
        P(),
        P(),
        P(),
        P(),
    )
    out_specs = P("coil", None, None, None, "slab", None)
    return jax.shard_map(
        per_device, mesh=mesh, in_specs=in_specs, out_specs=out_specs, check_vma=False
    )
```

profile of v0, /device:TPU:1, one launch (start us, length us, event | category | flops | bytes accessed | tf_op | source)
XLA Modules:
  0.0 170.5 jit_solution(17398881691764762360)
XLA Ops:
  0.0 1.1 fusion.25
  1.1 2.2 %collective-permute-start = (bf16[10,16,384]{2,1,0:T(8,128)(2,1)S(1)}, bf16[10,16,384]{2,1,0:T(8,128)(2,1)}, u32[]{:S(2)}, u32[]{:S(2)}) collective-permute-start(bf16[10,16,384]{2,1,0:T(8,128)(2,1)S(1)} %bitcast.186), channel_id=1, source_target_pairs={{0,8},{2,10},{8,16},{10,18},{16,24},{18,26},{24,28},{26,30},{28,20... | collective-permute-start | bytes 368648 | tf_op jit(solution)/shard_map/ppermute | solution.py:79
  3.3 1.5 collective-permute-start.22
  4.9 1.0 slice_bitcast_fusion.5
  5.9 7.8 %all-to-all-start = ((bf16[16,2,16,384]{3,2,1,0:T(8,128)(2,1)}), bf16[16,2,16,384]{3,2,1,0:T(8,128)(2,1)S(1)}, u32[]{:S(2)}, u32[]{:S(2)}) async-start(bf16[16,2,16,384]{3,2,1,0:T(8,128)(2,1)} %get-tuple-element.23), calls=%async_computation | async-start | bytes 786432 | tf_op jit(solution)/shard_map/all_to_all | solution.py:330
  15.7 1.4 collective-permute-start.2
  17.1 1.0 bitcast_dynamic-update-slice_fusion.11
  18.2 1.0 bitcast_dynamic-update-slice_fusion.10
  19.1 1.4 collective-permute-start.24
  20.6 1.6 bitcast_dynamic-update-slice_fusion.5
  22.3 1.6 bitcast_dynamic-update-slice_fusion.4
  23.8 2.6 %collective-permute-start.4 = (bf16[10,16,384]{2,1,0:T(8,128)(2,1)S(1)}, bf16[10,16,384]{2,1,0:T(8,128)(2,1)S(1)}, u32[]{:S(2)}, u32[]{:S(2)}) collective-permute-start(bf16[10,16,384]{2,1,0:T(8,128)(2,1)S(1)} %collective-permute-done.2), channel_id=1, source_target_pairs={{0,8},{2,10},{8,16},{10,18},{16,24},{18,26},{24,28},{26,30},{28,20... | collective-permute-start | bytes 368648 | tf_op jit(solution)/shard_map/ppermute | solution.py:79
  26.5 2.6 %collective-permute-start.26 = (bf16[10,16,384]{2,1,0:T(8,128)(2,1)}, bf16[10,16,384]{2,1,0:T(8,128)(2,1)S(1)}, u32[]{:S(2)}, u32[]{:S(2)}) collective-permute-start(bf16[10,16,384]{2,1,0:T(8,128)(2,1)} %collective-permute-done.24), channel_id=1, source_target_pairs={{0,8},{2,10},{8,16},{10,18},{16,24},{18,26},{24,28},{26,30},{28,20... | collective-permute-start | bytes 368648 | tf_op jit(solution)/shard_map/ppermute | solution.py:79
  29.7 1.8 %collective-permute-start.6 = (bf16[5,16,384]{2,1,0:T(8,128)(2,1)S(1)}, bf16[5,16,384]{2,1,0:T(8,128)(2,1)S(1)}, u32[]{:S(2)}, u32[]{:S(2)}) collective-permute-start(bf16[5,16,384]{2,1,0:T(8,128)(2,1)S(1)} %slice.208), channel_id=1, source_target_pairs={{0,8},{2,10},{8,16},{10,18},{16,24},{18,26},{24,28},{26,30},{28,20... | collective-permute-start | bytes 184328 | tf_op jit(solution)/shard_map/ppermute | solution.py:83
  31.5 1.0 collective-permute-start.7
  32.5 2.3 %collective-permute-done.6 = bf16[5,16,384]{2,1,0:T(8,128)(2,1)S(1)} collective-permute-done((bf16[5,16,384]{2,1,0:T(8,128)(2,1)S(1)}, bf16[5,16,384]{2,1,0:T(8,128)(2,1)S(1)}, u32[]{:S(2)}, u32[]{:S(2)}) %collective-permute-start.6) | collective-permute-done | bytes 61472 | tf_op jit(solution)/shard_map/ppermute | solution.py:83
  35.5 2.6 %collective-permute-start.8 = (bf16[8,10,16,384]{3,2,1,0:T(8,128)(2,1)S(1)}, bf16[8,10,16,384]{3,2,1,0:T(8,128)(2,1)}, u32[]{:S(2)}, u32[]{:S(2)}) collective-permute-start(bf16[8,10,16,384]{3,2,1,0:T(8,128)(2,1)S(1)} %fusion.16.mine), channel_id=1, source_target_pairs={{0,2},{2,0},{4,6},{6,4},{8,10},{10,8},{12,14},{14,12},{16,18},{18,... | collective-permute-start | bytes 2949128 | tf_op jit(solution)/shard_map/ppermute | solution.py:87
  38.1 1.6 bitcast_dynamic-update-slice_fusion.3
  39.6 5.2 %all-to-all-start.1 = ((bf16[16,2,16,384]{3,2,1,0:T(8,128)(2,1)}), bf16[16,2,16,384]{3,2,1,0:T(8,128)(2,1)S(1)}, u32[]{:S(2)}, u32[]{:S(2)}) async-start(bf16[16,2,16,384]{3,2,1,0:T(8,128)(2,1)} %get-tuple-element.24), calls=%async_computation.1 | async-start | bytes 786432 | tf_op jit(solution)/shard_map/all_to_all | solution.py:330
  44.9 1.6 bitcast_dynamic-update-slice_fusion.2
  46.4 1.4 collective-permute-start.28
  48.8 1.2 collective-permute-start.9
  50.7 1.5 bitcast_dynamic-update-slice_fusion
  52.3 0.8 collective-permute-done.28
  54.5 1.0 collective-permute-start.30
  56.3 1.2 collective-permute-start.31
  57.5 1.4 collective-permute-done.9.maps_b
  58.9 1.5 copy-done.7
  60.5 1.3 copy-done.9
  61.8 1.0 copy-done.11
  62.8 17.1 %gradient.2 = bf16[2,8,10,16,384]{4,3,2,1,0:T(8,128)(2,1)S(1)} custom-call(s32[17]{0:T(128)S(1)} %pad_add_fusion.slabs, bf16[8,10,16,384]{3,2,1,0:T(8,128)(2,1)S(1)} %fusion.16.mine, bf16[8,10,16,384]{3,2,1,0:T(8,128)(2,1)} %collective-permute-done.8.other, bf16[16,2,16,384]{3,2,1,0:T(8,128)(2,1)S(1)} %all-to-all-done.maps_a, ...), custom_call_target="tpu_custom_call" | custom-call | flops 10066329600 | bytes 8388608 | tf_op jit(solution)/shard_map/gradient/pallas_call | solution.py:183
  80.0 1.1 slice_bitcast_fusion.2
  81.0 2.5 %collective-permute-start.10 = (bf16[8,10,16,384]{3,2,1,0:T(8,128)(2,1)}, bf16[8,10,16,384]{3,2,1,0:T(8,128)(2,1)}, u32[]{:S(2)}, u32[]{:S(2)}) collective-permute-start(bf16[8,10,16,384]{3,2,1,0:T(8,128)(2,1)} %slice_bitcast_fusion.2), channel_id=1, source_target_pairs={{0,2},{2,0},{4,6},{6,4},{8,10},{10,8},{12,14},{14,12},{16,18},{18,... | collective-permute-start | bytes 2949128 | tf_op jit(solution)/shard_map/ppermute | solution.py:95
  83.5 1.0 copy-done.3
  84.5 17.0 %gradient.3 = bf16[2,8,10,16,384]{4,3,2,1,0:T(8,128)(2,1)S(1)} custom-call(s32[17]{0:T(128)S(1)} %pad_add_fusion.slabs, bf16[8,10,16,384]{3,2,1,0:T(8,128)(2,1)} %fusion.17.mine, bf16[8,10,16,384]{3,2,1,0:T(8,128)(2,1)} %collective-permute-done.30.other, bf16[16,2,16,384]{3,2,1,0:T(8,128)(2,1)S(1)} %copy-done.3, ...), custom_call_target="tpu_custom_call" | custom-call | flops 10066329600 | bytes 8388608 | tf_op jit(solution)/shard_map/gradient/pallas_call | solution.py:183
  101.6 1.1 slice_bitcast_fusion
  102.7 1.4 collective-permute-start.32
  104.8 1.5 reshape.89
  106.4 1.4 pad.9.clone
  108.6 1.7 %fusion.1 = bf16[8,10,16,384]{3,2,1,0:T(8,128)(2,1)S(1)} fusion(bf16[8,10,16,384]{3,2,1,0:T(8,128)(2,1)} %collective-permute-done.10, bf16[2,8,10,16,384]{4,3,2,1,0:T(8,128)(2,1)} %copy-done.1), kind=kLoop, calls=%fused_computation.3 | loop fusion | flops 1966080 | bytes 2949120 | tf_op jit(solution)/shard_map/convert_element_type | solution.py:91
  110.9 1.3 collective-permute-start.15
  112.1 1.4 fusion
  113.9 1.3 collective-permute-start.37
  115.2 1.5 collective-permute-start.16
  118.4 1.1 collective-permute-start.34
  119.5 1.3 collective-permute-done.12
  121.2 2.8 %collective-permute-done.34 = bf16[10,16,384]{2,1,0:T(8,128)(2,1)S(1)} collective-permute-done((bf16[10,16,384]{2,1,0:T(8,128)(2,1)S(1)}, bf16[10,16,384]{2,1,0:T(8,128)(2,1)S(1)}, u32[]{:S(2)}, u32[]{:S(2)}) %collective-permute-start.34) | collective-permute-done | bytes 122912 | tf_op jit(solution)/shard_map/ppermute | solution.py:108
  124.1 2.2 %collective-permute-done.13 = bf16[10,16,384]{2,1,0:T(8,128)(2,1)S(1)} collective-permute-done((bf16[10,16,384]{2,1,0:T(8,128)(2,1)S(1)}, bf16[10,16,384]{2,1,0:T(8,128)(2,1)S(1)}, u32[]{:S(2)}, u32[]{:S(2)}) %collective-permute-start.13) | collective-permute-done | bytes 122912 | tf_op jit(solution)/shard_map/ppermute | solution.py:108
  126.5 1.5 collective-permute-start.14
  128.8 1.4 collective-permute-start.39
  130.5 1.2 collective-permute-start.18
  131.7 1.0 collective-permute-done.39
  132.8 1.8 %collective-permute-start.40 = (bf16[10,16,384]{2,1,0:T(8,128)(2,1)S(1)}, bf16[10,16,384]{2,1,0:T(8,128)(2,1)S(1)}, u32[]{:S(2)}, u32[]{:S(2)}) collective-permute-start(bf16[10,16,384]{2,1,0:T(8,128)(2,1)S(1)} %fusion.3), channel_id=1, source_target_pairs={{0,4},{2,6},{8,0},{10,2},{16,8},{18,10},{24,16},{26,18},{28,24},{3... | collective-permute-start | bytes 368648 | tf_op jit(solution)/shard_map/ppermute | solution.py:109
  134.6 1.0 collective-permute-done.18
  135.7 8.1 %collective-permute-start.19 = (bf16[10,2,384]{2,1,0:T(2,128)(2,1)S(1)}, bf16[10,2,384]{2,1,0:T(2,128)(2,1)S(1)}, u32[]{:S(2)}, u32[]{:S(2)}) collective-permute-start(bf16[10,2,384]{2,1,0:T(2,128)(2,1)S(1)} %get-tuple-element.27), channel_id=1, source_target_pairs={{0,2},{2,4},{4,6},{6,8},{8,10},{10,12},{12,14},{14,16},{16,18},{18... | collective-permute-start | bytes 46088 | tf_op jit(solution)/shard_map/ppermute | solution.py:341
  143.8 1.9 %collective-permute-start.20 = (bf16[10,2,384]{2,1,0:T(2,128)(2,1)S(1)}, bf16[10,2,384]{2,1,0:T(2,128)(2,1)S(1)}, u32[]{:S(2)}, u32[]{:S(2)}) collective-permute-start(bf16[10,2,384]{2,1,0:T(2,128)(2,1)S(1)} %get-tuple-element.28), channel_id=1, source_target_pairs={{2,0},{4,2},{6,4},{8,6},{10,8},{12,10},{14,12},{16,14},{18,16},{20... | collective-permute-start | bytes 46088 | tf_op jit(solution)/shard_map/ppermute | solution.py:343
  145.9 3.6 %collective-permute-start.41 = (bf16[10,2,384]{2,1,0:T(2,128)(2,1)S(1)}, bf16[10,2,384]{2,1,0:T(2,128)(2,1)S(1)}, u32[]{:S(2)}, u32[]{:S(2)}) collective-permute-start(bf16[10,2,384]{2,1,0:T(2,128)(2,1)S(1)} %get-tuple-element.29), channel_id=1, source_target_pairs={{0,2},{2,4},{4,6},{6,8},{8,10},{10,12},{12,14},{14,16},{16,18},{18... | collective-permute-start | bytes 46088 | tf_op jit(solution)/shard_map/ppermute | solution.py:341
  149.5 1.9 %collective-permute-start.42 = (bf16[10,2,384]{2,1,0:T(2,128)(2,1)S(1)}, bf16[10,2,384]{2,1,0:T(2,128)(2,1)S(1)}, u32[]{:S(2)}, u32[]{:S(2)}) collective-permute-start(bf16[10,2,384]{2,1,0:T(2,128)(2,1)S(1)} %get-tuple-element.30), channel_id=1, source_target_pairs={{2,0},{4,2},{6,4},{8,6},{10,8},{12,10},{14,12},{16,14},{18,16},{20... | collective-permute-start | bytes 46088 | tf_op jit(solution)/shard_map/ppermute | solution.py:343
  151.6 1.3 collective-permute-start.21
  152.9 2.0 %collective-permute-done.42 = bf16[10,2,384]{2,1,0:T(2,128)(2,1)S(1)} collective-permute-done((bf16[10,2,384]{2,1,0:T(2,128)(2,1)S(1)}, bf16[10,2,384]{2,1,0:T(2,128)(2,1)S(1)}, u32[]{:S(2)}, u32[]{:S(2)}) %collective-permute-start.42) | collective-permute-done | bytes 15392 | tf_op jit(solution)/shard_map/ppermute | solution.py:343
  155.0 1.3 collective-permute-start.43
  156.3 1.4 collective-permute-done.21.other
  157.8 6.0 %convolutions.2 = bf16[10,16,384]{2,1,0:T(8,128)(2,1)S(1)} custom-call(s32[2]{0:T(128)S(1)} %add_convert_fusion.ends, bf16[10,20,384]{2,1,0:T(8,128)(2,1)S(1)} %pad_maximum_fusion.1.own, bf16[10,20,384]{2,1,0:T(8,128)(2,1)S(1)} %collective-permute-done.21.other, bf16[128,192]{1,0:T(8,128)(2,1)S(1)} %copy-done.4, f32[128,1]{1,0:T(8,128)S(1)} %copy-done.5, ...), custom_call_target="tpu_custom_call" | custom-call | flops 594542592 | bytes 1048576 | tf_op jit(solution)/shard_map/convolutions/pallas_call | solution.py:269
  163.8 6.0 %convolutions.3 = bf16[10,16,384]{2,1,0:T(8,128)(2,1)S(1)} custom-call(s32[2]{0:T(128)S(1)} %add_convert_fusion.ends, bf16[10,20,384]{2,1,0:T(8,128)(2,1)S(1)} %pad_maximum_fusion.2.own, bf16[10,20,384]{2,1,0:T(8,128)(2,1)S(1)} %collective-permute-done.43.other, bf16[128,192]{1,0:T(8,128)(2,1)S(1)} %copy-done.4, f32[128,1]{1,0:T(8,128)S(1)} %copy-done.5, ...), custom_call_target="tpu_custom_call" | custom-call | flops 594542592 | bytes 1048576 | tf_op jit(solution)/shard_map/convolutions/pallas_call | solution.py:269
  (140 shorter events, 14.6 us)
Async XLA Ops:
  0.0 4.8 %copy-start = (bf16[32,2,2,16,384]{4,3,2,1,0:T(8,128)(2,1)S(1)}, bf16[32,2,2,16,384]{4,3,2,1,0:T(8,128)(2,1)}, u32[]{:S(2)}) copy-start(bf16[32,2,2,16,384]{4,3,2,1,0:T(8,128)(2,1)} %param.14) | copy-start | bytes 4718596
  1.1 12.6 %copy-start.15 = (bf16[1,5,2,1,16,384]{5,4,3,2,1,0:T(8,128)(2,1)}, bf16[1,5,2,1,16,384]{5,4,3,2,1,0:T(8,128)(2,1)S(1)}, u32[]{:S(2)}) copy-start(bf16[1,5,2,1,16,384]{5,4,3,2,1,0:T(8,128)(2,1)S(1)} %get-tuple-element.25) | copy-start | bytes 368644
  1.1 13.9 %copy-start.13 = (bf16[1,5,2,1,16,384]{5,4,3,2,1,0:T(8,128)(2,1)}, bf16[1,5,2,1,16,384]{5,4,3,2,1,0:T(8,128)(2,1)S(1)}, u32[]{:S(2)}) copy-start(bf16[1,5,2,1,16,384]{5,4,3,2,1,0:T(8,128)(2,1)S(1)} %get-tuple-element.26) | copy-start | bytes 368644
  1.1 14.5 %collective-permute-start = (bf16[10,16,384]{2,1,0:T(8,128)(2,1)S(1)}, bf16[10,16,384]{2,1,0:T(8,128)(2,1)}, u32[]{:S(2)}, u32[]{:S(2)}) collective-permute-start(bf16[10,16,384]{2,1,0:T(8,128)(2,1)S(1)} %bitcast.186), channel_id=1, source_target_pairs={{0,8},{2,10},{8,16},{10,18},{16,24},{18,26},{24,28},{26,30},{28,20... | collective-permute-start | bytes 368648 | tf_op jit(solution)/shard_map/ppermute | solution.py:79
  3.3 14.7 %collective-permute-start.1 = (bf16[10,16,384]{2,1,0:T(8,128)(2,1)S(1)}, bf16[10,16,384]{2,1,0:T(8,128)(2,1)}, u32[]{:S(2)}, u32[]{:S(2)}) collective-permute-start(bf16[10,16,384]{2,1,0:T(8,128)(2,1)S(1)} %bitcast.187), channel_id=1, source_target_pairs={{0,4},{2,6},{8,0},{10,2},{16,8},{18,10},{24,16},{26,18},{28,24},{3... | collective-permute-start | bytes 368648 | tf_op jit(solution)/shard_map/ppermute | solution.py:80
  3.3 15.8 %collective-permute-start.22 = (bf16[10,16,384]{2,1,0:T(8,128)(2,1)S(1)}, bf16[10,16,384]{2,1,0:T(8,128)(2,1)}, u32[]{:S(2)}, u32[]{:S(2)}) collective-permute-start(bf16[10,16,384]{2,1,0:T(8,128)(2,1)S(1)} %bitcast.183), channel_id=1, source_target_pairs={{0,8},{2,10},{8,16},{10,18},{16,24},{18,26},{24,28},{26,30},{28,20... | collective-permute-start | bytes 368648 | tf_op jit(solution)/shard_map/ppermute | solution.py:79
  4.8 17.4 %collective-permute-start.23 = (bf16[10,16,384]{2,1,0:T(8,128)(2,1)S(1)}, bf16[10,16,384]{2,1,0:T(8,128)(2,1)}, u32[]{:S(2)}, u32[]{:S(2)}) collective-permute-start(bf16[10,16,384]{2,1,0:T(8,128)(2,1)S(1)} %bitcast.184), channel_id=1, source_target_pairs={{0,4},{2,6},{8,0},{10,2},{16,8},{18,10},{24,16},{26,18},{28,24},{3... | collective-permute-start | bytes 368648 | tf_op jit(solution)/shard_map/ppermute | solution.py:80
  4.8 8.9 %copy-start.19 = (s32[8]{0:T(128)S(1)}, s32[8]{0:T(128)}, u32[]{:S(2)}) copy-start(s32[8]{0:T(128)} %constant.104.clone) | copy-start | bytes 100
  4.8 8.9 %copy-start.17 = (bf16[64,10,3,3,3]{0,4,3,2,1:T(4,128)(2,1)S(1)}, bf16[64,10,3,3,3]{0,4,3,2,1:T(4,128)(2,1)}, u32[]{:S(2)}) copy-start(bf16[64,10,3,3,3]{0,4,3,2,1:T(4,128)(2,1)} %param.17) | copy-start | bytes 103684
  5.9 33.7 %all-to-all-start = ((bf16[16,2,16,384]{3,2,1,0:T(8,128)(2,1)}), bf16[16,2,16,384]{3,2,1,0:T(8,128)(2,1)S(1)}, u32[]{:S(2)}, u32[]{:S(2)}) async-start(bf16[16,2,16,384]{3,2,1,0:T(8,128)(2,1)} %get-tuple-element.23), calls=%async_computation | async-start | bytes 786432 | tf_op jit(solution)/shard_map/all_to_all | solution.py:330
  15.7 8.2 %collective-permute-start.2 = (bf16[10,16,384]{2,1,0:T(8,128)(2,1)}, bf16[10,16,384]{2,1,0:T(8,128)(2,1)S(1)}, u32[]{:S(2)}, u32[]{:S(2)}) collective-permute-start(bf16[10,16,384]{2,1,0:T(8,128)(2,1)} %collective-permute-done), channel_id=1, source_target_pairs={{0,8},{2,10},{8,16},{10,18},{16,24},{18,26},{24,28},{26,30},{28,20... | collective-permute-start | bytes 368648 | tf_op jit(solution)/shard_map/ppermute | solution.py:79
  18.0 8.4 %collective-permute-start.3 = (bf16[10,16,384]{2,1,0:T(8,128)(2,1)}, bf16[10,16,384]{2,1,0:T(8,128)(2,1)S(1)}, u32[]{:S(2)}, u32[]{:S(2)}) collective-permute-start(bf16[10,16,384]{2,1,0:T(8,128)(2,1)} %collective-permute-done.1), channel_id=1, source_target_pairs={{0,4},{2,6},{8,0},{10,2},{16,8},{18,10},{24,16},{26,18},{28,24},{3... | collective-permute-start | bytes 368648 | tf_op jit(solution)/shard_map/ppermute | solution.py:80
  19.1 7.3 %collective-permute-start.24 = (bf16[10,16,384]{2,1,0:T(8,128)(2,1)}, bf16[10,16,384]{2,1,0:T(8,128)(2,1)}, u32[]{:S(2)}, u32[]{:S(2)}) collective-permute-start(bf16[10,16,384]{2,1,0:T(8,128)(2,1)} %collective-permute-done.22), channel_id=1, source_target_pairs={{0,8},{2,10},{8,16},{10,18},{16,24},{18,26},{24,28},{26,30},{28,20... | collective-permute-start | bytes 368648 | tf_op jit(solution)/shard_map/ppermute | solution.py:79
  22.2 6.9 %collective-permute-start.25 = (bf16[10,16,384]{2,1,0:T(8,128)(2,1)}, bf16[10,16,384]{2,1,0:T(8,128)(2,1)}, u32[]{:S(2)}, u32[]{:S(2)}) collective-permute-start(bf16[10,16,384]{2,1,0:T(8,128)(2,1)} %collective-permute-done.23), channel_id=1, source_target_pairs={{0,4},{2,6},{8,0},{10,2},{16,8},{18,10},{24,16},{26,18},{28,24},{3... | collective-permute-start | bytes 368648 | tf_op jit(solution)/shard_map/ppermute | solution.py:80
  23.8 5.8 %collective-permute-start.4 = (bf16[10,16,384]{2,1,0:T(8,128)(2,1)S(1)}, bf16[10,16,384]{2,1,0:T(8,128)(2,1)S(1)}, u32[]{:S(2)}, u32[]{:S(2)}) collective-permute-start(bf16[10,16,384]{2,1,0:T(8,128)(2,1)S(1)} %collective-permute-done.2), channel_id=1, source_target_pairs={{0,8},{2,10},{8,16},{10,18},{16,24},{18,26},{24,28},{26,30},{28,20... | collective-permute-start | bytes 368648 | tf_op jit(solution)/shard_map/ppermute | solution.py:79
  26.5 5.0 %collective-permute-start.5 = (bf16[10,16,384]{2,1,0:T(8,128)(2,1)S(1)}, bf16[10,16,384]{2,1,0:T(8,128)(2,1)S(1)}, u32[]{:S(2)}, u32[]{:S(2)}) collective-permute-start(bf16[10,16,384]{2,1,0:T(8,128)(2,1)S(1)} %collective-permute-done.3), channel_id=1, source_target_pairs={{0,4},{2,6},{8,0},{10,2},{16,8},{18,10},{24,16},{26,18},{28,24},{3... | collective-permute-start | bytes 368648 | tf_op jit(solution)/shard_map/ppermute | solution.py:80
  26.5 20.0 %collective-permute-start.26 = (bf16[10,16,384]{2,1,0:T(8,128)(2,1)}, bf16[10,16,384]{2,1,0:T(8,128)(2,1)S(1)}, u32[]{:S(2)}, u32[]{:S(2)}) collective-permute-start(bf16[10,16,384]{2,1,0:T(8,128)(2,1)} %collective-permute-done.24), channel_id=1, source_target_pairs={{0,8},{2,10},{8,16},{10,18},{16,24},{18,26},{24,28},{26,30},{28,20... | collective-permute-start | bytes 368648 | tf_op jit(solution)/shard_map/ppermute | solution.py:79
  29.1 18.8 %collective-permute-start.27 = (bf16[10,16,384]{2,1,0:T(8,128)(2,1)}, bf16[10,16,384]{2,1,0:T(8,128)(2,1)}, u32[]{:S(2)}, u32[]{:S(2)}) collective-permute-start(bf16[10,16,384]{2,1,0:T(8,128)(2,1)} %collective-permute-done.25), channel_id=1, source_target_pairs={{0,4},{2,6},{8,0},{10,2},{16,8},{18,10},{24,16},{26,18},{28,24},{3... | collective-permute-start | bytes 368648 | tf_op jit(solution)/shard_map/ppermute | solution.py:80
  29.7 5.1 %collective-permute-start.6 = (bf16[5,16,384]{2,1,0:T(8,128)(2,1)S(1)}, bf16[5,16,384]{2,1,0:T(8,128)(2,1)S(1)}, u32[]{:S(2)}, u32[]{:S(2)}) collective-permute-start(bf16[5,16,384]{2,1,0:T(8,128)(2,1)S(1)} %slice.208), channel_id=1, source_target_pairs={{0,8},{2,10},{8,16},{10,18},{16,24},{18,26},{24,28},{26,30},{28,20... | collective-permute-start | bytes 184328 | tf_op jit(solution)/shard_map/ppermute | solution.py:83
  31.5 4.0 %collective-permute-start.7 = (bf16[5,16,384]{2,1,0:T(8,128)(2,1)S(1)}, bf16[5,16,384]{2,1,0:T(8,128)(2,1)S(1)}, u32[]{:S(2)}, u32[]{:S(2)}) collective-permute-start(bf16[5,16,384]{2,1,0:T(8,128)(2,1)S(1)} %slice.209), channel_id=1, source_target_pairs={{0,4},{2,6},{8,0},{10,2},{16,8},{18,10},{24,16},{26,18},{28,24},{3... | collective-permute-start | bytes 184328 | tf_op jit(solution)/shard_map/ppermute | solution.py:84
  35.5 23.5 %collective-permute-start.8 = (bf16[8,10,16,384]{3,2,1,0:T(8,128)(2,1)S(1)}, bf16[8,10,16,384]{3,2,1,0:T(8,128)(2,1)}, u32[]{:S(2)}, u32[]{:S(2)}) collective-permute-start(bf16[8,10,16,384]{3,2,1,0:T(8,128)(2,1)S(1)} %fusion.16.mine), channel_id=1, source_target_pairs={{0,2},{2,0},{4,6},{6,4},{8,10},{10,8},{12,14},{14,12},{16,18},{18,... | collective-permute-start | bytes 2949128 | tf_op jit(solution)/shard_map/ppermute | solution.py:87
  39.6 16.6 %all-to-all-start.1 = ((bf16[16,2,16,384]{3,2,1,0:T(8,128)(2,1)}), bf16[16,2,16,384]{3,2,1,0:T(8,128)(2,1)S(1)}, u32[]{:S(2)}, u32[]{:S(2)}) async-start(bf16[16,2,16,384]{3,2,1,0:T(8,128)(2,1)} %get-tuple-element.24), calls=%async_computation.1 | async-start | bytes 786432 | tf_op jit(solution)/shard_map/all_to_all | solution.py:330
  46.4 6.7 %collective-permute-start.28 = (bf16[5,16,384]{2,1,0:T(8,128)(2,1)S(1)}, bf16[5,16,384]{2,1,0:T(8,128)(2,1)S(1)}, u32[]{:S(2)}, u32[]{:S(2)}) collective-permute-start(bf16[5,16,384]{2,1,0:T(8,128)(2,1)S(1)} %slice.226), channel_id=1, source_target_pairs={{0,8},{2,10},{8,16},{10,18},{16,24},{18,26},{24,28},{26,30},{28,20... | collective-permute-start | bytes 184328 | tf_op jit(solution)/shard_map/ppermute | solution.py:83
  48.7 5.2 %collective-permute-start.29 = (bf16[5,16,384]{2,1,0:T(8,128)(2,1)S(1)}, bf16[5,16,384]{2,1,0:T(8,128)(2,1)S(1)}, u32[]{:S(2)}, u32[]{:S(2)}) collective-permute-start(bf16[5,16,384]{2,1,0:T(8,128)(2,1)S(1)} %slice.227), channel_id=1, source_target_pairs={{0,4},{2,6},{8,0},{10,2},{16,8},{18,10},{24,16},{26,18},{28,24},{3... | collective-permute-start | bytes 184328 | tf_op jit(solution)/shard_map/ppermute | solution.py:84
  48.8 10.1 %collective-permute-start.9 = (bf16[16,2,16,384]{3,2,1,0:T(8,128)(2,1)S(1)}, bf16[16,2,16,384]{3,2,1,0:T(8,128)(2,1)}, u32[]{:S(2)}, u32[]{:S(2)}) collective-permute-start(bf16[16,2,16,384]{3,2,1,0:T(8,128)(2,1)S(1)} %all-to-all-done.maps_a), channel_id=1, source_target_pairs={{0,1},{1,0},{2,3},{3,2},{4,5},{5,4},{6,7},{7,6},{8,9},{9,8},{10,11... | collective-permute-start | bytes 1179656 | tf_op jit(solution)/shard_map/ppermute | solution.py:331
  54.5 29.0 %collective-permute-start.30 = (bf16[8,10,16,384]{3,2,1,0:T(8,128)(2,1)}, bf16[8,10,16,384]{3,2,1,0:T(8,128)(2,1)}, u32[]{:S(2)}, u32[]{:S(2)}) collective-permute-start(bf16[8,10,16,384]{3,2,1,0:T(8,128)(2,1)} %fusion.17.mine), channel_id=1, source_target_pairs={{0,2},{2,0},{4,6},{6,4},{8,10},{10,8},{12,14},{14,12},{16,18},{18,... | collective-permute-start | bytes 2949128 | tf_op jit(solution)/shard_map/ppermute | solution.py:87
  56.3 23.7 %copy-start.2 = (bf16[16,2,16,384]{3,2,1,0:T(8,128)(2,1)}, bf16[16,2,16,384]{3,2,1,0:T(8,128)(2,1)S(1)}, u32[]{:S(2)}) copy-start(bf16[16,2,16,384]{3,2,1,0:T(8,128)(2,1)S(1)} %all-to-all-done.1.maps_a) | copy-start | bytes 1179652
  56.3 27.2 %collective-permute-start.31 = (bf16[16,2,16,384]{3,2,1,0:T(8,128)(2,1)S(1)}, bf16[16,2,16,384]{3,2,1,0:T(8,128)(2,1)S(1)}, u32[]{:S(2)}, u32[]{:S(2)}) collective-permute-start(bf16[16,2,16,384]{3,2,1,0:T(8,128)(2,1)S(1)} %all-to-all-done.1.maps_a), channel_id=1, source_target_pairs={{0,1},{1,0},{2,3},{3,2},{4,5},{5,4},{6,7},{7,6},{8,9},{9,8},{10,11... | collective-permute-start | bytes 1179656 | tf_op jit(solution)/shard_map/ppermute | solution.py:331
  58.9 1.5 copy-start.7
  79.9 3.6 %copy-start.1 = (bf16[2,8,10,16,384]{4,3,2,1,0:T(8,128)(2,1)}, bf16[2,8,10,16,384]{4,3,2,1,0:T(8,128)(2,1)S(1)}, u32[]{:S(2)}) copy-start(bf16[2,8,10,16,384]{4,3,2,1,0:T(8,128)(2,1)S(1)} %gradient.2) | copy-start | bytes 5898244
  79.9 3.6 %copy-start.10 = (bf16[768,768]{1,0:T(8,128)(2,1)S(1)}, bf16[768,768]{1,0:T(8,128)(2,1)}, u32[]{:S(2)}) copy-start(bf16[768,768]{1,0:T(8,128)(2,1)} %constant.102.clone.ty_f.ty_i) | copy-start | bytes 3538948
  80.0 3.6 %copy-start.12 = (bf16[512,512]{1,0:T(8,128)(2,1)S(1)}, bf16[512,512]{1,0:T(8,128)(2,1)}, u32[]{:S(2)}) copy-start(bf16[512,512]{1,0:T(8,128)(2,1)} %constant.103.clone.tz_f.tz_i) | copy-start | bytes 1572868
  81.0 27.6 %collective-permute-start.10 = (bf16[8,10,16,384]{3,2,1,0:T(8,128)(2,1)}, bf16[8,10,16,384]{3,2,1,0:T(8,128)(2,1)}, u32[]{:S(2)}, u32[]{:S(2)}) collective-permute-start(bf16[8,10,16,384]{3,2,1,0:T(8,128)(2,1)} %slice_bitcast_fusion.2), channel_id=1, source_target_pairs={{0,2},{2,0},{4,6},{6,4},{8,10},{10,8},{12,14},{14,12},{16,18},{18,... | collective-permute-start | bytes 2949128 | tf_op jit(solution)/shard_map/ppermute | solution.py:95
  101.6 2.5 %copy-start.18 = (bf16[10,64,3,3,3]{1,4,3,2,0:T(4,128)(2,1)S(1)}, bf16[10,64,3,3,3]{1,4,3,2,0:T(4,128)(2,1)}, u32[]{:S(2)}) copy-start(bf16[10,64,3,3,3]{1,4,3,2,0:T(4,128)(2,1)} %param.19) | copy-start | bytes 103684
  101.6 6.2 %copy-start.20 = (f32[64]{0:T(128)S(1)}, f32[64]{0:T(128)}, u32[]{:S(2)}) copy-start(f32[64]{0:T(128)} %param.18) | copy-start | bytes 772
  102.7 9.5 %collective-permute-start.32 = (bf16[8,10,16,384]{3,2,1,0:T(8,128)(2,1)}, bf16[8,10,16,384]{3,2,1,0:T(8,128)(2,1)}, u32[]{:S(2)}, u32[]{:S(2)}) collective-permute-start(bf16[8,10,16,384]{3,2,1,0:T(8,128)(2,1)} %slice_bitcast_fusion), channel_id=1, source_target_pairs={{0,2},{2,0},{4,6},{6,4},{8,10},{10,8},{12,14},{14,12},{16,18},{18,... | collective-permute-start | bytes 2949128 | tf_op jit(solution)/shard_map/ppermute | solution.py:95
  110.4 4.8 %collective-permute-start.11 = (bf16[5,16,384]{2,1,0:T(8,128)(2,1)S(1)}, bf16[5,16,384]{2,1,0:T(8,128)(2,1)S(1)}, u32[]{:S(2)}, u32[]{:S(2)}) collective-permute-start(bf16[5,16,384]{2,1,0:T(8,128)(2,1)S(1)} %get-tuple-element.11), channel_id=1, source_target_pairs={{0,8},{2,10},{8,16},{10,18},{16,24},{18,26},{24,28},{26,30},{28,20... | collective-permute-start | bytes 184328 | tf_op jit(solution)/shard_map/ppermute | solution.py:99
  110.9 4.3 %collective-permute-start.15 = (bf16[5,16,384]{2,1,0:T(8,128)(2,1)S(1)}, bf16[5,16,384]{2,1,0:T(8,128)(2,1)S(1)}, u32[]{:S(2)}, u32[]{:S(2)}) collective-permute-start(bf16[5,16,384]{2,1,0:T(8,128)(2,1)S(1)} %get-tuple-element.12), channel_id=1, source_target_pairs={{0,4},{2,6},{8,0},{10,2},{16,8},{18,10},{24,16},{26,18},{28,24},{3... | collective-permute-start | bytes 184328 | tf_op jit(solution)/shard_map/ppermute | solution.py:100
  113.6 3.4 %collective-permute-start.33 = (bf16[5,16,384]{2,1,0:T(8,128)(2,1)S(1)}, bf16[5,16,384]{2,1,0:T(8,128)(2,1)S(1)}, u32[]{:S(2)}, u32[]{:S(2)}) collective-permute-start(bf16[5,16,384]{2,1,0:T(8,128)(2,1)S(1)} %get-tuple-element.19), channel_id=1, source_target_pairs={{0,8},{2,10},{8,16},{10,18},{16,24},{18,26},{24,28},{26,30},{28,20... | collective-permute-start | bytes 184328 | tf_op jit(solution)/shard_map/ppermute | solution.py:99
  113.9 3.9 %collective-permute-start.37 = (bf16[5,16,384]{2,1,0:T(8,128)(2,1)S(1)}, bf16[5,16,384]{2,1,0:T(8,128)(2,1)S(1)}, u32[]{:S(2)}, u32[]{:S(2)}) collective-permute-start(bf16[5,16,384]{2,1,0:T(8,128)(2,1)S(1)} %get-tuple-element.20), channel_id=1, source_target_pairs={{0,4},{2,6},{8,0},{10,2},{16,8},{18,10},{24,16},{26,18},{28,24},{3... | collective-permute-start | bytes 184328 | tf_op jit(solution)/shard_map/ppermute | solution.py:100
  115.2 8.9 %collective-permute-start.16 = (bf16[10,16,384]{2,1,0:T(8,128)(2,1)S(1)}, bf16[10,16,384]{2,1,0:T(8,128)(2,1)S(1)}, u32[]{:S(2)}, u32[]{:S(2)}) collective-permute-start(bf16[10,16,384]{2,1,0:T(8,128)(2,1)S(1)} %pad_maximum_fusion.4), channel_id=1, source_target_pairs={{0,4},{2,6},{8,0},{10,2},{16,8},{18,10},{24,16},{26,18},{28,24},{3... | collective-permute-start | bytes 368648 | tf_op jit(solution)/shard_map/ppermute | solution.py:109
  116.7 18.9 %copy-start.16 = (bf16[1,5,2,1,16,384]{5,4,3,2,1,0:T(8,128)(2,1)S(1)}, bf16[1,5,2,1,16,384]{5,4,3,2,1,0:T(8,128)(2,1)}, u32[]{:S(2)}) copy-start(bf16[1,5,2,1,16,384]{5,4,3,2,1,0:T(8,128)(2,1)} %copy-done.15) | copy-start | bytes 368644
  116.7 4.1 %collective-permute-start.12 = (bf16[10,16,384]{2,1,0:T(8,128)(2,1)S(1)}, bf16[10,16,384]{2,1,0:T(8,128)(2,1)S(1)}, u32[]{:S(2)}, u32[]{:S(2)}) collective-permute-start(bf16[10,16,384]{2,1,0:T(8,128)(2,1)S(1)} %pad_maximum_fusion.3), channel_id=1, source_target_pairs={{0,8},{2,10},{8,16},{10,18},{16,24},{18,26},{24,28},{26,30},{28,20... | collective-permute-start | bytes 368648 | tf_op jit(solution)/shard_map/ppermute | solution.py:108
  117.9 27.9 %copy-start.14 = (bf16[1,5,2,1,16,384]{5,4,3,2,1,0:T(8,128)(2,1)S(1)}, bf16[1,5,2,1,16,384]{5,4,3,2,1,0:T(8,128)(2,1)}, u32[]{:S(2)}) copy-start(bf16[1,5,2,1,16,384]{5,4,3,2,1,0:T(8,128)(2,1)} %copy-done.13) | copy-start | bytes 368644
  117.9 10.0 %collective-permute-start.38 = (bf16[10,16,384]{2,1,0:T(8,128)(2,1)S(1)}, bf16[10,16,384]{2,1,0:T(8,128)(2,1)S(1)}, u32[]{:S(2)}, u32[]{:S(2)}) collective-permute-start(bf16[10,16,384]{2,1,0:T(8,128)(2,1)S(1)} %pad_maximum_fusion.6), channel_id=1, source_target_pairs={{0,4},{2,6},{8,0},{10,2},{16,8},{18,10},{24,16},{26,18},{28,24},{3... | collective-permute-start | bytes 368648 | tf_op jit(solution)/shard_map/ppermute | solution.py:109
  118.4 5.6 %collective-permute-start.34 = (bf16[10,16,384]{2,1,0:T(8,128)(2,1)S(1)}, bf16[10,16,384]{2,1,0:T(8,128)(2,1)S(1)}, u32[]{:S(2)}, u32[]{:S(2)}) collective-permute-start(bf16[10,16,384]{2,1,0:T(8,128)(2,1)S(1)} %pad_maximum_fusion.5), channel_id=1, source_target_pairs={{0,8},{2,10},{8,16},{10,18},{16,24},{18,26},{24,28},{26,30},{28,20... | collective-permute-start | bytes 368648 | tf_op jit(solution)/shard_map/ppermute | solution.py:108
  120.8 5.5 %collective-permute-start.13 = (bf16[10,16,384]{2,1,0:T(8,128)(2,1)S(1)}, bf16[10,16,384]{2,1,0:T(8,128)(2,1)S(1)}, u32[]{:S(2)}, u32[]{:S(2)}) collective-permute-start(bf16[10,16,384]{2,1,0:T(8,128)(2,1)S(1)} %fusion.11), channel_id=1, source_target_pairs={{0,8},{2,10},{8,16},{10,18},{16,24},{18,26},{24,28},{26,30},{28,20... | collective-permute-start | bytes 368648 | tf_op jit(solution)/shard_map/ppermute | solution.py:108
  124.0 33.8 %copy-start.4 = (bf16[128,192]{1,0:T(8,128)(2,1)S(1)}, bf16[128,192]{1,0:T(8,128)(2,1)}, u32[]{:S(2)}) copy-start(bf16[128,192]{1,0:T(8,128)(2,1)} %copy.23.w_first) | copy-start | bytes 147460
  124.0 33.8 %copy-start.5 = (f32[128,1]{1,0:T(8,128)S(1)}, f32[128,1]{1,0:T(8,128)}, u32[]{:S(2)}) copy-start(f32[128,1]{1,0:T(8,128)} %copy.24.b_first) | copy-start | bytes 1540
  124.0 33.8 %copy-start.6 = (bf16[3,3,16,128]{3,2,1,0:T(8,128)(2,1)S(1)}, bf16[3,3,16,128]{3,2,1,0:T(8,128)(2,1)}, u32[]{:S(2)}) copy-start(bf16[3,3,16,128]{3,2,1,0:T(8,128)(2,1)} %pad.9.clone) | copy-start | bytes 110596
  124.0 33.8 %copy-start.8 = (f32[10]{0:T(128)S(1)}, f32[10]{0:T(128)}, u32[]{:S(2)}) copy-start(f32[10]{0:T(128)} %b_second.3) | copy-start | bytes 124
  124.1 4.6 %collective-permute-start.35 = (bf16[10,16,384]{2,1,0:T(8,128)(2,1)S(1)}, bf16[10,16,384]{2,1,0:T(8,128)(2,1)S(1)}, u32[]{:S(2)}, u32[]{:S(2)}) collective-permute-start(bf16[10,16,384]{2,1,0:T(8,128)(2,1)S(1)} %fusion.4), channel_id=1, source_target_pairs={{0,8},{2,10},{8,16},{10,18},{16,24},{18,26},{24,28},{26,30},{28,20... | collective-permute-start | bytes 368648 | tf_op jit(solution)/shard_map/ppermute | solution.py:108
  126.4 4.1 %collective-permute-start.17 = (bf16[10,16,384]{2,1,0:T(8,128)(2,1)S(1)}, bf16[10,16,384]{2,1,0:T(8,128)(2,1)S(1)}, u32[]{:S(2)}, u32[]{:S(2)}) collective-permute-start(bf16[10,16,384]{2,1,0:T(8,128)(2,1)S(1)} %get-tuple-element.8), channel_id=1, source_target_pairs={{0,4},{2,6},{8,0},{10,2},{16,8},{18,10},{24,16},{26,18},{28,24},{3... | collective-permute-start | bytes 368648 | tf_op jit(solution)/shard_map/ppermute | solution.py:109
  126.5 8.1 %collective-permute-start.14 = (bf16[10,16,384]{2,1,0:T(8,128)(2,1)S(1)}, bf16[10,16,384]{2,1,0:T(8,128)(2,1)S(1)}, u32[]{:S(2)}, u32[]{:S(2)}) collective-permute-start(bf16[10,16,384]{2,1,0:T(8,128)(2,1)S(1)} %get-tuple-element.7), channel_id=1, source_target_pairs={{0,8},{2,10},{8,16},{10,18},{16,24},{18,26},{24,28},{26,30},{28,20... | collective-permute-start | bytes 368648 | tf_op jit(solution)/shard_map/ppermute | solution.py:108
  128.8 4.0 %collective-permute-start.39 = (bf16[10,16,384]{2,1,0:T(8,128)(2,1)S(1)}, bf16[10,16,384]{2,1,0:T(8,128)(2,1)S(1)}, u32[]{:S(2)}, u32[]{:S(2)}) collective-permute-start(bf16[10,16,384]{2,1,0:T(8,128)(2,1)S(1)} %get-tuple-element.16), channel_id=1, source_target_pairs={{0,4},{2,6},{8,0},{10,2},{16,8},{18,10},{24,16},{26,18},{28,24},{3... | collective-permute-start | bytes 368648 | tf_op jit(solution)/shard_map/ppermute | solution.py:109
  130.2 15.6 %collective-permute-start.36 = (bf16[10,16,384]{2,1,0:T(8,128)(2,1)S(1)}, bf16[10,16,384]{2,1,0:T(8,128)(2,1)S(1)}, u32[]{:S(2)}, u32[]{:S(2)}) collective-permute-start(bf16[10,16,384]{2,1,0:T(8,128)(2,1)S(1)} %get-tuple-element.15), channel_id=1, source_target_pairs={{0,8},{2,10},{8,16},{10,18},{16,24},{18,26},{24,28},{26,30},{28,20... | collective-permute-start | bytes 368648 | tf_op jit(solution)/shard_map/ppermute | solution.py:108
  130.5 5.1 %collective-permute-start.18 = (bf16[10,16,384]{2,1,0:T(8,128)(2,1)S(1)}, bf16[10,16,384]{2,1,0:T(8,128)(2,1)S(1)}, u32[]{:S(2)}, u32[]{:S(2)}) collective-permute-start(bf16[10,16,384]{2,1,0:T(8,128)(2,1)S(1)} %fusion.10), channel_id=1, source_target_pairs={{0,4},{2,6},{8,0},{10,2},{16,8},{18,10},{24,16},{26,18},{28,24},{3... | collective-permute-start | bytes 368648 | tf_op jit(solution)/shard_map/ppermute | solution.py:109
  132.8 13.0 %collective-permute-start.40 = (bf16[10,16,384]{2,1,0:T(8,128)(2,1)S(1)}, bf16[10,16,384]{2,1,0:T(8,128)(2,1)S(1)}, u32[]{:S(2)}, u32[]{:S(2)}) collective-permute-start(bf16[10,16,384]{2,1,0:T(8,128)(2,1)S(1)} %fusion.3), channel_id=1, source_target_pairs={{0,4},{2,6},{8,0},{10,2},{16,8},{18,10},{24,16},{26,18},{28,24},{3... | collective-permute-start | bytes 368648 | tf_op jit(solution)/shard_map/ppermute | solution.py:109
  135.7 15.7 %collective-permute-start.19 = (bf16[10,2,384]{2,1,0:T(2,128)(2,1)S(1)}, bf16[10,2,384]{2,1,0:T(2,128)(2,1)S(1)}, u32[]{:S(2)}, u32[]{:S(2)}) collective-permute-start(bf16[10,2,384]{2,1,0:T(2,128)(2,1)S(1)} %get-tuple-element.27), channel_id=1, source_target_pairs={{0,2},{2,4},{4,6},{6,8},{8,10},{10,12},{12,14},{14,16},{16,18},{18... | collective-permute-start | bytes 46088 | tf_op jit(solution)/shard_map/ppermute | solution.py:341
  143.8 7.7 %collective-permute-start.20 = (bf16[10,2,384]{2,1,0:T(2,128)(2,1)S(1)}, bf16[10,2,384]{2,1,0:T(2,128)(2,1)S(1)}, u32[]{:S(2)}, u32[]{:S(2)}) collective-permute-start(bf16[10,2,384]{2,1,0:T(2,128)(2,1)S(1)} %get-tuple-element.28), channel_id=1, source_target_pairs={{2,0},{4,2},{6,4},{8,6},{10,8},{12,10},{14,12},{16,14},{18,16},{20... | collective-permute-start | bytes 46088 | tf_op jit(solution)/shard_map/ppermute | solution.py:343
  145.9 7.0 %collective-permute-start.41 = (bf16[10,2,384]{2,1,0:T(2,128)(2,1)S(1)}, bf16[10,2,384]{2,1,0:T(2,128)(2,1)S(1)}, u32[]{:S(2)}, u32[]{:S(2)}) collective-permute-start(bf16[10,2,384]{2,1,0:T(2,128)(2,1)S(1)} %get-tuple-element.29), channel_id=1, source_target_pairs={{0,2},{2,4},{4,6},{6,8},{8,10},{10,12},{12,14},{14,16},{16,18},{18... | collective-permute-start | bytes 46088 | tf_op jit(solution)/shard_map/ppermute | solution.py:341
  149.5 5.3 %collective-permute-start.42 = (bf16[10,2,384]{2,1,0:T(2,128)(2,1)S(1)}, bf16[10,2,384]{2,1,0:T(2,128)(2,1)S(1)}, u32[]{:S(2)}, u32[]{:S(2)}) collective-permute-start(bf16[10,2,384]{2,1,0:T(2,128)(2,1)S(1)} %get-tuple-element.30), channel_id=1, source_target_pairs={{2,0},{4,2},{6,4},{8,6},{10,8},{12,10},{14,12},{16,14},{18,16},{20... | collective-permute-start | bytes 46088 | tf_op jit(solution)/shard_map/ppermute | solution.py:343
  151.6 6.2 %collective-permute-start.21 = (bf16[10,20,384]{2,1,0:T(8,128)(2,1)S(1)}, bf16[10,20,384]{2,1,0:T(8,128)(2,1)S(1)}, u32[]{:S(2)}, u32[]{:S(2)}) collective-permute-start(bf16[10,20,384]{2,1,0:T(8,128)(2,1)S(1)} %pad_maximum_fusion.1.own), channel_id=1, source_target_pairs={{0,1},{1,0},{2,3},{3,2},{4,5},{5,4},{6,7},{7,6},{8,9},{9,8},{10,11... | collective-permute-start | bytes 460808 | tf_op jit(solution)/shard_map/ppermute | solution.py:347
  155.0 8.8 %collective-permute-start.43 = (bf16[10,20,384]{2,1,0:T(8,128)(2,1)S(1)}, bf16[10,20,384]{2,1,0:T(8,128)(2,1)S(1)}, u32[]{:S(2)}, u32[]{:S(2)}) collective-permute-start(bf16[10,20,384]{2,1,0:T(8,128)(2,1)S(1)} %pad_maximum_fusion.2.own), channel_id=1, source_target_pairs={{0,1},{1,0},{2,3},{3,2},{4,5},{5,4},{6,7},{7,6},{8,9},{9,8},{10,11... | collective-permute-start | bytes 460808 | tf_op jit(solution)/shard_map/ppermute | solution.py:347
  (3 other events, 3.3 us)
where the time goes:
time: 174 us; the launch traced here: 170 us
  starting transfers between devices  71.1 us (41%)
  Pallas kernels  46.1 us (26%)
  local copies, waits for them, and re-layouts  26.7 us (15%)
  waiting for transfers between devices  20.1 us (12%)
  other arithmetic  5.86 us (3%)
    pallas_call x2, Pallas kernels, gradient(): pl.pallas_call(gradient_kernel, grid_spec=pltpu.PrefetchScalarGridSpec(nu...  34.2 us
    unnamed x58, local copies, waits for them, and re-layouts  18.3 us
    all_to_all x2, starting transfers between devices, paired(): lax.all_to_all(pairs[:, :, x], SLAB, split_axis=0, concat_axis=0, tiled=T...  13 us
    pallas_call x2, Pallas kernels, convolutions(): pl.pallas_call(convolution_kernel, in_specs=[smem, vmem, vmem, vmem, vmem...  11.9 us
    ppermute x2, starting transfers between devices, paired(): lax.ppermute(updated[:, rows - 2:], SLAB, up)  11.7 us
    ppermute x6, starting transfers between devices, ring_gather(): up = lax.ppermute(up, SLAB, ring.perm(1))  11.7 us
    ppermute x6, waiting for transfers between devices, ring_scatter(): up = lax.ppermute(above, SLAB, ring.perm(1))  7.03 us
    ppermute x6, starting transfers between devices, ring_scatter(): down = lax.ppermute(below, SLAB, ring.perm(-1))  6.34 us
  transfers between devices with their start and end apart: 46, of which 15 were waited for; matrix products, arithmetic and copies ran while one was open for 15% of the time, Pallas kernels for 24%

commit v1 on v0

--- a/solution.py
+++ b/solution.py
@@ -1,3 +1,4 @@
+import functools
 import math
 
 import jax
@@ -27,14 +28,24 @@
     return np.stack([upper, lower], axis=0).astype(ml_dtypes.bfloat16)
 
 
-def as_right(table):
-    length = table.shape[1]
-    return jnp.asarray(table.reshape(2 * length, 2 * length))
-
-
-def as_left(table):
-    length = table.shape[1]
-    return jnp.asarray(table.transpose(2, 3, 0, 1).reshape(2 * length, 2 * length))
+def split_tables(length, count, left, inverse):
+    table = dft_table(length, inverse)
+    part = length // count
+    out = []
+    for s in range(count):
+        if inverse:
+            piece = table[:, :part, :, s::count]
+        else:
+            piece = table[:, s::count, :, :part]
+        if left:
+            piece = piece.transpose(2, 3, 0, 1)
+        out.append(piece.reshape(2 * part, 2 * part))
+    return jnp.asarray(np.stack(out))
+
+
+def order(length, count):
+    taken = np.arange(length).reshape(-1, count).T.reshape(-1)
+    return np.eye(length, dtype=np.float32)[:, taken]
 
 
 class Ring:
@@ -45,21 +56,18 @@
         column = self.chips // 2
         self.order = [2 * i for i in range(column)] + [2 * i + 1 for i in reversed(range(column))]
 
-    def perm(self, step):
-        return [
-            (2 * self.order[i] + core, 2 * self.order[(i + step) % self.chips] + core)
-            for i in range(self.chips)
-            for core in range(2)
-        ]
+    def perm(self):
+        pairs = []
+        for i in range(self.chips):
+            for core, step in ((0, 1), (1, -1)):
+                pairs.append((2 * self.order[i] + core, 2 * self.order[(i + step) % self.chips] + core))
+        return pairs
 
     def siblings(self):
         return [(i, i ^ 1) for i in range(self.devices)]
 
-    def offsets(self):
-        out = [0]
-        for step in range(1, self.half):
-            out += [-step, step]
-        return out + [self.half]
+    def steps(self):
+        return [(step, True) for step in range(1, self.half)] + [(self.half, False)]
 
     def slabs(self):
         me = lax.axis_index(SLAB)
@@ -67,47 +75,68 @@
         column = self.chips // 2
         row = chip // 2
         place = jnp.where(chip % 2 == 0, row, self.chips - 1 - row)
-        at = (place + jnp.array(self.offsets(), jnp.int32) + self.chips) % self.chips
-        held = jnp.where(at < column, 2 * at, 2 * (self.chips - 1 - at) + 1)
-        return jnp.concatenate([2 * held + core, 2 * held + 1 - core]).astype(jnp.int32)
-
-
-def ring_gather(ring, own):
-    up = down = own
-    pieces = [own]
-    for _ in range(1, ring.half):
-        up = lax.ppermute(up, SLAB, ring.perm(1))
-        down = lax.ppermute(down, SLAB, ring.perm(-1))
-        pieces += [up, down]
-    cut = own.shape[0] // 2
-    up = lax.ppermute(up[:cut], SLAB, ring.perm(1))
-    down = lax.ppermute(down[cut:], SLAB, ring.perm(-1))
-    pieces.append(jnp.concatenate([up, down], axis=0))
-    mine = jnp.stack(pieces)
-    return mine, lax.ppermute(mine, SLAB, ring.siblings())
-
-
-def plus(a, b):
-    return (a.astype(F32) + b.astype(F32)).astype(BF16)
-
-
-def ring_scatter(ring, sums):
-    part = plus(sums[0], lax.ppermute(sums[1], SLAB, ring.siblings()))
-    index = {offset: i for i, offset in enumerate(ring.offsets())}
-    cut = part.shape[1] // 2
-    far = part[index[ring.half]]
-    up = lax.ppermute(far[:cut], SLAB, ring.perm(1))
-    down = lax.ppermute(far[cut:], SLAB, ring.perm(-1))
-    for step in range(ring.half - 1, 0, -1):
-        above, below = part[index[step]], part[index[-step]]
-        if step == ring.half - 1:
-            above = jnp.concatenate([plus(above[:cut], up), above[cut:]], axis=0)
-            below = jnp.concatenate([below[:cut], plus(below[cut:], down)], axis=0)
-        else:
-            above, below = plus(above, up), plus(below, down)
-        up = lax.ppermute(above, SLAB, ring.perm(1))
-        down = lax.ppermute(below, SLAB, ring.perm(-1))
-    return part[0].astype(F32) + up.astype(F32) + down.astype(F32)
+
+        def slab(offset, parity):
+            at = (place + offset + self.chips) % self.chips
+            return 2 * jnp.where(at < column, 2 * at, 2 * (self.chips - 1 - at) + 1) + parity
+
+        def handled(by, sign):
+            way = sign * (1 - 2 * by)
+            out = []
+            for step, both in self.steps():
+                out += [slab(way * step, by)] + ([slab(way * step, 1 - by)] if both else [])
+            return out
+
+        own = [slab(0, core), slab(0, 1 - core)]
+        gathered = own + handled(core, -1) + handled(1 - core, -1)
+        summed = own + handled(core, 1) + handled(1 - core, 1)
+        return jnp.stack(gathered + summed).astype(jnp.int32)
+
+
+def after(value, *earlier):
+    return lax.optimization_barrier((value,) + earlier)[0]
+
+
+class Gather:
+    def __init__(self, ring, mine):
+        self.ring = ring
+        self.held = self.own = jnp.concatenate([mine, lax.ppermute(mine, SLAB, ring.siblings())], axis=0)
+        self.kept, self.other = [], []
+
+    def step(self, *earlier):
+        both = self.ring.steps()[len(self.kept)][1]
+        held = self.held if both else self.held[:1]
+        self.held = lax.ppermute(after(held, *earlier) if earlier else held, SLAB, self.ring.perm())
+        self.kept.append(self.held)
+        self.other.append(lax.ppermute(self.held, SLAB, self.ring.siblings()))
+
+    def pieces(self):
+        return [self.own] + self.kept + self.other
+
+
+class Scatter:
+    def __init__(self, ring, own, kept, sent):
+        self.ring, self.own, self.kept = ring, own, kept
+        self.other = lax.ppermute(sent, SLAB, ring.siblings())
+        self.held = None
+        self.left = list(ring.steps())
+        self.end = kept.shape[0]
+
+    def step(self):
+        count = 2 if self.left.pop()[1] else 1
+        self.end -= count
+        total = self.kept[self.end : self.end + count].astype(F32) + self.other[self.end : self.end + count].astype(F32)
+        if self.held is not None:
+            got = self.held.astype(F32)
+            if got.shape[0] < count:
+                total = jnp.concatenate([total[:1] + got, total[1:]], axis=0)
+            else:
+                total = total + got
+        self.held = lax.ppermute(total.astype(BF16), SLAB, self.ring.perm())
+        return self.held
+
+    def chip(self):
+        return self.own.astype(F32) + self.held.astype(F32)
 
 
 def nt_dot(a, b):
@@ -118,93 +147,193 @@
     return lax.dot_general(a, b, (((1,), (0,)), ((), ())), preferred_element_type=F32)
 
 
-def gradient_kernel(
-    slabs, mine, other, maps_a, maps_b, measured, sampling, ty_f, tz_f, tz_i, ty_i, out, products, backs
-):
-    pieces, _, rows, ny = mine.shape
-    nz = 2 * pieces * rows
-    first = slabs[2 * pieces]
-    maps = (maps_a, maps_b)
-    for k in range(2 * pieces):
-        held = mine if k < pieces else other
+def gradient_kernel(images, coils, slabs, *refs):
+    held_images, refs = refs[:images], refs[images:]
+    maps, refs = refs[:coils], refs[coils:]
+    measured, sampling, ty_f, tz_f, tz_i, ty_i = refs[:6]
+    out, products, backs = refs[-5:-2], refs[-2], refs[-1]
+    rows, ny = held_images[0].shape[-2:]
+    nz = sampling.shape[-1]
+    count, half = nz // rows, rows // 2
+    my, mz = ny // 3, nz // 2
+    first = slabs[2 * count]
+    root = math.sqrt(0.75)
+
+    def pieces(arrays):
+        return [(array, i) for array in arrays for i in range(array.shape[0])]
+
+    def places(slab):
+        at = pl.multiple_of(slab * half, half)
+        return pl.ds(at, half), pl.ds(pl.multiple_of(at + mz, half), half)
+
+    def thirds(b0, b1, b2, sign):
+        add = [u + v for u, v in zip(b1, b2)]
+        low = [u - 0.5 * v for u, v in zip(b0, add)]
+        turn = [(sign * root) * (u - v) for u, v in zip(b1, b2)]
+        return (
+            (b0[0] + add[0], b0[1] + add[1]),
+            (low[0] - turn[1], low[1] + turn[0]),
+            (low[0] + turn[1], low[1] - turn[0]),
+        )
+
+    for k, (held, i) in enumerate(pieces(held_images)):
         slab = slabs[k]
-        at = pl.ds(pl.multiple_of(slab * rows, rows), rows)
-        real = held[k % pieces, 0].astype(F32)
-        imag = held[k % pieces, 1].astype(F32)
-        for c in range(2):
+        real = held[i, 0, 0].astype(F32)
+        imag = held[i, 0, 1].astype(F32)
+        for c in range(coils):
             m_real = maps[c][slab, 0].astype(F32)
             m_imag = maps[c][slab, 1].astype(F32)
-            products[c, at, :ny] = (m_real * real - m_imag * imag).astype(BF16)
-            products[c, at, ny:] = (m_real * imag + m_imag * real).astype(BF16)
+            p_real = m_real * real - m_imag * imag
+            p_imag = m_real * imag + m_imag * real
+            for parity, at in enumerate(places(slab)):
+                lines = slice(parity * half, (parity + 1) * half)
+                for j in range(3):
+                    cells = slice(j * my, (j + 1) * my)
+                    products[c, j, at, :my] = p_real[lines, cells]
+                    products[c, j, at, my:] = p_imag[lines, cells]
     mask = sampling[0, 0].astype(F32)
-    lefts = []
-    for c in range(2):
-        spectra = nt_dot(ty_f[...], products[c]).astype(BF16)
-        lefts.append(jnp.concatenate([spectra[:ny], spectra[ny:]], axis=1))
-    spectrum = nn_dot(jnp.concatenate(lefts, axis=0), tz_f[...])
-    residuals = []
-    for c in range(2):
+    folds = [[], []]
+    for c in range(coils):
+        parts = [nt_dot(ty_f[j], products[c, j].astype(BF16)) for j in range(3)]
+        parts = thirds(*[(part[:my], part[my:]) for part in parts], -1.0)
+        spectra = [jnp.concatenate([part[q].astype(BF16) for part in parts], axis=0) for q in range(2)]
+        halves = []
+        for j in range(2):
+            cells = slice(j * mz, (j + 1) * mz)
+            halves.append(nn_dot(jnp.concatenate([spectra[0][:, cells], spectra[1][:, cells]], axis=1), tz_f[j]))
         coil = first if c == 0 else 1 - first
-        spec = spectrum[c * ny : (c + 1) * ny]
-        seen = measured[0, coil, 0, :, 0].astype(F32)
-        residuals.append(
-            jnp.concatenate(
-                [(mask * (spec[:, :nz] - seen[0])).astype(BF16), (mask * (spec[:, nz:] - seen[1])).astype(BF16)],
-                axis=1,
-            )
-        )
-    depth = nt_dot(tz_i[...], jnp.concatenate(residuals, axis=0)).astype(BF16)
-    for c in range(2):
-        cols = slice(c * ny, (c + 1) * ny)
-        line = jnp.concatenate([depth[:nz, cols], depth[nz:, cols]], axis=1)
-        backs[c] = nn_dot(line, ty_i[...])
-    for k in range(2 * pieces):
-        slab = slabs[k]
-        at = pl.ds(pl.multiple_of(slab * rows, rows), rows)
-        real, imag = 0.0, 0.0
-        for c in range(2):
-            m_real = maps[c][slab, 0].astype(F32)
-            m_imag = maps[c][slab, 1].astype(F32)
-            b_real, b_imag = backs[c, at, :ny], backs[c, at, ny:]
-            real += m_real * b_real + m_imag * b_imag
-            imag += m_real * b_imag - m_imag * b_real
-        out[k // pieces, k % pieces, 0] = real.astype(BF16)
-        out[k // pieces, k % pieces, 1] = imag.astype(BF16)
-
-
-def gradient(where, mine, other, maps_a, maps_b, measured, sampling, tables, x):
-    pieces, channels, rows, ny = mine.shape
-    encodings = channels // 2
-    nz = 2 * pieces * rows
-    coils = 2
+        sums, differences = [], []
+        for q in range(2):
+            cells = slice(q * mz, (q + 1) * mz)
+            seen = measured[0, coil, 0, q, 0].astype(F32)
+            low = mask[:, :mz] * (halves[0][:, cells] + halves[1][:, cells] - seen[:, :mz])
+            high = mask[:, mz:] * (halves[0][:, cells] - halves[1][:, cells] - seen[:, mz:])
+            sums.append((low + high).astype(BF16))
+            differences.append((low - high).astype(BF16))
+        folds[0].append(jnp.concatenate(sums, axis=1))
+        folds[1].append(jnp.concatenate(differences, axis=1))
+    depths = [nt_dot(tz_i[j], jnp.concatenate(folds[j], axis=0)) for j in range(2)]
+    for c in range(coils):
+        lines = [[], [], []]
+        for j in range(2):
+            cut = lambda q, i: depths[j][q * mz : (q + 1) * mz, c * ny + i * my : c * ny + (i + 1) * my]
+            turned = thirds(*[(cut(0, i), cut(1, i)) for i in range(3)], 1.0)
+            for i in range(3):
+                lines[i].append(jnp.concatenate([turned[i][0].astype(BF16), turned[i][1].astype(BF16)], axis=1))
+        for i in range(3):
+            backs[c, i] = nn_dot(jnp.concatenate(lines[i], axis=0), ty_i[i])
+    for k, (held, i) in enumerate(pieces(out)):
+        slab = slabs[count + k]
+        for j in range(3):
+            cells = slice(j * my, (j + 1) * my)
+            real, imag = 0.0, 0.0
+            for c in range(coils):
+                m_real = maps[c][slab, 0, :, cells].astype(F32)
+                m_imag = maps[c][slab, 1, :, cells].astype(F32)
+                back = jnp.concatenate([backs[c, j, at, :] for at in places(slab)], axis=0)
+                real += m_real * back[:, :my] + m_imag * back[:, my:]
+                imag += m_real * back[:, my:] - m_imag * back[:, :my]
+            held[i, 0, :, cells] = real.astype(BF16)
+            held[i, 1, :, cells] = imag.astype(BF16)
+
+
+def gradient(where, images, maps, measured, sampling, tables, x):
+    _, _, channels, rows, ny = images[0].shape
+    nz = sampling.shape[-1]
+    n = len(maps)
+    far = (nz // rows - 2) // 2
     whole = lambda a: pl.BlockSpec(a.shape, lambda e, s: (0,) * a.ndim, pipeline_mode=pl.Buffered(1))
-    held = pl.BlockSpec((pieces, 2, rows, ny), lambda e, s: (0, e, 0, 0))
-    flops = 2 * encodings * coils * 2 * 4 * (nz * ny * ny + nz * nz * ny)
+    flops = channels * n * 2 * 4 * (nz * ny * ny + nz * nz * ny)
     return pl.pallas_call(
-        gradient_kernel,
+        functools.partial(gradient_kernel, len(images), n),
         grid_spec=pltpu.PrefetchScalarGridSpec(
             num_scalar_prefetch=1,
-            grid=(encodings,),
-            in_specs=[
-                held,
-                held,
-                whole(maps_a),
-                whole(maps_b),
-                pl.BlockSpec((1, coils, 1, 2, 1, ny, nz), lambda e, s: (0, 0, e, 0, x, 0, 0)),
+            grid=(channels // 2,),
+            in_specs=[pl.BlockSpec((a.shape[0], 1, 2, rows, ny), lambda e, s: (0, x, e, 0, 0)) for a in images]
+            + [whole(a) for a in maps]
+            + [
+                pl.BlockSpec((1, 2, 1, 2, 1, ny, nz), lambda e, s: (0, 0, e, 0, x, 0, 0)),
                 pl.BlockSpec((1, 1, ny, nz), lambda e, s: (0, e, 0, 0)),
             ]
             + [whole(t) for t in tables],
-            out_specs=pl.BlockSpec((2, pieces, 2, rows, ny), lambda e, s: (0, 0, e, 0, 0)),
+            out_specs=[pl.BlockSpec((m, 2, rows, ny), lambda e, s: (0, e, 0, 0)) for m in (2, far, far)],
             scratch_shapes=[
-                pltpu.VMEM((coils, nz, 2 * ny), BF16),
-                pltpu.VMEM((coils, nz, 2 * ny), F32),
+                pltpu.VMEM((n, 3, nz, 2 * ny // 3), F32),
+                pltpu.VMEM((n, 3, nz, 2 * ny // 3), F32),
             ],
         ),
-        out_shape=jax.ShapeDtypeStruct((2, pieces, channels, rows, ny), BF16),
+        out_shape=[jax.ShapeDtypeStruct((m, channels, rows, ny), BF16) for m in (2, far, far)],
         compiler_params=pltpu.CompilerParams(vmem_limit_bytes=40 * 2**20),
         cost_estimate=pl.CostEstimate(flops=flops, bytes_accessed=8 * 2**20, transcendentals=0),
         name="gradient",
-    )(where, mine, other, maps_a, maps_b, measured, sampling, *tables)
+    )(where, *images, *maps, measured, sampling, *tables)
+
+
+def reordered(value, along_z, along_y):
+    n, rows, ny = value.shape
+    block = along_z.shape[0]
+    flat = value.reshape(n * rows, ny)
+    out = []
+    for start in range(0, n * rows, block):
+        size = min(block, n * rows - start)
+        part = nn_dot(along_z[:size, :size], flat[start : start + size]).astype(BF16)
+        out.append(nn_dot(part, along_y).astype(BF16))
+    return jnp.concatenate(out, axis=0).reshape(n, rows, ny)
+
+
+def orders(rows, ny, back):
+    z, y = order(rows, 2), order(ny, 3)
+    along_z = np.kron(np.eye(8, dtype=np.float32), z if back else z.T)
+    return jnp.asarray(along_z, BF16), jnp.asarray(y.T if back else y, BF16)
+
+
+def prepare_kernel(which, image, maps, along_z, along_y, image_out, maps_out):
+    width, channels, rows, ny = image_out.shape
+    pairs = maps_out.shape[0]
+    picked = image[...].reshape((channels, width, rows, ny))
+    for x in range(width):
+        image_out[x] = reordered(picked[:, x], along_z[...], along_y[...])
+    for pair in range(pairs):
+        value = maps[2 * pair + which[0]].reshape((2 * width, rows, ny))
+        value = reordered(value, along_z[...], along_y[...])
+        for x in range(width):
+            for part in range(2):
+                maps_out[pair, x, part] = value[part * width + x]
+
+
+def prepare(which, current_image, coil_maps):
+    _, encodings, _, width, rows, ny = current_image.shape
+    vmem = pl.BlockSpec(memory_space=pltpu.VMEM)
+    smem = pl.BlockSpec(memory_space=pltpu.SMEM)
+    return pl.pallas_call(
+        prepare_kernel,
+        in_specs=[smem, vmem, vmem, vmem, vmem],
+        out_specs=[vmem, vmem],
+        out_shape=[
+            jax.ShapeDtypeStruct((width, 2 * encodings, rows, ny), BF16),
+            jax.ShapeDtypeStruct((coil_maps.shape[0] // 2, width, 2, rows, ny), BF16),
+        ],
+        compiler_params=pltpu.CompilerParams(vmem_limit_bytes=24 * 2**20),
+        name="prepare",
+    )(which, current_image, coil_maps, *orders(rows, ny, False))
+
+
+def update_kernel(image, chip, received, along_z, along_y, out):
+    for x in range(image.shape[0]):
+        value = image[x].astype(F32) - (chip[x] + received[x].astype(F32))
+        out[x] = reordered(value.astype(BF16), along_z[...], along_y[...])
+
+
+def update(image, chip, received):
+    vmem = pl.BlockSpec(memory_space=pltpu.VMEM)
+    return pl.pallas_call(
+        update_kernel,
+        in_specs=[vmem] * 5,
+        out_specs=vmem,
+        out_shape=jax.ShapeDtypeStruct(image.shape, BF16),
+        compiler_params=pltpu.CompilerParams(vmem_limit_bytes=16 * 2**20),
+        name="update",
+    )(image, chip, received, *orders(*image.shape[-2:], True))
 
 
 def shifted(value, step):
@@ -314,36 +443,38 @@
     _, encodings, _, width, rows, ny = current_image.shape
     nz = rows * devices
     channels = 2 * encodings
-    y_forward, y_inverse = dft_table(ny, False), dft_table(ny, True)
-    z_forward, z_inverse = dft_table(nz, False), dft_table(nz, True)
-    tables = (as_left(y_forward), as_right(z_forward), as_left(z_inverse), as_right(y_inverse))
+    tables = (
+        split_tables(ny, 3, True, False),
+        split_tables(nz, 2, False, False),
+        split_tables(nz, 2, True, True),
+        split_tables(ny, 3, False, True),
+    )
     where = jnp.concatenate([ring.slabs(), q[None].astype(jnp.int32)])
     swap = [(0, 1), (1, 0)]
-    pairs = coil_maps.reshape((devices, 2) + coil_maps.shape[1:])
-    pairs = lax.dynamic_index_in_dim(pairs, q, axis=1, keepdims=False)
     weights = convolution_weights(first_weight, first_bias, second_weight)
     ends = jnp.stack([me > 0, me < devices - 1]).astype(jnp.int32)
 
-    images = [current_image[0, :, :, x].reshape(channels, rows, ny) for x in range(width)]
-    maps, gathered = [], []
+    images, pairs = prepare(q[None].astype(jnp.int32), current_image, coil_maps)
+    gather = Gather(ring, images[None])
+    kept = lax.all_to_all(pairs, SLAB, split_axis=0, concat_axis=0, tiled=True)
+    for step in range(len(ring.steps())):
+        gather.step(*((kept,) if step == 2 else ()))
+    scatters = []
     for x in range(width):
-        kept = lax.all_to_all(pairs[:, :, x], SLAB, split_axis=0, concat_axis=0, tiled=True)
-        maps.append((kept, lax.ppermute(kept, COIL, swap)))
-        gathered.append(ring_gather(ring, images[x]))
+        maps = (kept[:, x], lax.ppermute(kept[:, x], COIL, swap))
+        scatters.append(Scatter(ring, *gradient(where, gather.pieces(), maps, measured, sampling, tables, x)))
+    for _ in ring.steps():
+        for scatter in scatters:
+            scatter.step()
+    chip = jnp.stack([scatter.chip() for scatter in scatters])
+    updated = update(images, chip[:, 0], lax.ppermute(chip[:, 1].astype(BF16), SLAB, ring.siblings()))
+    up = [(i, i + 1) for i in range(devices - 1)]
+    down = [(i + 1, i) for i in range(devices - 1)]
+    before = lax.ppermute(updated[:, :, rows - 2 :], SLAB, up)
+    behind = lax.ppermute(updated[:, :, :2], SLAB, down)
     refined = []
     for x in range(width):
-        sums = gradient(where, *gathered[x], *maps[x], measured, sampling, tables, x)
-        updated = (images[x].astype(F32) - ring_scatter(ring, sums)).astype(BF16)
-        up = [(i, i + 1) for i in range(devices - 1)]
-        down = [(i + 1, i) for i in range(devices - 1)]
-        bordered = jnp.concatenate(
-            [
-                lax.ppermute(updated[:, rows - 2 :], SLAB, up),
-                updated,
-                lax.ppermute(updated[:, :2], SLAB, down),
-            ],
-            axis=1,
-        )
+        bordered = jnp.concatenate([before[x], updated[x], behind[x]], axis=1)
         other = lax.ppermute(bordered, COIL, swap)
         refined.append(convolutions(ends, bordered, other, *weights, second_bias))
     out = jnp.stack(refined, axis=1).reshape(encodings, 2, width, rows, ny)
@@ -469,7 +600,7 @@
 
     def per_device(*args):
         coils, phase = args[2].shape[1], args[0].shape[0]
-        if phases == 2 and coils == 2 and phase == 1 and devices % 4 == 0 and args[0].shape[4] % 16 == 0:
+        if phases == 2 and coils == 2 and phase == 1 and devices % 4 == 0 and args[0].shape[4] % 16 == 0 and args[0].shape[5] % 384 == 0:
             return paired(*args)
         return on_device(*args)
 

time: 174 us -> 161 us (0.925); the launches traced: 170 us -> 160 us
  waiting for transfers between devices: 20.1 us -> 68.4 us
  starting transfers between devices: 71.1 us -> 34.5 us
  local copies, waits for them, and re-layouts: 26.7 us -> 11.2 us
  other arithmetic: 5.86 us -> 2.18 us
  Pallas kernels: 46.1 us -> 43.8 us
    ppermute x42 -> x24, waiting for transfers between devices: 17.9 us -> 63.4 us  [the longest x4 36 us: step(): lax.ppermute(after(held, *earlier) if earlier else held, SLAB, self.ring....]
    ppermute x42 -> x24, starting transfers between devices: 55.5 us -> 25.5 us  [the longest x4 6.94 us: step(): self.other.append(lax.ppermute(self.held, SLAB, self.ring.siblings()))]
    unnamed x58 -> x28, local copies, waits for them, and re-layouts: 18.3 us -> 7.76 us
    all_to_all x2 -> x1, starting transfers between devices: 13 us -> 7.33 us  [paired(): kept = lax.all_to_all(pairs, SLAB, split_axis=0, concat_axis=0, tiled=True)]
    ppermute x2, waiting for transfers between devices: 1.45 us -> 5.04 us  [paired(): other = lax.ppermute(bordered, COIL, swap)]
    convert_element_type x12 -> x7, other arithmetic: 3.73 us -> 0.48 us  [the longest x6 0.44 us: step(): self.held = lax.ppermute(total.astype(BF16), SLAB, self.ring.perm())]
    pallas_call x2 -> x4, Pallas kernels: 34.2 us -> 31.9 us  [the longest x2 26.7 us: gradient(): pl.pallas_call(functools.partial(gradient_kernel, len(images), n), grid_s...]
    squeeze x4, local copies, waits for them, and re-layouts: 3.23 us -> 1.27 us  [the longest x1 1.2 us: paired(): maps = (kept[:, x], lax.ppermute(kept[:, x], COIL, swap))]
  transfers between devices with their start and end apart: 46 -> 27, of which waited for: 15 -> 18; matrix products, arithmetic and copies ran while one was open for 15% -> 3% of each run, Pallas kernels for 24% -> 20%
where the time goes in v1:
time: 161 us; the launch traced here: 160 us
  waiting for transfers between devices  68.4 us (42%)
  Pallas kernels  43.8 us (27%)
  starting transfers between devices  34.5 us (21%)
  local copies, waits for them, and re-layouts  11.2 us (7%)
  other arithmetic  2.18 us (1%)
    ppermute x4, waiting for transfers between devices, step(): lax.ppermute(after(held, *earlier) if earlier else held, SLAB, self.ring....  36 us
    pallas_call x2, Pallas kernels, gradient(): pl.pallas_call(functools.partial(gradient_kernel, len(images), n), grid_s...  26.7 us
    ppermute x8, waiting for transfers between devices, step(): self.held = lax.ppermute(total.astype(BF16), SLAB, self.ring.perm())  17.8 us
    pallas_call x2, Pallas kernels, convolutions(): pl.pallas_call(convolution_kernel, in_specs=[smem, vmem, vmem, vmem, vmem...  11.9 us
    unnamed x28, local copies, waits for them, and re-layouts  7.76 us
    all_to_all x1, starting transfers between devices, paired(): kept = lax.all_to_all(pairs, SLAB, split_axis=0, concat_axis=0, tiled=True)  7.33 us
    ppermute x4, starting transfers between devices, step(): self.other.append(lax.ppermute(self.held, SLAB, self.ring.siblings()))  6.94 us
    ppermute x2, waiting for transfers between devices, paired(): other = lax.ppermute(bordered, COIL, swap)  5.04 us
  transfers between devices with their start and end apart: 27, of which 18 were waited for; matrix products, arithmetic and copies ran while one was open for 3% of the time, Pallas kernels for 20%

profile of v1, /device:TPU:1, one launch (start us, length us, event | category | flops | bytes accessed | tf_op | source)
XLA Modules:
  0.0 160.5 jit_solution(9299518696031162968)
XLA Ops:
  0.0 1.4 copy-done
  1.4 1.0 copy-done.1
  2.4 0.9 copy-done.3
  3.3 0.8 copy-done.4
  4.1 4.3 %prepare.1 = (bf16[2,10,16,384]{3,2,1,0:T(8,128)(2,1)S(1)}, bf16[16,2,2,16,384]{4,3,2,1,0:T(8,128)(2,1)}) custom-call(s32[1]{0:T(128)} %bitcast.2.which, bf16[1,5,2,2,16,384]{5,4,3,2,1,0:T(8,128)(2,1)S(1)} %copy-done.3, bf16[32,2,2,16,384]{4,3,2,1,0:T(8,128)(2,1)S(1)} %copy-done, bf16[128,128]{1,0:T(8,128)(2,1)S(1)} %copy-done.4, bf16[384,384]{1,0:T(8,128)(2,1)S(1)} %copy-done.1), custom_call_target="tpu_custom_call" | custom-call | tf_op jit(solution)/shard_map/prepare/pallas_call | solution.py:308
  8.4 7.3 %all-to-all-start = ((bf16[16,2,2,16,384]{4,3,2,1,0:T(8,128)(2,1)}), bf16[16,2,2,16,384]{4,3,2,1,0:T(8,128)(2,1)}, u32[]{:S(2)}, u32[]{:S(2)}) async-start(bf16[16,2,2,16,384]{4,3,2,1,0:T(8,128)(2,1)} %get-tuple-element.15), calls=%async_computation | async-start | bytes 1572864 | tf_op jit(solution)/shard_map/all_to_all | solution.py:459
  15.7 0.2 collective-permute-start
  15.9 1.3 collective-permute-done
  17.3 1.4 collective-permute-start.1
  18.7 17.4 %collective-permute-done.1.refs_1_ = bf16[2,2,10,16,384]{4,3,2,1,0:T(8,128)(2,1)S(1)} collective-permute-done((bf16[2,2,10,16,384]{4,3,2,1,0:T(8,128)(2,1)S(1)}, bf16[2,2,10,16,384]{4,3,2,1,0:T(8,128)(2,1)S(1)}, u32[]{:S(2)}, u32[]{:S(2)}) %collective-permute-start.1) | collective-permute-done | bytes 491552 | tf_op jit(solution)/shard_map/ppermute | solution.py:109
  36.2 11.7 %collective-permute-done.2.refs_2_ = bf16[2,2,10,16,384]{4,3,2,1,0:T(8,128)(2,1)S(1)} collective-permute-done((bf16[2,2,10,16,384]{4,3,2,1,0:T(8,128)(2,1)S(1)}, bf16[2,2,10,16,384]{4,3,2,1,0:T(8,128)(2,1)S(1)}, u32[]{:S(2)}, u32[]{:S(2)}) %collective-permute-start.2) | collective-permute-done | bytes 491552 | tf_op jit(solution)/shard_map/ppermute | solution.py:109
  47.9 1.7 %collective-permute-start.5 = (bf16[2,2,10,16,384]{4,3,2,1,0:T(8,128)(2,1)S(1)}, bf16[2,2,10,16,384]{4,3,2,1,0:T(8,128)(2,1)S(1)}, u32[]{:S(2)}, u32[]{:S(2)}) collective-permute-start(bf16[2,2,10,16,384]{4,3,2,1,0:T(8,128)(2,1)S(1)} %collective-permute-done.1.refs_1_), channel_id=1, source_target_pairs={{0,2},{2,0},{4,6},{6,4},{8,10},{10,8},{12,14},{14,12},{16,18},{18,... | collective-permute-start | bytes 1474568 | tf_op jit(solution)/shard_map/ppermute | solution.py:111
  49.6 6.3 %collective-permute-done.3.refs_3_ = bf16[2,2,10,16,384]{4,3,2,1,0:T(8,128)(2,1)S(1)} collective-permute-done((bf16[2,2,10,16,384]{4,3,2,1,0:T(8,128)(2,1)S(1)}, bf16[2,2,10,16,384]{4,3,2,1,0:T(8,128)(2,1)S(1)}, u32[]{:S(2)}, u32[]{:S(2)}) %collective-permute-start.3) | collective-permute-done | bytes 491552 | tf_op jit(solution)/shard_map/ppermute | solution.py:109
  55.9 0.7 slice.139
  56.6 2.5 %collective-permute-start.7 = (bf16[2,2,10,16,384]{4,3,2,1,0:T(8,128)(2,1)S(1)}, bf16[2,2,10,16,384]{4,3,2,1,0:T(8,128)(2,1)}, u32[]{:S(2)}, u32[]{:S(2)}) collective-permute-start(bf16[2,2,10,16,384]{4,3,2,1,0:T(8,128)(2,1)S(1)} %collective-permute-done.3.refs_3_), channel_id=1, source_target_pairs={{0,2},{2,0},{4,6},{6,4},{8,10},{10,8},{12,14},{14,12},{16,18},{18,... | collective-permute-start | bytes 1474568 | tf_op jit(solution)/shard_map/ppermute | solution.py:111
  59.1 1.2 slice_bitcast_fusion
  60.3 1.3 collective-permute-start.15
  61.6 0.6 collective-permute-done.4.refs_4_
  62.2 2.7 %collective-permute-start.8 = (bf16[1,2,10,16,384]{4,3,2,1,0:T(8,128)(2,1)}, bf16[1,2,10,16,384]{4,3,2,1,0:T(8,128)(2,1)}, u32[]{:S(2)}, u32[]{:S(2)}) collective-permute-start(bf16[1,2,10,16,384]{4,3,2,1,0:T(8,128)(2,1)} %collective-permute-done.4.refs_4_), channel_id=1, source_target_pairs={{0,2},{2,0},{4,6},{6,4},{8,10},{10,8},{12,14},{14,12},{16,18},{18,... | collective-permute-start | bytes 737288 | tf_op jit(solution)/shard_map/ppermute | solution.py:111
  64.9 0.1 concatenate.24.slabs
  65.1 0.8 dynamic-slice_bitcast_fusion.2
  65.9 1.3 collective-permute-start.9
  67.2 4.0 %collective-permute-done.15.refs_10_ = bf16[16,2,16,384]{3,2,1,0:T(8,128)(2,1)} collective-permute-done((bf16[16,2,16,384]{3,2,1,0:T(8,128)(2,1)S(1)}, bf16[16,2,16,384]{3,2,1,0:T(8,128)(2,1)}, u32[]{:S(2)}, u32[]{:S(2)}) %collective-permute-start.15) | collective-permute-done | bytes 393248 | tf_op jit(solution)/shard_map/ppermute | solution.py:464
  71.3 1.5 copy-done.6
  72.8 1.0 copy-done.9
  73.8 0.9 copy-done.10
  74.8 13.4 %gradient.3 = (bf16[2,10,16,384]{3,2,1,0:T(8,128)(2,1)S(1)}, bf16[7,10,16,384]{3,2,1,0:T(8,128)(2,1)S(1)}, bf16[7,10,16,384]{3,2,1,0:T(8,128)(2,1)S(1)}) custom-call(s32[33]{0:T(128)S(1)} %concatenate.24.slabs, bf16[2,2,10,16,384]{4,3,2,1,0:T(8,128)(2,1)S(1)} %pad_maximum_fusion.1.refs_0_, bf16[2,2,10,16,384]{4,3,2,1,0:T(8,128)(2,1)S(1)} %collective-permute-done.1.refs_1_, ...), custom_call_target="tpu_custom_call" | custom-call | flops 10066329600 | bytes 8388608 | tf_op jit(solution)/shard_map/gradient/pallas_call | solution.py:247
  88.2 1.2 collective-permute-start.16
  89.4 13.3 %gradient.2 = (bf16[2,10,16,384]{3,2,1,0:T(8,128)(2,1)S(1)}, bf16[7,10,16,384]{3,2,1,0:T(8,128)(2,1)S(1)}, bf16[7,10,16,384]{3,2,1,0:T(8,128)(2,1)S(1)}) custom-call(s32[33]{0:T(128)S(1)} %concatenate.24.slabs, bf16[2,2,10,16,384]{4,3,2,1,0:T(8,128)(2,1)S(1)} %pad_maximum_fusion.1.refs_0_, bf16[2,2,10,16,384]{4,3,2,1,0:T(8,128)(2,1)S(1)} %collective-permute-done.1.refs_1_, ...), custom_call_target="tpu_custom_call" | custom-call | flops 10066329600 | bytes 8388608 | tf_op jit(solution)/shard_map/gradient/pallas_call | solution.py:247
  102.7 0.2 collective-permute-start.10
  103.0 0.1 maximum_bitcast_fusion
  103.2 1.1 collective-permute-start.17
  104.4 0.8 collective-permute-done.10
  105.2 1.1 collective-permute-start.11
  106.4 1.6 collective-permute-done.17
  108.1 0.4 collective-permute-start.18
  108.4 1.6 %collective-permute-done.11 = bf16[1,10,16,384]{3,2,1,0:T(8,128)(2,1)S(1)} collective-permute-done((bf16[1,10,16,384]{3,2,1,0:T(8,128)(2,1)S(1)}, bf16[1,10,16,384]{3,2,1,0:T(8,128)(2,1)S(1)}, u32[]{:S(2)}, u32[]{:S(2)}) %collective-permute-start.11) | collective-permute-done | bytes 122912 | tf_op jit(solution)/shard_map/ppermute | solution.py:135
  110.1 0.4 collective-permute-start.12
  110.5 3.0 %collective-permute-done.18 = bf16[2,10,16,384]{3,2,1,0:T(8,128)(2,1)S(1)} collective-permute-done((bf16[2,10,16,384]{3,2,1,0:T(8,128)(2,1)S(1)}, bf16[2,10,16,384]{3,2,1,0:T(8,128)(2,1)S(1)}, u32[]{:S(2)}, u32[]{:S(2)}) %collective-permute-start.18) | collective-permute-done | bytes 245792 | tf_op jit(solution)/shard_map/ppermute | solution.py:135
  113.6 0.4 collective-permute-start.19
  113.9 2.2 %collective-permute-done.12 = bf16[2,10,16,384]{3,2,1,0:T(8,128)(2,1)S(1)} collective-permute-done((bf16[2,10,16,384]{3,2,1,0:T(8,128)(2,1)S(1)}, bf16[2,10,16,384]{3,2,1,0:T(8,128)(2,1)S(1)}, u32[]{:S(2)}, u32[]{:S(2)}) %collective-permute-start.12) | collective-permute-done | bytes 245792 | tf_op jit(solution)/shard_map/ppermute | solution.py:135
  116.2 0.4 collective-permute-start.13
  116.6 2.4 %collective-permute-done.19 = bf16[2,10,16,384]{3,2,1,0:T(8,128)(2,1)S(1)} collective-permute-done((bf16[2,10,16,384]{3,2,1,0:T(8,128)(2,1)S(1)}, bf16[2,10,16,384]{3,2,1,0:T(8,128)(2,1)S(1)}, u32[]{:S(2)}, u32[]{:S(2)}) %collective-permute-start.19) | collective-permute-done | bytes 245792 | tf_op jit(solution)/shard_map/ppermute | solution.py:135
  119.0 0.4 collective-permute-start.20
  119.4 2.2 %collective-permute-done.13 = bf16[2,10,16,384]{3,2,1,0:T(8,128)(2,1)S(1)} collective-permute-done((bf16[2,10,16,384]{3,2,1,0:T(8,128)(2,1)S(1)}, bf16[2,10,16,384]{3,2,1,0:T(8,128)(2,1)S(1)}, u32[]{:S(2)}, u32[]{:S(2)}) %collective-permute-start.13) | collective-permute-done | bytes 245792 | tf_op jit(solution)/shard_map/ppermute | solution.py:135
  121.7 0.4 collective-permute-start.14
  122.0 2.1 %collective-permute-done.20 = bf16[2,10,16,384]{3,2,1,0:T(8,128)(2,1)S(1)} collective-permute-done((bf16[2,10,16,384]{3,2,1,0:T(8,128)(2,1)S(1)}, bf16[2,10,16,384]{3,2,1,0:T(8,128)(2,1)S(1)}, u32[]{:S(2)}, u32[]{:S(2)}) %collective-permute-start.20) | collective-permute-done | bytes 245792 | tf_op jit(solution)/shard_map/ppermute | solution.py:135
  124.2 2.9 %collective-permute-done.14 = bf16[2,10,16,384]{3,2,1,0:T(8,128)(2,1)S(1)} collective-permute-done((bf16[2,10,16,384]{3,2,1,0:T(8,128)(2,1)S(1)}, bf16[2,10,16,384]{3,2,1,0:T(8,128)(2,1)S(1)}, u32[]{:S(2)}, u32[]{:S(2)}) %collective-permute-start.14) | collective-permute-done | bytes 245792 | tf_op jit(solution)/shard_map/ppermute | solution.py:135
  127.2 3.2 %collective-permute-start.21 = (bf16[2,10,16,384]{3,2,1,0:T(8,128)(2,1)S(1)}, bf16[2,10,16,384]{3,2,1,0:T(8,128)(2,1)S(1)}, u32[]{:S(2)}, u32[]{:S(2)}) collective-permute-start(bf16[2,10,16,384]{3,2,1,0:T(8,128)(2,1)S(1)} %fusion.3), channel_id=1, source_target_pairs={{0,2},{2,0},{4,6},{6,4},{8,10},{10,8},{12,14},{14,12},{16,18},{18,... | collective-permute-start | bytes 737288 | tf_op jit(solution)/shard_map/ppermute | solution.py:470
  130.6 0.1 reshape.22
  130.7 0.1 copy.37.w_first
  130.9 0.1 reshape.26
  131.1 0.1 copy.38.b_first
  131.3 0.3 collective-permute-done.21.received
  131.6 0.8 update.1
  132.5 3.2 %collective-permute-start.22 = (bf16[2,10,2,384]{3,2,1,0:T(2,128)(2,1)S(1)}, bf16[2,10,2,384]{3,2,1,0:T(2,128)(2,1)S(1)}, u32[]{:S(2)}, u32[]{:S(2)}) collective-permute-start(bf16[2,10,2,384]{3,2,1,0:T(2,128)(2,1)S(1)} %get-tuple-element.27), channel_id=1, source_target_pairs={{0,2},{2,4},{4,6},{6,8},{8,10},{10,12},{12,14},{14,16},{16,18},{18... | collective-permute-start | bytes 92168 | tf_op jit(solution)/shard_map/ppermute | solution.py:473
  135.7 2.1 %collective-permute-start.23 = (bf16[2,10,2,384]{3,2,1,0:T(2,128)(2,1)S(1)}, bf16[2,10,2,384]{3,2,1,0:T(2,128)(2,1)S(1)}, u32[]{:S(2)}, u32[]{:S(2)}) collective-permute-start(bf16[2,10,2,384]{3,2,1,0:T(2,128)(2,1)S(1)} %get-tuple-element.28), channel_id=1, source_target_pairs={{2,0},{4,2},{6,4},{8,6},{10,8},{12,10},{14,12},{16,14},{18,16},{20... | collective-permute-start | bytes 92168 | tf_op jit(solution)/shard_map/ppermute | solution.py:474
  137.8 3.1 %collective-permute-done.23 = bf16[2,10,2,384]{3,2,1,0:T(2,128)(2,1)S(1)} collective-permute-done((bf16[2,10,2,384]{3,2,1,0:T(2,128)(2,1)S(1)}, bf16[2,10,2,384]{3,2,1,0:T(2,128)(2,1)S(1)}, u32[]{:S(2)}, u32[]{:S(2)}) %collective-permute-start.23) | collective-permute-done | bytes 30752 | tf_op jit(solution)/shard_map/ppermute | solution.py:474
  141.0 1.3 collective-permute-start.24
  142.4 0.3 collective-permute-start.25
  142.8 5.0 %collective-permute-done.24.other = bf16[10,20,384]{2,1,0:T(8,128)(2,1)S(1)} collective-permute-done((bf16[10,20,384]{2,1,0:T(8,128)(2,1)S(1)}, bf16[10,20,384]{2,1,0:T(8,128)(2,1)S(1)}, u32[]{:S(2)}, u32[]{:S(2)}) %collective-permute-start.24) | collective-permute-done | bytes 153632 | tf_op jit(solution)/shard_map/ppermute | solution.py:478
  147.8 5.9 %convolutions.2 = bf16[10,16,384]{2,1,0:T(8,128)(2,1)S(1)} custom-call(s32[2]{0:T(128)S(1)} %add_convert_fusion.6.ends, bf16[10,20,384]{2,1,0:T(8,128)(2,1)S(1)} %pad_maximum_fusion.5.own, bf16[10,20,384]{2,1,0:T(8,128)(2,1)S(1)} %collective-permute-done.24.other, bf16[128,192]{1,0:T(8,128)(2,1)S(1)} %copy.37.w_first, f32[128,1]{1,0:T(8,128)S(1)} %copy.38.b_first, ...), custom_call_target="tpu_custom_call" | custom-call | flops 594542592 | bytes 1048576 | tf_op jit(solution)/shard_map/convolutions/pallas_call | solution.py:398
  153.8 6.0 %convolutions.3 = bf16[10,16,384]{2,1,0:T(8,128)(2,1)S(1)} custom-call(s32[2]{0:T(128)S(1)} %add_convert_fusion.6.ends, bf16[10,20,384]{2,1,0:T(8,128)(2,1)S(1)} %pad_maximum_fusion.6.own, bf16[10,20,384]{2,1,0:T(8,128)(2,1)S(1)} %collective-permute-done.25.other, bf16[128,192]{1,0:T(8,128)(2,1)S(1)} %copy.37.w_first, f32[128,1]{1,0:T(8,128)S(1)} %copy.38.b_first, ...), custom_call_target="tpu_custom_call" | custom-call | flops 594542592 | bytes 1048576 | tf_op jit(solution)/shard_map/convolutions/pallas_call | solution.py:398
  159.7 0.7 pad_maximum_fusion.4
  (66 shorter events, 1.8 us)
Async XLA Ops:
  0.0 1.4 copy-start
  1.4 1.0 copy-start.1
  2.4 0.9 copy-start.3
  3.3 0.8 copy-start.4
  8.4 39.5 %all-to-all-start = ((bf16[16,2,2,16,384]{4,3,2,1,0:T(8,128)(2,1)}), bf16[16,2,2,16,384]{4,3,2,1,0:T(8,128)(2,1)}, u32[]{:S(2)}, u32[]{:S(2)}) async-start(bf16[16,2,2,16,384]{4,3,2,1,0:T(8,128)(2,1)} %get-tuple-element.15), calls=%async_computation | async-start | bytes 1572864 | tf_op jit(solution)/shard_map/all_to_all | solution.py:459
  15.7 1.5 collective-permute-start
  17.3 18.9 %collective-permute-start.1 = (bf16[2,2,10,16,384]{4,3,2,1,0:T(8,128)(2,1)S(1)}, bf16[2,2,10,16,384]{4,3,2,1,0:T(8,128)(2,1)S(1)}, u32[]{:S(2)}, u32[]{:S(2)}) collective-permute-start(bf16[2,2,10,16,384]{4,3,2,1,0:T(8,128)(2,1)S(1)} %pad_maximum_fusion.1.refs_0_), channel_id=1, source_target_pairs={{0,8},{2,6},{8,16},{10,2},{16,24},{18,10},{24,28},{26,18},{28,20},... | collective-permute-start | bytes 1474568 | tf_op jit(solution)/shard_map/ppermute | solution.py:109
  36.2 11.7 %collective-permute-start.2 = (bf16[2,2,10,16,384]{4,3,2,1,0:T(8,128)(2,1)S(1)}, bf16[2,2,10,16,384]{4,3,2,1,0:T(8,128)(2,1)S(1)}, u32[]{:S(2)}, u32[]{:S(2)}) collective-permute-start(bf16[2,2,10,16,384]{4,3,2,1,0:T(8,128)(2,1)S(1)} %collective-permute-done.1.refs_1_), channel_id=1, source_target_pairs={{0,8},{2,6},{8,16},{10,2},{16,24},{18,10},{24,28},{26,18},{28,20},... | collective-permute-start | bytes 1474568 | tf_op jit(solution)/shard_map/ppermute | solution.py:109
  47.9 8.0 %collective-permute-start.3 = (bf16[2,2,10,16,384]{4,3,2,1,0:T(8,128)(2,1)S(1)}, bf16[2,2,10,16,384]{4,3,2,1,0:T(8,128)(2,1)S(1)}, u32[]{:S(2)}, u32[]{:S(2)}) collective-permute-start(bf16[2,2,10,16,384]{4,3,2,1,0:T(8,128)(2,1)S(1)} %collective-permute-done.2.refs_2_), channel_id=1, source_target_pairs={{0,8},{2,6},{8,16},{10,2},{16,24},{18,10},{24,28},{26,18},{28,20},... | collective-permute-start | bytes 1474568 | tf_op jit(solution)/shard_map/ppermute | solution.py:109
  47.9 18.0 %collective-permute-start.5 = (bf16[2,2,10,16,384]{4,3,2,1,0:T(8,128)(2,1)S(1)}, bf16[2,2,10,16,384]{4,3,2,1,0:T(8,128)(2,1)S(1)}, u32[]{:S(2)}, u32[]{:S(2)}) collective-permute-start(bf16[2,2,10,16,384]{4,3,2,1,0:T(8,128)(2,1)S(1)} %collective-permute-done.1.refs_1_), channel_id=1, source_target_pairs={{0,2},{2,0},{4,6},{6,4},{8,10},{10,8},{12,14},{14,12},{16,18},{18,... | collective-permute-start | bytes 1474568 | tf_op jit(solution)/shard_map/ppermute | solution.py:111
  49.6 17.6 %collective-permute-start.6 = (bf16[2,2,10,16,384]{4,3,2,1,0:T(8,128)(2,1)S(1)}, bf16[2,2,10,16,384]{4,3,2,1,0:T(8,128)(2,1)}, u32[]{:S(2)}, u32[]{:S(2)}) collective-permute-start(bf16[2,2,10,16,384]{4,3,2,1,0:T(8,128)(2,1)S(1)} %collective-permute-done.2.refs_2_), channel_id=1, source_target_pairs={{0,2},{2,0},{4,6},{6,4},{8,10},{10,8},{12,14},{14,12},{16,18},{18,... | collective-permute-start | bytes 1474568 | tf_op jit(solution)/shard_map/ppermute | solution.py:111
  56.6 5.7 %collective-permute-start.4 = (bf16[1,2,10,16,384]{4,3,2,1,0:T(8,128)(2,1)}, bf16[1,2,10,16,384]{4,3,2,1,0:T(8,128)(2,1)}, u32[]{:S(2)}, u32[]{:S(2)}) collective-permute-start(bf16[1,2,10,16,384]{4,3,2,1,0:T(8,128)(2,1)} %slice.139), channel_id=1, source_target_pairs={{0,8},{2,6},{8,16},{10,2},{16,24},{18,10},{24,28},{26,18},{28,20},... | collective-permute-start | bytes 737288 | tf_op jit(solution)/shard_map/ppermute | solution.py:109
  56.6 14.7 %collective-permute-start.7 = (bf16[2,2,10,16,384]{4,3,2,1,0:T(8,128)(2,1)S(1)}, bf16[2,2,10,16,384]{4,3,2,1,0:T(8,128)(2,1)}, u32[]{:S(2)}, u32[]{:S(2)}) collective-permute-start(bf16[2,2,10,16,384]{4,3,2,1,0:T(8,128)(2,1)S(1)} %collective-permute-done.3.refs_3_), channel_id=1, source_target_pairs={{0,2},{2,0},{4,6},{6,4},{8,10},{10,8},{12,14},{14,12},{16,18},{18,... | collective-permute-start | bytes 1474568 | tf_op jit(solution)/shard_map/ppermute | solution.py:111
  60.3 10.9 %collective-permute-start.15 = (bf16[16,2,16,384]{3,2,1,0:T(8,128)(2,1)S(1)}, bf16[16,2,16,384]{3,2,1,0:T(8,128)(2,1)}, u32[]{:S(2)}, u32[]{:S(2)}) collective-permute-start(bf16[16,2,16,384]{3,2,1,0:T(8,128)(2,1)S(1)} %get-tuple-element.23.refs_9_), channel_id=1, source_target_pairs={{0,1},{1,0},{2,3},{3,2},{4,5},{5,4},{6,7},{7,6},{8,9},{9,8},{10,11... | collective-permute-start | bytes 1179656 | tf_op jit(solution)/shard_map/ppermute | solution.py:464
  62.2 9.0 %collective-permute-start.8 = (bf16[1,2,10,16,384]{4,3,2,1,0:T(8,128)(2,1)}, bf16[1,2,10,16,384]{4,3,2,1,0:T(8,128)(2,1)}, u32[]{:S(2)}, u32[]{:S(2)}) collective-permute-start(bf16[1,2,10,16,384]{4,3,2,1,0:T(8,128)(2,1)} %collective-permute-done.4.refs_4_), channel_id=1, source_target_pairs={{0,2},{2,0},{4,6},{6,4},{8,10},{10,8},{12,14},{14,12},{16,18},{18,... | collective-permute-start | bytes 737288 | tf_op jit(solution)/shard_map/ppermute | solution.py:111
  65.9 23.5 %collective-permute-start.9 = (bf16[16,2,16,384]{3,2,1,0:T(8,128)(2,1)S(1)}, bf16[16,2,16,384]{3,2,1,0:T(8,128)(2,1)S(1)}, u32[]{:S(2)}, u32[]{:S(2)}) collective-permute-start(bf16[16,2,16,384]{3,2,1,0:T(8,128)(2,1)S(1)} %get-tuple-element.24.refs_9_), channel_id=1, source_target_pairs={{0,1},{1,0},{2,3},{3,2},{4,5},{5,4},{6,7},{7,6},{8,9},{9,8},{10,11... | collective-permute-start | bytes 1179656 | tf_op jit(solution)/shard_map/ppermute | solution.py:464
  71.3 1.5 copy-start.6
  72.8 1.0 copy-start.9
  73.8 0.9 copy-start.10
  74.7 14.7 %copy-start.7 = (s32[1,5,384,256]{3,2,1,0:T(8,128)S(1)}, s32[1,5,384,256]{3,2,1,0:T(8,128)}, u32[]{:S(2)}) copy-start(s32[1,5,384,256]{3,2,1,0:T(8,128)} %refs_12_.3) | copy-start | bytes 5898244
  88.2 14.9 %copy-start.11 = (bf16[10,64,3,3,3]{1,4,3,2,0:T(4,128)(2,1)S(1)}, bf16[10,64,3,3,3]{1,4,3,2,0:T(4,128)(2,1)}, u32[]{:S(2)}) copy-start(bf16[10,64,3,3,3]{1,4,3,2,0:T(4,128)(2,1)} %param.22) | copy-start | bytes 103684
  88.2 14.9 %collective-permute-start.16 = (bf16[7,10,16,384]{3,2,1,0:T(8,128)(2,1)S(1)}, bf16[7,10,16,384]{3,2,1,0:T(8,128)(2,1)S(1)}, u32[]{:S(2)}, u32[]{:S(2)}) collective-permute-start(bf16[7,10,16,384]{3,2,1,0:T(8,128)(2,1)S(1)} %get-tuple-element.22), channel_id=1, source_target_pairs={{0,2},{2,0},{4,6},{6,4},{8,10},{10,8},{12,14},{14,12},{16,18},{18,... | collective-permute-start | bytes 2580488 | tf_op jit(solution)/shard_map/ppermute | solution.py:120
  102.7 2.5 %collective-permute-start.10 = (bf16[7,10,16,384]{3,2,1,0:T(8,128)(2,1)S(1)}, bf16[7,10,16,384]{3,2,1,0:T(8,128)(2,1)S(1)}, u32[]{:S(2)}, u32[]{:S(2)}) collective-permute-start(bf16[7,10,16,384]{3,2,1,0:T(8,128)(2,1)S(1)} %get-tuple-element.19), channel_id=1, source_target_pairs={{0,2},{2,0},{4,6},{6,4},{8,10},{10,8},{12,14},{14,12},{16,18},{18,... | collective-permute-start | bytes 2580488 | tf_op jit(solution)/shard_map/ppermute | solution.py:120
  103.2 4.8 %collective-permute-start.17 = (bf16[1,10,16,384]{3,2,1,0:T(8,128)(2,1)S(1)}, bf16[1,10,16,384]{3,2,1,0:T(8,128)(2,1)S(1)}, u32[]{:S(2)}, u32[]{:S(2)}) collective-permute-start(bf16[1,10,16,384]{3,2,1,0:T(8,128)(2,1)S(1)} %add_convert_fusion.4), channel_id=1, source_target_pairs={{0,8},{2,6},{8,16},{10,2},{16,24},{18,10},{24,28},{26,18},{28,20},... | collective-permute-start | bytes 368648 | tf_op jit(solution)/shard_map/ppermute | solution.py:135
  105.2 4.8 %collective-permute-start.11 = (bf16[1,10,16,384]{3,2,1,0:T(8,128)(2,1)S(1)}, bf16[1,10,16,384]{3,2,1,0:T(8,128)(2,1)S(1)}, u32[]{:S(2)}, u32[]{:S(2)}) collective-permute-start(bf16[1,10,16,384]{3,2,1,0:T(8,128)(2,1)S(1)} %add_convert_fusion.5), channel_id=1, source_target_pairs={{0,8},{2,6},{8,16},{10,2},{16,24},{18,10},{24,28},{26,18},{28,20},... | collective-permute-start | bytes 368648 | tf_op jit(solution)/shard_map/ppermute | solution.py:135
  108.1 5.4 %collective-permute-start.18 = (bf16[2,10,16,384]{3,2,1,0:T(8,128)(2,1)S(1)}, bf16[2,10,16,384]{3,2,1,0:T(8,128)(2,1)S(1)}, u32[]{:S(2)}, u32[]{:S(2)}) collective-permute-start(bf16[2,10,16,384]{3,2,1,0:T(8,128)(2,1)S(1)} %pad_maximum_fusion.3), channel_id=1, source_target_pairs={{0,8},{2,6},{8,16},{10,2},{16,24},{18,10},{24,28},{26,18},{28,20},... | collective-permute-start | bytes 737288 | tf_op jit(solution)/shard_map/ppermute | solution.py:135
  110.1 6.0 %collective-permute-start.12 = (bf16[2,10,16,384]{3,2,1,0:T(8,128)(2,1)S(1)}, bf16[2,10,16,384]{3,2,1,0:T(8,128)(2,1)S(1)}, u32[]{:S(2)}, u32[]{:S(2)}) collective-permute-start(bf16[2,10,16,384]{3,2,1,0:T(8,128)(2,1)S(1)} %pad_maximum_fusion.2), channel_id=1, source_target_pairs={{0,8},{2,6},{8,16},{10,2},{16,24},{18,10},{24,28},{26,18},{28,20},... | collective-permute-start | bytes 737288 | tf_op jit(solution)/shard_map/ppermute | solution.py:135
  113.6 5.4 %collective-permute-start.19 = (bf16[2,10,16,384]{3,2,1,0:T(8,128)(2,1)S(1)}, bf16[2,10,16,384]{3,2,1,0:T(8,128)(2,1)S(1)}, u32[]{:S(2)}, u32[]{:S(2)}) collective-permute-start(bf16[2,10,16,384]{3,2,1,0:T(8,128)(2,1)S(1)} %add_convert_fusion.1), channel_id=1, source_target_pairs={{0,8},{2,6},{8,16},{10,2},{16,24},{18,10},{24,28},{26,18},{28,20},... | collective-permute-start | bytes 737288 | tf_op jit(solution)/shard_map/ppermute | solution.py:135
  116.2 5.4 %collective-permute-start.13 = (bf16[2,10,16,384]{3,2,1,0:T(8,128)(2,1)S(1)}, bf16[2,10,16,384]{3,2,1,0:T(8,128)(2,1)S(1)}, u32[]{:S(2)}, u32[]{:S(2)}) collective-permute-start(bf16[2,10,16,384]{3,2,1,0:T(8,128)(2,1)S(1)} %add_convert_fusion.3), channel_id=1, source_target_pairs={{0,8},{2,6},{8,16},{10,2},{16,24},{18,10},{24,28},{26,18},{28,20},... | collective-permute-start | bytes 737288 | tf_op jit(solution)/shard_map/ppermute | solution.py:135
  119.0 5.1 %collective-permute-start.20 = (bf16[2,10,16,384]{3,2,1,0:T(8,128)(2,1)S(1)}, bf16[2,10,16,384]{3,2,1,0:T(8,128)(2,1)S(1)}, u32[]{:S(2)}, u32[]{:S(2)}) collective-permute-start(bf16[2,10,16,384]{3,2,1,0:T(8,128)(2,1)S(1)} %add_convert_fusion), channel_id=1, source_target_pairs={{0,8},{2,6},{8,16},{10,2},{16,24},{18,10},{24,28},{26,18},{28,20},... | collective-permute-start | bytes 737288 | tf_op jit(solution)/shard_map/ppermute | solution.py:135
  121.7 5.4 %collective-permute-start.14 = (bf16[2,10,16,384]{3,2,1,0:T(8,128)(2,1)S(1)}, bf16[2,10,16,384]{3,2,1,0:T(8,128)(2,1)S(1)}, u32[]{:S(2)}, u32[]{:S(2)}) collective-permute-start(bf16[2,10,16,384]{3,2,1,0:T(8,128)(2,1)S(1)} %add_convert_fusion.2), channel_id=1, source_target_pairs={{0,8},{2,6},{8,16},{10,2},{16,24},{18,10},{24,28},{26,18},{28,20},... | collective-permute-start | bytes 737288 | tf_op jit(solution)/shard_map/ppermute | solution.py:135
  124.1 6.9 %copy-start.12 = (f32[64]{0:T(128)S(1)}, f32[64]{0:T(128)}, u32[]{:S(2)}) copy-start(f32[64]{0:T(128)} %param.21) | copy-start | bytes 772
  127.1 4.4 %copy-start.2 = (bf16[384,384]{1,0:T(8,128)(2,1)S(1)}, bf16[384,384]{1,0:T(8,128)(2,1)}, u32[]{:S(2)}) copy-start(bf16[384,384]{1,0:T(8,128)(2,1)} %constant.202.clone.along_y) | copy-start | bytes 884740
  127.1 4.4 %copy-start.5 = (bf16[128,128]{1,0:T(8,128)(2,1)S(1)}, bf16[128,128]{1,0:T(8,128)(2,1)}, u32[]{:S(2)}) copy-start(bf16[128,128]{1,0:T(8,128)(2,1)} %constant.201.clone.along_z) | copy-start | bytes 98308
  127.2 4.3 %collective-permute-start.21 = (bf16[2,10,16,384]{3,2,1,0:T(8,128)(2,1)S(1)}, bf16[2,10,16,384]{3,2,1,0:T(8,128)(2,1)S(1)}, u32[]{:S(2)}, u32[]{:S(2)}) collective-permute-start(bf16[2,10,16,384]{3,2,1,0:T(8,128)(2,1)S(1)} %fusion.3), channel_id=1, source_target_pairs={{0,2},{2,0},{4,6},{6,4},{8,10},{10,8},{12,14},{14,12},{16,18},{18,... | collective-permute-start | bytes 737288 | tf_op jit(solution)/shard_map/ppermute | solution.py:470
  131.2 16.6 %copy-start.8 = (f32[10]{0:T(128)S(1)}, f32[10]{0:T(128)}, u32[]{:S(2)}) copy-start(f32[10]{0:T(128)} %b_second.3) | copy-start | bytes 124
  132.5 5.3 %collective-permute-start.22 = (bf16[2,10,2,384]{3,2,1,0:T(2,128)(2,1)S(1)}, bf16[2,10,2,384]{3,2,1,0:T(2,128)(2,1)S(1)}, u32[]{:S(2)}, u32[]{:S(2)}) collective-permute-start(bf16[2,10,2,384]{3,2,1,0:T(2,128)(2,1)S(1)} %get-tuple-element.27), channel_id=1, source_target_pairs={{0,2},{2,4},{4,6},{6,8},{8,10},{10,12},{12,14},{14,16},{16,18},{18... | collective-permute-start | bytes 92168 | tf_op jit(solution)/shard_map/ppermute | solution.py:473
  135.7 5.2 %collective-permute-start.23 = (bf16[2,10,2,384]{3,2,1,0:T(2,128)(2,1)S(1)}, bf16[2,10,2,384]{3,2,1,0:T(2,128)(2,1)S(1)}, u32[]{:S(2)}, u32[]{:S(2)}) collective-permute-start(bf16[2,10,2,384]{3,2,1,0:T(2,128)(2,1)S(1)} %get-tuple-element.28), channel_id=1, source_target_pairs={{2,0},{4,2},{6,4},{8,6},{10,8},{12,10},{14,12},{16,14},{18,16},{20... | collective-permute-start | bytes 92168 | tf_op jit(solution)/shard_map/ppermute | solution.py:474
  141.0 6.8 %collective-permute-start.24 = (bf16[10,20,384]{2,1,0:T(8,128)(2,1)S(1)}, bf16[10,20,384]{2,1,0:T(8,128)(2,1)S(1)}, u32[]{:S(2)}, u32[]{:S(2)}) collective-permute-start(bf16[10,20,384]{2,1,0:T(8,128)(2,1)S(1)} %pad_maximum_fusion.5.own), channel_id=1, source_target_pairs={{0,1},{1,0},{2,3},{3,2},{4,5},{5,4},{6,7},{7,6},{8,9},{9,8},{10,11... | collective-permute-start | bytes 460808 | tf_op jit(solution)/shard_map/ppermute | solution.py:478
  142.4 11.4 %collective-permute-start.25 = (bf16[10,20,384]{2,1,0:T(8,128)(2,1)S(1)}, bf16[10,20,384]{2,1,0:T(8,128)(2,1)S(1)}, u32[]{:S(2)}, u32[]{:S(2)}) collective-permute-start(bf16[10,20,384]{2,1,0:T(8,128)(2,1)S(1)} %pad_maximum_fusion.6.own), channel_id=1, source_target_pairs={{0,1},{1,0},{2,3},{3,2},{4,5},{5,4},{6,7},{7,6},{8,9},{9,8},{10,11... | collective-permute-start | bytes 460808 | tf_op jit(solution)/shard_map/ppermute | solution.py:478

commit v2 on v1

--- a/solution.py
+++ b/solution.py
@@ -100,18 +100,23 @@
 class Gather:
     def __init__(self, ring, mine):
         self.ring = ring
-        self.held = self.own = jnp.concatenate([mine, lax.ppermute(mine, SLAB, ring.siblings())], axis=0)
+        self.first = lax.ppermute(mine, SLAB, ring.perm())
+        self.own = [mine, lax.ppermute(mine, SLAB, ring.siblings())]
+        self.held = None
         self.kept, self.other = [], []
 
     def step(self, *earlier):
         both = self.ring.steps()[len(self.kept)][1]
-        held = self.held if both else self.held[:1]
-        self.held = lax.ppermute(after(held, *earlier) if earlier else held, SLAB, self.ring.perm())
+        if self.held is None:
+            self.held = jnp.concatenate([self.first, lax.ppermute(self.own[1], SLAB, self.ring.perm())], axis=0)
+        else:
+            held = self.held if both else self.held[:1]
+            self.held = lax.ppermute(after(held, *earlier) if earlier else held, SLAB, self.ring.perm())
         self.kept.append(self.held)
         self.other.append(lax.ppermute(self.held, SLAB, self.ring.siblings()))
 
     def pieces(self):
-        return [self.own] + self.kept + self.other
+        return self.own + self.kept + self.other
 
 
 class Scatter:
@@ -151,7 +156,7 @@
     held_images, refs = refs[:images], refs[images:]
     maps, refs = refs[:coils], refs[coils:]
     measured, sampling, ty_f, tz_f, tz_i, ty_i = refs[:6]
-    out, products, backs = refs[-5:-2], refs[-2], refs[-1]
+    out, products, backs = refs[6:9], refs[9], refs[10]
     rows, ny = held_images[0].shape[-2:]
     nz = sampling.shape[-1]
     count, half = nz // rows, rows // 2
@@ -178,11 +183,11 @@
 
     for k, (held, i) in enumerate(pieces(held_images)):
         slab = slabs[k]
-        real = held[i, 0, 0].astype(F32)
-        imag = held[i, 0, 1].astype(F32)
+        real = held[i, 0].astype(F32)
+        imag = held[i, 1].astype(F32)
         for c in range(coils):
-            m_real = maps[c][slab, 0].astype(F32)
-            m_imag = maps[c][slab, 1].astype(F32)
+            m_real = maps[c][slab, 0, 0].astype(F32)
+            m_imag = maps[c][slab, 0, 1].astype(F32)
             p_real = m_real * real - m_imag * imag
             p_imag = m_real * imag + m_imag * real
             for parity, at in enumerate(places(slab)):
@@ -228,8 +233,8 @@
             cells = slice(j * my, (j + 1) * my)
             real, imag = 0.0, 0.0
             for c in range(coils):
-                m_real = maps[c][slab, 0, :, cells].astype(F32)
-                m_imag = maps[c][slab, 1, :, cells].astype(F32)
+                m_real = maps[c][slab, 0, 0, :, cells].astype(F32)
+                m_imag = maps[c][slab, 0, 1, :, cells].astype(F32)
                 back = jnp.concatenate([backs[c, j, at, :] for at in places(slab)], axis=0)
                 real += m_real * back[:, :my] + m_imag * back[:, my:]
                 imag += m_real * back[:, my:] - m_imag * back[:, :my]
@@ -238,7 +243,7 @@
 
 
 def gradient(where, images, maps, measured, sampling, tables, x):
-    _, _, channels, rows, ny = images[0].shape
+    _, channels, rows, ny = images[0].shape
     nz = sampling.shape[-1]
     n = len(maps)
     far = (nz // rows - 2) // 2
@@ -249,8 +254,12 @@
         grid_spec=pltpu.PrefetchScalarGridSpec(
             num_scalar_prefetch=1,
             grid=(channels // 2,),
-            in_specs=[pl.BlockSpec((a.shape[0], 1, 2, rows, ny), lambda e, s: (0, x, e, 0, 0)) for a in images]
-            + [whole(a) for a in maps]
+            in_specs=[pl.BlockSpec((a.shape[0], 2, rows, ny), lambda e, s: (0, e, 0, 0)) for a in images]
+            + [
+                pl.BlockSpec((a.shape[0], 1, 2, rows, ny), functools.partial(lambda at, e, s: (0, at, 0, 0, 0), at),
+                             pipeline_mode=pl.Buffered(1))
+                for a, at in maps
+            ]
             + [
                 pl.BlockSpec((1, 2, 1, 2, 1, ny, nz), lambda e, s: (0, 0, e, 0, x, 0, 0)),
                 pl.BlockSpec((1, 1, ny, nz), lambda e, s: (0, e, 0, 0)),
@@ -266,18 +275,17 @@
         compiler_params=pltpu.CompilerParams(vmem_limit_bytes=40 * 2**20),
         cost_estimate=pl.CostEstimate(flops=flops, bytes_accessed=8 * 2**20, transcendentals=0),
         name="gradient",
-    )(where, *images, *maps, measured, sampling, *tables)
+    )(where, *images, *[a for a, _ in maps], measured, sampling, *tables)
 
 
 def reordered(value, along_z, along_y):
     n, rows, ny = value.shape
     block = along_z.shape[0]
-    flat = value.reshape(n * rows, ny)
+    flat = nn_dot(value.reshape(n * rows, ny), along_y).astype(BF16)
     out = []
     for start in range(0, n * rows, block):
         size = min(block, n * rows - start)
-        part = nn_dot(along_z[:size, :size], flat[start : start + size]).astype(BF16)
-        out.append(nn_dot(part, along_y).astype(BF16))
+        out.append(nn_dot(along_z[:size, :size], flat[start : start + size]).astype(BF16))
     return jnp.concatenate(out, axis=0).reshape(n, rows, ny)
 
 
@@ -289,33 +297,49 @@
 
 def prepare_kernel(which, image, maps, along_z, along_y, image_out, maps_out):
     width, channels, rows, ny = image_out.shape
-    pairs = maps_out.shape[0]
-    picked = image[...].reshape((channels, width, rows, ny))
-    for x in range(width):
-        image_out[x] = reordered(picked[:, x], along_z[...], along_y[...])
-    for pair in range(pairs):
-        value = maps[2 * pair + which[0]].reshape((2 * width, rows, ny))
-        value = reordered(value, along_z[...], along_y[...])
+
+    @pl.when(pl.program_id(0) == 0)
+    def _():
+        picked = image[...].reshape((channels, width, rows, ny))
+        for x in range(width):
+            image_out[x] = reordered(picked[:, x], along_z[...], along_y[...])
+
+    count = maps_out.shape[0]
+    value = reordered(maps[:, 0].reshape((count * 2 * width, rows, ny)), along_z[...], along_y[...])
+    for pair in range(count):
         for x in range(width):
             for part in range(2):
-                maps_out[pair, x, part] = value[part * width + x]
+                maps_out[pair, x, part] = value[(pair * 2 + part) * width + x]
 
 
 def prepare(which, current_image, coil_maps):
     _, encodings, _, width, rows, ny = current_image.shape
-    vmem = pl.BlockSpec(memory_space=pltpu.VMEM)
-    smem = pl.BlockSpec(memory_space=pltpu.SMEM)
+    devices = coil_maps.shape[0] // 2
+    pairs = coil_maps.reshape((devices, 2) + coil_maps.shape[1:])
+    whole = lambda shape: pl.BlockSpec(shape, lambda i, t: (0,) * len(shape))
+    matrices = orders(rows, ny, False)
+    image_shape = (width, 2 * encodings, rows, ny)
+    steps = 4
+    group = (devices // steps, width, 2, rows, ny)
     return pl.pallas_call(
         prepare_kernel,
-        in_specs=[smem, vmem, vmem, vmem, vmem],
-        out_specs=[vmem, vmem],
+        grid_spec=pltpu.PrefetchScalarGridSpec(
+            num_scalar_prefetch=1,
+            grid=(steps,),
+            in_specs=[
+                whole(current_image.shape),
+                pl.BlockSpec((devices // steps, 1) + coil_maps.shape[1:], lambda i, t: (i, t[0], 0, 0, 0, 0)),
+            ]
+            + [whole(m.shape) for m in matrices],
+            out_specs=[whole(image_shape), pl.BlockSpec(group, lambda i, t: (i, 0, 0, 0, 0))],
+        ),
         out_shape=[
-            jax.ShapeDtypeStruct((width, 2 * encodings, rows, ny), BF16),
-            jax.ShapeDtypeStruct((coil_maps.shape[0] // 2, width, 2, rows, ny), BF16),
+            jax.ShapeDtypeStruct(image_shape, BF16),
+            jax.ShapeDtypeStruct((devices, width, 2, rows, ny), BF16),
         ],
-        compiler_params=pltpu.CompilerParams(vmem_limit_bytes=24 * 2**20),
+        compiler_params=pltpu.CompilerParams(vmem_limit_bytes=58 * 2**20),
         name="prepare",
-    )(which, current_image, coil_maps, *orders(rows, ny, False))
+    )(which, current_image, pairs, *matrices)
 
 
 def update_kernel(image, chip, received, along_z, along_y, out):
@@ -353,53 +377,58 @@
     return jnp.concatenate([ref[j, start : start + count, :] for j in range(ref.shape[0])], axis=1)
 
 
-def convolution_kernel(ends, own, other, w_first, b_first, w_second, b_second, out, stacked, result):
-    channels, depth, ny = own.shape
-    rows = depth - 4
+def convolution_kernel(ends, *refs):
+    sources, refs = (refs[:3], refs[3:6]), refs[6:]
+    w_first, b_first, w_second, b_second, out, stacked, result = refs
+    _, channels, rows, ny = sources[0][1].shape
+    depth = rows + 4
     group = stacked.shape[1] // depth
     lanes = result.shape[1] // rows
     stacked[...] = jnp.zeros_like(stacked)
-    for t, source in enumerate((own, other)):
+    for t, source in enumerate(sources):
         for i in range(channels):
-            value = source[i].astype(F32)
+            value = jnp.concatenate([part[0, i].astype(F32) for part in source], axis=0)
             for d in range(3):
                 line = value if d == 1 else shifted(value, d - 1)
                 put_strided(stacked, (d * 2 + t) * channels + i, depth, group, line)
+    features = w_first.shape[0] // 2
+    taps = w_second.shape[0] // 4
     partial = []
-    taps = w_second.shape[0] // 3
-    for z in range(rows + 2):
-        window = get_lines(stacked, z * group, 3 * group).astype(BF16)
+    for pair in range(rows // 2 + 1):
+        window = get_lines(stacked, 2 * pair * group, 4 * group).astype(BF16)
         hidden = jnp.maximum(nn_dot(w_first[...], window) + b_first[...], 0.0)
-        if z == 0:
-            hidden = hidden * ends[0].astype(F32)
-        if z == rows + 1:
-            hidden = hidden * ends[1].astype(F32)
+        if pair == 0:
+            hidden = jnp.concatenate([hidden[:features] * ends[0].astype(F32), hidden[features:]], axis=0)
+        if pair == rows // 2:
+            hidden = jnp.concatenate([hidden[:features], hidden[features:] * ends[1].astype(F32)], axis=0)
         partial.append(nn_dot(w_second[...], hidden.astype(BF16)))
-        if z >= 2:
-            total = partial[z - 2][:taps] + partial[z - 1][taps : 2 * taps] + partial[z][2 * taps :]
-            line = (
-                shifted(total[:lanes], -1) + total[lanes : 2 * lanes] + shifted(total[2 * lanes :], 1)
-            )
-            put_strided(result, z - 2, lanes, rows, line)
-            partial[z - 2] = None
+        if pair > 0:
+            for z in range(2):
+                total = partial[0][(2 + z) * taps : (3 + z) * taps] + partial[1][z * taps : (z + 1) * taps]
+                line = shifted(total[:lanes], -1) + total[lanes : 2 * lanes] + shifted(total[2 * lanes :], 1)
+                put_strided(result, 2 * pair - 2 + z, lanes, rows, line)
+            partial = partial[1:]
     for i in range(channels):
-        value = own[i].astype(F32)[2 : 2 + rows]
-        out[i] = (value + get_lines(result, i * rows, rows) + b_second[i]).astype(BF16)
-
-
-def convolutions(ends, own, other, w_first, b_first, w_second, b_second):
-    channels, depth, ny = own.shape
-    rows = depth - 4
-    group = w_first.shape[1] // 3
-    lanes = w_second.shape[0] // 9
-    vmem = pl.BlockSpec(memory_space=pltpu.VMEM)
+        value = sources[0][1][0, i].astype(F32)
+        out[0, i // 2, i % 2, 0] = (value + get_lines(result, i * rows, rows) + b_second[i]).astype(BF16)
+
+
+def convolutions(ends, parts, w_first, b_first, w_second, b_second, encodings):
+    width, channels, rows, ny = parts[1].shape
+    depth = rows + 4
+    group = w_first.shape[1] // 4
+    lanes = w_second.shape[0] // 12
     smem = pl.BlockSpec(memory_space=pltpu.SMEM)
-    flops = 2 * (rows + 2) * ny * (w_first.size + w_second.size)
+    whole = lambda a: pl.BlockSpec(a.shape, lambda x: (0,) * a.ndim)
+    flops = width * (rows + 2) * ny * (w_first.size + w_second.size)
     return pl.pallas_call(
         convolution_kernel,
-        in_specs=[smem, vmem, vmem, vmem, vmem, vmem, smem],
-        out_specs=vmem,
-        out_shape=jax.ShapeDtypeStruct((channels, rows, ny), BF16),
+        grid=(width,),
+        in_specs=[smem]
+        + [pl.BlockSpec((1,) + a.shape[1:], lambda x: (x, 0, 0, 0)) for a in parts]
+        + [whole(w_first), whole(b_first), whole(w_second), smem],
+        out_specs=pl.BlockSpec((1, encodings, 2, 1, rows, ny), lambda x: (0, 0, 0, x, 0, 0)),
+        out_shape=jax.ShapeDtypeStruct((1, encodings, 2, width, rows, ny), BF16),
         scratch_shapes=[
             pltpu.VMEM((ny // 128, depth * group, 128), F32),
             pltpu.VMEM((ny // 128, lanes * rows, 128), F32),
@@ -407,7 +436,7 @@
         compiler_params=pltpu.CompilerParams(vmem_limit_bytes=24 * 2**20),
         cost_estimate=pl.CostEstimate(flops=flops, bytes_accessed=2**20, transcendentals=0),
         name="convolutions",
-    )(ends, own, other, w_first, b_first, w_second, b_second)
+    )(ends, *parts, w_first, b_first, w_second, b_second)
 
 
 def round_up(value, unit):
@@ -428,12 +457,15 @@
     first = first.transpose(0, 1, 4, 5, 2, 3).reshape(2 * feat, 3, 6 * channels)
     group = round_up(6 * channels, 16)
     first = jnp.pad(first, ((0, 0), (0, 0), (0, group - 6 * channels))).reshape(2 * feat, 3 * group)
-    bias = jnp.concatenate([first_bias, first_bias])[:, None]
+    first = jnp.concatenate([jnp.pad(first, ((0, 0), (0, group))), jnp.pad(first, ((0, 0), (group, 0)))], axis=0)
+    bias = jnp.concatenate([first_bias] * 4)[:, None]
     second = jnp.stack([tap(second_weight, 1), tap(second_weight, ahead)], 1)
     second = second.transpose(3, 4, 0, 1, 2).reshape(3, 3, channels, 2 * feat)
     lanes = round_up(channels, 8)
-    second = jnp.pad(second, ((0, 0), (0, 0), (0, lanes - channels), (0, 0))).reshape(9 * lanes, 2 * feat)
-    return first, bias, second
+    second = jnp.pad(second, ((0, 0), (0, 0), (0, lanes - channels), (0, 0))).reshape(3, 3 * lanes, 2 * feat)
+    none = jnp.zeros_like(second[0])
+    line = lambda u: jnp.concatenate([second[u + 2 - r] if 0 <= u + 2 - r <= 2 else none for r in range(4)], axis=0)
+    return first, bias, jnp.concatenate([line(0), line(1)], axis=1)
 
 
 def paired(current_image, coil_maps, measured, sampling, first_weight, first_bias, second_weight, second_bias):
@@ -449,36 +481,46 @@
         split_tables(nz, 2, True, True),
         split_tables(ny, 3, False, True),
     )
-    where = jnp.concatenate([ring.slabs(), q[None].astype(jnp.int32)])
+    which = q[None].astype(jnp.int32)
+    where = jnp.concatenate([ring.slabs(), which])
     swap = [(0, 1), (1, 0)]
     weights = convolution_weights(first_weight, first_bias, second_weight)
     ends = jnp.stack([me > 0, me < devices - 1]).astype(jnp.int32)
 
-    images, pairs = prepare(q[None].astype(jnp.int32), current_image, coil_maps)
-    gather = Gather(ring, images[None])
-    kept = lax.all_to_all(pairs, SLAB, split_axis=0, concat_axis=0, tiled=True)
+    images, pairs = prepare(which, current_image, coil_maps)
+    gathers = [Gather(ring, images[x : x + 1]) for x in range(width)]
+    kept = lax.all_to_all(after(pairs, *[gather.own[1] for gather in gathers]), SLAB, split_axis=0, concat_axis=0, tiled=True)
+    halves = [kept[:, x : x + 1] for x in range(width)]
     for step in range(len(ring.steps())):
-        gather.step(*((kept,) if step == 2 else ()))
+        for gather in gathers:
+            gather.step(*((halves[step - 2],) if 2 <= step < 2 + width else ()))
+    swapped = [lax.ppermute(half, COIL, swap) for half in halves]
     scatters = []
     for x in range(width):
-        maps = (kept[:, x], lax.ppermute(kept[:, x], COIL, swap))
-        scatters.append(Scatter(ring, *gradient(where, gather.pieces(), maps, measured, sampling, tables, x)))
+        scatters.append(Scatter(ring, *gradient(where, gathers[x].pieces(), [(kept, x), (swapped[x], 0)], measured, sampling, tables, x)))
     for _ in ring.steps():
         for scatter in scatters:
             scatter.step()
     chip = jnp.stack([scatter.chip() for scatter in scatters])
     updated = update(images, chip[:, 0], lax.ppermute(chip[:, 1].astype(BF16), SLAB, ring.siblings()))
-    up = [(i, i + 1) for i in range(devices - 1)]
-    down = [(i + 1, i) for i in range(devices - 1)]
-    before = lax.ppermute(updated[:, :, rows - 2 :], SLAB, up)
-    behind = lax.ppermute(updated[:, :, :2], SLAB, down)
-    refined = []
-    for x in range(width):
-        bordered = jnp.concatenate([before[x], updated[x], behind[x]], axis=1)
-        other = lax.ppermute(bordered, COIL, swap)
-        refined.append(convolutions(ends, bordered, other, *weights, second_bias))
-    out = jnp.stack(refined, axis=1).reshape(encodings, 2, width, rows, ny)
-    return out[None]
+    both = (SLAB, COIL)
+    cross = lambda shift, flip: [
+        ((i * 2 + q), ((i + shift) * 2 + (q ^ flip)))
+        for i in range(devices)
+        for q in range(2)
+        if 0 <= i + shift < devices
+    ]
+    head, tail = updated[:, :, :2], updated[:, :, rows - 2 :]
+    phases = []
+    for flip in range(2):
+        phases.append(
+            [
+                lax.ppermute(tail, both, cross(1, flip)),
+                lax.ppermute(updated, both, cross(0, 1)) if flip else updated,
+                lax.ppermute(head, both, cross(-1, flip)),
+            ]
+        )
+    return convolutions(ends, phases[0] + phases[1], *weights, second_bias, encodings)
 
 
 def with_halo(cells, sides, width):

time: 161 us -> 149 us (0.925)
  waiting for transfers between devices: 68.4 us -> 39 us
  starting transfers between devices: 34.5 us -> 54.6 us
  Pallas kernels: 43.8 us -> 40.9 us
    ppermute x4 -> x6, waiting for transfers between devices: 36 us -> 5.77 us  [step(): lax.ppermute(after(held, *earlier) if earlier else held, SLAB, self.ring....]
    ppermute x7 -> x13, starting transfers between devices: 9.71 us -> 20 us  [the longest x2 7.07 us: paired(): lax.ppermute(tail, both, cross(1, flip))]
    ppermute x7 -> x13, waiting for transfers between devices: 13.4 us -> 20.2 us  [the longest x2 11.1 us: __init__(): self.first = lax.ppermute(mine, SLAB, ring.perm())]
    ppermute x8, starting transfers between devices: 4.45 us -> 10.6 us  [step(): self.held = lax.ppermute(total.astype(BF16), SLAB, self.ring.perm())]
    ppermute x4 -> x6, starting transfers between devices: 1.45 us -> 7.07 us  [step(): lax.ppermute(after(held, *earlier) if earlier else held, SLAB, self.ring....]
    ppermute x8, waiting for transfers between devices: 17.8 us -> 12.4 us  [step(): self.held = lax.ppermute(total.astype(BF16), SLAB, self.ring.perm())]
    unnamed x28 -> x26, local copies, waits for them, and re-layouts: 7.76 us -> 4.46 us
    pallas_call x3 -> x2, Pallas kernels: 16.2 us -> 14 us  [the longest x1 8.93 us: convolutions(): pl.pallas_call(convolution_kernel, grid=(width,), in_specs=[smem] + [pl.B...]
  transfers between devices with their start and end apart: 27 -> 39, of which waited for: 18 -> 20; matrix products, arithmetic and copies ran while one was open for 3% -> 5% of each run, Pallas kernels for 20% -> 18%
where the time goes in v2:
time: 149 us; the launch traced here: 148 us
  starting transfers between devices  54.6 us (37%)
  Pallas kernels  40.9 us (27%)
  waiting for transfers between devices  39 us (26%)
  local copies, waits for them, and re-layouts  11 us (7%)
  other arithmetic  1.98 us (1%)
    pallas_call x2, Pallas kernels, gradient(): pl.pallas_call(functools.partial(gradient_kernel, len(images), n), grid_s...  26.3 us
    ppermute x8, waiting for transfers between devices, step(): self.held = lax.ppermute(total.astype(BF16), SLAB, self.ring.perm())  12.4 us
    ppermute x2, waiting for transfers between devices, __init__(): self.first = lax.ppermute(mine, SLAB, ring.perm())  11.1 us
    ppermute x8, starting transfers between devices, step(): self.held = lax.ppermute(total.astype(BF16), SLAB, self.ring.perm())  10.6 us
    pallas_call x1, Pallas kernels, convolutions(): pl.pallas_call(convolution_kernel, grid=(width,), in_specs=[smem] + [pl.B...  8.93 us
    all_to_all x1, starting transfers between devices, paired(): lax.all_to_all(after(pairs, *[gather.own[1] for gather in gathers]), SLAB...  7.46 us
    ppermute x2, starting transfers between devices, paired(): lax.ppermute(tail, both, cross(1, flip))  7.07 us
    ppermute x6, starting transfers between devices, step(): lax.ppermute(after(held, *earlier) if earlier else held, SLAB, self.ring....  7.07 us
  transfers between devices with their start and end apart: 39, of which 20 were waited for; matrix products, arithmetic and copies ran while one was open for 5% of the time, Pallas kernels for 18%

profile of v2, /device:TPU:1, one launch (start us, length us, event | category | flops | bytes accessed | tf_op | source)
XLA Modules:
  0.0 148.2 jit_solution(5958522023994309939)
XLA Ops:
  0.0 5.0 %prepare.1 = (bf16[2,10,16,384]{3,2,1,0:T(8,128)(2,1)}, bf16[16,2,2,16,384]{4,3,2,1,0:T(8,128)(2,1)}) custom-call(s32[1]{0:T(128)} %bitcast.2.which, bf16[1,5,2,2,16,384]{5,4,3,2,1,0:T(8,128)(2,1)} %image.1, bf16[16,2,2,2,16,384]{5,4,3,2,1,0:T(8,128)(2,1)} %bitcast.69, bf16[128,128]{1,0:T(8,128)(2,1)} %constant.200.clone.along_z, ...), custom_call_target="tpu_custom_call" | custom-call | tf_op jit(solution)/shard_map/prepare/pallas_call | solution.py:324
  5.0 1.0 fusion.11
  6.1 0.5 collective-permute-start.4
  6.6 0.8 collective-permute-done.refs_1_
  7.6 7.5 %all-to-all-start = ((bf16[16,2,2,16,384]{4,3,2,1,0:T(8,128)(2,1)}), bf16[16,2,2,16,384]{4,3,2,1,0:T(8,128)(2,1)S(1)}, u32[]{:S(2)}, u32[]{:S(2)}) async-start(bf16[16,2,2,16,384]{4,3,2,1,0:T(8,128)(2,1)} %get-tuple-element.20), calls=%async_computation | async-start | bytes 1572864 | tf_op jit(solution)/shard_map/all_to_all | solution.py:492
  15.1 1.4 collective-permute-start.17
  16.4 1.2 collective-permute-start.1
  17.6 1.2 collective-permute-start.18
  18.8 1.2 collective-permute-start.2
  20.0 9.5 %collective-permute-done.17 = bf16[1,10,16,384]{3,2,1,0:T(8,128)(2,1)S(1)} collective-permute-done((bf16[1,10,16,384]{3,2,1,0:T(8,128)(2,1)S(1)}, bf16[1,10,16,384]{3,2,1,0:T(8,128)(2,1)S(1)}, u32[]{:S(2)}, u32[]{:S(2)}) %collective-permute-start.17) | collective-permute-done | bytes 122912 | tf_op jit(solution)/shard_map/ppermute | solution.py:103
  29.5 1.6 %collective-permute-done.1 = bf16[1,10,16,384]{3,2,1,0:T(8,128)(2,1)S(1)} collective-permute-done((bf16[1,10,16,384]{3,2,1,0:T(8,128)(2,1)S(1)}, bf16[1,10,16,384]{3,2,1,0:T(8,128)(2,1)S(1)}, u32[]{:S(2)}, u32[]{:S(2)}) %collective-permute-start.1) | collective-permute-done | bytes 122912 | tf_op jit(solution)/shard_map/ppermute | solution.py:103
  31.1 3.1 %collective-permute-done.18 = bf16[1,10,16,384]{3,2,1,0:T(8,128)(2,1)S(1)} collective-permute-done((bf16[1,10,16,384]{3,2,1,0:T(8,128)(2,1)S(1)}, bf16[1,10,16,384]{3,2,1,0:T(8,128)(2,1)S(1)}, u32[]{:S(2)}, u32[]{:S(2)}) %collective-permute-start.18) | collective-permute-done | bytes 122912 | tf_op jit(solution)/shard_map/ppermute | solution.py:111
  34.3 1.2 collective-permute-done.2
  35.5 3.9 %collective-permute-start.3 = (bf16[2,10,16,384]{3,2,1,0:T(8,128)(2,1)S(1)}, bf16[2,10,16,384]{3,2,1,0:T(8,128)(2,1)S(1)}, u32[]{:S(2)}, u32[]{:S(2)}) collective-permute-start(bf16[2,10,16,384]{3,2,1,0:T(8,128)(2,1)S(1)} %constant_dynamic-update-slice_fusion.refs_2_), channel_id=1, source_target_pairs={{0,8},{2,6},{8,16},{10,2},{16,24},{18,10},{24,28},{26,18},{28,20},... | collective-permute-start | bytes 737288 | tf_op jit(solution)/shard_map/ppermute | solution.py:114
  39.4 1.0 fusion.9
  40.4 3.2 %collective-permute-done.19.refs_3_ = bf16[2,10,16,384]{3,2,1,0:T(8,128)(2,1)S(1)} collective-permute-done((bf16[2,10,16,384]{3,2,1,0:T(8,128)(2,1)S(1)}, bf16[2,10,16,384]{3,2,1,0:T(8,128)(2,1)S(1)}, u32[]{:S(2)}, u32[]{:S(2)}) %collective-permute-start.19) | collective-permute-done | bytes 245792 | tf_op jit(solution)/shard_map/ppermute | solution.py:114
  43.6 1.4 collective-permute-start.22
  45.0 1.2 collective-permute-start.26
  46.3 1.1 collective-permute-start.5
  47.5 1.5 %collective-permute-done.20.refs_4_ = bf16[2,10,16,384]{3,2,1,0:T(8,128)(2,1)S(1)} collective-permute-done((bf16[2,10,16,384]{3,2,1,0:T(8,128)(2,1)S(1)}, bf16[2,10,16,384]{3,2,1,0:T(8,128)(2,1)S(1)}, u32[]{:S(2)}, u32[]{:S(2)}) %collective-permute-start.20) | collective-permute-done | bytes 245792 | tf_op jit(solution)/shard_map/ppermute | solution.py:114
  49.0 0.7 slice.152
  49.9 0.7 maximum_bitcast_fusion.3
  50.6 2.0 %collective-permute-start.23 = (bf16[2,10,16,384]{3,2,1,0:T(8,128)(2,1)S(1)}, bf16[2,10,16,384]{3,2,1,0:T(8,128)(2,1)S(1)}, u32[]{:S(2)}, u32[]{:S(2)}) collective-permute-start(bf16[2,10,16,384]{3,2,1,0:T(8,128)(2,1)S(1)} %collective-permute-done.19.refs_3_), channel_id=1, source_target_pairs={{0,2},{2,0},{4,6},{6,4},{8,10},{10,8},{12,14},{14,12},{16,18},{18,... | collective-permute-start | bytes 737288 | tf_op jit(solution)/shard_map/ppermute | solution.py:116
  52.6 0.6 collective-permute-start.24
  53.2 1.5 copy.20
  54.6 0.9 reshape.28
  55.7 1.8 %collective-permute-start.6 = (bf16[1,10,16,384]{3,2,1,0:T(8,128)(2,1)S(1)}, bf16[1,10,16,384]{3,2,1,0:T(8,128)(2,1)S(1)}, u32[]{:S(2)}, u32[]{:S(2)}) collective-permute-start(bf16[1,10,16,384]{3,2,1,0:T(8,128)(2,1)S(1)} %slice.144), channel_id=1, source_target_pairs={{0,8},{2,6},{8,16},{10,2},{16,24},{18,10},{24,28},{26,18},{28,20},... | collective-permute-start | bytes 368648 | tf_op jit(solution)/shard_map/ppermute | solution.py:114
  57.5 0.6 collective-permute-start.25
  58.2 0.8 dynamic-slice_bitcast_fusion.2
  59.1 1.0 collective-permute-done.6.refs_5_
  60.1 0.5 collective-permute-start.8
  60.7 1.2 collective-permute-start.11
  62.4 1.5 %copy-done.3 = s32[1,5,384,256]{3,2,1,0:T(8,128)S(1)} copy-done((s32[1,5,384,256]{3,2,1,0:T(8,128)S(1)}, s32[1,5,384,256]{3,2,1,0:T(8,128)}, u32[]{:S(2)}) %copy-start.3) | copy-done | bytes 1966104
  64.0 0.9 copy-done.6
  64.9 1.0 copy-done.8
  65.9 0.9 copy-done.9
  66.8 13.1 %gradient.3 = (bf16[2,10,16,384]{3,2,1,0:T(8,128)(2,1)S(1)}, bf16[7,10,16,384]{3,2,1,0:T(8,128)(2,1)S(1)}, bf16[7,10,16,384]{3,2,1,0:T(8,128)(2,1)S(1)}) custom-call(s32[33]{0:T(128)S(1)} %concatenate.32.slabs, bf16[1,10,16,384]{3,2,1,0:T(8,128)(2,1)S(1)} %get-tuple-element.35.refs_0_, bf16[1,10,16,384]{3,2,1,0:T(8,128)(2,1)S(1)} %copy-done.6, ...), custom_call_target="tpu_custom_call" | custom-call | flops 10066329600 | bytes 8388608 | tf_op jit(solution)/shard_map/gradient/pallas_call | solution.py:252
  80.4 13.2 %gradient.2 = (bf16[2,10,16,384]{3,2,1,0:T(8,128)(2,1)S(1)}, bf16[7,10,16,384]{3,2,1,0:T(8,128)(2,1)S(1)}, bf16[7,10,16,384]{3,2,1,0:T(8,128)(2,1)S(1)}) custom-call(s32[33]{0:T(128)S(1)} %concatenate.32.slabs, bf16[1,10,16,384]{3,2,1,0:T(8,128)(2,1)S(1)} %get-tuple-element.36.refs_0_, bf16[1,10,16,384]{3,2,1,0:T(8,128)(2,1)S(1)} %collective-permute-done.refs_1_, ...), custom_call_target="tpu_custom_call" | custom-call | flops 10066329600 | bytes 8388608 | tf_op jit(solution)/shard_map/gradient/pallas_call | solution.py:252
  94.2 1.8 %collective-permute-start.28 = (bf16[1,10,16,384]{3,2,1,0:T(8,128)(2,1)S(1)}, bf16[1,10,16,384]{3,2,1,0:T(8,128)(2,1)S(1)}, u32[]{:S(2)}, u32[]{:S(2)}) collective-permute-start(bf16[1,10,16,384]{3,2,1,0:T(8,128)(2,1)S(1)} %add_convert_fusion.4), channel_id=1, source_target_pairs={{0,8},{2,6},{8,16},{10,2},{16,24},{18,10},{24,28},{26,18},{28,20},... | collective-permute-start | bytes 368648 | tf_op jit(solution)/shard_map/ppermute | solution.py:140
  96.1 1.8 %collective-permute-start.13 = (bf16[1,10,16,384]{3,2,1,0:T(8,128)(2,1)S(1)}, bf16[1,10,16,384]{3,2,1,0:T(8,128)(2,1)S(1)}, u32[]{:S(2)}, u32[]{:S(2)}) collective-permute-start(bf16[1,10,16,384]{3,2,1,0:T(8,128)(2,1)S(1)} %add_convert_fusion.5), channel_id=1, source_target_pairs={{0,8},{2,6},{8,16},{10,2},{16,24},{18,10},{24,28},{26,18},{28,20},... | collective-permute-start | bytes 368648 | tf_op jit(solution)/shard_map/ppermute | solution.py:140
  98.0 0.9 collective-permute-done.28
  99.0 1.2 collective-permute-start.29
  100.1 0.6 collective-permute-done.13
  100.8 1.2 collective-permute-start.14
  102.0 2.3 %collective-permute-done.29 = bf16[2,10,16,384]{3,2,1,0:T(8,128)(2,1)S(1)} collective-permute-done((bf16[2,10,16,384]{3,2,1,0:T(8,128)(2,1)S(1)}, bf16[2,10,16,384]{3,2,1,0:T(8,128)(2,1)S(1)}, u32[]{:S(2)}, u32[]{:S(2)}) %collective-permute-start.29) | collective-permute-done | bytes 245792 | tf_op jit(solution)/shard_map/ppermute | solution.py:140
  104.5 1.2 collective-permute-start.30
  105.6 1.4 collective-permute-done.14
  107.1 1.2 collective-permute-start.15
  108.2 1.6 %collective-permute-done.30 = bf16[2,10,16,384]{3,2,1,0:T(8,128)(2,1)S(1)} collective-permute-done((bf16[2,10,16,384]{3,2,1,0:T(8,128)(2,1)S(1)}, bf16[2,10,16,384]{3,2,1,0:T(8,128)(2,1)S(1)}, u32[]{:S(2)}, u32[]{:S(2)}) %collective-permute-start.30) | collective-permute-done | bytes 245792 | tf_op jit(solution)/shard_map/ppermute | solution.py:140
  110.0 1.2 collective-permute-start.31
  111.1 1.4 collective-permute-done.15
  112.6 1.2 collective-permute-start.16
  113.7 1.3 collective-permute-done.31
  115.1 2.9 %collective-permute-done.16 = bf16[2,10,16,384]{3,2,1,0:T(8,128)(2,1)S(1)} collective-permute-done((bf16[2,10,16,384]{3,2,1,0:T(8,128)(2,1)S(1)}, bf16[2,10,16,384]{3,2,1,0:T(8,128)(2,1)S(1)}, u32[]{:S(2)}, u32[]{:S(2)}) %collective-permute-start.16) | collective-permute-done | bytes 245792 | tf_op jit(solution)/shard_map/ppermute | solution.py:140
  118.1 3.1 %collective-permute-start.32 = (bf16[2,10,16,384]{3,2,1,0:T(8,128)(2,1)S(1)}, bf16[2,10,16,384]{3,2,1,0:T(8,128)(2,1)S(1)}, u32[]{:S(2)}, u32[]{:S(2)}) collective-permute-start(bf16[2,10,16,384]{3,2,1,0:T(8,128)(2,1)S(1)} %fusion.5), channel_id=1, source_target_pairs={{0,2},{2,0},{4,6},{6,4},{8,10},{10,8},{12,14},{14,12},{16,18},{18,... | collective-permute-start | bytes 737288 | tf_op jit(solution)/shard_map/ppermute | solution.py:505
  121.8 0.6 collective-permute-done.32.received
  122.4 0.7 update.1.refs_1_
  123.4 4.2 %collective-permute-start.33 = (bf16[2,10,2,384]{3,2,1,0:T(2,128)(2,1)S(1)}, bf16[2,10,2,384]{3,2,1,0:T(2,128)(2,1)S(1)}, u32[]{:S(2)}, u32[]{:S(2)}) collective-permute-start(bf16[2,10,2,384]{3,2,1,0:T(2,128)(2,1)S(1)} %get-tuple-element.34), channel_id=1, source_target_pairs={{0,2},{1,3},{2,4},{3,5},{4,6},{5,7},{6,8},{7,9},{8,10},{9,11},{10,... | collective-permute-start | bytes 92168 | tf_op jit(solution)/shard_map/ppermute | solution.py:518
  127.6 2.9 %collective-permute-start.35 = (bf16[2,10,2,384]{3,2,1,0:T(2,128)(2,1)S(1)}, bf16[2,10,2,384]{3,2,1,0:T(2,128)(2,1)S(1)}, u32[]{:S(2)}, u32[]{:S(2)}) collective-permute-start(bf16[2,10,2,384]{3,2,1,0:T(2,128)(2,1)S(1)} %get-tuple-element.34), channel_id=1, source_target_pairs={{0,3},{1,2},{2,5},{3,4},{4,7},{5,6},{6,9},{7,8},{8,11},{9,10},{10,... | collective-permute-start | bytes 92168 | tf_op jit(solution)/shard_map/ppermute | solution.py:518
  130.5 2.6 %collective-permute-start.34 = (bf16[2,10,2,384]{3,2,1,0:T(2,128)(2,1)S(1)}, bf16[2,10,2,384]{3,2,1,0:T(2,128)(2,1)S(1)}, u32[]{:S(2)}, u32[]{:S(2)}) collective-permute-start(bf16[2,10,2,384]{3,2,1,0:T(2,128)(2,1)S(1)} %get-tuple-element.33), channel_id=1, source_target_pairs={{2,0},{3,1},{4,2},{5,3},{6,4},{7,5},{8,6},{9,7},{10,8},{11,9},{12,... | collective-permute-start | bytes 92168 | tf_op jit(solution)/shard_map/ppermute | solution.py:520
  133.1 2.1 %collective-permute-start.37 = (bf16[2,10,2,384]{3,2,1,0:T(2,128)(2,1)S(1)}, bf16[2,10,2,384]{3,2,1,0:T(2,128)(2,1)S(1)}, u32[]{:S(2)}, u32[]{:S(2)}) collective-permute-start(bf16[2,10,2,384]{3,2,1,0:T(2,128)(2,1)S(1)} %get-tuple-element.33), channel_id=1, source_target_pairs={{2,1},{3,0},{4,3},{5,2},{6,5},{7,4},{8,7},{9,6},{10,9},{11,8},{12,... | collective-permute-start | bytes 92168 | tf_op jit(solution)/shard_map/ppermute | solution.py:520
  135.4 0.7 collective-permute-done.34.refs_2_
  136.1 3.1 %collective-permute-done.37.refs_5_ = bf16[2,10,2,384]{3,2,1,0:T(2,128)(2,1)S(1)} collective-permute-done((bf16[2,10,2,384]{3,2,1,0:T(2,128)(2,1)S(1)}, bf16[2,10,2,384]{3,2,1,0:T(2,128)(2,1)S(1)}, u32[]{:S(2)}, u32[]{:S(2)}) %collective-permute-start.37) | collective-permute-done | bytes 30752 | tf_op jit(solution)/shard_map/ppermute | solution.py:520
  139.2 8.9 %convolutions.1 = bf16[1,5,2,2,16,384]{5,4,3,2,1,0:T(8,128)(2,1)} custom-call(s32[2]{0:T(128)S(1)} %add_convert_fusion.6.ends, bf16[2,10,2,384]{3,2,1,0:T(2,128)(2,1)S(1)} %collective-permute-done.33.refs_0_, bf16[2,10,16,384]{3,2,1,0:T(8,128)(2,1)S(1)} %update.1.refs_1_, bf16[2,10,2,384]{3,2,1,0:T(2,128)(2,1)S(1)} %collective-permute-done.34.refs_2_, ...), custom_call_target="tpu_custom_call" | custom-call | flops 1585446912 | bytes 1048576 | tf_op jit(solution)/shard_map/convolutions/pallas_call | solution.py:424
  (92 shorter events, 4.3 us)
Async XLA Ops:
  6.0 1.4 collective-permute-start
  6.1 1.5 collective-permute-start.4
  7.6 32.8 %copy-start.5 = (bf16[1,10,16,384]{3,2,1,0:T(8,128)(2,1)}, bf16[1,10,16,384]{3,2,1,0:T(8,128)(2,1)S(1)}, u32[]{:S(2)}) copy-start(bf16[1,10,16,384]{3,2,1,0:T(8,128)(2,1)S(1)} %collective-permute-done.4.refs_1_) | copy-start | bytes 368644
  7.6 39.7 %copy-start.10 = (bf16[10,64,3,3,3]{1,4,3,2,0:T(4,128)(2,1)S(1)}, bf16[10,64,3,3,3]{1,4,3,2,0:T(4,128)(2,1)}, u32[]{:S(2)}) copy-start(bf16[10,64,3,3,3]{1,4,3,2,0:T(4,128)(2,1)} %param.22) | copy-start | bytes 103684
  7.6 31.8 %all-to-all-start = ((bf16[16,2,2,16,384]{4,3,2,1,0:T(8,128)(2,1)}), bf16[16,2,2,16,384]{4,3,2,1,0:T(8,128)(2,1)S(1)}, u32[]{:S(2)}, u32[]{:S(2)}) async-start(bf16[16,2,2,16,384]{4,3,2,1,0:T(8,128)(2,1)} %get-tuple-element.20), calls=%async_computation | async-start | bytes 1572864 | tf_op jit(solution)/shard_map/all_to_all | solution.py:492
  15.1 14.4 %collective-permute-start.17 = (bf16[1,10,16,384]{3,2,1,0:T(8,128)(2,1)S(1)}, bf16[1,10,16,384]{3,2,1,0:T(8,128)(2,1)S(1)}, u32[]{:S(2)}, u32[]{:S(2)}) collective-permute-start(bf16[1,10,16,384]{3,2,1,0:T(8,128)(2,1)S(1)} %get-tuple-element.35.refs_0_), channel_id=1, source_target_pairs={{0,8},{2,6},{8,16},{10,2},{16,24},{18,10},{24,28},{26,18},{28,20},... | collective-permute-start | bytes 368648 | tf_op jit(solution)/shard_map/ppermute | solution.py:103
  16.4 14.7 %collective-permute-start.1 = (bf16[1,10,16,384]{3,2,1,0:T(8,128)(2,1)S(1)}, bf16[1,10,16,384]{3,2,1,0:T(8,128)(2,1)S(1)}, u32[]{:S(2)}, u32[]{:S(2)}) collective-permute-start(bf16[1,10,16,384]{3,2,1,0:T(8,128)(2,1)S(1)} %get-tuple-element.36.refs_0_), channel_id=1, source_target_pairs={{0,8},{2,6},{8,16},{10,2},{16,24},{18,10},{24,28},{26,18},{28,20},... | collective-permute-start | bytes 368648 | tf_op jit(solution)/shard_map/ppermute | solution.py:103
  17.6 16.6 %collective-permute-start.18 = (bf16[1,10,16,384]{3,2,1,0:T(8,128)(2,1)S(1)}, bf16[1,10,16,384]{3,2,1,0:T(8,128)(2,1)S(1)}, u32[]{:S(2)}, u32[]{:S(2)}) collective-permute-start(bf16[1,10,16,384]{3,2,1,0:T(8,128)(2,1)S(1)} %collective-permute-done.4.refs_1_), channel_id=1, source_target_pairs={{0,8},{2,6},{8,16},{10,2},{16,24},{18,10},{24,28},{26,18},{28,20},... | collective-permute-start | bytes 368648 | tf_op jit(solution)/shard_map/ppermute | solution.py:111
  18.8 16.7 %collective-permute-start.2 = (bf16[1,10,16,384]{3,2,1,0:T(8,128)(2,1)S(1)}, bf16[1,10,16,384]{3,2,1,0:T(8,128)(2,1)S(1)}, u32[]{:S(2)}, u32[]{:S(2)}) collective-permute-start(bf16[1,10,16,384]{3,2,1,0:T(8,128)(2,1)S(1)} %collective-permute-done.refs_1_), channel_id=1, source_target_pairs={{0,8},{2,6},{8,16},{10,2},{16,24},{18,10},{24,28},{26,18},{28,20},... | collective-permute-start | bytes 368648 | tf_op jit(solution)/shard_map/ppermute | solution.py:111
  34.2 9.4 %collective-permute-start.19 = (bf16[2,10,16,384]{3,2,1,0:T(8,128)(2,1)S(1)}, bf16[2,10,16,384]{3,2,1,0:T(8,128)(2,1)S(1)}, u32[]{:S(2)}, u32[]{:S(2)}) collective-permute-start(bf16[2,10,16,384]{3,2,1,0:T(8,128)(2,1)S(1)} %constant_dynamic-update-slice_fusion.2.refs_2_), channel_id=1, source_target_pairs={{0,8},{2,6},{8,16},{10,2},{16,24},{18,10},{24,28},{26,18},{28,20},... | collective-permute-start | bytes 737288 | tf_op jit(solution)/shard_map/ppermute | solution.py:114
  35.5 10.7 %collective-permute-start.3 = (bf16[2,10,16,384]{3,2,1,0:T(8,128)(2,1)S(1)}, bf16[2,10,16,384]{3,2,1,0:T(8,128)(2,1)S(1)}, u32[]{:S(2)}, u32[]{:S(2)}) collective-permute-start(bf16[2,10,16,384]{3,2,1,0:T(8,128)(2,1)S(1)} %constant_dynamic-update-slice_fusion.refs_2_), channel_id=1, source_target_pairs={{0,8},{2,6},{8,16},{10,2},{16,24},{18,10},{24,28},{26,18},{28,20},... | collective-permute-start | bytes 737288 | tf_op jit(solution)/shard_map/ppermute | solution.py:114
  43.6 5.3 %collective-permute-start.20 = (bf16[2,10,16,384]{3,2,1,0:T(8,128)(2,1)S(1)}, bf16[2,10,16,384]{3,2,1,0:T(8,128)(2,1)S(1)}, u32[]{:S(2)}, u32[]{:S(2)}) collective-permute-start(bf16[2,10,16,384]{3,2,1,0:T(8,128)(2,1)S(1)} %collective-permute-done.19.refs_3_), channel_id=1, source_target_pairs={{0,8},{2,6},{8,16},{10,2},{16,24},{18,10},{24,28},{26,18},{28,20},... | collective-permute-start | bytes 737288 | tf_op jit(solution)/shard_map/ppermute | solution.py:114
  43.6 12.1 %collective-permute-start.22 = (bf16[2,10,16,384]{3,2,1,0:T(8,128)(2,1)S(1)}, bf16[2,10,16,384]{3,2,1,0:T(8,128)(2,1)S(1)}, u32[]{:S(2)}, u32[]{:S(2)}) collective-permute-start(bf16[2,10,16,384]{3,2,1,0:T(8,128)(2,1)S(1)} %constant_dynamic-update-slice_fusion.2.refs_2_), channel_id=1, source_target_pairs={{0,2},{2,0},{4,6},{6,4},{8,10},{10,8},{12,14},{14,12},{16,18},{18,... | collective-permute-start | bytes 737288 | tf_op jit(solution)/shard_map/ppermute | solution.py:116
  45.0 15.6 %collective-permute-start.26 = (bf16[16,1,2,16,384]{4,3,2,1,0:T(8,128)(2,1)}, bf16[16,1,2,16,384]{4,3,2,1,0:T(8,128)(2,1)S(1)}, u32[]{:S(2)}, u32[]{:S(2)}) collective-permute-start(bf16[16,1,2,16,384]{4,3,2,1,0:T(8,128)(2,1)} %get-tuple-element.31), channel_id=1, source_target_pairs={{0,1},{1,0},{2,3},{3,2},{4,5},{5,4},{6,7},{7,6},{8,9},{9,8},{10,11... | collective-permute-start | bytes 1179656 | tf_op jit(solution)/shard_map/ppermute | solution.py:497
  46.3 6.3 %collective-permute-start.5 = (bf16[2,10,16,384]{3,2,1,0:T(8,128)(2,1)S(1)}, bf16[2,10,16,384]{3,2,1,0:T(8,128)(2,1)S(1)}, u32[]{:S(2)}, u32[]{:S(2)}) collective-permute-start(bf16[2,10,16,384]{3,2,1,0:T(8,128)(2,1)S(1)} %collective-permute-done.3.refs_3_), channel_id=1, source_target_pairs={{0,8},{2,6},{8,16},{10,2},{16,24},{18,10},{24,28},{26,18},{28,20},... | collective-permute-start | bytes 737288 | tf_op jit(solution)/shard_map/ppermute | solution.py:114
  49.6 7.9 %collective-permute-start.21 = (bf16[1,10,16,384]{3,2,1,0:T(8,128)(2,1)}, bf16[1,10,16,384]{3,2,1,0:T(8,128)(2,1)}, u32[]{:S(2)}, u32[]{:S(2)}) collective-permute-start(bf16[1,10,16,384]{3,2,1,0:T(8,128)(2,1)} %slice.152), channel_id=1, source_target_pairs={{0,8},{2,6},{8,16},{10,2},{16,24},{18,10},{24,28},{26,18},{28,20},... | collective-permute-start | bytes 368648 | tf_op jit(solution)/shard_map/ppermute | solution.py:114
  50.6 8.4 %collective-permute-start.23 = (bf16[2,10,16,384]{3,2,1,0:T(8,128)(2,1)S(1)}, bf16[2,10,16,384]{3,2,1,0:T(8,128)(2,1)S(1)}, u32[]{:S(2)}, u32[]{:S(2)}) collective-permute-start(bf16[2,10,16,384]{3,2,1,0:T(8,128)(2,1)S(1)} %collective-permute-done.19.refs_3_), channel_id=1, source_target_pairs={{0,2},{2,0},{4,6},{6,4},{8,10},{10,8},{12,14},{14,12},{16,18},{18,... | collective-permute-start | bytes 737288 | tf_op jit(solution)/shard_map/ppermute | solution.py:116
  52.6 9.6 %collective-permute-start.24 = (bf16[2,10,16,384]{3,2,1,0:T(8,128)(2,1)S(1)}, bf16[2,10,16,384]{3,2,1,0:T(8,128)(2,1)}, u32[]{:S(2)}, u32[]{:S(2)}) collective-permute-start(bf16[2,10,16,384]{3,2,1,0:T(8,128)(2,1)S(1)} %collective-permute-done.20.refs_4_), channel_id=1, source_target_pairs={{0,2},{2,0},{4,6},{6,4},{8,10},{10,8},{12,14},{14,12},{16,18},{18,... | collective-permute-start | bytes 737288 | tf_op jit(solution)/shard_map/ppermute | solution.py:116
  55.7 4.4 %collective-permute-start.6 = (bf16[1,10,16,384]{3,2,1,0:T(8,128)(2,1)S(1)}, bf16[1,10,16,384]{3,2,1,0:T(8,128)(2,1)S(1)}, u32[]{:S(2)}, u32[]{:S(2)}) collective-permute-start(bf16[1,10,16,384]{3,2,1,0:T(8,128)(2,1)S(1)} %slice.144), channel_id=1, source_target_pairs={{0,8},{2,6},{8,16},{10,2},{16,24},{18,10},{24,28},{26,18},{28,20},... | collective-permute-start | bytes 368648 | tf_op jit(solution)/shard_map/ppermute | solution.py:114
  57.5 4.4 %collective-permute-start.25 = (bf16[1,10,16,384]{3,2,1,0:T(8,128)(2,1)}, bf16[1,10,16,384]{3,2,1,0:T(8,128)(2,1)S(1)}, u32[]{:S(2)}, u32[]{:S(2)}) collective-permute-start(bf16[1,10,16,384]{3,2,1,0:T(8,128)(2,1)} %collective-permute-done.21.refs_5_), channel_id=1, source_target_pairs={{0,2},{2,0},{4,6},{6,4},{8,10},{10,8},{12,14},{14,12},{16,18},{18,... | collective-permute-start | bytes 368648 | tf_op jit(solution)/shard_map/ppermute | solution.py:116
  59.0 21.0 %collective-permute-start.7 = (bf16[2,10,16,384]{3,2,1,0:T(8,128)(2,1)S(1)}, bf16[2,10,16,384]{3,2,1,0:T(8,128)(2,1)S(1)}, u32[]{:S(2)}, u32[]{:S(2)}) collective-permute-start(bf16[2,10,16,384]{3,2,1,0:T(8,128)(2,1)S(1)} %constant_dynamic-update-slice_fusion.refs_2_), channel_id=1, source_target_pairs={{0,2},{2,0},{4,6},{6,4},{8,10},{10,8},{12,14},{14,12},{16,18},{18,... | collective-permute-start | bytes 737288 | tf_op jit(solution)/shard_map/ppermute | solution.py:116
  60.1 20.2 %collective-permute-start.8 = (bf16[2,10,16,384]{3,2,1,0:T(8,128)(2,1)S(1)}, bf16[2,10,16,384]{3,2,1,0:T(8,128)(2,1)S(1)}, u32[]{:S(2)}, u32[]{:S(2)}) collective-permute-start(bf16[2,10,16,384]{3,2,1,0:T(8,128)(2,1)S(1)} %collective-permute-done.3.refs_3_), channel_id=1, source_target_pairs={{0,2},{2,0},{4,6},{6,4},{8,10},{10,8},{12,14},{14,12},{16,18},{18,... | collective-permute-start | bytes 737288 | tf_op jit(solution)/shard_map/ppermute | solution.py:116
  60.7 19.7 %collective-permute-start.11 = (bf16[16,1,2,16,384]{4,3,2,1,0:T(8,128)(2,1)}, bf16[16,1,2,16,384]{4,3,2,1,0:T(8,128)(2,1)S(1)}, u32[]{:S(2)}, u32[]{:S(2)}) collective-permute-start(bf16[16,1,2,16,384]{4,3,2,1,0:T(8,128)(2,1)} %get-tuple-element.32), channel_id=1, source_target_pairs={{0,1},{1,0},{2,3},{3,2},{4,5},{5,4},{6,7},{7,6},{8,9},{9,8},{10,11... | collective-permute-start | bytes 1179656 | tf_op jit(solution)/shard_map/ppermute | solution.py:497
  61.9 18.5 %collective-permute-start.9 = (bf16[2,10,16,384]{3,2,1,0:T(8,128)(2,1)S(1)}, bf16[2,10,16,384]{3,2,1,0:T(8,128)(2,1)S(1)}, u32[]{:S(2)}, u32[]{:S(2)}) collective-permute-start(bf16[2,10,16,384]{3,2,1,0:T(8,128)(2,1)S(1)} %collective-permute-done.5.refs_4_), channel_id=1, source_target_pairs={{0,2},{2,0},{4,6},{6,4},{8,10},{10,8},{12,14},{14,12},{16,18},{18,... | collective-permute-start | bytes 737288 | tf_op jit(solution)/shard_map/ppermute | solution.py:116
  62.2 18.2 %collective-permute-start.10 = (bf16[1,10,16,384]{3,2,1,0:T(8,128)(2,1)S(1)}, bf16[1,10,16,384]{3,2,1,0:T(8,128)(2,1)S(1)}, u32[]{:S(2)}, u32[]{:S(2)}) collective-permute-start(bf16[1,10,16,384]{3,2,1,0:T(8,128)(2,1)S(1)} %collective-permute-done.6.refs_5_), channel_id=1, source_target_pairs={{0,2},{2,0},{4,6},{6,4},{8,10},{10,8},{12,14},{14,12},{16,18},{18,... | collective-permute-start | bytes 368648 | tf_op jit(solution)/shard_map/ppermute | solution.py:116
  62.4 1.5 %copy-start.3 = (s32[1,5,384,256]{3,2,1,0:T(8,128)S(1)}, s32[1,5,384,256]{3,2,1,0:T(8,128)}, u32[]{:S(2)}) copy-start(s32[1,5,384,256]{3,2,1,0:T(8,128)} %refs_13_.3) | copy-start | bytes 5898244
  64.0 0.9 copy-start.6
  64.9 1.0 copy-start.8
  65.9 0.9 copy-start.9
  66.8 13.6 %copy-start.4 = (s32[1,5,384,256]{3,2,1,0:T(8,128)S(1)}, s32[1,5,384,256]{3,2,1,0:T(8,128)}, u32[]{:S(2)}) copy-start(s32[1,5,384,256]{3,2,1,0:T(8,128)} %refs_13_.3) | copy-start | bytes 5898244
  80.0 14.2 %collective-permute-start.27 = (bf16[7,10,16,384]{3,2,1,0:T(8,128)(2,1)S(1)}, bf16[7,10,16,384]{3,2,1,0:T(8,128)(2,1)S(1)}, u32[]{:S(2)}, u32[]{:S(2)}) collective-permute-start(bf16[7,10,16,384]{3,2,1,0:T(8,128)(2,1)S(1)} %get-tuple-element.30), channel_id=1, source_target_pairs={{0,2},{2,0},{4,6},{6,4},{8,10},{10,8},{12,14},{14,12},{16,18},{18,... | collective-permute-start | bytes 2580488 | tf_op jit(solution)/shard_map/ppermute | solution.py:125
  93.5 2.5 %collective-permute-start.12 = (bf16[7,10,16,384]{3,2,1,0:T(8,128)(2,1)S(1)}, bf16[7,10,16,384]{3,2,1,0:T(8,128)(2,1)S(1)}, u32[]{:S(2)}, u32[]{:S(2)}) collective-permute-start(bf16[7,10,16,384]{3,2,1,0:T(8,128)(2,1)S(1)} %get-tuple-element.25), channel_id=1, source_target_pairs={{0,2},{2,0},{4,6},{6,4},{8,10},{10,8},{12,14},{14,12},{16,18},{18,... | collective-permute-start | bytes 2580488 | tf_op jit(solution)/shard_map/ppermute | solution.py:125
  94.2 4.7 %collective-permute-start.28 = (bf16[1,10,16,384]{3,2,1,0:T(8,128)(2,1)S(1)}, bf16[1,10,16,384]{3,2,1,0:T(8,128)(2,1)S(1)}, u32[]{:S(2)}, u32[]{:S(2)}) collective-permute-start(bf16[1,10,16,384]{3,2,1,0:T(8,128)(2,1)S(1)} %add_convert_fusion.4), channel_id=1, source_target_pairs={{0,8},{2,6},{8,16},{10,2},{16,24},{18,10},{24,28},{26,18},{28,20},... | collective-permute-start | bytes 368648 | tf_op jit(solution)/shard_map/ppermute | solution.py:140
  96.1 4.7 %collective-permute-start.13 = (bf16[1,10,16,384]{3,2,1,0:T(8,128)(2,1)S(1)}, bf16[1,10,16,384]{3,2,1,0:T(8,128)(2,1)S(1)}, u32[]{:S(2)}, u32[]{:S(2)}) collective-permute-start(bf16[1,10,16,384]{3,2,1,0:T(8,128)(2,1)S(1)} %add_convert_fusion.5), channel_id=1, source_target_pairs={{0,8},{2,6},{8,16},{10,2},{16,24},{18,10},{24,28},{26,18},{28,20},... | collective-permute-start | bytes 368648 | tf_op jit(solution)/shard_map/ppermute | solution.py:140
  99.0 5.4 %collective-permute-start.29 = (bf16[2,10,16,384]{3,2,1,0:T(8,128)(2,1)S(1)}, bf16[2,10,16,384]{3,2,1,0:T(8,128)(2,1)S(1)}, u32[]{:S(2)}, u32[]{:S(2)}) collective-permute-start(bf16[2,10,16,384]{3,2,1,0:T(8,128)(2,1)S(1)} %pad_maximum_fusion.2), channel_id=1, source_target_pairs={{0,8},{2,6},{8,16},{10,2},{16,24},{18,10},{24,28},{26,18},{28,20},... | collective-permute-start | bytes 737288 | tf_op jit(solution)/shard_map/ppermute | solution.py:140
  100.8 6.2 %collective-permute-start.14 = (bf16[2,10,16,384]{3,2,1,0:T(8,128)(2,1)S(1)}, bf16[2,10,16,384]{3,2,1,0:T(8,128)(2,1)S(1)}, u32[]{:S(2)}, u32[]{:S(2)}) collective-permute-start(bf16[2,10,16,384]{3,2,1,0:T(8,128)(2,1)S(1)} %pad_maximum_fusion.1), channel_id=1, source_target_pairs={{0,8},{2,6},{8,16},{10,2},{16,24},{18,10},{24,28},{26,18},{28,20},... | collective-permute-start | bytes 737288 | tf_op jit(solution)/shard_map/ppermute | solution.py:140
  104.5 5.4 %collective-permute-start.30 = (bf16[2,10,16,384]{3,2,1,0:T(8,128)(2,1)S(1)}, bf16[2,10,16,384]{3,2,1,0:T(8,128)(2,1)S(1)}, u32[]{:S(2)}, u32[]{:S(2)}) collective-permute-start(bf16[2,10,16,384]{3,2,1,0:T(8,128)(2,1)S(1)} %add_convert_fusion.1), channel_id=1, source_target_pairs={{0,8},{2,6},{8,16},{10,2},{16,24},{18,10},{24,28},{26,18},{28,20},... | collective-permute-start | bytes 737288 | tf_op jit(solution)/shard_map/ppermute | solution.py:140
  107.1 5.4 %collective-permute-start.15 = (bf16[2,10,16,384]{3,2,1,0:T(8,128)(2,1)S(1)}, bf16[2,10,16,384]{3,2,1,0:T(8,128)(2,1)S(1)}, u32[]{:S(2)}, u32[]{:S(2)}) collective-permute-start(bf16[2,10,16,384]{3,2,1,0:T(8,128)(2,1)S(1)} %add_convert_fusion.3), channel_id=1, source_target_pairs={{0,8},{2,6},{8,16},{10,2},{16,24},{18,10},{24,28},{26,18},{28,20},... | collective-permute-start | bytes 737288 | tf_op jit(solution)/shard_map/ppermute | solution.py:140
  110.0 11.3 %copy-start.11 = (f32[64]{0:T(128)S(1)}, f32[64]{0:T(128)}, u32[]{:S(2)}) copy-start(f32[64]{0:T(128)} %param.21) | copy-start | bytes 772
  110.0 5.1 %collective-permute-start.31 = (bf16[2,10,16,384]{3,2,1,0:T(8,128)(2,1)S(1)}, bf16[2,10,16,384]{3,2,1,0:T(8,128)(2,1)S(1)}, u32[]{:S(2)}, u32[]{:S(2)}) collective-permute-start(bf16[2,10,16,384]{3,2,1,0:T(8,128)(2,1)S(1)} %add_convert_fusion), channel_id=1, source_target_pairs={{0,8},{2,6},{8,16},{10,2},{16,24},{18,10},{24,28},{26,18},{28,20},... | collective-permute-start | bytes 737288 | tf_op jit(solution)/shard_map/ppermute | solution.py:140
  112.6 5.4 %collective-permute-start.16 = (bf16[2,10,16,384]{3,2,1,0:T(8,128)(2,1)S(1)}, bf16[2,10,16,384]{3,2,1,0:T(8,128)(2,1)S(1)}, u32[]{:S(2)}, u32[]{:S(2)}) collective-permute-start(bf16[2,10,16,384]{3,2,1,0:T(8,128)(2,1)S(1)} %add_convert_fusion.2), channel_id=1, source_target_pairs={{0,8},{2,6},{8,16},{10,2},{16,24},{18,10},{24,28},{26,18},{28,20},... | collective-permute-start | bytes 737288 | tf_op jit(solution)/shard_map/ppermute | solution.py:140
  118.1 4.4 %copy-start = (bf16[2,10,16,384]{3,2,1,0:T(8,128)(2,1)S(1)}, bf16[2,10,16,384]{3,2,1,0:T(8,128)(2,1)}, u32[]{:S(2)}) copy-start(bf16[2,10,16,384]{3,2,1,0:T(8,128)(2,1)} %get-tuple-element.18.image) | copy-start | bytes 737284
  118.1 4.3 %copy-start.1 = (bf16[384,384]{1,0:T(8,128)(2,1)S(1)}, bf16[384,384]{1,0:T(8,128)(2,1)}, u32[]{:S(2)}) copy-start(bf16[384,384]{1,0:T(8,128)(2,1)} %constant.203.clone.along_y) | copy-start | bytes 884740
  118.1 4.3 %copy-start.2 = (bf16[128,128]{1,0:T(8,128)(2,1)S(1)}, bf16[128,128]{1,0:T(8,128)(2,1)}, u32[]{:S(2)}) copy-start(bf16[128,128]{1,0:T(8,128)(2,1)} %constant.202.clone.along_z) | copy-start | bytes 98308
  118.1 4.3 %collective-permute-start.32 = (bf16[2,10,16,384]{3,2,1,0:T(8,128)(2,1)S(1)}, bf16[2,10,16,384]{3,2,1,0:T(8,128)(2,1)S(1)}, u32[]{:S(2)}, u32[]{:S(2)}) collective-permute-start(bf16[2,10,16,384]{3,2,1,0:T(8,128)(2,1)S(1)} %fusion.5), channel_id=1, source_target_pairs={{0,2},{2,0},{4,6},{6,4},{8,10},{10,8},{12,14},{14,12},{16,18},{18,... | collective-permute-start | bytes 737288 | tf_op jit(solution)/shard_map/ppermute | solution.py:505
  121.4 17.8 %copy-start.7 = (f32[10]{0:T(128)S(1)}, f32[10]{0:T(128)}, u32[]{:S(2)}) copy-start(f32[10]{0:T(128)} %refs_9_.1) | copy-start | bytes 124
  123.1 16.1 %collective-permute-start.36 = (bf16[2,10,16,384]{3,2,1,0:T(8,128)(2,1)S(1)}, bf16[2,10,16,384]{3,2,1,0:T(8,128)(2,1)S(1)}, u32[]{:S(2)}, u32[]{:S(2)}) collective-permute-start(bf16[2,10,16,384]{3,2,1,0:T(8,128)(2,1)S(1)} %update.1.refs_1_), channel_id=1, source_target_pairs={{0,1},{1,0},{2,3},{3,2},{4,5},{5,4},{6,7},{7,6},{8,9},{9,8},{10,11... | collective-permute-start | bytes 737288 | tf_op jit(solution)/shard_map/ppermute | solution.py:519
  123.4 12.0 %collective-permute-start.33 = (bf16[2,10,2,384]{3,2,1,0:T(2,128)(2,1)S(1)}, bf16[2,10,2,384]{3,2,1,0:T(2,128)(2,1)S(1)}, u32[]{:S(2)}, u32[]{:S(2)}) collective-permute-start(bf16[2,10,2,384]{3,2,1,0:T(2,128)(2,1)S(1)} %get-tuple-element.34), channel_id=1, source_target_pairs={{0,2},{1,3},{2,4},{3,5},{4,6},{5,7},{6,8},{7,9},{8,10},{9,11},{10,... | collective-permute-start | bytes 92168 | tf_op jit(solution)/shard_map/ppermute | solution.py:518
  127.6 8.5 %collective-permute-start.35 = (bf16[2,10,2,384]{3,2,1,0:T(2,128)(2,1)S(1)}, bf16[2,10,2,384]{3,2,1,0:T(2,128)(2,1)S(1)}, u32[]{:S(2)}, u32[]{:S(2)}) collective-permute-start(bf16[2,10,2,384]{3,2,1,0:T(2,128)(2,1)S(1)} %get-tuple-element.34), channel_id=1, source_target_pairs={{0,3},{1,2},{2,5},{3,4},{4,7},{5,6},{6,9},{7,8},{8,11},{9,10},{10,... | collective-permute-start | bytes 92168 | tf_op jit(solution)/shard_map/ppermute | solution.py:518
  130.5 5.6 %collective-permute-start.34 = (bf16[2,10,2,384]{3,2,1,0:T(2,128)(2,1)S(1)}, bf16[2,10,2,384]{3,2,1,0:T(2,128)(2,1)S(1)}, u32[]{:S(2)}, u32[]{:S(2)}) collective-permute-start(bf16[2,10,2,384]{3,2,1,0:T(2,128)(2,1)S(1)} %get-tuple-element.33), channel_id=1, source_target_pairs={{2,0},{3,1},{4,2},{5,3},{6,4},{7,5},{8,6},{9,7},{10,8},{11,9},{12,... | collective-permute-start | bytes 92168 | tf_op jit(solution)/shard_map/ppermute | solution.py:520
  133.1 6.1 %collective-permute-start.37 = (bf16[2,10,2,384]{3,2,1,0:T(2,128)(2,1)S(1)}, bf16[2,10,2,384]{3,2,1,0:T(2,128)(2,1)S(1)}, u32[]{:S(2)}, u32[]{:S(2)}) collective-permute-start(bf16[2,10,2,384]{3,2,1,0:T(2,128)(2,1)S(1)} %get-tuple-element.33), channel_id=1, source_target_pairs={{2,1},{3,0},{4,3},{5,2},{6,5},{7,4},{8,7},{9,6},{10,9},{11,8},{12,... | collective-permute-start | bytes 92168 | tf_op jit(solution)/shard_map/ppermute | solution.py:520

commit v3 on v2

--- a/solution.py
+++ b/solution.py
@@ -40,7 +40,7 @@
         if left:
             piece = piece.transpose(2, 3, 0, 1)
         out.append(piece.reshape(2 * part, 2 * part))
-    return jnp.asarray(np.stack(out))
+    return np.stack(out)
 
 
 def order(length, count):
@@ -155,8 +155,9 @@
 def gradient_kernel(images, coils, slabs, *refs):
     held_images, refs = refs[:images], refs[images:]
     maps, refs = refs[:coils], refs[coils:]
-    measured, sampling, ty_f, tz_f, tz_i, ty_i = refs[:6]
-    out, products, backs = refs[6:9], refs[9], refs[10]
+    measured, sampling, tables = refs[:3]
+    out, products, backs = refs[3:6], refs[6], refs[7]
+    ty_f, tz_f, tz_i, ty_i = [0, 1, 2], [3, 4], [5, 6], [7, 8, 9]
     rows, ny = held_images[0].shape[-2:]
     nz = sampling.shape[-1]
     count, half = nz // rows, rows // 2
@@ -181,11 +182,11 @@
             (low[0] + turn[1], low[1] - turn[0]),
         )
 
-    for k, (held, i) in enumerate(pieces(held_images)):
-        slab = slabs[k]
-        real = held[i, 0].astype(F32)
-        imag = held[i, 1].astype(F32)
-        for c in range(coils):
+    def product(c):
+        for k, (held, i) in enumerate(pieces(held_images)):
+            slab = slabs[k]
+            real = held[i, 0].astype(F32)
+            imag = held[i, 1].astype(F32)
             m_real = maps[c][slab, 0, 0].astype(F32)
             m_imag = maps[c][slab, 0, 1].astype(F32)
             p_real = m_real * real - m_imag * imag
@@ -196,17 +197,24 @@
                     cells = slice(j * my, (j + 1) * my)
                     products[c, j, at, :my] = p_real[lines, cells]
                     products[c, j, at, my:] = p_imag[lines, cells]
-    mask = sampling[0, 0].astype(F32)
-    folds = [[], []]
-    for c in range(coils):
-        parts = [nt_dot(ty_f[j], products[c, j].astype(BF16)) for j in range(3)]
+
+    def to_frequency_y(c):
+        return [nt_dot(tables[ty_f[j]], products[c, j].astype(BF16)) for j in range(3)]
+
+    def spectra_of(parts):
         parts = thirds(*[(part[:my], part[my:]) for part in parts], -1.0)
-        spectra = [jnp.concatenate([part[q].astype(BF16) for part in parts], axis=0) for q in range(2)]
+        return [jnp.concatenate([part[q].astype(BF16) for part in parts], axis=0) for q in range(2)]
+
+    def to_frequency_z(spectra):
         halves = []
         for j in range(2):
             cells = slice(j * mz, (j + 1) * mz)
-            halves.append(nn_dot(jnp.concatenate([spectra[0][:, cells], spectra[1][:, cells]], axis=1), tz_f[j]))
+            halves.append(nn_dot(jnp.concatenate([spectra[0][:, cells], spectra[1][:, cells]], axis=1), tables[tz_f[j]]))
+        return halves
+
+    def residual_of(c, halves):
         coil = first if c == 0 else 1 - first
+        mask = sampling[0, 0].astype(F32)
         sums, differences = [], []
         for q in range(2):
             cells = slice(q * mz, (q + 1) * mz)
@@ -215,18 +223,39 @@
             high = mask[:, mz:] * (halves[0][:, cells] - halves[1][:, cells] - seen[:, mz:])
             sums.append((low + high).astype(BF16))
             differences.append((low - high).astype(BF16))
-        folds[0].append(jnp.concatenate(sums, axis=1))
-        folds[1].append(jnp.concatenate(differences, axis=1))
-    depths = [nt_dot(tz_i[j], jnp.concatenate(folds[j], axis=0)) for j in range(2)]
-    for c in range(coils):
+        return jnp.concatenate(sums, axis=1), jnp.concatenate(differences, axis=1)
+
+    def to_depth(folds):
+        return [nt_dot(tables[tz_i[j]], folds[j]) for j in range(2)]
+
+    def lines_of(depths):
         lines = [[], [], []]
         for j in range(2):
-            cut = lambda q, i: depths[j][q * mz : (q + 1) * mz, c * ny + i * my : c * ny + (i + 1) * my]
+            cut = lambda q, i: depths[j][q * mz : (q + 1) * mz, i * my : (i + 1) * my]
             turned = thirds(*[(cut(0, i), cut(1, i)) for i in range(3)], 1.0)
             for i in range(3):
                 lines[i].append(jnp.concatenate([turned[i][0].astype(BF16), turned[i][1].astype(BF16)], axis=1))
+        return [jnp.concatenate(line, axis=0) for line in lines]
+
+    def to_image(c, lines):
         for i in range(3):
-            backs[c, i] = nn_dot(jnp.concatenate(lines[i], axis=0), ty_i[i])
+            backs[c, i] = nn_dot(lines[i], tables[ty_i[i]])
+
+    stages = [
+        lambda c, _: product(c),
+        lambda c, _: to_frequency_y(c),
+        lambda c, value: spectra_of(value),
+        lambda c, value: to_frequency_z(value),
+        lambda c, value: residual_of(c, value),
+        lambda c, value: to_depth(value),
+        lambda c, value: lines_of(value),
+        lambda c, value: to_image(c, value),
+    ]
+    held_values = [None] * coils
+    for step in range(len(stages) + coils - 1):
+        for c in range(coils):
+            if 0 <= step - c < len(stages):
+                held_values[c] = stages[step - c](c, held_values[c])
     for k, (held, i) in enumerate(pieces(out)):
         slab = slabs[count + k]
         for j in range(3):
@@ -264,7 +293,7 @@
                 pl.BlockSpec((1, 2, 1, 2, 1, ny, nz), lambda e, s: (0, 0, e, 0, x, 0, 0)),
                 pl.BlockSpec((1, 1, ny, nz), lambda e, s: (0, e, 0, 0)),
             ]
-            + [whole(t) for t in tables],
+            + [whole(tables)],
             out_specs=[pl.BlockSpec((m, 2, rows, ny), lambda e, s: (0, e, 0, 0)) for m in (2, far, far)],
             scratch_shapes=[
                 pltpu.VMEM((n, 3, nz, 2 * ny // 3), F32),
@@ -275,7 +304,7 @@
         compiler_params=pltpu.CompilerParams(vmem_limit_bytes=40 * 2**20),
         cost_estimate=pl.CostEstimate(flops=flops, bytes_accessed=8 * 2**20, transcendentals=0),
         name="gradient",
-    )(where, *images, *[a for a, _ in maps], measured, sampling, *tables)
+    )(where, *images, *[a for a, _ in maps], measured, sampling, tables)
 
 
 def reordered(value, along_z, along_y):
@@ -295,51 +324,54 @@
     return jnp.asarray(along_z, BF16), jnp.asarray(y.T if back else y, BF16)
 
 
-def prepare_kernel(which, image, maps, along_z, along_y, image_out, maps_out):
-    width, channels, rows, ny = image_out.shape
-
-    @pl.when(pl.program_id(0) == 0)
-    def _():
-        picked = image[...].reshape((channels, width, rows, ny))
-        for x in range(width):
-            image_out[x] = reordered(picked[:, x], along_z[...], along_y[...])
-
-    count = maps_out.shape[0]
+def prepare_image_kernel(image, along_z, along_y, earlier, out):
+    width, channels, rows, ny = out.shape
+    picked = image[...].reshape((channels, width, rows, ny))
+    for x in range(width):
+        out[x] = reordered(picked[:, x], along_z[...], along_y[...])
+
+
+def prepare_image(current_image, earlier):
+    _, encodings, _, width, rows, ny = current_image.shape
+    vmem = pl.BlockSpec(memory_space=pltpu.VMEM)
+    return pl.pallas_call(
+        prepare_image_kernel,
+        in_specs=[vmem, vmem, vmem, pl.BlockSpec(memory_space=pl.ANY)],
+        out_specs=vmem,
+        out_shape=jax.ShapeDtypeStruct((width, 2 * encodings, rows, ny), BF16),
+        compiler_params=pltpu.CompilerParams(vmem_limit_bytes=16 * 2**20),
+        name="prepare_image",
+    )(current_image, *orders(rows, ny, False), earlier)
+
+
+def prepare_maps_kernel(which, maps, along_z, along_y, out):
+    count, width, _, rows, ny = out.shape
     value = reordered(maps[:, 0].reshape((count * 2 * width, rows, ny)), along_z[...], along_y[...])
     for pair in range(count):
         for x in range(width):
             for part in range(2):
-                maps_out[pair, x, part] = value[(pair * 2 + part) * width + x]
-
-
-def prepare(which, current_image, coil_maps):
-    _, encodings, _, width, rows, ny = current_image.shape
-    devices = coil_maps.shape[0] // 2
+                out[pair, x, part] = value[(pair * 2 + part) * width + x]
+
+
+def prepare_maps(which, coil_maps):
+    coils, _, width, rows, ny = coil_maps.shape
+    devices = coils // 2
     pairs = coil_maps.reshape((devices, 2) + coil_maps.shape[1:])
-    whole = lambda shape: pl.BlockSpec(shape, lambda i, t: (0,) * len(shape))
     matrices = orders(rows, ny, False)
-    image_shape = (width, 2 * encodings, rows, ny)
-    steps = 4
-    group = (devices // steps, width, 2, rows, ny)
+    steps = 2
     return pl.pallas_call(
-        prepare_kernel,
+        prepare_maps_kernel,
         grid_spec=pltpu.PrefetchScalarGridSpec(
             num_scalar_prefetch=1,
             grid=(steps,),
-            in_specs=[
-                whole(current_image.shape),
-                pl.BlockSpec((devices // steps, 1) + coil_maps.shape[1:], lambda i, t: (i, t[0], 0, 0, 0, 0)),
-            ]
-            + [whole(m.shape) for m in matrices],
-            out_specs=[whole(image_shape), pl.BlockSpec(group, lambda i, t: (i, 0, 0, 0, 0))],
+            in_specs=[pl.BlockSpec((devices // steps, 1) + coil_maps.shape[1:], lambda i, t: (i, t[0], 0, 0, 0, 0))]
+            + [pl.BlockSpec(m.shape, lambda i, t: (0, 0)) for m in matrices],
+            out_specs=pl.BlockSpec((devices // steps, width, 2, rows, ny), lambda i, t: (i, 0, 0, 0, 0)),
         ),
-        out_shape=[
-            jax.ShapeDtypeStruct(image_shape, BF16),
-            jax.ShapeDtypeStruct((devices, width, 2, rows, ny), BF16),
-        ],
+        out_shape=jax.ShapeDtypeStruct((devices, width, 2, rows, ny), BF16),
         compiler_params=pltpu.CompilerParams(vmem_limit_bytes=58 * 2**20),
-        name="prepare",
-    )(which, current_image, pairs, *matrices)
+        name="prepare_maps",
+    )(which, pairs, *matrices)
 
 
 def update_kernel(image, chip, received, along_z, along_y, out):
@@ -378,16 +410,16 @@
 
 
 def convolution_kernel(ends, *refs):
-    sources, refs = (refs[:3], refs[3:6]), refs[6:]
+    sources, refs = refs[:2], refs[2:]
     w_first, b_first, w_second, b_second, out, stacked, result = refs
-    _, channels, rows, ny = sources[0][1].shape
-    depth = rows + 4
+    channels, depth, ny = sources[0].shape
+    rows = depth - 4
     group = stacked.shape[1] // depth
     lanes = result.shape[1] // rows
     stacked[...] = jnp.zeros_like(stacked)
     for t, source in enumerate(sources):
         for i in range(channels):
-            value = jnp.concatenate([part[0, i].astype(F32) for part in source], axis=0)
+            value = source[i].astype(F32)
             for d in range(3):
                 line = value if d == 1 else shifted(value, d - 1)
                 put_strided(stacked, (d * 2 + t) * channels + i, depth, group, line)
@@ -409,26 +441,23 @@
                 put_strided(result, 2 * pair - 2 + z, lanes, rows, line)
             partial = partial[1:]
     for i in range(channels):
-        value = sources[0][1][0, i].astype(F32)
-        out[0, i // 2, i % 2, 0] = (value + get_lines(result, i * rows, rows) + b_second[i]).astype(BF16)
-
-
-def convolutions(ends, parts, w_first, b_first, w_second, b_second, encodings):
-    width, channels, rows, ny = parts[1].shape
-    depth = rows + 4
+        value = sources[0][i].astype(F32)[2 : 2 + rows]
+        out[i] = (value + get_lines(result, i * rows, rows) + b_second[i]).astype(BF16)
+
+
+def convolutions(ends, own, other, w_first, b_first, w_second, b_second):
+    channels, depth, ny = own.shape
+    rows = depth - 4
     group = w_first.shape[1] // 4
     lanes = w_second.shape[0] // 12
+    vmem = pl.BlockSpec(memory_space=pltpu.VMEM)
     smem = pl.BlockSpec(memory_space=pltpu.SMEM)
-    whole = lambda a: pl.BlockSpec(a.shape, lambda x: (0,) * a.ndim)
-    flops = width * (rows + 2) * ny * (w_first.size + w_second.size)
+    flops = (rows + 2) * ny * (w_first.size + w_second.size)
     return pl.pallas_call(
         convolution_kernel,
-        grid=(width,),
-        in_specs=[smem]
-        + [pl.BlockSpec((1,) + a.shape[1:], lambda x: (x, 0, 0, 0)) for a in parts]
-        + [whole(w_first), whole(b_first), whole(w_second), smem],
-        out_specs=pl.BlockSpec((1, encodings, 2, 1, rows, ny), lambda x: (0, 0, 0, x, 0, 0)),
-        out_shape=jax.ShapeDtypeStruct((1, encodings, 2, width, rows, ny), BF16),
+        in_specs=[smem, vmem, vmem, vmem, vmem, vmem, smem],
+        out_specs=vmem,
+        out_shape=jax.ShapeDtypeStruct((channels, rows, ny), BF16),
         scratch_shapes=[
             pltpu.VMEM((ny // 128, depth * group, 128), F32),
             pltpu.VMEM((ny // 128, lanes * rows, 128), F32),
@@ -436,7 +465,7 @@
         compiler_params=pltpu.CompilerParams(vmem_limit_bytes=24 * 2**20),
         cost_estimate=pl.CostEstimate(flops=flops, bytes_accessed=2**20, transcendentals=0),
         name="convolutions",
-    )(ends, *parts, w_first, b_first, w_second, b_second)
+    )(ends, own, other, w_first, b_first, w_second, b_second)
 
 
 def round_up(value, unit):
@@ -475,52 +504,49 @@
     _, encodings, _, width, rows, ny = current_image.shape
     nz = rows * devices
     channels = 2 * encodings
-    tables = (
-        split_tables(ny, 3, True, False),
-        split_tables(nz, 2, False, False),
-        split_tables(nz, 2, True, True),
-        split_tables(ny, 3, False, True),
+    tables = jnp.asarray(
+        np.concatenate(
+            [
+                split_tables(ny, 3, True, False),
+                split_tables(nz, 2, False, False),
+                split_tables(nz, 2, True, True),
+                split_tables(ny, 3, False, True),
+            ]
+        )
     )
     which = q[None].astype(jnp.int32)
     where = jnp.concatenate([ring.slabs(), which])
     swap = [(0, 1), (1, 0)]
+    mask = sampling.astype(BF16)
     weights = convolution_weights(first_weight, first_bias, second_weight)
     ends = jnp.stack([me > 0, me < devices - 1]).astype(jnp.int32)
 
-    images, pairs = prepare(which, current_image, coil_maps)
+    pairs = prepare_maps(which, coil_maps)
+    images = prepare_image(current_image, pairs)
     gathers = [Gather(ring, images[x : x + 1]) for x in range(width)]
-    kept = lax.all_to_all(after(pairs, *[gather.own[1] for gather in gathers]), SLAB, split_axis=0, concat_axis=0, tiled=True)
+    kept = lax.all_to_all(pairs, SLAB, split_axis=0, concat_axis=0, tiled=True)
     halves = [kept[:, x : x + 1] for x in range(width)]
     for step in range(len(ring.steps())):
         for gather in gathers:
-            gather.step(*((halves[step - 2],) if 2 <= step < 2 + width else ()))
+            gather.step(*(weights + (mask,) if step == 1 else (halves[step - 2],) if 2 <= step < 2 + width else ()))
     swapped = [lax.ppermute(half, COIL, swap) for half in halves]
     scatters = []
     for x in range(width):
-        scatters.append(Scatter(ring, *gradient(where, gathers[x].pieces(), [(kept, x), (swapped[x], 0)], measured, sampling, tables, x)))
+        scatters.append(Scatter(ring, *gradient(where, gathers[x].pieces(), [(kept, x), (swapped[x], 0)], measured, mask, tables, x)))
     for _ in ring.steps():
         for scatter in scatters:
             scatter.step()
     chip = jnp.stack([scatter.chip() for scatter in scatters])
     updated = update(images, chip[:, 0], lax.ppermute(chip[:, 1].astype(BF16), SLAB, ring.siblings()))
-    both = (SLAB, COIL)
-    cross = lambda shift, flip: [
-        ((i * 2 + q), ((i + shift) * 2 + (q ^ flip)))
-        for i in range(devices)
-        for q in range(2)
-        if 0 <= i + shift < devices
-    ]
-    head, tail = updated[:, :, :2], updated[:, :, rows - 2 :]
-    phases = []
-    for flip in range(2):
-        phases.append(
-            [
-                lax.ppermute(tail, both, cross(1, flip)),
-                lax.ppermute(updated, both, cross(0, 1)) if flip else updated,
-                lax.ppermute(head, both, cross(-1, flip)),
-            ]
-        )
-    return convolutions(ends, phases[0] + phases[1], *weights, second_bias, encodings)
+    up = [(i, i + 1) for i in range(devices - 1)]
+    down = [(i + 1, i) for i in range(devices - 1)]
+    before = lax.ppermute(updated[:, :, rows - 2 :], SLAB, up)
+    behind = lax.ppermute(updated[:, :, :2], SLAB, down)
+    refined = []
+    for x in range(width):
+        bordered = jnp.concatenate([before[x], updated[x], behind[x]], axis=1)
+        refined.append(convolutions(ends, bordered, lax.ppermute(bordered, COIL, swap), *weights, second_bias))
+    return jnp.stack(refined, axis=1).reshape(current_image.shape)
 
 
 def with_halo(cells, sides, width):
@@ -637,12 +663,17 @@
     return refined.astype(jnp.bfloat16).reshape(updated.shape)
 
 
+def fits(shape, devices):
+    rows, ny = shape[4:]
+    return rows % 16 == 0 and ny % 384 == 0 and 2 * ny == 3 * rows * devices
+
+
 def solution(mesh):
     devices, phases = mesh.shape[SLAB], mesh.shape[COIL]
 
     def per_device(*args):
         coils, phase = args[2].shape[1], args[0].shape[0]
-        if phases == 2 and coils == 2 and phase == 1 and devices % 4 == 0 and args[0].shape[4] % 16 == 0 and args[0].shape[5] % 384 == 0:
+        if phases == 2 and coils == 2 and phase == 1 and devices % 4 == 0 and fits(args[0].shape, devices):
             return paired(*args)
         return on_device(*args)
 

time: 149 us -> 140 us (0.940)
  Pallas kernels: 40.9 us -> 37.1 us
  local copies, waits for them, and re-layouts: 11 us -> 7.53 us
  waiting for transfers between devices: 39 us -> 36 us
  other arithmetic: 1.98 us -> 3.93 us
    ppermute x8, waiting for transfers between devices: 12.4 us -> 7.79 us  [step(): self.held = lax.ppermute(total.astype(BF16), SLAB, self.ring.perm())]
    ppermute x5 -> x4, starting transfers between devices: 12 us -> 7.6 us  [the longest x1 3.9 us: paired(): before = lax.ppermute(updated[:, :, rows - 2:], SLAB, up)]
    ppermute x5 -> x4, waiting for transfers between devices: 3.78 us -> 8.1 us  [the longest x2 5.04 us: paired(): lax.ppermute(bordered, COIL, swap)]
    ppermute x2, waiting for transfers between devices: 11.1 us -> 7.37 us  [__init__(): self.first = lax.ppermute(mine, SLAB, ring.perm())]
    ppermute x8, starting transfers between devices: 10.6 us -> 14.3 us  [step(): self.held = lax.ppermute(total.astype(BF16), SLAB, self.ring.perm())]
    ppermute x6, waiting for transfers between devices: 5.77 us -> 9.22 us  [step(): lax.ppermute(after(held, *earlier) if earlier else held, SLAB, self.ring....]
    pallas_call x2, Pallas kernels: 26.3 us -> 23.8 us  [gradient(): pl.pallas_call(functools.partial(gradient_kernel, len(images), n), grid_s...]
    all_to_all x1, starting transfers between devices: 7.46 us -> 5.24 us  [paired(): kept = lax.all_to_all(pairs, SLAB, split_axis=0, concat_axis=0, tiled=True)]
  transfers between devices with their start and end apart: 39 -> 38, of which waited for: 20 -> 18; matrix products, arithmetic and copies ran while one was open for 5% -> 5% of each run, Pallas kernels for 18% -> 20%
where the time goes in v3:
time: 140 us
  starting transfers between devices  54.5 us (39%)
  Pallas kernels  37.1 us (26%)
  waiting for transfers between devices  36 us (26%)
  local copies, waits for them, and re-layouts  7.53 us (5%)
  other arithmetic  3.93 us (3%)
    pallas_call x2, Pallas kernels, gradient(): pl.pallas_call(functools.partial(gradient_kernel, len(images), n), grid_s...  23.8 us
    ppermute x8, starting transfers between devices, step(): self.held = lax.ppermute(total.astype(BF16), SLAB, self.ring.perm())  14.3 us
    ppermute x6, waiting for transfers between devices, step(): lax.ppermute(after(held, *earlier) if earlier else held, SLAB, self.ring....  9.22 us
    pallas_call x2, Pallas kernels, convolutions(): pl.pallas_call(convolution_kernel, in_specs=[smem, vmem, vmem, vmem, vmem...  8.85 us
    ppermute x6, starting transfers between devices, step(): lax.ppermute(after(held, *earlier) if earlier else held, SLAB, self.ring....  8.17 us
    ppermute x8, waiting for transfers between devices, step(): self.held = lax.ppermute(total.astype(BF16), SLAB, self.ring.perm())  7.79 us
    ppermute x2, waiting for transfers between devices, __init__(): self.first = lax.ppermute(mine, SLAB, ring.perm())  7.37 us
    ppermute x8, starting transfers between devices, step(): self.other.append(lax.ppermute(self.held, SLAB, self.ring.siblings()))  5.32 us
  transfers between devices with their start and end apart: 38, of which 18 were waited for; matrix products, arithmetic and copies ran while one was open for 5% of the time, Pallas kernels for 20%

profile of v3, /device:TPU:1, one launch (start us, length us, event | category | flops | bytes accessed | tf_op | source)
XLA Modules:
  0.0 139.6 jit_solution(1361588430161962494)
XLA Ops:
  0.0 3.1 %prepare_maps.1.earlier = bf16[16,2,2,16,384]{4,3,2,1,0:T(8,128)(2,1)} custom-call(s32[1]{0:T(128)} %bitcast.2.which, bf16[16,2,2,2,16,384]{5,4,3,2,1,0:T(8,128)(2,1)} %bitcast.89, bf16[128,128]{1,0:T(8,128)(2,1)} %constant.197.clone.along_z, bf16[384,384]{1,0:T(8,128)(2,1)} %constant.198.clone.along_y), custom_call_target="tpu_custom_call" | custom-call | tf_op jit(solution)/shard_map/prepare_maps/pallas_call | solution.py:362
  3.2 0.7 prepare_image.1.image
  4.0 2.7 %collective-permute-start.17 = (bf16[1,10,16,384]{3,2,1,0:T(8,128)(2,1)S(1)}, bf16[1,10,16,384]{3,2,1,0:T(8,128)(2,1)S(1)}, u32[]{:S(2)}, u32[]{:S(2)}) collective-permute-start(bf16[1,10,16,384]{3,2,1,0:T(8,128)(2,1)S(1)} %get-tuple-element.35.refs_0_), channel_id=1, source_target_pairs={{0,8},{2,6},{8,16},{10,2},{16,24},{18,10},{24,28},{26,18},{28,20},... | collective-permute-start | bytes 368648 | tf_op jit(solution)/shard_map/ppermute | solution.py:103
  6.7 5.2 %all-to-all-start = ((bf16[16,2,2,16,384]{4,3,2,1,0:T(8,128)(2,1)}), bf16[16,2,2,16,384]{4,3,2,1,0:T(8,128)(2,1)S(1)}, u32[]{:S(2)}, u32[]{:S(2)}) async-start(bf16[16,2,2,16,384]{4,3,2,1,0:T(8,128)(2,1)} %prepare_maps.1.earlier), calls=%async_computation | async-start | bytes 1572864 | tf_op jit(solution)/shard_map/all_to_all | solution.py:527
  12.1 1.6 %collective-permute-start.1 = (bf16[1,10,16,384]{3,2,1,0:T(8,128)(2,1)S(1)}, bf16[1,10,16,384]{3,2,1,0:T(8,128)(2,1)}, u32[]{:S(2)}, u32[]{:S(2)}) collective-permute-start(bf16[1,10,16,384]{3,2,1,0:T(8,128)(2,1)S(1)} %get-tuple-element.36.refs_0_), channel_id=1, source_target_pairs={{0,8},{2,6},{8,16},{10,2},{16,24},{18,10},{24,28},{26,18},{28,20},... | collective-permute-start | bytes 368648 | tf_op jit(solution)/shard_map/ppermute | solution.py:103
  14.8 1.7 %convert_element_type.117.refs_13_ = bf16[1,5,384,256]{3,2,1,0:T(8,128)(2,1)S(1)} convert(s32[1,5,384,256]{3,2,1,0:T(8,128)} %param.18) | non-fusion elementwise | flops 491520 | bytes 2949120 | tf_op jit(solution)/shard_map/convert_element_type | solution.py:520
  16.5 1.2 collective-permute-start.18
  17.8 1.2 collective-permute-start.2
  19.0 7.4 %collective-permute-done.1 = bf16[1,10,16,384]{3,2,1,0:T(8,128)(2,1)} collective-permute-done((bf16[1,10,16,384]{3,2,1,0:T(8,128)(2,1)S(1)}, bf16[1,10,16,384]{3,2,1,0:T(8,128)(2,1)}, u32[]{:S(2)}, u32[]{:S(2)}) %collective-permute-start.1) | collective-permute-done | bytes 122912 | tf_op jit(solution)/shard_map/ppermute | solution.py:103
  26.4 0.9 constant_dynamic-update-slice_fusion.1
  27.3 0.6 collective-permute-done.18
  28.0 1.4 %collective-permute-start.19 = (bf16[2,10,16,384]{3,2,1,0:T(8,128)(2,1)S(1)}, bf16[2,10,16,384]{3,2,1,0:T(8,128)(2,1)}, u32[]{:S(2)}, u32[]{:S(2)}) collective-permute-start(bf16[2,10,16,384]{3,2,1,0:T(8,128)(2,1)S(1)} %constant_dynamic-update-slice_fusion.2.refs_2_), channel_id=1, source_target_pairs={{0,8},{2,6},{8,16},{10,2},{16,24},{18,10},{24,28},{26,18},{28,20},... | collective-permute-start | bytes 737288 | tf_op jit(solution)/shard_map/ppermute | solution.py:114
  29.4 1.6 %collective-permute-done.2 = bf16[1,10,16,384]{3,2,1,0:T(8,128)(2,1)S(1)} collective-permute-done((bf16[1,10,16,384]{3,2,1,0:T(8,128)(2,1)S(1)}, bf16[1,10,16,384]{3,2,1,0:T(8,128)(2,1)S(1)}, u32[]{:S(2)}, u32[]{:S(2)}) %collective-permute-start.2) | collective-permute-done | bytes 122912 | tf_op jit(solution)/shard_map/ppermute | solution.py:111
  31.1 3.9 %collective-permute-start.3 = (bf16[2,10,16,384]{3,2,1,0:T(8,128)(2,1)S(1)}, bf16[2,10,16,384]{3,2,1,0:T(8,128)(2,1)}, u32[]{:S(2)}, u32[]{:S(2)}) collective-permute-start(bf16[2,10,16,384]{3,2,1,0:T(8,128)(2,1)S(1)} %constant_dynamic-update-slice_fusion.refs_2_), channel_id=1, source_target_pairs={{0,8},{2,6},{8,16},{10,2},{16,24},{18,10},{24,28},{26,18},{28,20},... | collective-permute-start | bytes 737288 | tf_op jit(solution)/shard_map/ppermute | solution.py:114
  35.0 1.0 fusion.9
  36.0 3.3 %collective-permute-done.19.refs_3_ = bf16[2,10,16,384]{3,2,1,0:T(8,128)(2,1)} collective-permute-done((bf16[2,10,16,384]{3,2,1,0:T(8,128)(2,1)S(1)}, bf16[2,10,16,384]{3,2,1,0:T(8,128)(2,1)}, u32[]{:S(2)}, u32[]{:S(2)}) %collective-permute-start.19) | collective-permute-done | bytes 245792 | tf_op jit(solution)/shard_map/ppermute | solution.py:114
  39.3 2.3 %collective-permute-done.3.refs_3_ = bf16[2,10,16,384]{3,2,1,0:T(8,128)(2,1)} collective-permute-done((bf16[2,10,16,384]{3,2,1,0:T(8,128)(2,1)S(1)}, bf16[2,10,16,384]{3,2,1,0:T(8,128)(2,1)}, u32[]{:S(2)}, u32[]{:S(2)}) %collective-permute-start.3) | collective-permute-done | bytes 245792 | tf_op jit(solution)/shard_map/ppermute | solution.py:114
  41.6 1.2 collective-permute-start.26
  42.9 1.9 %collective-permute-start.22 = (bf16[2,10,16,384]{3,2,1,0:T(8,128)(2,1)S(1)}, bf16[2,10,16,384]{3,2,1,0:T(8,128)(2,1)S(1)}, u32[]{:S(2)}, u32[]{:S(2)}) collective-permute-start(bf16[2,10,16,384]{3,2,1,0:T(8,128)(2,1)S(1)} %constant_dynamic-update-slice_fusion.2.refs_2_), channel_id=1, source_target_pairs={{0,2},{2,0},{4,6},{6,4},{8,10},{10,8},{12,14},{14,12},{16,18},{18,... | collective-permute-start | bytes 737288 | tf_op jit(solution)/shard_map/ppermute | solution.py:116
  44.9 1.1 collective-permute-start.21
  46.0 1.6 %collective-permute-done.4.refs_4_ = bf16[2,10,16,384]{3,2,1,0:T(8,128)(2,1)S(1)} collective-permute-done((bf16[2,10,16,384]{3,2,1,0:T(8,128)(2,1)}, bf16[2,10,16,384]{3,2,1,0:T(8,128)(2,1)S(1)}, u32[]{:S(2)}, u32[]{:S(2)}) %collective-permute-start.4) | collective-permute-done | bytes 245792 | tf_op jit(solution)/shard_map/ppermute | solution.py:114
  47.6 1.5 %collective-permute-start.24 = (bf16[2,10,16,384]{3,2,1,0:T(8,128)(2,1)S(1)}, bf16[2,10,16,384]{3,2,1,0:T(8,128)(2,1)}, u32[]{:S(2)}, u32[]{:S(2)}) collective-permute-start(bf16[2,10,16,384]{3,2,1,0:T(8,128)(2,1)S(1)} %collective-permute-done.20.refs_4_), channel_id=1, source_target_pairs={{0,2},{2,0},{4,6},{6,4},{8,10},{10,8},{12,14},{14,12},{16,18},{18,... | collective-permute-start | bytes 737288 | tf_op jit(solution)/shard_map/ppermute | solution.py:116
  49.0 0.6 slice.169
  49.7 0.7 copy-done.5
  50.4 1.7 %collective-permute-start.5 = (bf16[1,10,16,384]{3,2,1,0:T(8,128)(2,1)}, bf16[1,10,16,384]{3,2,1,0:T(8,128)(2,1)}, u32[]{:S(2)}, u32[]{:S(2)}) collective-permute-start(bf16[1,10,16,384]{3,2,1,0:T(8,128)(2,1)} %slice.169), channel_id=1, source_target_pairs={{0,8},{2,6},{8,16},{10,2},{16,24},{18,10},{24,28},{26,18},{28,20},... | collective-permute-start | bytes 368648 | tf_op jit(solution)/shard_map/ppermute | solution.py:114
  52.3 0.6 collective-permute-start.6
  52.8 1.9 %collective-permute-done.5.refs_5_ = bf16[1,10,16,384]{3,2,1,0:T(8,128)(2,1)} collective-permute-done((bf16[1,10,16,384]{3,2,1,0:T(8,128)(2,1)}, bf16[1,10,16,384]{3,2,1,0:T(8,128)(2,1)}, u32[]{:S(2)}, u32[]{:S(2)}) %collective-permute-start.5) | collective-permute-done | bytes 122912 | tf_op jit(solution)/shard_map/ppermute | solution.py:114
  54.7 0.9 collective-permute-start.7
  55.6 1.2 collective-permute-start.10
  56.8 0.3 collective-permute-start.8
  57.3 0.9 copy-done.6
  58.3 0.9 copy-done.10
  59.2 1.3 copy-done.12
  60.5 12.2 %gradient.3 = (bf16[2,10,16,384]{3,2,1,0:T(8,128)(2,1)S(1)}, bf16[7,10,16,384]{3,2,1,0:T(8,128)(2,1)S(1)}, bf16[7,10,16,384]{3,2,1,0:T(8,128)(2,1)S(1)}) custom-call(s32[33]{0:T(128)S(1)} %concatenate.39.slabs, bf16[1,10,16,384]{3,2,1,0:T(8,128)(2,1)S(1)} %get-tuple-element.35.refs_0_, bf16[1,10,16,384]{3,2,1,0:T(8,128)(2,1)S(1)} %copy-done.10, ...), custom_call_target="tpu_custom_call" | custom-call | flops 10066329600 | bytes 8388608 | tf_op jit(solution)/shard_map/gradient/pallas_call | solution.py:281
  72.7 0.4 collective-permute-start.27
  73.1 11.6 %gradient.2 = (bf16[2,10,16,384]{3,2,1,0:T(8,128)(2,1)S(1)}, bf16[7,10,16,384]{3,2,1,0:T(8,128)(2,1)S(1)}, bf16[7,10,16,384]{3,2,1,0:T(8,128)(2,1)S(1)}) custom-call(s32[33]{0:T(128)S(1)} %concatenate.39.slabs, bf16[1,10,16,384]{3,2,1,0:T(8,128)(2,1)S(1)} %get-tuple-element.36.refs_0_, bf16[1,10,16,384]{3,2,1,0:T(8,128)(2,1)S(1)} %copy-done.8, ...), custom_call_target="tpu_custom_call" | custom-call | flops 10066329600 | bytes 8388608 | tf_op jit(solution)/shard_map/gradient/pallas_call | solution.py:281
  84.7 0.3 collective-permute-start.11
  85.1 1.8 %collective-permute-start.28 = (bf16[1,10,16,384]{3,2,1,0:T(8,128)(2,1)S(1)}, bf16[1,10,16,384]{3,2,1,0:T(8,128)(2,1)S(1)}, u32[]{:S(2)}, u32[]{:S(2)}) collective-permute-start(bf16[1,10,16,384]{3,2,1,0:T(8,128)(2,1)S(1)} %add_convert_fusion.4), channel_id=1, source_target_pairs={{0,8},{2,6},{8,16},{10,2},{16,24},{18,10},{24,28},{26,18},{28,20},... | collective-permute-start | bytes 368648 | tf_op jit(solution)/shard_map/ppermute | solution.py:140
  87.2 1.8 %collective-permute-start.12 = (bf16[1,10,16,384]{3,2,1,0:T(8,128)(2,1)S(1)}, bf16[1,10,16,384]{3,2,1,0:T(8,128)(2,1)S(1)}, u32[]{:S(2)}, u32[]{:S(2)}) collective-permute-start(bf16[1,10,16,384]{3,2,1,0:T(8,128)(2,1)S(1)} %add_convert_fusion.5), channel_id=1, source_target_pairs={{0,8},{2,6},{8,16},{10,2},{16,24},{18,10},{24,28},{26,18},{28,20},... | collective-permute-start | bytes 368648 | tf_op jit(solution)/shard_map/ppermute | solution.py:140
  89.2 1.8 %collective-permute-start.29 = (bf16[2,10,16,384]{3,2,1,0:T(8,128)(2,1)S(1)}, bf16[2,10,16,384]{3,2,1,0:T(8,128)(2,1)S(1)}, u32[]{:S(2)}, u32[]{:S(2)}) collective-permute-start(bf16[2,10,16,384]{3,2,1,0:T(8,128)(2,1)S(1)} %pad_maximum_fusion.2), channel_id=1, source_target_pairs={{0,8},{2,6},{8,16},{10,2},{16,24},{18,10},{24,28},{26,18},{28,20},... | collective-permute-start | bytes 737288 | tf_op jit(solution)/shard_map/ppermute | solution.py:140
  91.0 0.3 collective-permute-done.12
  91.4 1.8 %collective-permute-start.13 = (bf16[2,10,16,384]{3,2,1,0:T(8,128)(2,1)S(1)}, bf16[2,10,16,384]{3,2,1,0:T(8,128)(2,1)S(1)}, u32[]{:S(2)}, u32[]{:S(2)}) collective-permute-start(bf16[2,10,16,384]{3,2,1,0:T(8,128)(2,1)S(1)} %pad_maximum_fusion.1), channel_id=1, source_target_pairs={{0,8},{2,6},{8,16},{10,2},{16,24},{18,10},{24,28},{26,18},{28,20},... | collective-permute-start | bytes 737288 | tf_op jit(solution)/shard_map/ppermute | solution.py:140
  93.2 1.4 %collective-permute-done.29 = bf16[2,10,16,384]{3,2,1,0:T(8,128)(2,1)S(1)} collective-permute-done((bf16[2,10,16,384]{3,2,1,0:T(8,128)(2,1)S(1)}, bf16[2,10,16,384]{3,2,1,0:T(8,128)(2,1)S(1)}, u32[]{:S(2)}, u32[]{:S(2)}) %collective-permute-start.29) | collective-permute-done | bytes 245792 | tf_op jit(solution)/shard_map/ppermute | solution.py:140
  94.7 1.8 %collective-permute-start.30 = (bf16[2,10,16,384]{3,2,1,0:T(8,128)(2,1)S(1)}, bf16[2,10,16,384]{3,2,1,0:T(8,128)(2,1)S(1)}, u32[]{:S(2)}, u32[]{:S(2)}) collective-permute-start(bf16[2,10,16,384]{3,2,1,0:T(8,128)(2,1)S(1)} %add_convert_fusion.1), channel_id=1, source_target_pairs={{0,8},{2,6},{8,16},{10,2},{16,24},{18,10},{24,28},{26,18},{28,20},... | collective-permute-start | bytes 737288 | tf_op jit(solution)/shard_map/ppermute | solution.py:140
  96.5 0.8 collective-permute-done.13
  97.3 1.8 %collective-permute-start.14 = (bf16[2,10,16,384]{3,2,1,0:T(8,128)(2,1)S(1)}, bf16[2,10,16,384]{3,2,1,0:T(8,128)(2,1)S(1)}, u32[]{:S(2)}, u32[]{:S(2)}) collective-permute-start(bf16[2,10,16,384]{3,2,1,0:T(8,128)(2,1)S(1)} %add_convert_fusion.3), channel_id=1, source_target_pairs={{0,8},{2,6},{8,16},{10,2},{16,24},{18,10},{24,28},{26,18},{28,20},... | collective-permute-start | bytes 737288 | tf_op jit(solution)/shard_map/ppermute | solution.py:140
  99.1 1.0 collective-permute-done.30
  100.2 1.8 %collective-permute-start.31 = (bf16[2,10,16,384]{3,2,1,0:T(8,128)(2,1)S(1)}, bf16[2,10,16,384]{3,2,1,0:T(8,128)(2,1)S(1)}, u32[]{:S(2)}, u32[]{:S(2)}) collective-permute-start(bf16[2,10,16,384]{3,2,1,0:T(8,128)(2,1)S(1)} %add_convert_fusion), channel_id=1, source_target_pairs={{0,8},{2,6},{8,16},{10,2},{16,24},{18,10},{24,28},{26,18},{28,20},... | collective-permute-start | bytes 737288 | tf_op jit(solution)/shard_map/ppermute | solution.py:140
  102.0 0.8 collective-permute-done.14
  102.8 1.8 %collective-permute-start.15 = (bf16[2,10,16,384]{3,2,1,0:T(8,128)(2,1)S(1)}, bf16[2,10,16,384]{3,2,1,0:T(8,128)(2,1)S(1)}, u32[]{:S(2)}, u32[]{:S(2)}) collective-permute-start(bf16[2,10,16,384]{3,2,1,0:T(8,128)(2,1)S(1)} %add_convert_fusion.2), channel_id=1, source_target_pairs={{0,8},{2,6},{8,16},{10,2},{16,24},{18,10},{24,28},{26,18},{28,20},... | collective-permute-start | bytes 737288 | tf_op jit(solution)/shard_map/ppermute | solution.py:140
  104.6 0.7 collective-permute-done.31
  105.4 2.8 %collective-permute-done.15 = bf16[2,10,16,384]{3,2,1,0:T(8,128)(2,1)S(1)} collective-permute-done((bf16[2,10,16,384]{3,2,1,0:T(8,128)(2,1)S(1)}, bf16[2,10,16,384]{3,2,1,0:T(8,128)(2,1)S(1)}, u32[]{:S(2)}, u32[]{:S(2)}) %collective-permute-start.15) | collective-permute-done | bytes 245792 | tf_op jit(solution)/shard_map/ppermute | solution.py:140
  108.3 3.8 %collective-permute-start.32 = (bf16[2,10,16,384]{3,2,1,0:T(8,128)(2,1)S(1)}, bf16[2,10,16,384]{3,2,1,0:T(8,128)(2,1)S(1)}, u32[]{:S(2)}, u32[]{:S(2)}) collective-permute-start(bf16[2,10,16,384]{3,2,1,0:T(8,128)(2,1)S(1)} %fusion.5), channel_id=1, source_target_pairs={{0,2},{2,0},{4,6},{6,4},{8,10},{10,8},{12,14},{14,12},{16,18},{18,... | collective-permute-start | bytes 737288 | tf_op jit(solution)/shard_map/ppermute | solution.py:540
  112.3 0.9 collective-permute-done.32.received
  113.2 0.7 update.1
  114.0 3.9 %collective-permute-start.33 = (bf16[2,10,2,384]{3,2,1,0:T(2,128)(2,1)S(1)}, bf16[2,10,2,384]{3,2,1,0:T(2,128)(2,1)S(1)}, u32[]{:S(2)}, u32[]{:S(2)}) collective-permute-start(bf16[2,10,2,384]{3,2,1,0:T(2,128)(2,1)S(1)} %get-tuple-element.33), channel_id=1, source_target_pairs={{0,2},{2,4},{4,6},{6,8},{8,10},{10,12},{12,14},{14,16},{16,18},{18... | collective-permute-start | bytes 92168 | tf_op jit(solution)/shard_map/ppermute | solution.py:543
  117.9 2.1 %collective-permute-start.34 = (bf16[2,10,2,384]{3,2,1,0:T(2,128)(2,1)S(1)}, bf16[2,10,2,384]{3,2,1,0:T(2,128)(2,1)S(1)}, u32[]{:S(2)}, u32[]{:S(2)}) collective-permute-start(bf16[2,10,2,384]{3,2,1,0:T(2,128)(2,1)S(1)} %get-tuple-element.34), channel_id=1, source_target_pairs={{2,0},{4,2},{6,4},{8,6},{10,8},{12,10},{14,12},{16,14},{18,16},{20... | collective-permute-start | bytes 92168 | tf_op jit(solution)/shard_map/ppermute | solution.py:544
  120.1 3.1 %collective-permute-done.34 = bf16[2,10,2,384]{3,2,1,0:T(2,128)(2,1)S(1)} collective-permute-done((bf16[2,10,2,384]{3,2,1,0:T(2,128)(2,1)S(1)}, bf16[2,10,2,384]{3,2,1,0:T(2,128)(2,1)S(1)}, u32[]{:S(2)}, u32[]{:S(2)}) %collective-permute-start.34) | collective-permute-done | bytes 30752 | tf_op jit(solution)/shard_map/ppermute | solution.py:544
  123.3 0.3 collective-permute-start.35
  123.6 1.3 collective-permute-start.36
  125.0 5.0 %collective-permute-done.35.refs_1_ = bf16[10,20,384]{2,1,0:T(8,128)(2,1)S(1)} collective-permute-done((bf16[10,20,384]{2,1,0:T(8,128)(2,1)S(1)}, bf16[10,20,384]{2,1,0:T(8,128)(2,1)S(1)}, u32[]{:S(2)}, u32[]{:S(2)}) %collective-permute-start.35) | collective-permute-done | bytes 153632 | tf_op jit(solution)/shard_map/ppermute | solution.py:548
  130.0 4.4 %convolutions.2 = bf16[10,16,384]{2,1,0:T(8,128)(2,1)S(1)} custom-call(s32[2]{0:T(128)S(1)} %add_convert_fusion.6.ends, bf16[10,20,384]{2,1,0:T(8,128)(2,1)S(1)} %pad_maximum_fusion.4.refs_0_, bf16[10,20,384]{2,1,0:T(8,128)(2,1)S(1)} %collective-permute-done.35.refs_1_, bf16[256,256]{1,0:T(8,128)(2,1)S(1)} %fusion.8.refs_2_, f32[256,1]{1,0:T(8,128)S(1)} %copy.25.refs_3_, ...), custom_call_target="tpu_custom_call" | custom-call | flops 792723456 | bytes 1048576 | tf_op jit(solution)/shard_map/convolutions/pallas_call | solution.py:456
  134.5 4.4 %convolutions.3 = bf16[10,16,384]{2,1,0:T(8,128)(2,1)S(1)} custom-call(s32[2]{0:T(128)S(1)} %add_convert_fusion.6.ends, bf16[10,20,384]{2,1,0:T(8,128)(2,1)S(1)} %pad_maximum_fusion.5.refs_0_, bf16[10,20,384]{2,1,0:T(8,128)(2,1)S(1)} %collective-permute-done.36.refs_1_, bf16[256,256]{1,0:T(8,128)(2,1)S(1)} %fusion.8.refs_2_, f32[256,1]{1,0:T(8,128)S(1)} %copy.25.refs_3_, ...), custom_call_target="tpu_custom_call" | custom-call | flops 792723456 | bytes 1048576 | tf_op jit(solution)/shard_map/convolutions/pallas_call | solution.py:456
  138.9 0.7 pad_maximum_fusion.3
  (109 shorter events, 3.5 us)
Async XLA Ops:
  0.0 3.2 %copy-start.3 = (bf16[128,128]{1,0:T(8,128)(2,1)S(1)}, bf16[128,128]{1,0:T(8,128)(2,1)}, u32[]{:S(2)}) copy-start(bf16[128,128]{1,0:T(8,128)(2,1)} %constant.197.clone.along_z) | copy-start | bytes 98308
  0.0 3.2 %copy-start = (bf16[384,384]{1,0:T(8,128)(2,1)S(1)}, bf16[384,384]{1,0:T(8,128)(2,1)}, u32[]{:S(2)}) copy-start(bf16[384,384]{1,0:T(8,128)(2,1)} %constant.198.clone.along_y) | copy-start | bytes 884740
  0.0 3.2 %copy-start.2 = (bf16[1,5,2,2,16,384]{5,4,3,2,1,0:T(8,128)(2,1)S(1)}, bf16[1,5,2,2,16,384]{5,4,3,2,1,0:T(8,128)(2,1)}, u32[]{:S(2)}) copy-start(bf16[1,5,2,2,16,384]{5,4,3,2,1,0:T(8,128)(2,1)} %image.1) | copy-start | bytes 737284
  3.2 10.5 %copy-start.14 = (bf16[64,10,3,3,3]{0,4,3,2,1:T(4,128)(2,1)S(1)}, bf16[64,10,3,3,3]{0,4,3,2,1:T(4,128)(2,1)}, u32[]{:S(2)}) copy-start(bf16[64,10,3,3,3]{0,4,3,2,1:T(4,128)(2,1)} %param.19) | copy-start | bytes 103684
  3.8 10.4 %copy-start.15 = (bf16[10,64,3,3,3]{1,4,3,2,0:T(4,128)(2,1)S(1)}, bf16[10,64,3,3,3]{1,4,3,2,0:T(4,128)(2,1)}, u32[]{:S(2)}) copy-start(bf16[10,64,3,3,3]{1,4,3,2,0:T(4,128)(2,1)} %param.21) | copy-start | bytes 103684
  3.9 10.8 %copy-start.16 = (f32[64]{0:T(128)S(1)}, f32[64]{0:T(128)}, u32[]{:S(2)}) copy-start(f32[64]{0:T(128)} %param.20) | copy-start | bytes 772
  3.9 12.6 %collective-permute-start.16 = (bf16[1,10,16,384]{3,2,1,0:T(8,128)(2,1)S(1)}, bf16[1,10,16,384]{3,2,1,0:T(8,128)(2,1)S(1)}, u32[]{:S(2)}, u32[]{:S(2)}) collective-permute-start(bf16[1,10,16,384]{3,2,1,0:T(8,128)(2,1)S(1)} %get-tuple-element.35.refs_0_), channel_id=1, source_target_pairs={{0,2},{2,0},{4,6},{6,4},{8,10},{10,8},{12,14},{14,12},{16,18},{18,... | collective-permute-start | bytes 368648 | tf_op jit(solution)/shard_map/ppermute | solution.py:104
  4.0 13.8 %collective-permute-start.17 = (bf16[1,10,16,384]{3,2,1,0:T(8,128)(2,1)S(1)}, bf16[1,10,16,384]{3,2,1,0:T(8,128)(2,1)S(1)}, u32[]{:S(2)}, u32[]{:S(2)}) collective-permute-start(bf16[1,10,16,384]{3,2,1,0:T(8,128)(2,1)S(1)} %get-tuple-element.35.refs_0_), channel_id=1, source_target_pairs={{0,8},{2,6},{8,16},{10,2},{16,24},{18,10},{24,28},{26,18},{28,20},... | collective-permute-start | bytes 368648 | tf_op jit(solution)/shard_map/ppermute | solution.py:103
  6.7 28.3 %all-to-all-start = ((bf16[16,2,2,16,384]{4,3,2,1,0:T(8,128)(2,1)}), bf16[16,2,2,16,384]{4,3,2,1,0:T(8,128)(2,1)S(1)}, u32[]{:S(2)}, u32[]{:S(2)}) async-start(bf16[16,2,2,16,384]{4,3,2,1,0:T(8,128)(2,1)} %prepare_maps.1.earlier), calls=%async_computation | async-start | bytes 1572864 | tf_op jit(solution)/shard_map/all_to_all | solution.py:527
  11.9 5.9 %collective-permute-start = (bf16[1,10,16,384]{3,2,1,0:T(8,128)(2,1)S(1)}, bf16[1,10,16,384]{3,2,1,0:T(8,128)(2,1)S(1)}, u32[]{:S(2)}, u32[]{:S(2)}) collective-permute-start(bf16[1,10,16,384]{3,2,1,0:T(8,128)(2,1)S(1)} %get-tuple-element.36.refs_0_), channel_id=1, source_target_pairs={{0,2},{2,0},{4,6},{6,4},{8,10},{10,8},{12,14},{14,12},{16,18},{18,... | collective-permute-start | bytes 368648 | tf_op jit(solution)/shard_map/ppermute | solution.py:104
  12.1 14.3 %collective-permute-start.1 = (bf16[1,10,16,384]{3,2,1,0:T(8,128)(2,1)S(1)}, bf16[1,10,16,384]{3,2,1,0:T(8,128)(2,1)}, u32[]{:S(2)}, u32[]{:S(2)}) collective-permute-start(bf16[1,10,16,384]{3,2,1,0:T(8,128)(2,1)S(1)} %get-tuple-element.36.refs_0_), channel_id=1, source_target_pairs={{0,8},{2,6},{8,16},{10,2},{16,24},{18,10},{24,28},{26,18},{28,20},... | collective-permute-start | bytes 368648 | tf_op jit(solution)/shard_map/ppermute | solution.py:103
  16.5 22.8 %copy-start.9 = (bf16[1,10,16,384]{3,2,1,0:T(8,128)(2,1)}, bf16[1,10,16,384]{3,2,1,0:T(8,128)(2,1)S(1)}, u32[]{:S(2)}) copy-start(bf16[1,10,16,384]{3,2,1,0:T(8,128)(2,1)S(1)} %collective-permute-done.16.refs_1_) | copy-start | bytes 368644
  16.5 11.4 %collective-permute-start.18 = (bf16[1,10,16,384]{3,2,1,0:T(8,128)(2,1)S(1)}, bf16[1,10,16,384]{3,2,1,0:T(8,128)(2,1)S(1)}, u32[]{:S(2)}, u32[]{:S(2)}) collective-permute-start(bf16[1,10,16,384]{3,2,1,0:T(8,128)(2,1)S(1)} %collective-permute-done.16.refs_1_), channel_id=1, source_target_pairs={{0,8},{2,6},{8,16},{10,2},{16,24},{18,10},{24,28},{26,18},{28,20},... | collective-permute-start | bytes 368648 | tf_op jit(solution)/shard_map/ppermute | solution.py:111
  17.8 21.5 %copy-start.7 = (bf16[1,10,16,384]{3,2,1,0:T(8,128)(2,1)}, bf16[1,10,16,384]{3,2,1,0:T(8,128)(2,1)S(1)}, u32[]{:S(2)}) copy-start(bf16[1,10,16,384]{3,2,1,0:T(8,128)(2,1)S(1)} %collective-permute-done.refs_1_) | copy-start | bytes 368644
  17.8 13.2 %collective-permute-start.2 = (bf16[1,10,16,384]{3,2,1,0:T(8,128)(2,1)S(1)}, bf16[1,10,16,384]{3,2,1,0:T(8,128)(2,1)S(1)}, u32[]{:S(2)}, u32[]{:S(2)}) collective-permute-start(bf16[1,10,16,384]{3,2,1,0:T(8,128)(2,1)S(1)} %collective-permute-done.refs_1_), channel_id=1, source_target_pairs={{0,8},{2,6},{8,16},{10,2},{16,24},{18,10},{24,28},{26,18},{28,20},... | collective-permute-start | bytes 368648 | tf_op jit(solution)/shard_map/ppermute | solution.py:111
  28.0 11.3 %collective-permute-start.19 = (bf16[2,10,16,384]{3,2,1,0:T(8,128)(2,1)S(1)}, bf16[2,10,16,384]{3,2,1,0:T(8,128)(2,1)}, u32[]{:S(2)}, u32[]{:S(2)}) collective-permute-start(bf16[2,10,16,384]{3,2,1,0:T(8,128)(2,1)S(1)} %constant_dynamic-update-slice_fusion.2.refs_2_), channel_id=1, source_target_pairs={{0,8},{2,6},{8,16},{10,2},{16,24},{18,10},{24,28},{26,18},{28,20},... | collective-permute-start | bytes 737288 | tf_op jit(solution)/shard_map/ppermute | solution.py:114
  31.1 10.6 %collective-permute-start.3 = (bf16[2,10,16,384]{3,2,1,0:T(8,128)(2,1)S(1)}, bf16[2,10,16,384]{3,2,1,0:T(8,128)(2,1)}, u32[]{:S(2)}, u32[]{:S(2)}) collective-permute-start(bf16[2,10,16,384]{3,2,1,0:T(8,128)(2,1)S(1)} %constant_dynamic-update-slice_fusion.refs_2_), channel_id=1, source_target_pairs={{0,8},{2,6},{8,16},{10,2},{16,24},{18,10},{24,28},{26,18},{28,20},... | collective-permute-start | bytes 737288 | tf_op jit(solution)/shard_map/ppermute | solution.py:114
  39.3 5.6 %collective-permute-start.20 = (bf16[2,10,16,384]{3,2,1,0:T(8,128)(2,1)}, bf16[2,10,16,384]{3,2,1,0:T(8,128)(2,1)S(1)}, u32[]{:S(2)}, u32[]{:S(2)}) collective-permute-start(bf16[2,10,16,384]{3,2,1,0:T(8,128)(2,1)} %collective-permute-done.19.refs_3_), channel_id=1, source_target_pairs={{0,8},{2,6},{8,16},{10,2},{16,24},{18,10},{24,28},{26,18},{28,20},... | collective-permute-start | bytes 737288 | tf_op jit(solution)/shard_map/ppermute | solution.py:114
  41.6 6.0 %collective-permute-start.4 = (bf16[2,10,16,384]{3,2,1,0:T(8,128)(2,1)}, bf16[2,10,16,384]{3,2,1,0:T(8,128)(2,1)S(1)}, u32[]{:S(2)}, u32[]{:S(2)}) collective-permute-start(bf16[2,10,16,384]{3,2,1,0:T(8,128)(2,1)} %collective-permute-done.3.refs_3_), channel_id=1, source_target_pairs={{0,8},{2,6},{8,16},{10,2},{16,24},{18,10},{24,28},{26,18},{28,20},... | collective-permute-start | bytes 737288 | tf_op jit(solution)/shard_map/ppermute | solution.py:114
  41.6 14.0 %collective-permute-start.26 = (bf16[16,1,2,16,384]{4,3,2,1,0:T(8,128)(2,1)}, bf16[16,1,2,16,384]{4,3,2,1,0:T(8,128)(2,1)}, u32[]{:S(2)}, u32[]{:S(2)}) collective-permute-start(bf16[16,1,2,16,384]{4,3,2,1,0:T(8,128)(2,1)} %get-tuple-element.29), channel_id=1, source_target_pairs={{0,1},{1,0},{2,3},{3,2},{4,5},{5,4},{6,7},{7,6},{8,9},{9,8},{10,11... | collective-permute-start | bytes 1179656 | tf_op jit(solution)/shard_map/ppermute | solution.py:532
  42.9 6.8 %collective-permute-start.22 = (bf16[2,10,16,384]{3,2,1,0:T(8,128)(2,1)S(1)}, bf16[2,10,16,384]{3,2,1,0:T(8,128)(2,1)S(1)}, u32[]{:S(2)}, u32[]{:S(2)}) collective-permute-start(bf16[2,10,16,384]{3,2,1,0:T(8,128)(2,1)S(1)} %constant_dynamic-update-slice_fusion.2.refs_2_), channel_id=1, source_target_pairs={{0,2},{2,0},{4,6},{6,4},{8,10},{10,8},{12,14},{14,12},{16,18},{18,... | collective-permute-start | bytes 737288 | tf_op jit(solution)/shard_map/ppermute | solution.py:116
  44.8 7.5 %collective-permute-start.23 = (bf16[2,10,16,384]{3,2,1,0:T(8,128)(2,1)}, bf16[2,10,16,384]{3,2,1,0:T(8,128)(2,1)}, u32[]{:S(2)}, u32[]{:S(2)}) collective-permute-start(bf16[2,10,16,384]{3,2,1,0:T(8,128)(2,1)} %collective-permute-done.19.refs_3_), channel_id=1, source_target_pairs={{0,2},{2,0},{4,6},{6,4},{8,10},{10,8},{12,14},{14,12},{16,18},{18,... | collective-permute-start | bytes 737288 | tf_op jit(solution)/shard_map/ppermute | solution.py:116
  44.9 7.3 %collective-permute-start.21 = (bf16[1,10,16,384]{3,2,1,0:T(8,128)(2,1)S(1)}, bf16[1,10,16,384]{3,2,1,0:T(8,128)(2,1)}, u32[]{:S(2)}, u32[]{:S(2)}) collective-permute-start(bf16[1,10,16,384]{3,2,1,0:T(8,128)(2,1)S(1)} %slice.178), channel_id=1, source_target_pairs={{0,8},{2,6},{8,16},{10,2},{16,24},{18,10},{24,28},{26,18},{28,20},... | collective-permute-start | bytes 368648 | tf_op jit(solution)/shard_map/ppermute | solution.py:114
  47.6 9.5 %collective-permute-start.24 = (bf16[2,10,16,384]{3,2,1,0:T(8,128)(2,1)S(1)}, bf16[2,10,16,384]{3,2,1,0:T(8,128)(2,1)}, u32[]{:S(2)}, u32[]{:S(2)}) collective-permute-start(bf16[2,10,16,384]{3,2,1,0:T(8,128)(2,1)S(1)} %collective-permute-done.20.refs_4_), channel_id=1, source_target_pairs={{0,2},{2,0},{4,6},{6,4},{8,10},{10,8},{12,14},{14,12},{16,18},{18,... | collective-permute-start | bytes 737288 | tf_op jit(solution)/shard_map/ppermute | solution.py:116
  49.7 0.7 copy-start.5
  50.4 4.3 %collective-permute-start.5 = (bf16[1,10,16,384]{3,2,1,0:T(8,128)(2,1)}, bf16[1,10,16,384]{3,2,1,0:T(8,128)(2,1)}, u32[]{:S(2)}, u32[]{:S(2)}) collective-permute-start(bf16[1,10,16,384]{3,2,1,0:T(8,128)(2,1)} %slice.169), channel_id=1, source_target_pairs={{0,8},{2,6},{8,16},{10,2},{16,24},{18,10},{24,28},{26,18},{28,20},... | collective-permute-start | bytes 368648 | tf_op jit(solution)/shard_map/ppermute | solution.py:114
  52.1 4.7 %collective-permute-start.25 = (bf16[1,10,16,384]{3,2,1,0:T(8,128)(2,1)}, bf16[1,10,16,384]{3,2,1,0:T(8,128)(2,1)}, u32[]{:S(2)}, u32[]{:S(2)}) collective-permute-start(bf16[1,10,16,384]{3,2,1,0:T(8,128)(2,1)} %collective-permute-done.21.refs_5_), channel_id=1, source_target_pairs={{0,2},{2,0},{4,6},{6,4},{8,10},{10,8},{12,14},{14,12},{16,18},{18,... | collective-permute-start | bytes 368648 | tf_op jit(solution)/shard_map/ppermute | solution.py:116
  52.3 20.5 %collective-permute-start.6 = (bf16[2,10,16,384]{3,2,1,0:T(8,128)(2,1)S(1)}, bf16[2,10,16,384]{3,2,1,0:T(8,128)(2,1)S(1)}, u32[]{:S(2)}, u32[]{:S(2)}) collective-permute-start(bf16[2,10,16,384]{3,2,1,0:T(8,128)(2,1)S(1)} %constant_dynamic-update-slice_fusion.refs_2_), channel_id=1, source_target_pairs={{0,2},{2,0},{4,6},{6,4},{8,10},{10,8},{12,14},{14,12},{16,18},{18,... | collective-permute-start | bytes 737288 | tf_op jit(solution)/shard_map/ppermute | solution.py:116
  54.7 18.4 %collective-permute-start.7 = (bf16[2,10,16,384]{3,2,1,0:T(8,128)(2,1)}, bf16[2,10,16,384]{3,2,1,0:T(8,128)(2,1)S(1)}, u32[]{:S(2)}, u32[]{:S(2)}) collective-permute-start(bf16[2,10,16,384]{3,2,1,0:T(8,128)(2,1)} %collective-permute-done.3.refs_3_), channel_id=1, source_target_pairs={{0,2},{2,0},{4,6},{6,4},{8,10},{10,8},{12,14},{14,12},{16,18},{18,... | collective-permute-start | bytes 737288 | tf_op jit(solution)/shard_map/ppermute | solution.py:116
  55.6 17.5 %collective-permute-start.10 = (bf16[16,1,2,16,384]{4,3,2,1,0:T(8,128)(2,1)}, bf16[16,1,2,16,384]{4,3,2,1,0:T(8,128)(2,1)S(1)}, u32[]{:S(2)}, u32[]{:S(2)}) collective-permute-start(bf16[16,1,2,16,384]{4,3,2,1,0:T(8,128)(2,1)} %get-tuple-element.30), channel_id=1, source_target_pairs={{0,1},{1,0},{2,3},{3,2},{4,5},{5,4},{6,7},{7,6},{8,9},{9,8},{10,11... | collective-permute-start | bytes 1179656 | tf_op jit(solution)/shard_map/ppermute | solution.py:532
  56.8 16.3 %collective-permute-start.8 = (bf16[2,10,16,384]{3,2,1,0:T(8,128)(2,1)S(1)}, bf16[2,10,16,384]{3,2,1,0:T(8,128)(2,1)S(1)}, u32[]{:S(2)}, u32[]{:S(2)}) collective-permute-start(bf16[2,10,16,384]{3,2,1,0:T(8,128)(2,1)S(1)} %collective-permute-done.4.refs_4_), channel_id=1, source_target_pairs={{0,2},{2,0},{4,6},{6,4},{8,10},{10,8},{12,14},{14,12},{16,18},{18,... | collective-permute-start | bytes 737288 | tf_op jit(solution)/shard_map/ppermute | solution.py:116
  57.1 16.0 %collective-permute-start.9 = (bf16[1,10,16,384]{3,2,1,0:T(8,128)(2,1)}, bf16[1,10,16,384]{3,2,1,0:T(8,128)(2,1)S(1)}, u32[]{:S(2)}, u32[]{:S(2)}) collective-permute-start(bf16[1,10,16,384]{3,2,1,0:T(8,128)(2,1)} %collective-permute-done.5.refs_5_), channel_id=1, source_target_pairs={{0,2},{2,0},{4,6},{6,4},{8,10},{10,8},{12,14},{14,12},{16,18},{18,... | collective-permute-start | bytes 368648 | tf_op jit(solution)/shard_map/ppermute | solution.py:116
  57.3 0.9 copy-start.6
  58.3 0.9 copy-start.10
  59.2 1.3 copy-start.12
  60.5 12.6 %copy-start.8 = (bf16[1,10,16,384]{3,2,1,0:T(8,128)(2,1)S(1)}, bf16[1,10,16,384]{3,2,1,0:T(8,128)(2,1)}, u32[]{:S(2)}) copy-start(bf16[1,10,16,384]{3,2,1,0:T(8,128)(2,1)} %copy-done.7) | copy-start | bytes 368644
  60.5 12.6 %copy-start.13 = (bf16[10,256,256]{2,1,0:T(8,128)(2,1)S(1)}, bf16[10,256,256]{2,1,0:T(8,128)(2,1)}, u32[]{:S(2)}) copy-start(bf16[10,256,256]{2,1,0:T(8,128)(2,1)} %constant.196.clone.refs_14_) | copy-start | bytes 3932164
  72.7 12.3 %collective-permute-start.27 = (bf16[7,10,16,384]{3,2,1,0:T(8,128)(2,1)S(1)}, bf16[7,10,16,384]{3,2,1,0:T(8,128)(2,1)S(1)}, u32[]{:S(2)}, u32[]{:S(2)}) collective-permute-start(bf16[7,10,16,384]{3,2,1,0:T(8,128)(2,1)S(1)} %get-tuple-element.28), channel_id=1, source_target_pairs={{0,2},{2,0},{4,6},{6,4},{8,10},{10,8},{12,14},{14,12},{16,18},{18,... | collective-permute-start | bytes 2580488 | tf_op jit(solution)/shard_map/ppermute | solution.py:125
  84.7 2.5 %collective-permute-start.11 = (bf16[7,10,16,384]{3,2,1,0:T(8,128)(2,1)S(1)}, bf16[7,10,16,384]{3,2,1,0:T(8,128)(2,1)S(1)}, u32[]{:S(2)}, u32[]{:S(2)}) collective-permute-start(bf16[7,10,16,384]{3,2,1,0:T(8,128)(2,1)S(1)} %get-tuple-element.22), channel_id=1, source_target_pairs={{0,2},{2,0},{4,6},{6,4},{8,10},{10,8},{12,14},{14,12},{16,18},{18,... | collective-permute-start | bytes 2580488 | tf_op jit(solution)/shard_map/ppermute | solution.py:125
  85.1 4.1 %collective-permute-start.28 = (bf16[1,10,16,384]{3,2,1,0:T(8,128)(2,1)S(1)}, bf16[1,10,16,384]{3,2,1,0:T(8,128)(2,1)S(1)}, u32[]{:S(2)}, u32[]{:S(2)}) collective-permute-start(bf16[1,10,16,384]{3,2,1,0:T(8,128)(2,1)S(1)} %add_convert_fusion.4), channel_id=1, source_target_pairs={{0,8},{2,6},{8,16},{10,2},{16,24},{18,10},{24,28},{26,18},{28,20},... | collective-permute-start | bytes 368648 | tf_op jit(solution)/shard_map/ppermute | solution.py:140
  87.2 4.1 %collective-permute-start.12 = (bf16[1,10,16,384]{3,2,1,0:T(8,128)(2,1)S(1)}, bf16[1,10,16,384]{3,2,1,0:T(8,128)(2,1)S(1)}, u32[]{:S(2)}, u32[]{:S(2)}) collective-permute-start(bf16[1,10,16,384]{3,2,1,0:T(8,128)(2,1)S(1)} %add_convert_fusion.5), channel_id=1, source_target_pairs={{0,8},{2,6},{8,16},{10,2},{16,24},{18,10},{24,28},{26,18},{28,20},... | collective-permute-start | bytes 368648 | tf_op jit(solution)/shard_map/ppermute | solution.py:140
  89.2 5.4 %collective-permute-start.29 = (bf16[2,10,16,384]{3,2,1,0:T(8,128)(2,1)S(1)}, bf16[2,10,16,384]{3,2,1,0:T(8,128)(2,1)S(1)}, u32[]{:S(2)}, u32[]{:S(2)}) collective-permute-start(bf16[2,10,16,384]{3,2,1,0:T(8,128)(2,1)S(1)} %pad_maximum_fusion.2), channel_id=1, source_target_pairs={{0,8},{2,6},{8,16},{10,2},{16,24},{18,10},{24,28},{26,18},{28,20},... | collective-permute-start | bytes 737288 | tf_op jit(solution)/shard_map/ppermute | solution.py:140
  91.4 5.9 %collective-permute-start.13 = (bf16[2,10,16,384]{3,2,1,0:T(8,128)(2,1)S(1)}, bf16[2,10,16,384]{3,2,1,0:T(8,128)(2,1)S(1)}, u32[]{:S(2)}, u32[]{:S(2)}) collective-permute-start(bf16[2,10,16,384]{3,2,1,0:T(8,128)(2,1)S(1)} %pad_maximum_fusion.1), channel_id=1, source_target_pairs={{0,8},{2,6},{8,16},{10,2},{16,24},{18,10},{24,28},{26,18},{28,20},... | collective-permute-start | bytes 737288 | tf_op jit(solution)/shard_map/ppermute | solution.py:140
  94.7 5.4 %collective-permute-start.30 = (bf16[2,10,16,384]{3,2,1,0:T(8,128)(2,1)S(1)}, bf16[2,10,16,384]{3,2,1,0:T(8,128)(2,1)S(1)}, u32[]{:S(2)}, u32[]{:S(2)}) collective-permute-start(bf16[2,10,16,384]{3,2,1,0:T(8,128)(2,1)S(1)} %add_convert_fusion.1), channel_id=1, source_target_pairs={{0,8},{2,6},{8,16},{10,2},{16,24},{18,10},{24,28},{26,18},{28,20},... | collective-permute-start | bytes 737288 | tf_op jit(solution)/shard_map/ppermute | solution.py:140
  97.3 5.4 %collective-permute-start.14 = (bf16[2,10,16,384]{3,2,1,0:T(8,128)(2,1)S(1)}, bf16[2,10,16,384]{3,2,1,0:T(8,128)(2,1)S(1)}, u32[]{:S(2)}, u32[]{:S(2)}) collective-permute-start(bf16[2,10,16,384]{3,2,1,0:T(8,128)(2,1)S(1)} %add_convert_fusion.3), channel_id=1, source_target_pairs={{0,8},{2,6},{8,16},{10,2},{16,24},{18,10},{24,28},{26,18},{28,20},... | collective-permute-start | bytes 737288 | tf_op jit(solution)/shard_map/ppermute | solution.py:140
  100.2 5.1 %collective-permute-start.31 = (bf16[2,10,16,384]{3,2,1,0:T(8,128)(2,1)S(1)}, bf16[2,10,16,384]{3,2,1,0:T(8,128)(2,1)S(1)}, u32[]{:S(2)}, u32[]{:S(2)}) collective-permute-start(bf16[2,10,16,384]{3,2,1,0:T(8,128)(2,1)S(1)} %add_convert_fusion), channel_id=1, source_target_pairs={{0,8},{2,6},{8,16},{10,2},{16,24},{18,10},{24,28},{26,18},{28,20},... | collective-permute-start | bytes 737288 | tf_op jit(solution)/shard_map/ppermute | solution.py:140
  102.8 5.4 %collective-permute-start.15 = (bf16[2,10,16,384]{3,2,1,0:T(8,128)(2,1)S(1)}, bf16[2,10,16,384]{3,2,1,0:T(8,128)(2,1)S(1)}, u32[]{:S(2)}, u32[]{:S(2)}) collective-permute-start(bf16[2,10,16,384]{3,2,1,0:T(8,128)(2,1)S(1)} %add_convert_fusion.2), channel_id=1, source_target_pairs={{0,8},{2,6},{8,16},{10,2},{16,24},{18,10},{24,28},{26,18},{28,20},... | collective-permute-start | bytes 737288 | tf_op jit(solution)/shard_map/ppermute | solution.py:140
  105.3 7.9 %copy-start.1 = (bf16[384,384]{1,0:T(8,128)(2,1)S(1)}, bf16[384,384]{1,0:T(8,128)(2,1)}, u32[]{:S(2)}) copy-start(bf16[384,384]{1,0:T(8,128)(2,1)} %constant.200.clone.along_y) | copy-start | bytes 884740
  105.4 7.9 %copy-start.4 = (bf16[128,128]{1,0:T(8,128)(2,1)S(1)}, bf16[128,128]{1,0:T(8,128)(2,1)}, u32[]{:S(2)}) copy-start(bf16[128,128]{1,0:T(8,128)(2,1)} %constant.199.clone.along_z) | copy-start | bytes 98308
  108.3 4.9 %collective-permute-start.32 = (bf16[2,10,16,384]{3,2,1,0:T(8,128)(2,1)S(1)}, bf16[2,10,16,384]{3,2,1,0:T(8,128)(2,1)S(1)}, u32[]{:S(2)}, u32[]{:S(2)}) collective-permute-start(bf16[2,10,16,384]{3,2,1,0:T(8,128)(2,1)S(1)} %fusion.5), channel_id=1, source_target_pairs={{0,2},{2,0},{4,6},{6,4},{8,10},{10,8},{12,14},{14,12},{16,18},{18,... | collective-permute-start | bytes 737288 | tf_op jit(solution)/shard_map/ppermute | solution.py:540
  112.2 17.8 %copy-start.11 = (f32[10]{0:T(128)S(1)}, f32[10]{0:T(128)}, u32[]{:S(2)}) copy-start(f32[10]{0:T(128)} %refs_5_.3) | copy-start | bytes 124
  114.0 6.1 %collective-permute-start.33 = (bf16[2,10,2,384]{3,2,1,0:T(2,128)(2,1)S(1)}, bf16[2,10,2,384]{3,2,1,0:T(2,128)(2,1)S(1)}, u32[]{:S(2)}, u32[]{:S(2)}) collective-permute-start(bf16[2,10,2,384]{3,2,1,0:T(2,128)(2,1)S(1)} %get-tuple-element.33), channel_id=1, source_target_pairs={{0,2},{2,4},{4,6},{6,8},{8,10},{10,12},{12,14},{14,16},{16,18},{18... | collective-permute-start | bytes 92168 | tf_op jit(solution)/shard_map/ppermute | solution.py:543
  117.9 5.2 %collective-permute-start.34 = (bf16[2,10,2,384]{3,2,1,0:T(2,128)(2,1)S(1)}, bf16[2,10,2,384]{3,2,1,0:T(2,128)(2,1)S(1)}, u32[]{:S(2)}, u32[]{:S(2)}) collective-permute-start(bf16[2,10,2,384]{3,2,1,0:T(2,128)(2,1)S(1)} %get-tuple-element.34), channel_id=1, source_target_pairs={{2,0},{4,2},{6,4},{8,6},{10,8},{12,10},{14,12},{16,14},{18,16},{20... | collective-permute-start | bytes 92168 | tf_op jit(solution)/shard_map/ppermute | solution.py:544
  123.3 6.8 %collective-permute-start.35 = (bf16[10,20,384]{2,1,0:T(8,128)(2,1)S(1)}, bf16[10,20,384]{2,1,0:T(8,128)(2,1)S(1)}, u32[]{:S(2)}, u32[]{:S(2)}) collective-permute-start(bf16[10,20,384]{2,1,0:T(8,128)(2,1)S(1)} %pad_maximum_fusion.4.refs_0_), channel_id=1, source_target_pairs={{0,1},{1,0},{2,3},{3,2},{4,5},{5,4},{6,7},{7,6},{8,9},{9,8},{10,11... | collective-permute-start | bytes 460808 | tf_op jit(solution)/shard_map/ppermute | solution.py:548
  123.6 10.9 %collective-permute-start.36 = (bf16[10,20,384]{2,1,0:T(8,128)(2,1)S(1)}, bf16[10,20,384]{2,1,0:T(8,128)(2,1)S(1)}, u32[]{:S(2)}, u32[]{:S(2)}) collective-permute-start(bf16[10,20,384]{2,1,0:T(8,128)(2,1)S(1)} %pad_maximum_fusion.5.refs_0_), channel_id=1, source_target_pairs={{0,1},{1,0},{2,3},{3,2},{4,5},{5,4},{6,7},{7,6},{8,9},{9,8},{10,11... | collective-permute-start | bytes 460808 | tf_op jit(solution)/shard_map/ppermute | solution.py:548

commit v4 on v3

--- a/solution.py
+++ b/solution.py
@@ -410,16 +410,19 @@
 
 
 def convolution_kernel(ends, *refs):
-    sources, refs = refs[:2], refs[2:]
+    sources, refs = (refs[:2], refs[2:4]), refs[4:]
     w_first, b_first, w_second, b_second, out, stacked, result = refs
-    channels, depth, ny = sources[0].shape
-    rows = depth - 4
+    _, channels, rows, ny = sources[0][0].shape
+    depth = rows + 4
     group = stacked.shape[1] // depth
     lanes = result.shape[1] // rows
-    stacked[...] = jnp.zeros_like(stacked)
-    for t, source in enumerate(sources):
+    nothing = jnp.zeros((depth, ny), F32)
+    for i in range(6 * channels, group):
+        put_strided(stacked, i, depth, group, nothing)
+    for t, (cells, edges) in enumerate(sources):
         for i in range(channels):
-            value = source[i].astype(F32)
+            edge = edges[0, i].astype(F32)
+            value = jnp.concatenate([edge[:2], cells[0, i].astype(F32), edge[2:]], axis=0)
             for d in range(3):
                 line = value if d == 1 else shifted(value, d - 1)
                 put_strided(stacked, (d * 2 + t) * channels + i, depth, group, line)
@@ -441,31 +444,33 @@
                 put_strided(result, 2 * pair - 2 + z, lanes, rows, line)
             partial = partial[1:]
     for i in range(channels):
-        value = sources[0][i].astype(F32)[2 : 2 + rows]
-        out[i] = (value + get_lines(result, i * rows, rows) + b_second[i]).astype(BF16)
-
-
-def convolutions(ends, own, other, w_first, b_first, w_second, b_second):
-    channels, depth, ny = own.shape
-    rows = depth - 4
+        value = sources[0][0][0, i].astype(F32)
+        out[0, i // 2, i % 2, 0] = (value + get_lines(result, i * rows, rows) + b_second[i]).astype(BF16)
+
+
+def convolutions(ends, parts, w_first, b_first, w_second, b_second, shape):
+    width, _, rows, ny = parts[0].shape
     group = w_first.shape[1] // 4
     lanes = w_second.shape[0] // 12
-    vmem = pl.BlockSpec(memory_space=pltpu.VMEM)
     smem = pl.BlockSpec(memory_space=pltpu.SMEM)
-    flops = (rows + 2) * ny * (w_first.size + w_second.size)
+    whole = lambda a: pl.BlockSpec(a.shape, lambda x: (0,) * a.ndim)
+    flops = width * (rows + 2) * ny * (w_first.size + w_second.size)
     return pl.pallas_call(
         convolution_kernel,
-        in_specs=[smem, vmem, vmem, vmem, vmem, vmem, smem],
-        out_specs=vmem,
-        out_shape=jax.ShapeDtypeStruct((channels, rows, ny), BF16),
+        grid=(width,),
+        in_specs=[smem]
+        + [pl.BlockSpec((1,) + a.shape[1:], lambda x: (x, 0, 0, 0)) for a in parts]
+        + [whole(w_first), whole(b_first), whole(w_second), smem],
+        out_specs=pl.BlockSpec((1,) + shape[1:3] + (1,) + shape[4:], lambda x: (0, 0, 0, x, 0, 0)),
+        out_shape=jax.ShapeDtypeStruct(shape, BF16),
         scratch_shapes=[
-            pltpu.VMEM((ny // 128, depth * group, 128), F32),
+            pltpu.VMEM((ny // 128, (rows + 4) * group, 128), F32),
             pltpu.VMEM((ny // 128, lanes * rows, 128), F32),
         ],
         compiler_params=pltpu.CompilerParams(vmem_limit_bytes=24 * 2**20),
         cost_estimate=pl.CostEstimate(flops=flops, bytes_accessed=2**20, transcendentals=0),
         name="convolutions",
-    )(ends, own, other, w_first, b_first, w_second, b_second)
+    )(ends, *parts, w_first, b_first, w_second, b_second)
 
 
 def round_up(value, unit):
@@ -525,14 +530,13 @@
     images = prepare_image(current_image, pairs)
     gathers = [Gather(ring, images[x : x + 1]) for x in range(width)]
     kept = lax.all_to_all(pairs, SLAB, split_axis=0, concat_axis=0, tiled=True)
-    halves = [kept[:, x : x + 1] for x in range(width)]
     for step in range(len(ring.steps())):
         for gather in gathers:
-            gather.step(*(weights + (mask,) if step == 1 else (halves[step - 2],) if 2 <= step < 2 + width else ()))
-    swapped = [lax.ppermute(half, COIL, swap) for half in halves]
+            gather.step(*(weights + (mask,) if step == 1 else (kept,) if step == 2 else ()))
+    swapped = lax.ppermute(kept, COIL, swap)
     scatters = []
     for x in range(width):
-        scatters.append(Scatter(ring, *gradient(where, gathers[x].pieces(), [(kept, x), (swapped[x], 0)], measured, mask, tables, x)))
+        scatters.append(Scatter(ring, *gradient(where, gathers[x].pieces(), [(kept, x), (swapped, x)], measured, mask, tables, x)))
     for _ in ring.steps():
         for scatter in scatters:
             scatter.step()
@@ -540,13 +544,12 @@
     updated = update(images, chip[:, 0], lax.ppermute(chip[:, 1].astype(BF16), SLAB, ring.siblings()))
     up = [(i, i + 1) for i in range(devices - 1)]
     down = [(i + 1, i) for i in range(devices - 1)]
-    before = lax.ppermute(updated[:, :, rows - 2 :], SLAB, up)
-    behind = lax.ppermute(updated[:, :, :2], SLAB, down)
-    refined = []
-    for x in range(width):
-        bordered = jnp.concatenate([before[x], updated[x], behind[x]], axis=1)
-        refined.append(convolutions(ends, bordered, lax.ppermute(bordered, COIL, swap), *weights, second_bias))
-    return jnp.stack(refined, axis=1).reshape(current_image.shape)
+    other = lax.ppermute(updated, COIL, swap)
+    edges = jnp.concatenate(
+        [lax.ppermute(updated[:, :, rows - 2 :], SLAB, up), lax.ppermute(updated[:, :, :2], SLAB, down)], axis=2
+    )
+    parts = (updated, edges, other, lax.ppermute(edges, COIL, swap))
+    return convolutions(ends, parts, *weights, second_bias, current_image.shape)
 
 
 def with_halo(cells, sides, width):

time: 140 us -> 137 us (0.979); the launches traced: 140 us -> 135 us
  waiting for transfers between devices: 36 us -> 33.5 us
    ppermute x6 -> x5, waiting for transfers between devices: 8.11 us -> 4.5 us  [the longest x1 2.56 us: paired(): parts = (updated, edges, other, lax.ppermute(edges, COIL, swap))]
    ppermute x2, waiting for transfers between devices: 2.27 us -> 0.64 us  [step(): lax.ppermute(self.own[1], SLAB, self.ring.perm())]
    ppermute x6 -> x5, starting transfers between devices: 10.1 us -> 9.85 us  [the longest x1 3.91 us: paired(): lax.ppermute(updated[:, :, rows - 2:], SLAB, up)]
    pallas_call x2 -> x1, Pallas kernels: 8.85 us -> 8.97 us  [convolutions(): pl.pallas_call(convolution_kernel, grid=(width,), in_specs=[smem] + [pl.B...]
    unnamed x36 -> x40, local copies, waits for them, and re-layouts: 4.85 us -> 4.86 us
  transfers between devices with their start and end apart: 38 -> 37, of which waited for: 18 -> 20; matrix products, arithmetic and copies ran while one was open for 5% -> 4% of each run, Pallas kernels for 20% -> 18%
where the time goes in v4:
time: 137 us; the launch traced here: 135 us
  starting transfers between devices  54.1 us (39%)
  Pallas kernels  37.4 us (27%)
  waiting for transfers between devices  33.5 us (24%)
  local copies, waits for them, and re-layouts  6.5 us (5%)
  other arithmetic  3.12 us (2%)
    pallas_call x2, Pallas kernels, gradient(): pl.pallas_call(functools.partial(gradient_kernel, len(images), n), grid_s...  23.9 us
    ppermute x8, starting transfers between devices, step(): self.held = lax.ppermute(total.astype(BF16), SLAB, self.ring.perm())  14.2 us
    ppermute x6, waiting for transfers between devices, step(): lax.ppermute(after(held, *earlier) if earlier else held, SLAB, self.ring....  10.5 us
    pallas_call x1, Pallas kernels, convolutions(): pl.pallas_call(convolution_kernel, grid=(width,), in_specs=[smem] + [pl.B...  8.97 us
    ppermute x8, waiting for transfers between devices, step(): self.held = lax.ppermute(total.astype(BF16), SLAB, self.ring.perm())  8.12 us
    ppermute x6, starting transfers between devices, step(): lax.ppermute(after(held, *earlier) if earlier else held, SLAB, self.ring....  7.6 us
    ppermute x2, waiting for transfers between devices, __init__(): self.first = lax.ppermute(mine, SLAB, ring.perm())  7.37 us
    ppermute x8, starting transfers between devices, step(): self.other.append(lax.ppermute(self.held, SLAB, self.ring.siblings()))  6.05 us
  transfers between devices with their start and end apart: 37, of which 20 were waited for; matrix products, arithmetic and copies ran while one was open for 4% of the time, Pallas kernels for 18%

profile of v4, /device:TPU:1, one launch (start us, length us, event | category | flops | bytes accessed | tf_op | source)
XLA Modules:
  0.0 135.1 jit_solution(5602303373688413567)
XLA Ops:
  0.0 3.2 %prepare_maps.1.earlier = bf16[16,2,2,16,384]{4,3,2,1,0:T(8,128)(2,1)} custom-call(s32[1]{0:T(128)} %bitcast.2.which, bf16[16,2,2,2,16,384]{5,4,3,2,1,0:T(8,128)(2,1)} %bitcast.69, bf16[128,128]{1,0:T(8,128)(2,1)} %constant.197.clone.along_z, bf16[384,384]{1,0:T(8,128)(2,1)} %constant.198.clone.along_y), custom_call_target="tpu_custom_call" | custom-call | tf_op jit(solution)/shard_map/prepare_maps/pallas_call | solution.py:362
  3.2 0.7 prepare_image.1.image
  4.0 2.7 %collective-permute-start.17 = (bf16[1,10,16,384]{3,2,1,0:T(8,128)(2,1)S(1)}, bf16[1,10,16,384]{3,2,1,0:T(8,128)(2,1)S(1)}, u32[]{:S(2)}, u32[]{:S(2)}) collective-permute-start(bf16[1,10,16,384]{3,2,1,0:T(8,128)(2,1)S(1)} %get-tuple-element.27.refs_0_), channel_id=1, source_target_pairs={{0,8},{2,6},{8,16},{10,2},{16,24},{18,10},{24,28},{26,18},{28,20},... | collective-permute-start | bytes 368648 | tf_op jit(solution)/shard_map/ppermute | solution.py:103
  6.7 5.2 %all-to-all-start = ((bf16[16,2,2,16,384]{4,3,2,1,0:T(8,128)(2,1)}), bf16[16,2,2,16,384]{4,3,2,1,0:T(8,128)(2,1)S(1)}, u32[]{:S(2)}, u32[]{:S(2)}) async-start(bf16[16,2,2,16,384]{4,3,2,1,0:T(8,128)(2,1)} %prepare_maps.1.earlier), calls=%async_computation | async-start | bytes 1572864 | tf_op jit(solution)/shard_map/all_to_all | solution.py:532
  11.9 0.2 collective-permute-start
  12.1 1.6 %collective-permute-start.1 = (bf16[1,10,16,384]{3,2,1,0:T(8,128)(2,1)S(1)}, bf16[1,10,16,384]{3,2,1,0:T(8,128)(2,1)}, u32[]{:S(2)}, u32[]{:S(2)}) collective-permute-start(bf16[1,10,16,384]{3,2,1,0:T(8,128)(2,1)S(1)} %get-tuple-element.28.refs_0_), channel_id=1, source_target_pairs={{0,8},{2,6},{8,16},{10,2},{16,24},{18,10},{24,28},{26,18},{28,20},... | collective-permute-start | bytes 368648 | tf_op jit(solution)/shard_map/ppermute | solution.py:103
  14.4 0.1 reshape.28
  14.8 1.7 %convert_element_type.117.refs_13_ = bf16[1,5,384,256]{3,2,1,0:T(8,128)(2,1)S(1)} convert(s32[1,5,384,256]{3,2,1,0:T(8,128)} %param.18) | non-fusion elementwise | flops 491520 | bytes 2949120 | tf_op jit(solution)/shard_map/convert_element_type | solution.py:525
  16.6 1.2 collective-permute-start.18
  17.8 1.2 collective-permute-start.2
  19.1 7.4 %collective-permute-done.1 = bf16[1,10,16,384]{3,2,1,0:T(8,128)(2,1)} collective-permute-done((bf16[1,10,16,384]{3,2,1,0:T(8,128)(2,1)S(1)}, bf16[1,10,16,384]{3,2,1,0:T(8,128)(2,1)}, u32[]{:S(2)}, u32[]{:S(2)}) %collective-permute-start.1) | collective-permute-done | bytes 122912 | tf_op jit(solution)/shard_map/ppermute | solution.py:103
  26.4 0.9 constant_dynamic-update-slice_fusion.1
  27.4 0.6 collective-permute-done.18
  28.0 1.4 %collective-permute-start.19 = (bf16[2,10,16,384]{3,2,1,0:T(8,128)(2,1)S(1)}, bf16[2,10,16,384]{3,2,1,0:T(8,128)(2,1)}, u32[]{:S(2)}, u32[]{:S(2)}) collective-permute-start(bf16[2,10,16,384]{3,2,1,0:T(8,128)(2,1)S(1)} %constant_dynamic-update-slice_fusion.2.refs_2_), channel_id=1, source_target_pairs={{0,8},{2,6},{8,16},{10,2},{16,24},{18,10},{24,28},{26,18},{28,20},... | collective-permute-start | bytes 737288 | tf_op jit(solution)/shard_map/ppermute | solution.py:114
  29.4 1.2 all-to-all-done.refs_10_
  30.6 1.2 collective-permute-start.10
  31.9 4.4 %collective-permute-start.3 = (bf16[2,10,16,384]{3,2,1,0:T(8,128)(2,1)S(1)}, bf16[2,10,16,384]{3,2,1,0:T(8,128)(2,1)S(1)}, u32[]{:S(2)}, u32[]{:S(2)}) collective-permute-start(bf16[2,10,16,384]{3,2,1,0:T(8,128)(2,1)S(1)} %constant_dynamic-update-slice_fusion.refs_2_), channel_id=1, source_target_pairs={{0,8},{2,6},{8,16},{10,2},{16,24},{18,10},{24,28},{26,18},{28,20},... | collective-permute-start | bytes 737288 | tf_op jit(solution)/shard_map/ppermute | solution.py:114
  36.2 3.1 %collective-permute-done.19.refs_3_ = bf16[2,10,16,384]{3,2,1,0:T(8,128)(2,1)} collective-permute-done((bf16[2,10,16,384]{3,2,1,0:T(8,128)(2,1)S(1)}, bf16[2,10,16,384]{3,2,1,0:T(8,128)(2,1)}, u32[]{:S(2)}, u32[]{:S(2)}) %collective-permute-start.19) | collective-permute-done | bytes 245792 | tf_op jit(solution)/shard_map/ppermute | solution.py:114
  39.3 2.6 %collective-permute-done.3.refs_3_ = bf16[2,10,16,384]{3,2,1,0:T(8,128)(2,1)S(1)} collective-permute-done((bf16[2,10,16,384]{3,2,1,0:T(8,128)(2,1)S(1)}, bf16[2,10,16,384]{3,2,1,0:T(8,128)(2,1)S(1)}, u32[]{:S(2)}, u32[]{:S(2)}) %collective-permute-start.3) | collective-permute-done | bytes 245792 | tf_op jit(solution)/shard_map/ppermute | solution.py:114
  41.9 2.7 %collective-permute-start.22 = (bf16[2,10,16,384]{3,2,1,0:T(8,128)(2,1)S(1)}, bf16[2,10,16,384]{3,2,1,0:T(8,128)(2,1)S(1)}, u32[]{:S(2)}, u32[]{:S(2)}) collective-permute-start(bf16[2,10,16,384]{3,2,1,0:T(8,128)(2,1)S(1)} %constant_dynamic-update-slice_fusion.2.refs_2_), channel_id=1, source_target_pairs={{0,2},{2,0},{4,6},{6,4},{8,10},{10,8},{12,14},{14,12},{16,18},{18,... | collective-permute-start | bytes 737288 | tf_op jit(solution)/shard_map/ppermute | solution.py:116
  44.6 0.3 collective-permute-done.20.refs_4_
  45.0 2.5 %collective-permute-done.4.refs_4_ = bf16[2,10,16,384]{3,2,1,0:T(8,128)(2,1)S(1)} collective-permute-done((bf16[2,10,16,384]{3,2,1,0:T(8,128)(2,1)S(1)}, bf16[2,10,16,384]{3,2,1,0:T(8,128)(2,1)S(1)}, u32[]{:S(2)}, u32[]{:S(2)}) %collective-permute-start.4) | collective-permute-done | bytes 245792 | tf_op jit(solution)/shard_map/ppermute | solution.py:114
  47.6 1.5 %collective-permute-start.24 = (bf16[2,10,16,384]{3,2,1,0:T(8,128)(2,1)S(1)}, bf16[2,10,16,384]{3,2,1,0:T(8,128)(2,1)}, u32[]{:S(2)}, u32[]{:S(2)}) collective-permute-start(bf16[2,10,16,384]{3,2,1,0:T(8,128)(2,1)S(1)} %collective-permute-done.20.refs_4_), channel_id=1, source_target_pairs={{0,2},{2,0},{4,6},{6,4},{8,10},{10,8},{12,14},{14,12},{16,18},{18,... | collective-permute-start | bytes 737288 | tf_op jit(solution)/shard_map/ppermute | solution.py:116
  49.1 0.7 slice.136
  49.7 0.7 copy-done.7
  50.4 1.7 %collective-permute-start.5 = (bf16[1,10,16,384]{3,2,1,0:T(8,128)(2,1)}, bf16[1,10,16,384]{3,2,1,0:T(8,128)(2,1)}, u32[]{:S(2)}, u32[]{:S(2)}) collective-permute-start(bf16[1,10,16,384]{3,2,1,0:T(8,128)(2,1)} %slice.136), channel_id=1, source_target_pairs={{0,8},{2,6},{8,16},{10,2},{16,24},{18,10},{24,28},{26,18},{28,20},... | collective-permute-start | bytes 368648 | tf_op jit(solution)/shard_map/ppermute | solution.py:114
  52.3 0.5 collective-permute-start.6
  52.9 1.9 %collective-permute-done.5.refs_5_ = bf16[1,10,16,384]{3,2,1,0:T(8,128)(2,1)} collective-permute-done((bf16[1,10,16,384]{3,2,1,0:T(8,128)(2,1)}, bf16[1,10,16,384]{3,2,1,0:T(8,128)(2,1)}, u32[]{:S(2)}, u32[]{:S(2)}) %collective-permute-start.5) | collective-permute-done | bytes 122912 | tf_op jit(solution)/shard_map/ppermute | solution.py:114
  54.8 0.8 collective-permute-start.7
  55.6 0.5 collective-permute-start.9
  56.1 0.9 copy-done.8
  57.1 0.9 copy-done.12
  58.0 1.3 copy-done.14
  59.3 11.7 %gradient.3 = (bf16[2,10,16,384]{3,2,1,0:T(8,128)(2,1)S(1)}, bf16[7,10,16,384]{3,2,1,0:T(8,128)(2,1)S(1)}, bf16[7,10,16,384]{3,2,1,0:T(8,128)(2,1)S(1)}) custom-call(s32[33]{0:T(128)S(1)} %concatenate.35.slabs, bf16[1,10,16,384]{3,2,1,0:T(8,128)(2,1)S(1)} %get-tuple-element.27.refs_0_, bf16[1,10,16,384]{3,2,1,0:T(8,128)(2,1)S(1)} %copy-done.12, ...), custom_call_target="tpu_custom_call" | custom-call | flops 10066329600 | bytes 8388608 | tf_op jit(solution)/shard_map/gradient/pallas_call | solution.py:281
  71.1 0.2 collective-permute-start.26
  71.3 12.2 %gradient.2 = (bf16[2,10,16,384]{3,2,1,0:T(8,128)(2,1)S(1)}, bf16[7,10,16,384]{3,2,1,0:T(8,128)(2,1)S(1)}, bf16[7,10,16,384]{3,2,1,0:T(8,128)(2,1)S(1)}) custom-call(s32[33]{0:T(128)S(1)} %concatenate.35.slabs, bf16[1,10,16,384]{3,2,1,0:T(8,128)(2,1)S(1)} %get-tuple-element.28.refs_0_, bf16[1,10,16,384]{3,2,1,0:T(8,128)(2,1)S(1)} %copy-done.10, ...), custom_call_target="tpu_custom_call" | custom-call | flops 10066329600 | bytes 8388608 | tf_op jit(solution)/shard_map/gradient/pallas_call | solution.py:281
  83.4 0.5 collective-permute-start.11
  84.0 1.8 %collective-permute-start.27 = (bf16[1,10,16,384]{3,2,1,0:T(8,128)(2,1)S(1)}, bf16[1,10,16,384]{3,2,1,0:T(8,128)(2,1)S(1)}, u32[]{:S(2)}, u32[]{:S(2)}) collective-permute-start(bf16[1,10,16,384]{3,2,1,0:T(8,128)(2,1)S(1)} %add_convert_fusion.4), channel_id=1, source_target_pairs={{0,8},{2,6},{8,16},{10,2},{16,24},{18,10},{24,28},{26,18},{28,20},... | collective-permute-start | bytes 368648 | tf_op jit(solution)/shard_map/ppermute | solution.py:140
  86.0 1.8 %collective-permute-start.12 = (bf16[1,10,16,384]{3,2,1,0:T(8,128)(2,1)S(1)}, bf16[1,10,16,384]{3,2,1,0:T(8,128)(2,1)S(1)}, u32[]{:S(2)}, u32[]{:S(2)}) collective-permute-start(bf16[1,10,16,384]{3,2,1,0:T(8,128)(2,1)S(1)} %add_convert_fusion.5), channel_id=1, source_target_pairs={{0,8},{2,6},{8,16},{10,2},{16,24},{18,10},{24,28},{26,18},{28,20},... | collective-permute-start | bytes 368648 | tf_op jit(solution)/shard_map/ppermute | solution.py:140
  87.9 0.2 collective-permute-done.27
  88.1 1.8 %collective-permute-start.28 = (bf16[2,10,16,384]{3,2,1,0:T(8,128)(2,1)S(1)}, bf16[2,10,16,384]{3,2,1,0:T(8,128)(2,1)S(1)}, u32[]{:S(2)}, u32[]{:S(2)}) collective-permute-start(bf16[2,10,16,384]{3,2,1,0:T(8,128)(2,1)S(1)} %pad_maximum_fusion.2), channel_id=1, source_target_pairs={{0,8},{2,6},{8,16},{10,2},{16,24},{18,10},{24,28},{26,18},{28,20},... | collective-permute-start | bytes 737288 | tf_op jit(solution)/shard_map/ppermute | solution.py:140
  89.9 0.2 collective-permute-done.12
  90.2 1.8 %collective-permute-start.13 = (bf16[2,10,16,384]{3,2,1,0:T(8,128)(2,1)S(1)}, bf16[2,10,16,384]{3,2,1,0:T(8,128)(2,1)S(1)}, u32[]{:S(2)}, u32[]{:S(2)}) collective-permute-start(bf16[2,10,16,384]{3,2,1,0:T(8,128)(2,1)S(1)} %pad_maximum_fusion.1), channel_id=1, source_target_pairs={{0,8},{2,6},{8,16},{10,2},{16,24},{18,10},{24,28},{26,18},{28,20},... | collective-permute-start | bytes 737288 | tf_op jit(solution)/shard_map/ppermute | solution.py:140
  91.9 1.6 %collective-permute-done.28 = bf16[2,10,16,384]{3,2,1,0:T(8,128)(2,1)S(1)} collective-permute-done((bf16[2,10,16,384]{3,2,1,0:T(8,128)(2,1)S(1)}, bf16[2,10,16,384]{3,2,1,0:T(8,128)(2,1)S(1)}, u32[]{:S(2)}, u32[]{:S(2)}) %collective-permute-start.28) | collective-permute-done | bytes 245792 | tf_op jit(solution)/shard_map/ppermute | solution.py:140
  93.6 1.8 %collective-permute-start.29 = (bf16[2,10,16,384]{3,2,1,0:T(8,128)(2,1)S(1)}, bf16[2,10,16,384]{3,2,1,0:T(8,128)(2,1)S(1)}, u32[]{:S(2)}, u32[]{:S(2)}) collective-permute-start(bf16[2,10,16,384]{3,2,1,0:T(8,128)(2,1)S(1)} %add_convert_fusion.1), channel_id=1, source_target_pairs={{0,8},{2,6},{8,16},{10,2},{16,24},{18,10},{24,28},{26,18},{28,20},... | collective-permute-start | bytes 737288 | tf_op jit(solution)/shard_map/ppermute | solution.py:140
  95.4 0.8 collective-permute-done.13
  96.3 1.8 %collective-permute-start.14 = (bf16[2,10,16,384]{3,2,1,0:T(8,128)(2,1)S(1)}, bf16[2,10,16,384]{3,2,1,0:T(8,128)(2,1)S(1)}, u32[]{:S(2)}, u32[]{:S(2)}) collective-permute-start(bf16[2,10,16,384]{3,2,1,0:T(8,128)(2,1)S(1)} %add_convert_fusion.3), channel_id=1, source_target_pairs={{0,8},{2,6},{8,16},{10,2},{16,24},{18,10},{24,28},{26,18},{28,20},... | collective-permute-start | bytes 737288 | tf_op jit(solution)/shard_map/ppermute | solution.py:140
  98.0 1.0 collective-permute-done.29
  99.1 1.8 %collective-permute-start.30 = (bf16[2,10,16,384]{3,2,1,0:T(8,128)(2,1)S(1)}, bf16[2,10,16,384]{3,2,1,0:T(8,128)(2,1)S(1)}, u32[]{:S(2)}, u32[]{:S(2)}) collective-permute-start(bf16[2,10,16,384]{3,2,1,0:T(8,128)(2,1)S(1)} %add_convert_fusion), channel_id=1, source_target_pairs={{0,8},{2,6},{8,16},{10,2},{16,24},{18,10},{24,28},{26,18},{28,20},... | collective-permute-start | bytes 737288 | tf_op jit(solution)/shard_map/ppermute | solution.py:140
  100.9 0.8 collective-permute-done.14
  101.8 1.8 %collective-permute-start.15 = (bf16[2,10,16,384]{3,2,1,0:T(8,128)(2,1)S(1)}, bf16[2,10,16,384]{3,2,1,0:T(8,128)(2,1)S(1)}, u32[]{:S(2)}, u32[]{:S(2)}) collective-permute-start(bf16[2,10,16,384]{3,2,1,0:T(8,128)(2,1)S(1)} %add_convert_fusion.2), channel_id=1, source_target_pairs={{0,8},{2,6},{8,16},{10,2},{16,24},{18,10},{24,28},{26,18},{28,20},... | collective-permute-start | bytes 737288 | tf_op jit(solution)/shard_map/ppermute | solution.py:140
  103.5 0.7 collective-permute-done.30
  104.3 2.8 %collective-permute-done.15 = bf16[2,10,16,384]{3,2,1,0:T(8,128)(2,1)S(1)} collective-permute-done((bf16[2,10,16,384]{3,2,1,0:T(8,128)(2,1)S(1)}, bf16[2,10,16,384]{3,2,1,0:T(8,128)(2,1)S(1)}, u32[]{:S(2)}, u32[]{:S(2)}) %collective-permute-start.15) | collective-permute-done | bytes 245792 | tf_op jit(solution)/shard_map/ppermute | solution.py:140
  107.3 3.6 %collective-permute-start.31 = (bf16[2,10,16,384]{3,2,1,0:T(8,128)(2,1)S(1)}, bf16[2,10,16,384]{3,2,1,0:T(8,128)(2,1)S(1)}, u32[]{:S(2)}, u32[]{:S(2)}) collective-permute-start(bf16[2,10,16,384]{3,2,1,0:T(8,128)(2,1)S(1)} %fusion.5), channel_id=1, source_target_pairs={{0,2},{2,0},{4,6},{6,4},{8,10},{10,8},{12,14},{14,12},{16,18},{18,... | collective-permute-start | bytes 737288 | tf_op jit(solution)/shard_map/ppermute | solution.py:544
  110.9 1.1 collective-permute-done.31.received
  112.0 0.7 update.1.refs_0_
  112.7 3.9 %collective-permute-start.32 = (bf16[2,10,2,384]{3,2,1,0:T(2,128)(2,1)S(1)}, bf16[2,10,2,384]{3,2,1,0:T(2,128)(2,1)S(1)}, u32[]{:S(2)}, u32[]{:S(2)}) collective-permute-start(bf16[2,10,2,384]{3,2,1,0:T(2,128)(2,1)S(1)} %get-tuple-element.25), channel_id=1, source_target_pairs={{0,2},{2,4},{4,6},{6,8},{8,10},{10,12},{12,14},{14,16},{16,18},{18... | collective-permute-start | bytes 92168 | tf_op jit(solution)/shard_map/ppermute | solution.py:549
  116.7 2.1 %collective-permute-start.33 = (bf16[2,10,2,384]{3,2,1,0:T(2,128)(2,1)S(1)}, bf16[2,10,2,384]{3,2,1,0:T(2,128)(2,1)S(1)}, u32[]{:S(2)}, u32[]{:S(2)}) collective-permute-start(bf16[2,10,2,384]{3,2,1,0:T(2,128)(2,1)S(1)} %get-tuple-element.26), channel_id=1, source_target_pairs={{2,0},{4,2},{6,4},{8,6},{10,8},{12,10},{14,12},{16,14},{18,16},{20... | collective-permute-start | bytes 92168 | tf_op jit(solution)/shard_map/ppermute | solution.py:549
  118.8 1.3 collective-permute-start.34
  120.1 0.1 copy.23.refs_5_
  120.2 1.9 %collective-permute-done.33 = bf16[2,10,2,384]{3,2,1,0:T(2,128)(2,1)S(1)} collective-permute-done((bf16[2,10,2,384]{3,2,1,0:T(2,128)(2,1)S(1)}, bf16[2,10,2,384]{3,2,1,0:T(2,128)(2,1)S(1)}, u32[]{:S(2)}, u32[]{:S(2)}) %collective-permute-start.33) | collective-permute-done | bytes 30752 | tf_op jit(solution)/shard_map/ppermute | solution.py:549
  122.2 1.3 collective-permute-start.35
  123.6 2.6 %collective-permute-done.35.refs_3_ = bf16[2,10,4,384]{3,2,1,0:T(4,128)(2,1)S(1)} collective-permute-done((bf16[2,10,4,384]{3,2,1,0:T(4,128)(2,1)S(1)}, bf16[2,10,4,384]{3,2,1,0:T(4,128)(2,1)S(1)}, u32[]{:S(2)}, u32[]{:S(2)}) %collective-permute-start.35) | collective-permute-done | bytes 61472 | tf_op jit(solution)/shard_map/ppermute | solution.py:551
  126.2 9.0 %convolutions.1 = bf16[1,5,2,2,16,384]{5,4,3,2,1,0:T(8,128)(2,1)} custom-call(s32[2]{0:T(128)S(1)} %add_convert_fusion.6.ends, bf16[2,10,16,384]{3,2,1,0:T(8,128)(2,1)S(1)} %update.1.refs_0_, bf16[2,10,4,384]{3,2,1,0:T(4,128)(2,1)S(1)} %pad_maximum_fusion.3.refs_1_, bf16[2,10,16,384]{3,2,1,0:T(8,128)(2,1)S(1)} %collective-permute-done.34.refs_2_, ...), custom_call_target="tpu_custom_call" | custom-call | flops 1585446912 | bytes 1048576 | tf_op jit(solution)/shard_map/convolutions/pallas_call | solution.py:458
  (104 shorter events, 2.6 us)
Async XLA Ops:
  0.0 3.2 %copy-start.3 = (bf16[128,128]{1,0:T(8,128)(2,1)S(1)}, bf16[128,128]{1,0:T(8,128)(2,1)}, u32[]{:S(2)}) copy-start(bf16[128,128]{1,0:T(8,128)(2,1)} %constant.197.clone.along_z) | copy-start | bytes 98308
  0.0 3.2 %copy-start = (bf16[384,384]{1,0:T(8,128)(2,1)S(1)}, bf16[384,384]{1,0:T(8,128)(2,1)}, u32[]{:S(2)}) copy-start(bf16[384,384]{1,0:T(8,128)(2,1)} %constant.198.clone.along_y) | copy-start | bytes 884740
  0.0 3.2 %copy-start.2 = (bf16[1,5,2,2,16,384]{5,4,3,2,1,0:T(8,128)(2,1)S(1)}, bf16[1,5,2,2,16,384]{5,4,3,2,1,0:T(8,128)(2,1)}, u32[]{:S(2)}) copy-start(bf16[1,5,2,2,16,384]{5,4,3,2,1,0:T(8,128)(2,1)} %image.1) | copy-start | bytes 737284
  3.2 10.5 %copy-start.16 = (bf16[64,10,3,3,3]{0,4,3,2,1:T(4,128)(2,1)S(1)}, bf16[64,10,3,3,3]{0,4,3,2,1:T(4,128)(2,1)}, u32[]{:S(2)}) copy-start(bf16[64,10,3,3,3]{0,4,3,2,1:T(4,128)(2,1)} %param.19) | copy-start | bytes 103684
  3.9 10.4 %copy-start.17 = (bf16[10,64,3,3,3]{1,4,3,2,0:T(4,128)(2,1)S(1)}, bf16[10,64,3,3,3]{1,4,3,2,0:T(4,128)(2,1)}, u32[]{:S(2)}) copy-start(bf16[10,64,3,3,3]{1,4,3,2,0:T(4,128)(2,1)} %param.21) | copy-start | bytes 103684
  3.9 10.8 %copy-start.18 = (f32[64]{0:T(128)S(1)}, f32[64]{0:T(128)}, u32[]{:S(2)}) copy-start(f32[64]{0:T(128)} %param.20) | copy-start | bytes 772
  3.9 12.6 %collective-permute-start.16 = (bf16[1,10,16,384]{3,2,1,0:T(8,128)(2,1)S(1)}, bf16[1,10,16,384]{3,2,1,0:T(8,128)(2,1)S(1)}, u32[]{:S(2)}, u32[]{:S(2)}) collective-permute-start(bf16[1,10,16,384]{3,2,1,0:T(8,128)(2,1)S(1)} %get-tuple-element.27.refs_0_), channel_id=1, source_target_pairs={{0,2},{2,0},{4,6},{6,4},{8,10},{10,8},{12,14},{14,12},{16,18},{18,... | collective-permute-start | bytes 368648 | tf_op jit(solution)/shard_map/ppermute | solution.py:104
  4.0 13.8 %collective-permute-start.17 = (bf16[1,10,16,384]{3,2,1,0:T(8,128)(2,1)S(1)}, bf16[1,10,16,384]{3,2,1,0:T(8,128)(2,1)S(1)}, u32[]{:S(2)}, u32[]{:S(2)}) collective-permute-start(bf16[1,10,16,384]{3,2,1,0:T(8,128)(2,1)S(1)} %get-tuple-element.27.refs_0_), channel_id=1, source_target_pairs={{0,8},{2,6},{8,16},{10,2},{16,24},{18,10},{24,28},{26,18},{28,20},... | collective-permute-start | bytes 368648 | tf_op jit(solution)/shard_map/ppermute | solution.py:103
  6.7 23.9 %all-to-all-start = ((bf16[16,2,2,16,384]{4,3,2,1,0:T(8,128)(2,1)}), bf16[16,2,2,16,384]{4,3,2,1,0:T(8,128)(2,1)S(1)}, u32[]{:S(2)}, u32[]{:S(2)}) async-start(bf16[16,2,2,16,384]{4,3,2,1,0:T(8,128)(2,1)} %prepare_maps.1.earlier), calls=%async_computation | async-start | bytes 1572864 | tf_op jit(solution)/shard_map/all_to_all | solution.py:532
  11.9 5.9 %collective-permute-start = (bf16[1,10,16,384]{3,2,1,0:T(8,128)(2,1)S(1)}, bf16[1,10,16,384]{3,2,1,0:T(8,128)(2,1)S(1)}, u32[]{:S(2)}, u32[]{:S(2)}) collective-permute-start(bf16[1,10,16,384]{3,2,1,0:T(8,128)(2,1)S(1)} %get-tuple-element.28.refs_0_), channel_id=1, source_target_pairs={{0,2},{2,0},{4,6},{6,4},{8,10},{10,8},{12,14},{14,12},{16,18},{18,... | collective-permute-start | bytes 368648 | tf_op jit(solution)/shard_map/ppermute | solution.py:104
  12.1 14.3 %collective-permute-start.1 = (bf16[1,10,16,384]{3,2,1,0:T(8,128)(2,1)S(1)}, bf16[1,10,16,384]{3,2,1,0:T(8,128)(2,1)}, u32[]{:S(2)}, u32[]{:S(2)}) collective-permute-start(bf16[1,10,16,384]{3,2,1,0:T(8,128)(2,1)S(1)} %get-tuple-element.28.refs_0_), channel_id=1, source_target_pairs={{0,8},{2,6},{8,16},{10,2},{16,24},{18,10},{24,28},{26,18},{28,20},... | collective-permute-start | bytes 368648 | tf_op jit(solution)/shard_map/ppermute | solution.py:103
  16.5 22.8 %copy-start.11 = (bf16[1,10,16,384]{3,2,1,0:T(8,128)(2,1)}, bf16[1,10,16,384]{3,2,1,0:T(8,128)(2,1)S(1)}, u32[]{:S(2)}) copy-start(bf16[1,10,16,384]{3,2,1,0:T(8,128)(2,1)S(1)} %collective-permute-done.16.refs_1_) | copy-start | bytes 368644
  16.6 11.4 %collective-permute-start.18 = (bf16[1,10,16,384]{3,2,1,0:T(8,128)(2,1)S(1)}, bf16[1,10,16,384]{3,2,1,0:T(8,128)(2,1)S(1)}, u32[]{:S(2)}, u32[]{:S(2)}) collective-permute-start(bf16[1,10,16,384]{3,2,1,0:T(8,128)(2,1)S(1)} %collective-permute-done.16.refs_1_), channel_id=1, source_target_pairs={{0,8},{2,6},{8,16},{10,2},{16,24},{18,10},{24,28},{26,18},{28,20},... | collective-permute-start | bytes 368648 | tf_op jit(solution)/shard_map/ppermute | solution.py:111
  17.8 21.5 %copy-start.9 = (bf16[1,10,16,384]{3,2,1,0:T(8,128)(2,1)}, bf16[1,10,16,384]{3,2,1,0:T(8,128)(2,1)S(1)}, u32[]{:S(2)}) copy-start(bf16[1,10,16,384]{3,2,1,0:T(8,128)(2,1)S(1)} %collective-permute-done.refs_1_) | copy-start | bytes 368644
  17.8 14.0 %collective-permute-start.2 = (bf16[1,10,16,384]{3,2,1,0:T(8,128)(2,1)S(1)}, bf16[1,10,16,384]{3,2,1,0:T(8,128)(2,1)S(1)}, u32[]{:S(2)}, u32[]{:S(2)}) collective-permute-start(bf16[1,10,16,384]{3,2,1,0:T(8,128)(2,1)S(1)} %collective-permute-done.refs_1_), channel_id=1, source_target_pairs={{0,8},{2,6},{8,16},{10,2},{16,24},{18,10},{24,28},{26,18},{28,20},... | collective-permute-start | bytes 368648 | tf_op jit(solution)/shard_map/ppermute | solution.py:111
  28.0 11.3 %collective-permute-start.19 = (bf16[2,10,16,384]{3,2,1,0:T(8,128)(2,1)S(1)}, bf16[2,10,16,384]{3,2,1,0:T(8,128)(2,1)}, u32[]{:S(2)}, u32[]{:S(2)}) collective-permute-start(bf16[2,10,16,384]{3,2,1,0:T(8,128)(2,1)S(1)} %constant_dynamic-update-slice_fusion.2.refs_2_), channel_id=1, source_target_pairs={{0,8},{2,6},{8,16},{10,2},{16,24},{18,10},{24,28},{26,18},{28,20},... | collective-permute-start | bytes 737288 | tf_op jit(solution)/shard_map/ppermute | solution.py:114
  30.6 25.5 %collective-permute-start.10 = (bf16[16,2,2,16,384]{4,3,2,1,0:T(8,128)(2,1)S(1)}, bf16[16,2,2,16,384]{4,3,2,1,0:T(8,128)(2,1)}, u32[]{:S(2)}, u32[]{:S(2)}) collective-permute-start(bf16[16,2,2,16,384]{4,3,2,1,0:T(8,128)(2,1)S(1)} %all-to-all-done.refs_10_), channel_id=1, source_target_pairs={{0,1},{1,0},{2,3},{3,2},{4,5},{5,4},{6,7},{7,6},{8,9},{9,8},{10,11... | collective-permute-start | bytes 2359304 | tf_op jit(solution)/shard_map/ppermute | solution.py:536
  31.9 10.1 %collective-permute-start.3 = (bf16[2,10,16,384]{3,2,1,0:T(8,128)(2,1)S(1)}, bf16[2,10,16,384]{3,2,1,0:T(8,128)(2,1)S(1)}, u32[]{:S(2)}, u32[]{:S(2)}) collective-permute-start(bf16[2,10,16,384]{3,2,1,0:T(8,128)(2,1)S(1)} %constant_dynamic-update-slice_fusion.refs_2_), channel_id=1, source_target_pairs={{0,8},{2,6},{8,16},{10,2},{16,24},{18,10},{24,28},{26,18},{28,20},... | collective-permute-start | bytes 737288 | tf_op jit(solution)/shard_map/ppermute | solution.py:114
  39.3 5.7 %collective-permute-start.20 = (bf16[2,10,16,384]{3,2,1,0:T(8,128)(2,1)}, bf16[2,10,16,384]{3,2,1,0:T(8,128)(2,1)S(1)}, u32[]{:S(2)}, u32[]{:S(2)}) collective-permute-start(bf16[2,10,16,384]{3,2,1,0:T(8,128)(2,1)} %collective-permute-done.19.refs_3_), channel_id=1, source_target_pairs={{0,8},{2,6},{8,16},{10,2},{16,24},{18,10},{24,28},{26,18},{28,20},... | collective-permute-start | bytes 737288 | tf_op jit(solution)/shard_map/ppermute | solution.py:114
  41.9 7.8 %copy-start.5 = (bf16[2,10,16,384]{3,2,1,0:T(8,128)(2,1)}, bf16[2,10,16,384]{3,2,1,0:T(8,128)(2,1)S(1)}, u32[]{:S(2)}) copy-start(bf16[2,10,16,384]{3,2,1,0:T(8,128)(2,1)S(1)} %collective-permute-done.3.refs_3_) | copy-start | bytes 737284
  41.9 5.7 %collective-permute-start.4 = (bf16[2,10,16,384]{3,2,1,0:T(8,128)(2,1)S(1)}, bf16[2,10,16,384]{3,2,1,0:T(8,128)(2,1)S(1)}, u32[]{:S(2)}, u32[]{:S(2)}) collective-permute-start(bf16[2,10,16,384]{3,2,1,0:T(8,128)(2,1)S(1)} %collective-permute-done.3.refs_3_), channel_id=1, source_target_pairs={{0,8},{2,6},{8,16},{10,2},{16,24},{18,10},{24,28},{26,18},{28,20},... | collective-permute-start | bytes 737288 | tf_op jit(solution)/shard_map/ppermute | solution.py:114
  41.9 7.8 %collective-permute-start.22 = (bf16[2,10,16,384]{3,2,1,0:T(8,128)(2,1)S(1)}, bf16[2,10,16,384]{3,2,1,0:T(8,128)(2,1)S(1)}, u32[]{:S(2)}, u32[]{:S(2)}) collective-permute-start(bf16[2,10,16,384]{3,2,1,0:T(8,128)(2,1)S(1)} %constant_dynamic-update-slice_fusion.2.refs_2_), channel_id=1, source_target_pairs={{0,2},{2,0},{4,6},{6,4},{8,10},{10,8},{12,14},{14,12},{16,18},{18,... | collective-permute-start | bytes 737288 | tf_op jit(solution)/shard_map/ppermute | solution.py:116
  44.6 7.7 %collective-permute-start.23 = (bf16[2,10,16,384]{3,2,1,0:T(8,128)(2,1)}, bf16[2,10,16,384]{3,2,1,0:T(8,128)(2,1)}, u32[]{:S(2)}, u32[]{:S(2)}) collective-permute-start(bf16[2,10,16,384]{3,2,1,0:T(8,128)(2,1)} %collective-permute-done.19.refs_3_), channel_id=1, source_target_pairs={{0,2},{2,0},{4,6},{6,4},{8,10},{10,8},{12,14},{14,12},{16,18},{18,... | collective-permute-start | bytes 737288 | tf_op jit(solution)/shard_map/ppermute | solution.py:116
  45.0 7.2 %collective-permute-start.21 = (bf16[1,10,16,384]{3,2,1,0:T(8,128)(2,1)S(1)}, bf16[1,10,16,384]{3,2,1,0:T(8,128)(2,1)}, u32[]{:S(2)}, u32[]{:S(2)}) collective-permute-start(bf16[1,10,16,384]{3,2,1,0:T(8,128)(2,1)S(1)} %slice.144), channel_id=1, source_target_pairs={{0,8},{2,6},{8,16},{10,2},{16,24},{18,10},{24,28},{26,18},{28,20},... | collective-permute-start | bytes 368648 | tf_op jit(solution)/shard_map/ppermute | solution.py:114
  47.6 8.0 %collective-permute-start.24 = (bf16[2,10,16,384]{3,2,1,0:T(8,128)(2,1)S(1)}, bf16[2,10,16,384]{3,2,1,0:T(8,128)(2,1)}, u32[]{:S(2)}, u32[]{:S(2)}) collective-permute-start(bf16[2,10,16,384]{3,2,1,0:T(8,128)(2,1)S(1)} %collective-permute-done.20.refs_4_), channel_id=1, source_target_pairs={{0,2},{2,0},{4,6},{6,4},{8,10},{10,8},{12,14},{14,12},{16,18},{18,... | collective-permute-start | bytes 737288 | tf_op jit(solution)/shard_map/ppermute | solution.py:116
  49.7 0.7 copy-start.7
  50.4 4.4 %collective-permute-start.5 = (bf16[1,10,16,384]{3,2,1,0:T(8,128)(2,1)}, bf16[1,10,16,384]{3,2,1,0:T(8,128)(2,1)}, u32[]{:S(2)}, u32[]{:S(2)}) collective-permute-start(bf16[1,10,16,384]{3,2,1,0:T(8,128)(2,1)} %slice.136), channel_id=1, source_target_pairs={{0,8},{2,6},{8,16},{10,2},{16,24},{18,10},{24,28},{26,18},{28,20},... | collective-permute-start | bytes 368648 | tf_op jit(solution)/shard_map/ppermute | solution.py:114
  52.2 3.5 %collective-permute-start.25 = (bf16[1,10,16,384]{3,2,1,0:T(8,128)(2,1)}, bf16[1,10,16,384]{3,2,1,0:T(8,128)(2,1)}, u32[]{:S(2)}, u32[]{:S(2)}) collective-permute-start(bf16[1,10,16,384]{3,2,1,0:T(8,128)(2,1)} %collective-permute-done.21.refs_5_), channel_id=1, source_target_pairs={{0,2},{2,0},{4,6},{6,4},{8,10},{10,8},{12,14},{14,12},{16,18},{18,... | collective-permute-start | bytes 368648 | tf_op jit(solution)/shard_map/ppermute | solution.py:116
  52.3 18.9 %copy-start.6 = (bf16[2,10,16,384]{3,2,1,0:T(8,128)(2,1)S(1)}, bf16[2,10,16,384]{3,2,1,0:T(8,128)(2,1)}, u32[]{:S(2)}) copy-start(bf16[2,10,16,384]{3,2,1,0:T(8,128)(2,1)} %copy-done.5) | copy-start | bytes 737284
  52.3 18.9 %collective-permute-start.6 = (bf16[2,10,16,384]{3,2,1,0:T(8,128)(2,1)S(1)}, bf16[2,10,16,384]{3,2,1,0:T(8,128)(2,1)S(1)}, u32[]{:S(2)}, u32[]{:S(2)}) collective-permute-start(bf16[2,10,16,384]{3,2,1,0:T(8,128)(2,1)S(1)} %constant_dynamic-update-slice_fusion.refs_2_), channel_id=1, source_target_pairs={{0,2},{2,0},{4,6},{6,4},{8,10},{10,8},{12,14},{14,12},{16,18},{18,... | collective-permute-start | bytes 737288 | tf_op jit(solution)/shard_map/ppermute | solution.py:116
  54.8 16.4 %collective-permute-start.7 = (bf16[2,10,16,384]{3,2,1,0:T(8,128)(2,1)}, bf16[2,10,16,384]{3,2,1,0:T(8,128)(2,1)S(1)}, u32[]{:S(2)}, u32[]{:S(2)}) collective-permute-start(bf16[2,10,16,384]{3,2,1,0:T(8,128)(2,1)} %copy-done.5), channel_id=1, source_target_pairs={{0,2},{2,0},{4,6},{6,4},{8,10},{10,8},{12,14},{14,12},{16,18},{18,... | collective-permute-start | bytes 737288 | tf_op jit(solution)/shard_map/ppermute | solution.py:116
  55.6 15.6 %collective-permute-start.8 = (bf16[2,10,16,384]{3,2,1,0:T(8,128)(2,1)S(1)}, bf16[2,10,16,384]{3,2,1,0:T(8,128)(2,1)S(1)}, u32[]{:S(2)}, u32[]{:S(2)}) collective-permute-start(bf16[2,10,16,384]{3,2,1,0:T(8,128)(2,1)S(1)} %collective-permute-done.4.refs_4_), channel_id=1, source_target_pairs={{0,2},{2,0},{4,6},{6,4},{8,10},{10,8},{12,14},{14,12},{16,18},{18,... | collective-permute-start | bytes 737288 | tf_op jit(solution)/shard_map/ppermute | solution.py:116
  55.6 15.6 %collective-permute-start.9 = (bf16[1,10,16,384]{3,2,1,0:T(8,128)(2,1)}, bf16[1,10,16,384]{3,2,1,0:T(8,128)(2,1)S(1)}, u32[]{:S(2)}, u32[]{:S(2)}) collective-permute-start(bf16[1,10,16,384]{3,2,1,0:T(8,128)(2,1)} %collective-permute-done.5.refs_5_), channel_id=1, source_target_pairs={{0,2},{2,0},{4,6},{6,4},{8,10},{10,8},{12,14},{14,12},{16,18},{18,... | collective-permute-start | bytes 368648 | tf_op jit(solution)/shard_map/ppermute | solution.py:116
  56.1 0.9 copy-start.8
  57.1 0.9 copy-start.12
  58.0 1.3 copy-start.14
  59.3 12.0 %copy-start.10 = (bf16[1,10,16,384]{3,2,1,0:T(8,128)(2,1)S(1)}, bf16[1,10,16,384]{3,2,1,0:T(8,128)(2,1)}, u32[]{:S(2)}) copy-start(bf16[1,10,16,384]{3,2,1,0:T(8,128)(2,1)} %copy-done.9) | copy-start | bytes 368644
  59.3 12.0 %copy-start.15 = (bf16[10,256,256]{2,1,0:T(8,128)(2,1)S(1)}, bf16[10,256,256]{2,1,0:T(8,128)(2,1)}, u32[]{:S(2)}) copy-start(bf16[10,256,256]{2,1,0:T(8,128)(2,1)} %constant.196.clone.refs_14_) | copy-start | bytes 3932164
  71.1 12.9 %collective-permute-start.26 = (bf16[7,10,16,384]{3,2,1,0:T(8,128)(2,1)S(1)}, bf16[7,10,16,384]{3,2,1,0:T(8,128)(2,1)S(1)}, u32[]{:S(2)}, u32[]{:S(2)}) collective-permute-start(bf16[7,10,16,384]{3,2,1,0:T(8,128)(2,1)S(1)} %get-tuple-element.24), channel_id=1, source_target_pairs={{0,2},{2,0},{4,6},{6,4},{8,10},{10,8},{12,14},{14,12},{16,18},{18,... | collective-permute-start | bytes 2580488 | tf_op jit(solution)/shard_map/ppermute | solution.py:125
  83.4 2.5 %collective-permute-start.11 = (bf16[7,10,16,384]{3,2,1,0:T(8,128)(2,1)S(1)}, bf16[7,10,16,384]{3,2,1,0:T(8,128)(2,1)S(1)}, u32[]{:S(2)}, u32[]{:S(2)}) collective-permute-start(bf16[7,10,16,384]{3,2,1,0:T(8,128)(2,1)S(1)} %get-tuple-element.19), channel_id=1, source_target_pairs={{0,2},{2,0},{4,6},{6,4},{8,10},{10,8},{12,14},{14,12},{16,18},{18,... | collective-permute-start | bytes 2580488 | tf_op jit(solution)/shard_map/ppermute | solution.py:125
  84.0 4.1 %collective-permute-start.27 = (bf16[1,10,16,384]{3,2,1,0:T(8,128)(2,1)S(1)}, bf16[1,10,16,384]{3,2,1,0:T(8,128)(2,1)S(1)}, u32[]{:S(2)}, u32[]{:S(2)}) collective-permute-start(bf16[1,10,16,384]{3,2,1,0:T(8,128)(2,1)S(1)} %add_convert_fusion.4), channel_id=1, source_target_pairs={{0,8},{2,6},{8,16},{10,2},{16,24},{18,10},{24,28},{26,18},{28,20},... | collective-permute-start | bytes 368648 | tf_op jit(solution)/shard_map/ppermute | solution.py:140
  86.0 4.1 %collective-permute-start.12 = (bf16[1,10,16,384]{3,2,1,0:T(8,128)(2,1)S(1)}, bf16[1,10,16,384]{3,2,1,0:T(8,128)(2,1)S(1)}, u32[]{:S(2)}, u32[]{:S(2)}) collective-permute-start(bf16[1,10,16,384]{3,2,1,0:T(8,128)(2,1)S(1)} %add_convert_fusion.5), channel_id=1, source_target_pairs={{0,8},{2,6},{8,16},{10,2},{16,24},{18,10},{24,28},{26,18},{28,20},... | collective-permute-start | bytes 368648 | tf_op jit(solution)/shard_map/ppermute | solution.py:140
  88.1 5.4 %collective-permute-start.28 = (bf16[2,10,16,384]{3,2,1,0:T(8,128)(2,1)S(1)}, bf16[2,10,16,384]{3,2,1,0:T(8,128)(2,1)S(1)}, u32[]{:S(2)}, u32[]{:S(2)}) collective-permute-start(bf16[2,10,16,384]{3,2,1,0:T(8,128)(2,1)S(1)} %pad_maximum_fusion.2), channel_id=1, source_target_pairs={{0,8},{2,6},{8,16},{10,2},{16,24},{18,10},{24,28},{26,18},{28,20},... | collective-permute-start | bytes 737288 | tf_op jit(solution)/shard_map/ppermute | solution.py:140
  90.2 6.0 %collective-permute-start.13 = (bf16[2,10,16,384]{3,2,1,0:T(8,128)(2,1)S(1)}, bf16[2,10,16,384]{3,2,1,0:T(8,128)(2,1)S(1)}, u32[]{:S(2)}, u32[]{:S(2)}) collective-permute-start(bf16[2,10,16,384]{3,2,1,0:T(8,128)(2,1)S(1)} %pad_maximum_fusion.1), channel_id=1, source_target_pairs={{0,8},{2,6},{8,16},{10,2},{16,24},{18,10},{24,28},{26,18},{28,20},... | collective-permute-start | bytes 737288 | tf_op jit(solution)/shard_map/ppermute | solution.py:140
  93.6 5.4 %collective-permute-start.29 = (bf16[2,10,16,384]{3,2,1,0:T(8,128)(2,1)S(1)}, bf16[2,10,16,384]{3,2,1,0:T(8,128)(2,1)S(1)}, u32[]{:S(2)}, u32[]{:S(2)}) collective-permute-start(bf16[2,10,16,384]{3,2,1,0:T(8,128)(2,1)S(1)} %add_convert_fusion.1), channel_id=1, source_target_pairs={{0,8},{2,6},{8,16},{10,2},{16,24},{18,10},{24,28},{26,18},{28,20},... | collective-permute-start | bytes 737288 | tf_op jit(solution)/shard_map/ppermute | solution.py:140
  96.3 5.4 %collective-permute-start.14 = (bf16[2,10,16,384]{3,2,1,0:T(8,128)(2,1)S(1)}, bf16[2,10,16,384]{3,2,1,0:T(8,128)(2,1)S(1)}, u32[]{:S(2)}, u32[]{:S(2)}) collective-permute-start(bf16[2,10,16,384]{3,2,1,0:T(8,128)(2,1)S(1)} %add_convert_fusion.3), channel_id=1, source_target_pairs={{0,8},{2,6},{8,16},{10,2},{16,24},{18,10},{24,28},{26,18},{28,20},... | collective-permute-start | bytes 737288 | tf_op jit(solution)/shard_map/ppermute | solution.py:140
  99.1 5.1 %collective-permute-start.30 = (bf16[2,10,16,384]{3,2,1,0:T(8,128)(2,1)S(1)}, bf16[2,10,16,384]{3,2,1,0:T(8,128)(2,1)S(1)}, u32[]{:S(2)}, u32[]{:S(2)}) collective-permute-start(bf16[2,10,16,384]{3,2,1,0:T(8,128)(2,1)S(1)} %add_convert_fusion), channel_id=1, source_target_pairs={{0,8},{2,6},{8,16},{10,2},{16,24},{18,10},{24,28},{26,18},{28,20},... | collective-permute-start | bytes 737288 | tf_op jit(solution)/shard_map/ppermute | solution.py:140
  101.8 5.4 %collective-permute-start.15 = (bf16[2,10,16,384]{3,2,1,0:T(8,128)(2,1)S(1)}, bf16[2,10,16,384]{3,2,1,0:T(8,128)(2,1)S(1)}, u32[]{:S(2)}, u32[]{:S(2)}) collective-permute-start(bf16[2,10,16,384]{3,2,1,0:T(8,128)(2,1)S(1)} %add_convert_fusion.2), channel_id=1, source_target_pairs={{0,8},{2,6},{8,16},{10,2},{16,24},{18,10},{24,28},{26,18},{28,20},... | collective-permute-start | bytes 737288 | tf_op jit(solution)/shard_map/ppermute | solution.py:140
  104.3 7.7 %copy-start.1 = (bf16[384,384]{1,0:T(8,128)(2,1)S(1)}, bf16[384,384]{1,0:T(8,128)(2,1)}, u32[]{:S(2)}) copy-start(bf16[384,384]{1,0:T(8,128)(2,1)} %constant.200.clone.along_y) | copy-start | bytes 884740
  104.3 7.7 %copy-start.4 = (bf16[128,128]{1,0:T(8,128)(2,1)S(1)}, bf16[128,128]{1,0:T(8,128)(2,1)}, u32[]{:S(2)}) copy-start(bf16[128,128]{1,0:T(8,128)(2,1)} %constant.199.clone.along_z) | copy-start | bytes 98308
  107.3 18.9 %copy-start.13 = (f32[10]{0:T(128)S(1)}, f32[10]{0:T(128)}, u32[]{:S(2)}) copy-start(f32[10]{0:T(128)} %refs_7_.1) | copy-start | bytes 124
  107.3 4.7 %collective-permute-start.31 = (bf16[2,10,16,384]{3,2,1,0:T(8,128)(2,1)S(1)}, bf16[2,10,16,384]{3,2,1,0:T(8,128)(2,1)S(1)}, u32[]{:S(2)}, u32[]{:S(2)}) collective-permute-start(bf16[2,10,16,384]{3,2,1,0:T(8,128)(2,1)S(1)} %fusion.5), channel_id=1, source_target_pairs={{0,2},{2,0},{4,6},{6,4},{8,10},{10,8},{12,14},{14,12},{16,18},{18,... | collective-permute-start | bytes 737288 | tf_op jit(solution)/shard_map/ppermute | solution.py:544
  112.7 7.5 %collective-permute-start.32 = (bf16[2,10,2,384]{3,2,1,0:T(2,128)(2,1)S(1)}, bf16[2,10,2,384]{3,2,1,0:T(2,128)(2,1)S(1)}, u32[]{:S(2)}, u32[]{:S(2)}) collective-permute-start(bf16[2,10,2,384]{3,2,1,0:T(2,128)(2,1)S(1)} %get-tuple-element.25), channel_id=1, source_target_pairs={{0,2},{2,4},{4,6},{6,8},{8,10},{10,12},{12,14},{14,16},{16,18},{18... | collective-permute-start | bytes 92168 | tf_op jit(solution)/shard_map/ppermute | solution.py:549
  116.7 5.5 %collective-permute-start.33 = (bf16[2,10,2,384]{3,2,1,0:T(2,128)(2,1)S(1)}, bf16[2,10,2,384]{3,2,1,0:T(2,128)(2,1)S(1)}, u32[]{:S(2)}, u32[]{:S(2)}) collective-permute-start(bf16[2,10,2,384]{3,2,1,0:T(2,128)(2,1)S(1)} %get-tuple-element.26), channel_id=1, source_target_pairs={{2,0},{4,2},{6,4},{8,6},{10,8},{12,10},{14,12},{16,14},{18,16},{20... | collective-permute-start | bytes 92168 | tf_op jit(solution)/shard_map/ppermute | solution.py:549
  118.8 7.4 %collective-permute-start.34 = (bf16[2,10,16,384]{3,2,1,0:T(8,128)(2,1)S(1)}, bf16[2,10,16,384]{3,2,1,0:T(8,128)(2,1)S(1)}, u32[]{:S(2)}, u32[]{:S(2)}) collective-permute-start(bf16[2,10,16,384]{3,2,1,0:T(8,128)(2,1)S(1)} %update.1.refs_0_), channel_id=1, source_target_pairs={{0,1},{1,0},{2,3},{3,2},{4,5},{5,4},{6,7},{7,6},{8,9},{9,8},{10,11... | collective-permute-start | bytes 737288 | tf_op jit(solution)/shard_map/ppermute | solution.py:547
  122.2 3.9 %collective-permute-start.35 = (bf16[2,10,4,384]{3,2,1,0:T(4,128)(2,1)S(1)}, bf16[2,10,4,384]{3,2,1,0:T(4,128)(2,1)S(1)}, u32[]{:S(2)}, u32[]{:S(2)}) collective-permute-start(bf16[2,10,4,384]{3,2,1,0:T(4,128)(2,1)S(1)} %pad_maximum_fusion.3.refs_1_), channel_id=1, source_target_pairs={{0,1},{1,0},{2,3},{3,2},{4,5},{5,4},{6,7},{7,6},{8,9},{9,8},{10,11... | collective-permute-start | bytes 184328 | tf_op jit(solution)/shard_map/ppermute | solution.py:551

commit v5 on v4

--- a/solution.py
+++ b/solution.py
@@ -301,7 +301,7 @@
             ],
         ),
         out_shape=[jax.ShapeDtypeStruct((m, channels, rows, ny), BF16) for m in (2, far, far)],
-        compiler_params=pltpu.CompilerParams(vmem_limit_bytes=40 * 2**20),
+        compiler_params=pltpu.CompilerParams(vmem_limit_bytes=46 * 2**20),
         cost_estimate=pl.CostEstimate(flops=flops, bytes_accessed=8 * 2**20, transcendentals=0),
         name="gradient",
     )(where, *images, *[a for a, _ in maps], measured, sampling, tables)
@@ -358,7 +358,7 @@
     devices = coils // 2
     pairs = coil_maps.reshape((devices, 2) + coil_maps.shape[1:])
     matrices = orders(rows, ny, False)
-    steps = 2
+    steps = 1
     return pl.pallas_call(
         prepare_maps_kernel,
         grid_spec=pltpu.PrefetchScalarGridSpec(
@@ -400,37 +400,39 @@
     return jnp.concatenate([edge, value[..., :-1]], axis=-1)
 
 
-def put_strided(ref, start, count, stride, value):
-    for j in range(ref.shape[0]):
-        ref[j, pl.ds(start, count, stride=stride), :] = value[:, j * 128 : (j + 1) * 128]
-
-
-def get_lines(ref, start, count):
-    return jnp.concatenate([ref[j, start : start + count, :] for j in range(ref.shape[0])], axis=1)
+def put_strided(ref, first, start, count, stride, value):
+    for j in range(value.shape[1] // 128):
+        ref[first + j, pl.ds(start, count, stride=stride), :] = value[:, j * 128 : (j + 1) * 128]
+
+
+def get_lines(ref, chunks, start, count):
+    return jnp.concatenate([ref[j, start : start + count, :] for j in chunks], axis=1)
 
 
 def convolution_kernel(ends, *refs):
     sources, refs = (refs[:2], refs[2:4]), refs[4:]
     w_first, b_first, w_second, b_second, out, stacked, result = refs
-    _, channels, rows, ny = sources[0][0].shape
+    width, channels, rows, ny = sources[0][0].shape
     depth = rows + 4
     group = stacked.shape[1] // depth
     lanes = result.shape[1] // rows
+    chunks = ny // 128
     nothing = jnp.zeros((depth, ny), F32)
-    for i in range(6 * channels, group):
-        put_strided(stacked, i, depth, group, nothing)
-    for t, (cells, edges) in enumerate(sources):
-        for i in range(channels):
-            edge = edges[0, i].astype(F32)
-            value = jnp.concatenate([edge[:2], cells[0, i].astype(F32), edge[2:]], axis=0)
-            for d in range(3):
-                line = value if d == 1 else shifted(value, d - 1)
-                put_strided(stacked, (d * 2 + t) * channels + i, depth, group, line)
+    for x in range(width):
+        for i in range(6 * channels, group):
+            put_strided(stacked, x * chunks, i, depth, group, nothing)
+        for t, (cells, edges) in enumerate(sources):
+            for i in range(channels):
+                edge = edges[x, i].astype(F32)
+                value = jnp.concatenate([edge[:2], cells[x, i].astype(F32), edge[2:]], axis=0)
+                for d in range(3):
+                    line = value if d == 1 else shifted(value, d - 1)
+                    put_strided(stacked, x * chunks, (d * 2 + t) * channels + i, depth, group, line)
     features = w_first.shape[0] // 2
     taps = w_second.shape[0] // 4
     partial = []
     for pair in range(rows // 2 + 1):
-        window = get_lines(stacked, 2 * pair * group, 4 * group).astype(BF16)
+        window = get_lines(stacked, range(width * chunks), 2 * pair * group, 4 * group).astype(BF16)
         hidden = jnp.maximum(nn_dot(w_first[...], window) + b_first[...], 0.0)
         if pair == 0:
             hidden = jnp.concatenate([hidden[:features] * ends[0].astype(F32), hidden[features:]], axis=0)
@@ -439,13 +441,17 @@
         partial.append(nn_dot(w_second[...], hidden.astype(BF16)))
         if pair > 0:
             for z in range(2):
-                total = partial[0][(2 + z) * taps : (3 + z) * taps] + partial[1][z * taps : (z + 1) * taps]
-                line = shifted(total[:lanes], -1) + total[lanes : 2 * lanes] + shifted(total[2 * lanes :], 1)
-                put_strided(result, 2 * pair - 2 + z, lanes, rows, line)
+                both = partial[0][(2 + z) * taps : (3 + z) * taps] + partial[1][z * taps : (z + 1) * taps]
+                for x in range(width):
+                    total = both[:, x * ny : (x + 1) * ny]
+                    line = shifted(total[:lanes], -1) + total[lanes : 2 * lanes] + shifted(total[2 * lanes :], 1)
+                    put_strided(result, x * chunks, 2 * pair - 2 + z, lanes, rows, line)
             partial = partial[1:]
-    for i in range(channels):
-        value = sources[0][0][0, i].astype(F32)
-        out[0, i // 2, i % 2, 0] = (value + get_lines(result, i * rows, rows) + b_second[i]).astype(BF16)
+    for x in range(width):
+        for i in range(channels):
+            value = sources[0][0][x, i].astype(F32)
+            added = get_lines(result, range(x * chunks, (x + 1) * chunks), i * rows, rows)
+            out[0, i // 2, i % 2, x] = (value + added + b_second[i]).astype(BF16)
 
 
 def convolutions(ends, parts, w_first, b_first, w_second, b_second, shape):
@@ -453,19 +459,16 @@
     group = w_first.shape[1] // 4
     lanes = w_second.shape[0] // 12
     smem = pl.BlockSpec(memory_space=pltpu.SMEM)
-    whole = lambda a: pl.BlockSpec(a.shape, lambda x: (0,) * a.ndim)
+    vmem = pl.BlockSpec(memory_space=pltpu.VMEM)
     flops = width * (rows + 2) * ny * (w_first.size + w_second.size)
     return pl.pallas_call(
         convolution_kernel,
-        grid=(width,),
-        in_specs=[smem]
-        + [pl.BlockSpec((1,) + a.shape[1:], lambda x: (x, 0, 0, 0)) for a in parts]
-        + [whole(w_first), whole(b_first), whole(w_second), smem],
-        out_specs=pl.BlockSpec((1,) + shape[1:3] + (1,) + shape[4:], lambda x: (0, 0, 0, x, 0, 0)),
+        in_specs=[smem] + [vmem] * (len(parts) + 3) + [smem],
+        out_specs=vmem,
         out_shape=jax.ShapeDtypeStruct(shape, BF16),
         scratch_shapes=[
-            pltpu.VMEM((ny // 128, (rows + 4) * group, 128), F32),
-            pltpu.VMEM((ny // 128, lanes * rows, 128), F32),
+            pltpu.VMEM((width * ny // 128, (rows + 4) * group, 128), F32),
+            pltpu.VMEM((width * ny // 128, lanes * rows, 128), F32),
         ],
         compiler_params=pltpu.CompilerParams(vmem_limit_bytes=24 * 2**20),
         cost_estimate=pl.CostEstimate(flops=flops, bytes_accessed=2**20, transcendentals=0),

time: 137 us -> 135 us (0.985)
  Pallas kernels: 37.4 us -> 35.3 us
    pallas_call x1, Pallas kernels: 8.97 us -> 6.99 us  [convolutions(): pl.pallas_call(convolution_kernel, in_specs=[smem] + [vmem] * (len(parts)...]
where the time goes in v5:
time: 135 us; the launch traced here: 133 us
  starting transfers between devices  54.1 us (40%)
  Pallas kernels  35.3 us (26%)
  waiting for transfers between devices  33.5 us (25%)
  local copies, waits for them, and re-layouts  6.5 us (5%)
  other arithmetic  3.12 us (2%)
    pallas_call x2, Pallas kernels, gradient(): pl.pallas_call(functools.partial(gradient_kernel, len(images), n), grid_s...  23.9 us
    ppermute x8, starting transfers between devices, step(): self.held = lax.ppermute(total.astype(BF16), SLAB, self.ring.perm())  14.1 us
    ppermute x6, waiting for transfers between devices, step(): lax.ppermute(after(held, *earlier) if earlier else held, SLAB, self.ring....  10.5 us
    ppermute x8, waiting for transfers between devices, step(): self.held = lax.ppermute(total.astype(BF16), SLAB, self.ring.perm())  8.18 us
    ppermute x6, starting transfers between devices, step(): lax.ppermute(after(held, *earlier) if earlier else held, SLAB, self.ring....  7.6 us
    ppermute x2, waiting for transfers between devices, __init__(): self.first = lax.ppermute(mine, SLAB, ring.perm())  7.37 us
    pallas_call x1, Pallas kernels, convolutions(): pl.pallas_call(convolution_kernel, in_specs=[smem] + [vmem] * (len(parts)...  6.99 us
    ppermute x8, starting transfers between devices, step(): self.other.append(lax.ppermute(self.held, SLAB, self.ring.siblings()))  6.05 us
  transfers between devices with their start and end apart: 37, of which 20 were waited for; matrix products, arithmetic and copies ran while one was open for 4% of the time, Pallas kernels for 18%

profile of v5, /device:TPU:1, one launch (start us, length us, event | category | flops | bytes accessed | tf_op | source)
XLA Modules:
  0.0 133.1 jit_solution(4563214844973851595)
XLA Ops:
  0.0 3.1 %prepare_maps.1.earlier = bf16[16,2,2,16,384]{4,3,2,1,0:T(8,128)(2,1)} custom-call(s32[1]{0:T(128)} %bitcast.2.which, bf16[16,2,2,2,16,384]{5,4,3,2,1,0:T(8,128)(2,1)} %bitcast.69, bf16[128,128]{1,0:T(8,128)(2,1)} %constant.197.clone.along_z, bf16[384,384]{1,0:T(8,128)(2,1)} %constant.198.clone.along_y), custom_call_target="tpu_custom_call" | custom-call | tf_op jit(solution)/shard_map/prepare_maps/pallas_call | solution.py:362
  3.1 0.7 prepare_image.1.image
  3.9 2.7 %collective-permute-start.17 = (bf16[1,10,16,384]{3,2,1,0:T(8,128)(2,1)S(1)}, bf16[1,10,16,384]{3,2,1,0:T(8,128)(2,1)S(1)}, u32[]{:S(2)}, u32[]{:S(2)}) collective-permute-start(bf16[1,10,16,384]{3,2,1,0:T(8,128)(2,1)S(1)} %get-tuple-element.27.refs_0_), channel_id=1, source_target_pairs={{0,8},{2,6},{8,16},{10,2},{16,24},{18,10},{24,28},{26,18},{28,20},... | collective-permute-start | bytes 368648 | tf_op jit(solution)/shard_map/ppermute | solution.py:103
  6.6 5.2 %all-to-all-start = ((bf16[16,2,2,16,384]{4,3,2,1,0:T(8,128)(2,1)}), bf16[16,2,2,16,384]{4,3,2,1,0:T(8,128)(2,1)S(1)}, u32[]{:S(2)}, u32[]{:S(2)}) async-start(bf16[16,2,2,16,384]{4,3,2,1,0:T(8,128)(2,1)} %prepare_maps.1.earlier), calls=%async_computation | async-start | bytes 1572864 | tf_op jit(solution)/shard_map/all_to_all | solution.py:535
  11.8 0.2 collective-permute-start
  12.0 1.6 %collective-permute-start.1 = (bf16[1,10,16,384]{3,2,1,0:T(8,128)(2,1)S(1)}, bf16[1,10,16,384]{3,2,1,0:T(8,128)(2,1)}, u32[]{:S(2)}, u32[]{:S(2)}) collective-permute-start(bf16[1,10,16,384]{3,2,1,0:T(8,128)(2,1)S(1)} %get-tuple-element.28.refs_0_), channel_id=1, source_target_pairs={{0,8},{2,6},{8,16},{10,2},{16,24},{18,10},{24,28},{26,18},{28,20},... | collective-permute-start | bytes 368648 | tf_op jit(solution)/shard_map/ppermute | solution.py:103
  14.3 0.1 reshape.28
  14.7 1.7 %convert_element_type.117.refs_13_ = bf16[1,5,384,256]{3,2,1,0:T(8,128)(2,1)S(1)} convert(s32[1,5,384,256]{3,2,1,0:T(8,128)} %param.18) | non-fusion elementwise | flops 491520 | bytes 2949120 | tf_op jit(solution)/shard_map/convert_element_type | solution.py:528
  16.4 1.2 collective-permute-start.18
  17.7 1.2 collective-permute-start.2
  19.0 7.4 %collective-permute-done.1 = bf16[1,10,16,384]{3,2,1,0:T(8,128)(2,1)} collective-permute-done((bf16[1,10,16,384]{3,2,1,0:T(8,128)(2,1)S(1)}, bf16[1,10,16,384]{3,2,1,0:T(8,128)(2,1)}, u32[]{:S(2)}, u32[]{:S(2)}) %collective-permute-start.1) | collective-permute-done | bytes 122912 | tf_op jit(solution)/shard_map/ppermute | solution.py:103
  26.3 0.9 constant_dynamic-update-slice_fusion.1
  27.2 0.6 collective-permute-done.18
  27.9 1.4 %collective-permute-start.19 = (bf16[2,10,16,384]{3,2,1,0:T(8,128)(2,1)S(1)}, bf16[2,10,16,384]{3,2,1,0:T(8,128)(2,1)}, u32[]{:S(2)}, u32[]{:S(2)}) collective-permute-start(bf16[2,10,16,384]{3,2,1,0:T(8,128)(2,1)S(1)} %constant_dynamic-update-slice_fusion.2.refs_2_), channel_id=1, source_target_pairs={{0,8},{2,6},{8,16},{10,2},{16,24},{18,10},{24,28},{26,18},{28,20},... | collective-permute-start | bytes 737288 | tf_op jit(solution)/shard_map/ppermute | solution.py:114
  29.3 1.2 all-to-all-done.refs_10_
  30.5 1.2 collective-permute-start.10
  31.8 4.4 %collective-permute-start.3 = (bf16[2,10,16,384]{3,2,1,0:T(8,128)(2,1)S(1)}, bf16[2,10,16,384]{3,2,1,0:T(8,128)(2,1)S(1)}, u32[]{:S(2)}, u32[]{:S(2)}) collective-permute-start(bf16[2,10,16,384]{3,2,1,0:T(8,128)(2,1)S(1)} %constant_dynamic-update-slice_fusion.refs_2_), channel_id=1, source_target_pairs={{0,8},{2,6},{8,16},{10,2},{16,24},{18,10},{24,28},{26,18},{28,20},... | collective-permute-start | bytes 737288 | tf_op jit(solution)/shard_map/ppermute | solution.py:114
  36.1 3.1 %collective-permute-done.19.refs_3_ = bf16[2,10,16,384]{3,2,1,0:T(8,128)(2,1)} collective-permute-done((bf16[2,10,16,384]{3,2,1,0:T(8,128)(2,1)S(1)}, bf16[2,10,16,384]{3,2,1,0:T(8,128)(2,1)}, u32[]{:S(2)}, u32[]{:S(2)}) %collective-permute-start.19) | collective-permute-done | bytes 245792 | tf_op jit(solution)/shard_map/ppermute | solution.py:114
  39.2 2.6 %collective-permute-done.3.refs_3_ = bf16[2,10,16,384]{3,2,1,0:T(8,128)(2,1)S(1)} collective-permute-done((bf16[2,10,16,384]{3,2,1,0:T(8,128)(2,1)S(1)}, bf16[2,10,16,384]{3,2,1,0:T(8,128)(2,1)S(1)}, u32[]{:S(2)}, u32[]{:S(2)}) %collective-permute-start.3) | collective-permute-done | bytes 245792 | tf_op jit(solution)/shard_map/ppermute | solution.py:114
  41.8 2.7 %collective-permute-start.22 = (bf16[2,10,16,384]{3,2,1,0:T(8,128)(2,1)S(1)}, bf16[2,10,16,384]{3,2,1,0:T(8,128)(2,1)S(1)}, u32[]{:S(2)}, u32[]{:S(2)}) collective-permute-start(bf16[2,10,16,384]{3,2,1,0:T(8,128)(2,1)S(1)} %constant_dynamic-update-slice_fusion.2.refs_2_), channel_id=1, source_target_pairs={{0,2},{2,0},{4,6},{6,4},{8,10},{10,8},{12,14},{14,12},{16,18},{18,... | collective-permute-start | bytes 737288 | tf_op jit(solution)/shard_map/ppermute | solution.py:116
  44.5 0.3 collective-permute-done.20.refs_4_
  44.9 2.5 %collective-permute-done.4.refs_4_ = bf16[2,10,16,384]{3,2,1,0:T(8,128)(2,1)S(1)} collective-permute-done((bf16[2,10,16,384]{3,2,1,0:T(8,128)(2,1)S(1)}, bf16[2,10,16,384]{3,2,1,0:T(8,128)(2,1)S(1)}, u32[]{:S(2)}, u32[]{:S(2)}) %collective-permute-start.4) | collective-permute-done | bytes 245792 | tf_op jit(solution)/shard_map/ppermute | solution.py:114
  47.5 1.5 %collective-permute-start.24 = (bf16[2,10,16,384]{3,2,1,0:T(8,128)(2,1)S(1)}, bf16[2,10,16,384]{3,2,1,0:T(8,128)(2,1)}, u32[]{:S(2)}, u32[]{:S(2)}) collective-permute-start(bf16[2,10,16,384]{3,2,1,0:T(8,128)(2,1)S(1)} %collective-permute-done.20.refs_4_), channel_id=1, source_target_pairs={{0,2},{2,0},{4,6},{6,4},{8,10},{10,8},{12,14},{14,12},{16,18},{18,... | collective-permute-start | bytes 737288 | tf_op jit(solution)/shard_map/ppermute | solution.py:116
  49.0 0.7 slice.136
  49.6 0.7 copy-done.7
  50.3 1.7 %collective-permute-start.5 = (bf16[1,10,16,384]{3,2,1,0:T(8,128)(2,1)}, bf16[1,10,16,384]{3,2,1,0:T(8,128)(2,1)}, u32[]{:S(2)}, u32[]{:S(2)}) collective-permute-start(bf16[1,10,16,384]{3,2,1,0:T(8,128)(2,1)} %slice.136), channel_id=1, source_target_pairs={{0,8},{2,6},{8,16},{10,2},{16,24},{18,10},{24,28},{26,18},{28,20},... | collective-permute-start | bytes 368648 | tf_op jit(solution)/shard_map/ppermute | solution.py:114
  52.2 0.5 collective-permute-start.6
  52.8 1.9 %collective-permute-done.5.refs_5_ = bf16[1,10,16,384]{3,2,1,0:T(8,128)(2,1)} collective-permute-done((bf16[1,10,16,384]{3,2,1,0:T(8,128)(2,1)}, bf16[1,10,16,384]{3,2,1,0:T(8,128)(2,1)}, u32[]{:S(2)}, u32[]{:S(2)}) %collective-permute-start.5) | collective-permute-done | bytes 122912 | tf_op jit(solution)/shard_map/ppermute | solution.py:114
  54.7 0.8 collective-permute-start.7
  55.5 0.5 collective-permute-start.9
  56.0 0.9 copy-done.8
  57.0 0.9 copy-done.12
  57.9 1.3 copy-done.14
  59.2 11.7 %gradient.3 = (bf16[2,10,16,384]{3,2,1,0:T(8,128)(2,1)S(1)}, bf16[7,10,16,384]{3,2,1,0:T(8,128)(2,1)S(1)}, bf16[7,10,16,384]{3,2,1,0:T(8,128)(2,1)S(1)}) custom-call(s32[33]{0:T(128)S(1)} %concatenate.35.slabs, bf16[1,10,16,384]{3,2,1,0:T(8,128)(2,1)S(1)} %get-tuple-element.27.refs_0_, bf16[1,10,16,384]{3,2,1,0:T(8,128)(2,1)S(1)} %copy-done.12, ...), custom_call_target="tpu_custom_call" | custom-call | flops 10066329600 | bytes 8388608 | tf_op jit(solution)/shard_map/gradient/pallas_call | solution.py:281
  71.0 0.2 collective-permute-start.26
  71.2 12.2 %gradient.2 = (bf16[2,10,16,384]{3,2,1,0:T(8,128)(2,1)S(1)}, bf16[7,10,16,384]{3,2,1,0:T(8,128)(2,1)S(1)}, bf16[7,10,16,384]{3,2,1,0:T(8,128)(2,1)S(1)}) custom-call(s32[33]{0:T(128)S(1)} %concatenate.35.slabs, bf16[1,10,16,384]{3,2,1,0:T(8,128)(2,1)S(1)} %get-tuple-element.28.refs_0_, bf16[1,10,16,384]{3,2,1,0:T(8,128)(2,1)S(1)} %copy-done.10, ...), custom_call_target="tpu_custom_call" | custom-call | flops 10066329600 | bytes 8388608 | tf_op jit(solution)/shard_map/gradient/pallas_call | solution.py:281
  83.3 0.5 collective-permute-start.11
  83.9 1.8 %collective-permute-start.27 = (bf16[1,10,16,384]{3,2,1,0:T(8,128)(2,1)S(1)}, bf16[1,10,16,384]{3,2,1,0:T(8,128)(2,1)S(1)}, u32[]{:S(2)}, u32[]{:S(2)}) collective-permute-start(bf16[1,10,16,384]{3,2,1,0:T(8,128)(2,1)S(1)} %add_convert_fusion.4), channel_id=1, source_target_pairs={{0,8},{2,6},{8,16},{10,2},{16,24},{18,10},{24,28},{26,18},{28,20},... | collective-permute-start | bytes 368648 | tf_op jit(solution)/shard_map/ppermute | solution.py:140
  85.9 1.8 %collective-permute-start.12 = (bf16[1,10,16,384]{3,2,1,0:T(8,128)(2,1)S(1)}, bf16[1,10,16,384]{3,2,1,0:T(8,128)(2,1)S(1)}, u32[]{:S(2)}, u32[]{:S(2)}) collective-permute-start(bf16[1,10,16,384]{3,2,1,0:T(8,128)(2,1)S(1)} %add_convert_fusion.5), channel_id=1, source_target_pairs={{0,8},{2,6},{8,16},{10,2},{16,24},{18,10},{24,28},{26,18},{28,20},... | collective-permute-start | bytes 368648 | tf_op jit(solution)/shard_map/ppermute | solution.py:140
  87.8 0.2 collective-permute-done.27
  88.1 1.8 %collective-permute-start.28 = (bf16[2,10,16,384]{3,2,1,0:T(8,128)(2,1)S(1)}, bf16[2,10,16,384]{3,2,1,0:T(8,128)(2,1)S(1)}, u32[]{:S(2)}, u32[]{:S(2)}) collective-permute-start(bf16[2,10,16,384]{3,2,1,0:T(8,128)(2,1)S(1)} %pad_maximum_fusion.2), channel_id=1, source_target_pairs={{0,8},{2,6},{8,16},{10,2},{16,24},{18,10},{24,28},{26,18},{28,20},... | collective-permute-start | bytes 737288 | tf_op jit(solution)/shard_map/ppermute | solution.py:140
  89.8 0.2 collective-permute-done.12
  90.1 1.8 %collective-permute-start.13 = (bf16[2,10,16,384]{3,2,1,0:T(8,128)(2,1)S(1)}, bf16[2,10,16,384]{3,2,1,0:T(8,128)(2,1)S(1)}, u32[]{:S(2)}, u32[]{:S(2)}) collective-permute-start(bf16[2,10,16,384]{3,2,1,0:T(8,128)(2,1)S(1)} %pad_maximum_fusion.1), channel_id=1, source_target_pairs={{0,8},{2,6},{8,16},{10,2},{16,24},{18,10},{24,28},{26,18},{28,20},... | collective-permute-start | bytes 737288 | tf_op jit(solution)/shard_map/ppermute | solution.py:140
  91.8 1.6 %collective-permute-done.28 = bf16[2,10,16,384]{3,2,1,0:T(8,128)(2,1)S(1)} collective-permute-done((bf16[2,10,16,384]{3,2,1,0:T(8,128)(2,1)S(1)}, bf16[2,10,16,384]{3,2,1,0:T(8,128)(2,1)S(1)}, u32[]{:S(2)}, u32[]{:S(2)}) %collective-permute-start.28) | collective-permute-done | bytes 245792 | tf_op jit(solution)/shard_map/ppermute | solution.py:140
  93.5 1.8 %collective-permute-start.29 = (bf16[2,10,16,384]{3,2,1,0:T(8,128)(2,1)S(1)}, bf16[2,10,16,384]{3,2,1,0:T(8,128)(2,1)S(1)}, u32[]{:S(2)}, u32[]{:S(2)}) collective-permute-start(bf16[2,10,16,384]{3,2,1,0:T(8,128)(2,1)S(1)} %add_convert_fusion.1), channel_id=1, source_target_pairs={{0,8},{2,6},{8,16},{10,2},{16,24},{18,10},{24,28},{26,18},{28,20},... | collective-permute-start | bytes 737288 | tf_op jit(solution)/shard_map/ppermute | solution.py:140
  95.3 0.8 collective-permute-done.13
  96.2 1.8 %collective-permute-start.14 = (bf16[2,10,16,384]{3,2,1,0:T(8,128)(2,1)S(1)}, bf16[2,10,16,384]{3,2,1,0:T(8,128)(2,1)S(1)}, u32[]{:S(2)}, u32[]{:S(2)}) collective-permute-start(bf16[2,10,16,384]{3,2,1,0:T(8,128)(2,1)S(1)} %add_convert_fusion.3), channel_id=1, source_target_pairs={{0,8},{2,6},{8,16},{10,2},{16,24},{18,10},{24,28},{26,18},{28,20},... | collective-permute-start | bytes 737288 | tf_op jit(solution)/shard_map/ppermute | solution.py:140
  97.9 1.0 collective-permute-done.29
  99.0 1.8 %collective-permute-start.30 = (bf16[2,10,16,384]{3,2,1,0:T(8,128)(2,1)S(1)}, bf16[2,10,16,384]{3,2,1,0:T(8,128)(2,1)S(1)}, u32[]{:S(2)}, u32[]{:S(2)}) collective-permute-start(bf16[2,10,16,384]{3,2,1,0:T(8,128)(2,1)S(1)} %add_convert_fusion), channel_id=1, source_target_pairs={{0,8},{2,6},{8,16},{10,2},{16,24},{18,10},{24,28},{26,18},{28,20},... | collective-permute-start | bytes 737288 | tf_op jit(solution)/shard_map/ppermute | solution.py:140
  100.8 0.8 collective-permute-done.14
  101.7 1.8 %collective-permute-start.15 = (bf16[2,10,16,384]{3,2,1,0:T(8,128)(2,1)S(1)}, bf16[2,10,16,384]{3,2,1,0:T(8,128)(2,1)S(1)}, u32[]{:S(2)}, u32[]{:S(2)}) collective-permute-start(bf16[2,10,16,384]{3,2,1,0:T(8,128)(2,1)S(1)} %add_convert_fusion.2), channel_id=1, source_target_pairs={{0,8},{2,6},{8,16},{10,2},{16,24},{18,10},{24,28},{26,18},{28,20},... | collective-permute-start | bytes 737288 | tf_op jit(solution)/shard_map/ppermute | solution.py:140
  103.4 0.7 collective-permute-done.30
  104.2 2.8 %collective-permute-done.15 = bf16[2,10,16,384]{3,2,1,0:T(8,128)(2,1)S(1)} collective-permute-done((bf16[2,10,16,384]{3,2,1,0:T(8,128)(2,1)S(1)}, bf16[2,10,16,384]{3,2,1,0:T(8,128)(2,1)S(1)}, u32[]{:S(2)}, u32[]{:S(2)}) %collective-permute-start.15) | collective-permute-done | bytes 245792 | tf_op jit(solution)/shard_map/ppermute | solution.py:140
  107.2 3.6 %collective-permute-start.31 = (bf16[2,10,16,384]{3,2,1,0:T(8,128)(2,1)S(1)}, bf16[2,10,16,384]{3,2,1,0:T(8,128)(2,1)S(1)}, u32[]{:S(2)}, u32[]{:S(2)}) collective-permute-start(bf16[2,10,16,384]{3,2,1,0:T(8,128)(2,1)S(1)} %fusion.5), channel_id=1, source_target_pairs={{0,2},{2,0},{4,6},{6,4},{8,10},{10,8},{12,14},{14,12},{16,18},{18,... | collective-permute-start | bytes 737288 | tf_op jit(solution)/shard_map/ppermute | solution.py:547
  110.8 1.1 collective-permute-done.31.received
  111.9 0.7 update.1.refs_0_
  112.6 3.9 %collective-permute-start.32 = (bf16[2,10,2,384]{3,2,1,0:T(2,128)(2,1)S(1)}, bf16[2,10,2,384]{3,2,1,0:T(2,128)(2,1)S(1)}, u32[]{:S(2)}, u32[]{:S(2)}) collective-permute-start(bf16[2,10,2,384]{3,2,1,0:T(2,128)(2,1)S(1)} %get-tuple-element.25), channel_id=1, source_target_pairs={{0,2},{2,4},{4,6},{6,8},{8,10},{10,12},{12,14},{14,16},{16,18},{18... | collective-permute-start | bytes 92168 | tf_op jit(solution)/shard_map/ppermute | solution.py:552
  116.6 2.1 %collective-permute-start.33 = (bf16[2,10,2,384]{3,2,1,0:T(2,128)(2,1)S(1)}, bf16[2,10,2,384]{3,2,1,0:T(2,128)(2,1)S(1)}, u32[]{:S(2)}, u32[]{:S(2)}) collective-permute-start(bf16[2,10,2,384]{3,2,1,0:T(2,128)(2,1)S(1)} %get-tuple-element.26), channel_id=1, source_target_pairs={{2,0},{4,2},{6,4},{8,6},{10,8},{12,10},{14,12},{16,14},{18,16},{20... | collective-permute-start | bytes 92168 | tf_op jit(solution)/shard_map/ppermute | solution.py:552
  118.7 1.3 collective-permute-start.34
  120.0 0.1 copy.23.refs_5_
  120.1 1.9 %collective-permute-done.33 = bf16[2,10,2,384]{3,2,1,0:T(2,128)(2,1)S(1)} collective-permute-done((bf16[2,10,2,384]{3,2,1,0:T(2,128)(2,1)S(1)}, bf16[2,10,2,384]{3,2,1,0:T(2,128)(2,1)S(1)}, u32[]{:S(2)}, u32[]{:S(2)}) %collective-permute-start.33) | collective-permute-done | bytes 30752 | tf_op jit(solution)/shard_map/ppermute | solution.py:552
  122.1 1.3 collective-permute-start.35
  123.5 2.5 %collective-permute-done.35.refs_3_ = bf16[2,10,4,384]{3,2,1,0:T(4,128)(2,1)S(1)} collective-permute-done((bf16[2,10,4,384]{3,2,1,0:T(4,128)(2,1)S(1)}, bf16[2,10,4,384]{3,2,1,0:T(4,128)(2,1)S(1)}, u32[]{:S(2)}, u32[]{:S(2)}) %collective-permute-start.35) | collective-permute-done | bytes 61472 | tf_op jit(solution)/shard_map/ppermute | solution.py:554
  126.1 7.0 %convolutions.1 = bf16[1,5,2,2,16,384]{5,4,3,2,1,0:T(8,128)(2,1)} custom-call(s32[2]{0:T(128)S(1)} %add_convert_fusion.6.ends, bf16[2,10,16,384]{3,2,1,0:T(8,128)(2,1)S(1)} %update.1.refs_0_, bf16[2,10,4,384]{3,2,1,0:T(4,128)(2,1)S(1)} %pad_maximum_fusion.3.refs_1_, bf16[2,10,16,384]{3,2,1,0:T(8,128)(2,1)S(1)} %collective-permute-done.34.refs_2_, ...), custom_call_target="tpu_custom_call" | custom-call | flops 1585446912 | bytes 1048576 | tf_op jit(solution)/shard_map/convolutions/pallas_call | solution.py:464
  (104 shorter events, 2.6 us)
Async XLA Ops:
  0.0 3.1 %copy-start.3 = (bf16[128,128]{1,0:T(8,128)(2,1)S(1)}, bf16[128,128]{1,0:T(8,128)(2,1)}, u32[]{:S(2)}) copy-start(bf16[128,128]{1,0:T(8,128)(2,1)} %constant.197.clone.along_z) | copy-start | bytes 98308
  0.0 3.1 %copy-start = (bf16[384,384]{1,0:T(8,128)(2,1)S(1)}, bf16[384,384]{1,0:T(8,128)(2,1)}, u32[]{:S(2)}) copy-start(bf16[384,384]{1,0:T(8,128)(2,1)} %constant.198.clone.along_y) | copy-start | bytes 884740
  0.0 3.1 %copy-start.2 = (bf16[1,5,2,2,16,384]{5,4,3,2,1,0:T(8,128)(2,1)S(1)}, bf16[1,5,2,2,16,384]{5,4,3,2,1,0:T(8,128)(2,1)}, u32[]{:S(2)}) copy-start(bf16[1,5,2,2,16,384]{5,4,3,2,1,0:T(8,128)(2,1)} %image.1) | copy-start | bytes 737284
  3.1 10.5 %copy-start.16 = (bf16[64,10,3,3,3]{0,4,3,2,1:T(4,128)(2,1)S(1)}, bf16[64,10,3,3,3]{0,4,3,2,1:T(4,128)(2,1)}, u32[]{:S(2)}) copy-start(bf16[64,10,3,3,3]{0,4,3,2,1:T(4,128)(2,1)} %param.19) | copy-start | bytes 103684
  3.8 10.4 %copy-start.17 = (bf16[10,64,3,3,3]{1,4,3,2,0:T(4,128)(2,1)S(1)}, bf16[10,64,3,3,3]{1,4,3,2,0:T(4,128)(2,1)}, u32[]{:S(2)}) copy-start(bf16[10,64,3,3,3]{1,4,3,2,0:T(4,128)(2,1)} %param.21) | copy-start | bytes 103684
  3.8 10.8 %copy-start.18 = (f32[64]{0:T(128)S(1)}, f32[64]{0:T(128)}, u32[]{:S(2)}) copy-start(f32[64]{0:T(128)} %param.20) | copy-start | bytes 772
  3.8 12.6 %collective-permute-start.16 = (bf16[1,10,16,384]{3,2,1,0:T(8,128)(2,1)S(1)}, bf16[1,10,16,384]{3,2,1,0:T(8,128)(2,1)S(1)}, u32[]{:S(2)}, u32[]{:S(2)}) collective-permute-start(bf16[1,10,16,384]{3,2,1,0:T(8,128)(2,1)S(1)} %get-tuple-element.27.refs_0_), channel_id=1, source_target_pairs={{0,2},{2,0},{4,6},{6,4},{8,10},{10,8},{12,14},{14,12},{16,18},{18,... | collective-permute-start | bytes 368648 | tf_op jit(solution)/shard_map/ppermute | solution.py:104
  3.9 13.7 %collective-permute-start.17 = (bf16[1,10,16,384]{3,2,1,0:T(8,128)(2,1)S(1)}, bf16[1,10,16,384]{3,2,1,0:T(8,128)(2,1)S(1)}, u32[]{:S(2)}, u32[]{:S(2)}) collective-permute-start(bf16[1,10,16,384]{3,2,1,0:T(8,128)(2,1)S(1)} %get-tuple-element.27.refs_0_), channel_id=1, source_target_pairs={{0,8},{2,6},{8,16},{10,2},{16,24},{18,10},{24,28},{26,18},{28,20},... | collective-permute-start | bytes 368648 | tf_op jit(solution)/shard_map/ppermute | solution.py:103
  6.6 23.9 %all-to-all-start = ((bf16[16,2,2,16,384]{4,3,2,1,0:T(8,128)(2,1)}), bf16[16,2,2,16,384]{4,3,2,1,0:T(8,128)(2,1)S(1)}, u32[]{:S(2)}, u32[]{:S(2)}) async-start(bf16[16,2,2,16,384]{4,3,2,1,0:T(8,128)(2,1)} %prepare_maps.1.earlier), calls=%async_computation | async-start | bytes 1572864 | tf_op jit(solution)/shard_map/all_to_all | solution.py:535
  11.8 5.9 %collective-permute-start = (bf16[1,10,16,384]{3,2,1,0:T(8,128)(2,1)S(1)}, bf16[1,10,16,384]{3,2,1,0:T(8,128)(2,1)S(1)}, u32[]{:S(2)}, u32[]{:S(2)}) collective-permute-start(bf16[1,10,16,384]{3,2,1,0:T(8,128)(2,1)S(1)} %get-tuple-element.28.refs_0_), channel_id=1, source_target_pairs={{0,2},{2,0},{4,6},{6,4},{8,10},{10,8},{12,14},{14,12},{16,18},{18,... | collective-permute-start | bytes 368648 | tf_op jit(solution)/shard_map/ppermute | solution.py:104
  12.0 14.3 %collective-permute-start.1 = (bf16[1,10,16,384]{3,2,1,0:T(8,128)(2,1)S(1)}, bf16[1,10,16,384]{3,2,1,0:T(8,128)(2,1)}, u32[]{:S(2)}, u32[]{:S(2)}) collective-permute-start(bf16[1,10,16,384]{3,2,1,0:T(8,128)(2,1)S(1)} %get-tuple-element.28.refs_0_), channel_id=1, source_target_pairs={{0,8},{2,6},{8,16},{10,2},{16,24},{18,10},{24,28},{26,18},{28,20},... | collective-permute-start | bytes 368648 | tf_op jit(solution)/shard_map/ppermute | solution.py:103
  16.4 22.8 %copy-start.11 = (bf16[1,10,16,384]{3,2,1,0:T(8,128)(2,1)}, bf16[1,10,16,384]{3,2,1,0:T(8,128)(2,1)S(1)}, u32[]{:S(2)}) copy-start(bf16[1,10,16,384]{3,2,1,0:T(8,128)(2,1)S(1)} %collective-permute-done.16.refs_1_) | copy-start | bytes 368644
  16.4 11.4 %collective-permute-start.18 = (bf16[1,10,16,384]{3,2,1,0:T(8,128)(2,1)S(1)}, bf16[1,10,16,384]{3,2,1,0:T(8,128)(2,1)S(1)}, u32[]{:S(2)}, u32[]{:S(2)}) collective-permute-start(bf16[1,10,16,384]{3,2,1,0:T(8,128)(2,1)S(1)} %collective-permute-done.16.refs_1_), channel_id=1, source_target_pairs={{0,8},{2,6},{8,16},{10,2},{16,24},{18,10},{24,28},{26,18},{28,20},... | collective-permute-start | bytes 368648 | tf_op jit(solution)/shard_map/ppermute | solution.py:111
  17.7 21.5 %copy-start.9 = (bf16[1,10,16,384]{3,2,1,0:T(8,128)(2,1)}, bf16[1,10,16,384]{3,2,1,0:T(8,128)(2,1)S(1)}, u32[]{:S(2)}) copy-start(bf16[1,10,16,384]{3,2,1,0:T(8,128)(2,1)S(1)} %collective-permute-done.refs_1_) | copy-start | bytes 368644
  17.7 14.0 %collective-permute-start.2 = (bf16[1,10,16,384]{3,2,1,0:T(8,128)(2,1)S(1)}, bf16[1,10,16,384]{3,2,1,0:T(8,128)(2,1)S(1)}, u32[]{:S(2)}, u32[]{:S(2)}) collective-permute-start(bf16[1,10,16,384]{3,2,1,0:T(8,128)(2,1)S(1)} %collective-permute-done.refs_1_), channel_id=1, source_target_pairs={{0,8},{2,6},{8,16},{10,2},{16,24},{18,10},{24,28},{26,18},{28,20},... | collective-permute-start | bytes 368648 | tf_op jit(solution)/shard_map/ppermute | solution.py:111
  27.9 11.3 %collective-permute-start.19 = (bf16[2,10,16,384]{3,2,1,0:T(8,128)(2,1)S(1)}, bf16[2,10,16,384]{3,2,1,0:T(8,128)(2,1)}, u32[]{:S(2)}, u32[]{:S(2)}) collective-permute-start(bf16[2,10,16,384]{3,2,1,0:T(8,128)(2,1)S(1)} %constant_dynamic-update-slice_fusion.2.refs_2_), channel_id=1, source_target_pairs={{0,8},{2,6},{8,16},{10,2},{16,24},{18,10},{24,28},{26,18},{28,20},... | collective-permute-start | bytes 737288 | tf_op jit(solution)/shard_map/ppermute | solution.py:114
  30.5 25.5 %collective-permute-start.10 = (bf16[16,2,2,16,384]{4,3,2,1,0:T(8,128)(2,1)S(1)}, bf16[16,2,2,16,384]{4,3,2,1,0:T(8,128)(2,1)}, u32[]{:S(2)}, u32[]{:S(2)}) collective-permute-start(bf16[16,2,2,16,384]{4,3,2,1,0:T(8,128)(2,1)S(1)} %all-to-all-done.refs_10_), channel_id=1, source_target_pairs={{0,1},{1,0},{2,3},{3,2},{4,5},{5,4},{6,7},{7,6},{8,9},{9,8},{10,11... | collective-permute-start | bytes 2359304 | tf_op jit(solution)/shard_map/ppermute | solution.py:539
  31.8 10.1 %collective-permute-start.3 = (bf16[2,10,16,384]{3,2,1,0:T(8,128)(2,1)S(1)}, bf16[2,10,16,384]{3,2,1,0:T(8,128)(2,1)S(1)}, u32[]{:S(2)}, u32[]{:S(2)}) collective-permute-start(bf16[2,10,16,384]{3,2,1,0:T(8,128)(2,1)S(1)} %constant_dynamic-update-slice_fusion.refs_2_), channel_id=1, source_target_pairs={{0,8},{2,6},{8,16},{10,2},{16,24},{18,10},{24,28},{26,18},{28,20},... | collective-permute-start | bytes 737288 | tf_op jit(solution)/shard_map/ppermute | solution.py:114
  39.2 5.7 %collective-permute-start.20 = (bf16[2,10,16,384]{3,2,1,0:T(8,128)(2,1)}, bf16[2,10,16,384]{3,2,1,0:T(8,128)(2,1)S(1)}, u32[]{:S(2)}, u32[]{:S(2)}) collective-permute-start(bf16[2,10,16,384]{3,2,1,0:T(8,128)(2,1)} %collective-permute-done.19.refs_3_), channel_id=1, source_target_pairs={{0,8},{2,6},{8,16},{10,2},{16,24},{18,10},{24,28},{26,18},{28,20},... | collective-permute-start | bytes 737288 | tf_op jit(solution)/shard_map/ppermute | solution.py:114
  41.8 7.8 %copy-start.5 = (bf16[2,10,16,384]{3,2,1,0:T(8,128)(2,1)}, bf16[2,10,16,384]{3,2,1,0:T(8,128)(2,1)S(1)}, u32[]{:S(2)}) copy-start(bf16[2,10,16,384]{3,2,1,0:T(8,128)(2,1)S(1)} %collective-permute-done.3.refs_3_) | copy-start | bytes 737284
  41.8 5.7 %collective-permute-start.4 = (bf16[2,10,16,384]{3,2,1,0:T(8,128)(2,1)S(1)}, bf16[2,10,16,384]{3,2,1,0:T(8,128)(2,1)S(1)}, u32[]{:S(2)}, u32[]{:S(2)}) collective-permute-start(bf16[2,10,16,384]{3,2,1,0:T(8,128)(2,1)S(1)} %collective-permute-done.3.refs_3_), channel_id=1, source_target_pairs={{0,8},{2,6},{8,16},{10,2},{16,24},{18,10},{24,28},{26,18},{28,20},... | collective-permute-start | bytes 737288 | tf_op jit(solution)/shard_map/ppermute | solution.py:114
  41.8 7.8 %collective-permute-start.22 = (bf16[2,10,16,384]{3,2,1,0:T(8,128)(2,1)S(1)}, bf16[2,10,16,384]{3,2,1,0:T(8,128)(2,1)S(1)}, u32[]{:S(2)}, u32[]{:S(2)}) collective-permute-start(bf16[2,10,16,384]{3,2,1,0:T(8,128)(2,1)S(1)} %constant_dynamic-update-slice_fusion.2.refs_2_), channel_id=1, source_target_pairs={{0,2},{2,0},{4,6},{6,4},{8,10},{10,8},{12,14},{14,12},{16,18},{18,... | collective-permute-start | bytes 737288 | tf_op jit(solution)/shard_map/ppermute | solution.py:116
  44.5 7.7 %collective-permute-start.23 = (bf16[2,10,16,384]{3,2,1,0:T(8,128)(2,1)}, bf16[2,10,16,384]{3,2,1,0:T(8,128)(2,1)}, u32[]{:S(2)}, u32[]{:S(2)}) collective-permute-start(bf16[2,10,16,384]{3,2,1,0:T(8,128)(2,1)} %collective-permute-done.19.refs_3_), channel_id=1, source_target_pairs={{0,2},{2,0},{4,6},{6,4},{8,10},{10,8},{12,14},{14,12},{16,18},{18,... | collective-permute-start | bytes 737288 | tf_op jit(solution)/shard_map/ppermute | solution.py:116
  44.9 7.2 %collective-permute-start.21 = (bf16[1,10,16,384]{3,2,1,0:T(8,128)(2,1)S(1)}, bf16[1,10,16,384]{3,2,1,0:T(8,128)(2,1)}, u32[]{:S(2)}, u32[]{:S(2)}) collective-permute-start(bf16[1,10,16,384]{3,2,1,0:T(8,128)(2,1)S(1)} %slice.144), channel_id=1, source_target_pairs={{0,8},{2,6},{8,16},{10,2},{16,24},{18,10},{24,28},{26,18},{28,20},... | collective-permute-start | bytes 368648 | tf_op jit(solution)/shard_map/ppermute | solution.py:114
  47.5 8.0 %collective-permute-start.24 = (bf16[2,10,16,384]{3,2,1,0:T(8,128)(2,1)S(1)}, bf16[2,10,16,384]{3,2,1,0:T(8,128)(2,1)}, u32[]{:S(2)}, u32[]{:S(2)}) collective-permute-start(bf16[2,10,16,384]{3,2,1,0:T(8,128)(2,1)S(1)} %collective-permute-done.20.refs_4_), channel_id=1, source_target_pairs={{0,2},{2,0},{4,6},{6,4},{8,10},{10,8},{12,14},{14,12},{16,18},{18,... | collective-permute-start | bytes 737288 | tf_op jit(solution)/shard_map/ppermute | solution.py:116
  49.6 0.7 copy-start.7
  50.3 4.4 %collective-permute-start.5 = (bf16[1,10,16,384]{3,2,1,0:T(8,128)(2,1)}, bf16[1,10,16,384]{3,2,1,0:T(8,128)(2,1)}, u32[]{:S(2)}, u32[]{:S(2)}) collective-permute-start(bf16[1,10,16,384]{3,2,1,0:T(8,128)(2,1)} %slice.136), channel_id=1, source_target_pairs={{0,8},{2,6},{8,16},{10,2},{16,24},{18,10},{24,28},{26,18},{28,20},... | collective-permute-start | bytes 368648 | tf_op jit(solution)/shard_map/ppermute | solution.py:114
  52.1 3.5 %collective-permute-start.25 = (bf16[1,10,16,384]{3,2,1,0:T(8,128)(2,1)}, bf16[1,10,16,384]{3,2,1,0:T(8,128)(2,1)}, u32[]{:S(2)}, u32[]{:S(2)}) collective-permute-start(bf16[1,10,16,384]{3,2,1,0:T(8,128)(2,1)} %collective-permute-done.21.refs_5_), channel_id=1, source_target_pairs={{0,2},{2,0},{4,6},{6,4},{8,10},{10,8},{12,14},{14,12},{16,18},{18,... | collective-permute-start | bytes 368648 | tf_op jit(solution)/shard_map/ppermute | solution.py:116
  52.2 18.9 %copy-start.6 = (bf16[2,10,16,384]{3,2,1,0:T(8,128)(2,1)S(1)}, bf16[2,10,16,384]{3,2,1,0:T(8,128)(2,1)}, u32[]{:S(2)}) copy-start(bf16[2,10,16,384]{3,2,1,0:T(8,128)(2,1)} %copy-done.5) | copy-start | bytes 737284
  52.2 18.9 %collective-permute-start.6 = (bf16[2,10,16,384]{3,2,1,0:T(8,128)(2,1)S(1)}, bf16[2,10,16,384]{3,2,1,0:T(8,128)(2,1)S(1)}, u32[]{:S(2)}, u32[]{:S(2)}) collective-permute-start(bf16[2,10,16,384]{3,2,1,0:T(8,128)(2,1)S(1)} %constant_dynamic-update-slice_fusion.refs_2_), channel_id=1, source_target_pairs={{0,2},{2,0},{4,6},{6,4},{8,10},{10,8},{12,14},{14,12},{16,18},{18,... | collective-permute-start | bytes 737288 | tf_op jit(solution)/shard_map/ppermute | solution.py:116
  54.7 16.4 %collective-permute-start.7 = (bf16[2,10,16,384]{3,2,1,0:T(8,128)(2,1)}, bf16[2,10,16,384]{3,2,1,0:T(8,128)(2,1)S(1)}, u32[]{:S(2)}, u32[]{:S(2)}) collective-permute-start(bf16[2,10,16,384]{3,2,1,0:T(8,128)(2,1)} %copy-done.5), channel_id=1, source_target_pairs={{0,2},{2,0},{4,6},{6,4},{8,10},{10,8},{12,14},{14,12},{16,18},{18,... | collective-permute-start | bytes 737288 | tf_op jit(solution)/shard_map/ppermute | solution.py:116
  55.5 15.6 %collective-permute-start.8 = (bf16[2,10,16,384]{3,2,1,0:T(8,128)(2,1)S(1)}, bf16[2,10,16,384]{3,2,1,0:T(8,128)(2,1)S(1)}, u32[]{:S(2)}, u32[]{:S(2)}) collective-permute-start(bf16[2,10,16,384]{3,2,1,0:T(8,128)(2,1)S(1)} %collective-permute-done.4.refs_4_), channel_id=1, source_target_pairs={{0,2},{2,0},{4,6},{6,4},{8,10},{10,8},{12,14},{14,12},{16,18},{18,... | collective-permute-start | bytes 737288 | tf_op jit(solution)/shard_map/ppermute | solution.py:116
  55.5 15.6 %collective-permute-start.9 = (bf16[1,10,16,384]{3,2,1,0:T(8,128)(2,1)}, bf16[1,10,16,384]{3,2,1,0:T(8,128)(2,1)S(1)}, u32[]{:S(2)}, u32[]{:S(2)}) collective-permute-start(bf16[1,10,16,384]{3,2,1,0:T(8,128)(2,1)} %collective-permute-done.5.refs_5_), channel_id=1, source_target_pairs={{0,2},{2,0},{4,6},{6,4},{8,10},{10,8},{12,14},{14,12},{16,18},{18,... | collective-permute-start | bytes 368648 | tf_op jit(solution)/shard_map/ppermute | solution.py:116
  56.0 0.9 copy-start.8
  57.0 0.9 copy-start.12
  57.9 1.3 copy-start.14
  59.2 12.0 %copy-start.10 = (bf16[1,10,16,384]{3,2,1,0:T(8,128)(2,1)S(1)}, bf16[1,10,16,384]{3,2,1,0:T(8,128)(2,1)}, u32[]{:S(2)}) copy-start(bf16[1,10,16,384]{3,2,1,0:T(8,128)(2,1)} %copy-done.9) | copy-start | bytes 368644
  59.2 12.0 %copy-start.15 = (bf16[10,256,256]{2,1,0:T(8,128)(2,1)S(1)}, bf16[10,256,256]{2,1,0:T(8,128)(2,1)}, u32[]{:S(2)}) copy-start(bf16[10,256,256]{2,1,0:T(8,128)(2,1)} %constant.196.clone.refs_14_) | copy-start | bytes 3932164
  71.0 12.9 %collective-permute-start.26 = (bf16[7,10,16,384]{3,2,1,0:T(8,128)(2,1)S(1)}, bf16[7,10,16,384]{3,2,1,0:T(8,128)(2,1)S(1)}, u32[]{:S(2)}, u32[]{:S(2)}) collective-permute-start(bf16[7,10,16,384]{3,2,1,0:T(8,128)(2,1)S(1)} %get-tuple-element.24), channel_id=1, source_target_pairs={{0,2},{2,0},{4,6},{6,4},{8,10},{10,8},{12,14},{14,12},{16,18},{18,... | collective-permute-start | bytes 2580488 | tf_op jit(solution)/shard_map/ppermute | solution.py:125
  83.3 2.5 %collective-permute-start.11 = (bf16[7,10,16,384]{3,2,1,0:T(8,128)(2,1)S(1)}, bf16[7,10,16,384]{3,2,1,0:T(8,128)(2,1)S(1)}, u32[]{:S(2)}, u32[]{:S(2)}) collective-permute-start(bf16[7,10,16,384]{3,2,1,0:T(8,128)(2,1)S(1)} %get-tuple-element.19), channel_id=1, source_target_pairs={{0,2},{2,0},{4,6},{6,4},{8,10},{10,8},{12,14},{14,12},{16,18},{18,... | collective-permute-start | bytes 2580488 | tf_op jit(solution)/shard_map/ppermute | solution.py:125
  83.9 4.1 %collective-permute-start.27 = (bf16[1,10,16,384]{3,2,1,0:T(8,128)(2,1)S(1)}, bf16[1,10,16,384]{3,2,1,0:T(8,128)(2,1)S(1)}, u32[]{:S(2)}, u32[]{:S(2)}) collective-permute-start(bf16[1,10,16,384]{3,2,1,0:T(8,128)(2,1)S(1)} %add_convert_fusion.4), channel_id=1, source_target_pairs={{0,8},{2,6},{8,16},{10,2},{16,24},{18,10},{24,28},{26,18},{28,20},... | collective-permute-start | bytes 368648 | tf_op jit(solution)/shard_map/ppermute | solution.py:140
  85.9 4.1 %collective-permute-start.12 = (bf16[1,10,16,384]{3,2,1,0:T(8,128)(2,1)S(1)}, bf16[1,10,16,384]{3,2,1,0:T(8,128)(2,1)S(1)}, u32[]{:S(2)}, u32[]{:S(2)}) collective-permute-start(bf16[1,10,16,384]{3,2,1,0:T(8,128)(2,1)S(1)} %add_convert_fusion.5), channel_id=1, source_target_pairs={{0,8},{2,6},{8,16},{10,2},{16,24},{18,10},{24,28},{26,18},{28,20},... | collective-permute-start | bytes 368648 | tf_op jit(solution)/shard_map/ppermute | solution.py:140
  88.1 5.4 %collective-permute-start.28 = (bf16[2,10,16,384]{3,2,1,0:T(8,128)(2,1)S(1)}, bf16[2,10,16,384]{3,2,1,0:T(8,128)(2,1)S(1)}, u32[]{:S(2)}, u32[]{:S(2)}) collective-permute-start(bf16[2,10,16,384]{3,2,1,0:T(8,128)(2,1)S(1)} %pad_maximum_fusion.2), channel_id=1, source_target_pairs={{0,8},{2,6},{8,16},{10,2},{16,24},{18,10},{24,28},{26,18},{28,20},... | collective-permute-start | bytes 737288 | tf_op jit(solution)/shard_map/ppermute | solution.py:140
  90.1 6.0 %collective-permute-start.13 = (bf16[2,10,16,384]{3,2,1,0:T(8,128)(2,1)S(1)}, bf16[2,10,16,384]{3,2,1,0:T(8,128)(2,1)S(1)}, u32[]{:S(2)}, u32[]{:S(2)}) collective-permute-start(bf16[2,10,16,384]{3,2,1,0:T(8,128)(2,1)S(1)} %pad_maximum_fusion.1), channel_id=1, source_target_pairs={{0,8},{2,6},{8,16},{10,2},{16,24},{18,10},{24,28},{26,18},{28,20},... | collective-permute-start | bytes 737288 | tf_op jit(solution)/shard_map/ppermute | solution.py:140
  93.5 5.4 %collective-permute-start.29 = (bf16[2,10,16,384]{3,2,1,0:T(8,128)(2,1)S(1)}, bf16[2,10,16,384]{3,2,1,0:T(8,128)(2,1)S(1)}, u32[]{:S(2)}, u32[]{:S(2)}) collective-permute-start(bf16[2,10,16,384]{3,2,1,0:T(8,128)(2,1)S(1)} %add_convert_fusion.1), channel_id=1, source_target_pairs={{0,8},{2,6},{8,16},{10,2},{16,24},{18,10},{24,28},{26,18},{28,20},... | collective-permute-start | bytes 737288 | tf_op jit(solution)/shard_map/ppermute | solution.py:140
  96.2 5.4 %collective-permute-start.14 = (bf16[2,10,16,384]{3,2,1,0:T(8,128)(2,1)S(1)}, bf16[2,10,16,384]{3,2,1,0:T(8,128)(2,1)S(1)}, u32[]{:S(2)}, u32[]{:S(2)}) collective-permute-start(bf16[2,10,16,384]{3,2,1,0:T(8,128)(2,1)S(1)} %add_convert_fusion.3), channel_id=1, source_target_pairs={{0,8},{2,6},{8,16},{10,2},{16,24},{18,10},{24,28},{26,18},{28,20},... | collective-permute-start | bytes 737288 | tf_op jit(solution)/shard_map/ppermute | solution.py:140
  99.0 5.1 %collective-permute-start.30 = (bf16[2,10,16,384]{3,2,1,0:T(8,128)(2,1)S(1)}, bf16[2,10,16,384]{3,2,1,0:T(8,128)(2,1)S(1)}, u32[]{:S(2)}, u32[]{:S(2)}) collective-permute-start(bf16[2,10,16,384]{3,2,1,0:T(8,128)(2,1)S(1)} %add_convert_fusion), channel_id=1, source_target_pairs={{0,8},{2,6},{8,16},{10,2},{16,24},{18,10},{24,28},{26,18},{28,20},... | collective-permute-start | bytes 737288 | tf_op jit(solution)/shard_map/ppermute | solution.py:140
  101.7 5.4 %collective-permute-start.15 = (bf16[2,10,16,384]{3,2,1,0:T(8,128)(2,1)S(1)}, bf16[2,10,16,384]{3,2,1,0:T(8,128)(2,1)S(1)}, u32[]{:S(2)}, u32[]{:S(2)}) collective-permute-start(bf16[2,10,16,384]{3,2,1,0:T(8,128)(2,1)S(1)} %add_convert_fusion.2), channel_id=1, source_target_pairs={{0,8},{2,6},{8,16},{10,2},{16,24},{18,10},{24,28},{26,18},{28,20},... | collective-permute-start | bytes 737288 | tf_op jit(solution)/shard_map/ppermute | solution.py:140
  104.2 7.7 %copy-start.1 = (bf16[384,384]{1,0:T(8,128)(2,1)S(1)}, bf16[384,384]{1,0:T(8,128)(2,1)}, u32[]{:S(2)}) copy-start(bf16[384,384]{1,0:T(8,128)(2,1)} %constant.200.clone.along_y) | copy-start | bytes 884740
  104.2 7.7 %copy-start.4 = (bf16[128,128]{1,0:T(8,128)(2,1)S(1)}, bf16[128,128]{1,0:T(8,128)(2,1)}, u32[]{:S(2)}) copy-start(bf16[128,128]{1,0:T(8,128)(2,1)} %constant.199.clone.along_z) | copy-start | bytes 98308
  107.2 18.9 %copy-start.13 = (f32[10]{0:T(128)S(1)}, f32[10]{0:T(128)}, u32[]{:S(2)}) copy-start(f32[10]{0:T(128)} %refs_7_.1) | copy-start | bytes 124
  107.2 4.7 %collective-permute-start.31 = (bf16[2,10,16,384]{3,2,1,0:T(8,128)(2,1)S(1)}, bf16[2,10,16,384]{3,2,1,0:T(8,128)(2,1)S(1)}, u32[]{:S(2)}, u32[]{:S(2)}) collective-permute-start(bf16[2,10,16,384]{3,2,1,0:T(8,128)(2,1)S(1)} %fusion.5), channel_id=1, source_target_pairs={{0,2},{2,0},{4,6},{6,4},{8,10},{10,8},{12,14},{14,12},{16,18},{18,... | collective-permute-start | bytes 737288 | tf_op jit(solution)/shard_map/ppermute | solution.py:547
  112.6 7.5 %collective-permute-start.32 = (bf16[2,10,2,384]{3,2,1,0:T(2,128)(2,1)S(1)}, bf16[2,10,2,384]{3,2,1,0:T(2,128)(2,1)S(1)}, u32[]{:S(2)}, u32[]{:S(2)}) collective-permute-start(bf16[2,10,2,384]{3,2,1,0:T(2,128)(2,1)S(1)} %get-tuple-element.25), channel_id=1, source_target_pairs={{0,2},{2,4},{4,6},{6,8},{8,10},{10,12},{12,14},{14,16},{16,18},{18... | collective-permute-start | bytes 92168 | tf_op jit(solution)/shard_map/ppermute | solution.py:552
  116.6 5.5 %collective-permute-start.33 = (bf16[2,10,2,384]{3,2,1,0:T(2,128)(2,1)S(1)}, bf16[2,10,2,384]{3,2,1,0:T(2,128)(2,1)S(1)}, u32[]{:S(2)}, u32[]{:S(2)}) collective-permute-start(bf16[2,10,2,384]{3,2,1,0:T(2,128)(2,1)S(1)} %get-tuple-element.26), channel_id=1, source_target_pairs={{2,0},{4,2},{6,4},{8,6},{10,8},{12,10},{14,12},{16,14},{18,16},{20... | collective-permute-start | bytes 92168 | tf_op jit(solution)/shard_map/ppermute | solution.py:552
  118.7 7.4 %collective-permute-start.34 = (bf16[2,10,16,384]{3,2,1,0:T(8,128)(2,1)S(1)}, bf16[2,10,16,384]{3,2,1,0:T(8,128)(2,1)S(1)}, u32[]{:S(2)}, u32[]{:S(2)}) collective-permute-start(bf16[2,10,16,384]{3,2,1,0:T(8,128)(2,1)S(1)} %update.1.refs_0_), channel_id=1, source_target_pairs={{0,1},{1,0},{2,3},{3,2},{4,5},{5,4},{6,7},{7,6},{8,9},{9,8},{10,11... | collective-permute-start | bytes 737288 | tf_op jit(solution)/shard_map/ppermute | solution.py:550
  122.1 3.9 %collective-permute-start.35 = (bf16[2,10,4,384]{3,2,1,0:T(4,128)(2,1)S(1)}, bf16[2,10,4,384]{3,2,1,0:T(4,128)(2,1)S(1)}, u32[]{:S(2)}, u32[]{:S(2)}) collective-permute-start(bf16[2,10,4,384]{3,2,1,0:T(4,128)(2,1)S(1)} %pad_maximum_fusion.3.refs_1_), channel_id=1, source_target_pairs={{0,1},{1,0},{2,3},{3,2},{4,5},{5,4},{6,7},{7,6},{8,9},{9,8},{10,11... | collective-permute-start | bytes 184328 | tf_op jit(solution)/shard_map/ppermute | solution.py:554

commit v6 on v5

--- a/solution.py
+++ b/solution.py
@@ -28,15 +28,12 @@
     return np.stack([upper, lower], axis=0).astype(ml_dtypes.bfloat16)
 
 
-def split_tables(length, count, left, inverse):
-    table = dft_table(length, inverse)
+def split_tables(length, count, left):
+    table = dft_table(length, False)
     part = length // count
     out = []
     for s in range(count):
-        if inverse:
-            piece = table[:, :part, :, s::count]
-        else:
-            piece = table[:, s::count, :, :part]
+        piece = table[:, s::count, :, :part]
         if left:
             piece = piece.transpose(2, 3, 0, 1)
         out.append(piece.reshape(2 * part, 2 * part))
@@ -157,7 +154,7 @@
     maps, refs = refs[:coils], refs[coils:]
     measured, sampling, tables = refs[:3]
     out, products, backs = refs[3:6], refs[6], refs[7]
-    ty_f, tz_f, tz_i, ty_i = [0, 1, 2], [3, 4], [5, 6], [7, 8, 9]
+    in_y, in_z = [0, 1, 2], [3, 4]
     rows, ny = held_images[0].shape[-2:]
     nz = sampling.shape[-1]
     count, half = nz // rows, rows // 2
@@ -199,7 +196,7 @@
                     products[c, j, at, my:] = p_imag[lines, cells]
 
     def to_frequency_y(c):
-        return [nt_dot(tables[ty_f[j]], products[c, j].astype(BF16)) for j in range(3)]
+        return [nt_dot(tables[in_y[j]], products[c, j].astype(BF16)) for j in range(3)]
 
     def spectra_of(parts):
         parts = thirds(*[(part[:my], part[my:]) for part in parts], -1.0)
@@ -209,7 +206,7 @@
         halves = []
         for j in range(2):
             cells = slice(j * mz, (j + 1) * mz)
-            halves.append(nn_dot(jnp.concatenate([spectra[0][:, cells], spectra[1][:, cells]], axis=1), tables[tz_f[j]]))
+            halves.append(nn_dot(jnp.concatenate([spectra[0][:, cells], spectra[1][:, cells]], axis=1), tables[in_z[j]]))
         return halves
 
     def residual_of(c, halves):
@@ -226,7 +223,7 @@
         return jnp.concatenate(sums, axis=1), jnp.concatenate(differences, axis=1)
 
     def to_depth(folds):
-        return [nt_dot(tables[tz_i[j]], folds[j]) for j in range(2)]
+        return [nt_dot(tables[in_z[j]], folds[j]) for j in range(2)]
 
     def lines_of(depths):
         lines = [[], [], []]
@@ -239,7 +236,7 @@
 
     def to_image(c, lines):
         for i in range(3):
-            backs[c, i] = nn_dot(lines[i], tables[ty_i[i]])
+            backs[c, i] = nn_dot(lines[i], tables[in_y[i]])
 
     stages = [
         lambda c, _: product(c),
@@ -301,7 +298,7 @@
             ],
         ),
         out_shape=[jax.ShapeDtypeStruct((m, channels, rows, ny), BF16) for m in (2, far, far)],
-        compiler_params=pltpu.CompilerParams(vmem_limit_bytes=46 * 2**20),
+        compiler_params=pltpu.CompilerParams(vmem_limit_bytes=52 * 2**20),
         cost_estimate=pl.CostEstimate(flops=flops, bytes_accessed=8 * 2**20, transcendentals=0),
         name="gradient",
     )(where, *images, *[a for a, _ in maps], measured, sampling, tables)
@@ -512,16 +509,7 @@
     _, encodings, _, width, rows, ny = current_image.shape
     nz = rows * devices
     channels = 2 * encodings
-    tables = jnp.asarray(
-        np.concatenate(
-            [
-                split_tables(ny, 3, True, False),
-                split_tables(nz, 2, False, False),
-                split_tables(nz, 2, True, True),
-                split_tables(ny, 3, False, True),
-            ]
-        )
-    )
+    tables = jnp.asarray(np.concatenate([split_tables(ny, 3, True), split_tables(nz, 2, False)]))
     which = q[None].astype(jnp.int32)
     where = jnp.concatenate([ring.slabs(), which])
     swap = [(0, 1), (1, 0)]

time: 135 us -> 132 us (0.978)
  local copies, waits for them, and re-layouts: 6.5 us -> 1.77 us
  waiting for transfers between devices: 33.5 us -> 35.2 us
  Pallas kernels: 35.3 us -> 36.8 us
    unnamed x40 -> x28, local copies, waits for them, and re-layouts: 4.86 us -> 0.78 us
    pallas_call x2, Pallas kernels: 23.9 us -> 25.5 us  [gradient(): pl.pallas_call(functools.partial(gradient_kernel, len(images), n), grid_s...]
  transfers between devices with their start and end apart: 37 -> 37, of which waited for: 20 -> 19; matrix products, arithmetic and copies ran while one was open for 4% -> 3% of each run, Pallas kernels for 18% -> 19%
where the time goes in v6:
time: 132 us; the launch traced here: 131 us
  starting transfers between devices  53.1 us (40%)
  Pallas kernels  36.8 us (28%)
  waiting for transfers between devices  35.2 us (27%)
  other arithmetic  3.48 us (3%)
  local copies, waits for them, and re-layouts  1.77 us (1%)
    pallas_call x2, Pallas kernels, gradient(): pl.pallas_call(functools.partial(gradient_kernel, len(images), n), grid_s...  25.5 us
    ppermute x8, starting transfers between devices, step(): self.held = lax.ppermute(total.astype(BF16), SLAB, self.ring.perm())  14 us
    ppermute x6, waiting for transfers between devices, step(): lax.ppermute(after(held, *earlier) if earlier else held, SLAB, self.ring....  10.3 us
    ppermute x8, waiting for transfers between devices, step(): self.held = lax.ppermute(total.astype(BF16), SLAB, self.ring.perm())  8.11 us
    ppermute x2, waiting for transfers between devices, __init__(): self.first = lax.ppermute(mine, SLAB, ring.perm())  7.92 us
    ppermute x6, starting transfers between devices, step(): lax.ppermute(after(held, *earlier) if earlier else held, SLAB, self.ring....  7.44 us
    pallas_call x1, Pallas kernels, convolutions(): pl.pallas_call(convolution_kernel, in_specs=[smem] + [vmem] * (len(parts)...  6.94 us
    ppermute x8, starting transfers between devices, step(): self.other.append(lax.ppermute(self.held, SLAB, self.ring.siblings()))  5.64 us
  transfers between devices with their start and end apart: 37, of which 19 were waited for; matrix products, arithmetic and copies ran while one was open for 3% of the time, Pallas kernels for 19%

profile of v6, /device:TPU:1, one launch (start us, length us, event | category | flops | bytes accessed | tf_op | source)
XLA Modules:
  0.0 130.8 jit_solution(12636332966273398055)
XLA Ops:
  0.0 3.0 %prepare_maps.1.earlier = bf16[16,2,2,16,384]{4,3,2,1,0:T(8,128)(2,1)} custom-call(s32[1]{0:T(128)} %bitcast.2.which, bf16[16,2,2,2,16,384]{5,4,3,2,1,0:T(8,128)(2,1)} %bitcast.69, bf16[128,128]{1,0:T(8,128)(2,1)} %constant.197.clone.along_z, bf16[384,384]{1,0:T(8,128)(2,1)} %constant.198.clone.along_y), custom_call_target="tpu_custom_call" | custom-call | tf_op jit(solution)/shard_map/prepare_maps/pallas_call | solution.py:359
  3.1 0.7 prepare_image.1.image
  3.8 0.1 collective-permute-start.16
  3.9 2.7 %collective-permute-start.17 = (bf16[1,10,16,384]{3,2,1,0:T(8,128)(2,1)S(1)}, bf16[1,10,16,384]{3,2,1,0:T(8,128)(2,1)S(1)}, u32[]{:S(2)}, u32[]{:S(2)}) collective-permute-start(bf16[1,10,16,384]{3,2,1,0:T(8,128)(2,1)S(1)} %get-tuple-element.27.refs_0_), channel_id=1, source_target_pairs={{0,8},{2,6},{8,16},{10,2},{16,24},{18,10},{24,28},{26,18},{28,20},... | collective-permute-start | bytes 368648 | tf_op jit(solution)/shard_map/ppermute | solution.py:100
  6.6 5.2 %all-to-all-start = ((bf16[16,2,2,16,384]{4,3,2,1,0:T(8,128)(2,1)}), bf16[16,2,2,16,384]{4,3,2,1,0:T(8,128)(2,1)}, u32[]{:S(2)}, u32[]{:S(2)}) async-start(bf16[16,2,2,16,384]{4,3,2,1,0:T(8,128)(2,1)} %prepare_maps.1.earlier), calls=%async_computation | async-start | bytes 1572864 | tf_op jit(solution)/shard_map/all_to_all | solution.py:523
  11.8 0.2 collective-permute-start
  12.0 1.5 %collective-permute-start.1 = (bf16[1,10,16,384]{3,2,1,0:T(8,128)(2,1)S(1)}, bf16[1,10,16,384]{3,2,1,0:T(8,128)(2,1)S(1)}, u32[]{:S(2)}, u32[]{:S(2)}) collective-permute-start(bf16[1,10,16,384]{3,2,1,0:T(8,128)(2,1)S(1)} %get-tuple-element.28.refs_0_), channel_id=1, source_target_pairs={{0,8},{2,6},{8,16},{10,2},{16,24},{18,10},{24,28},{26,18},{28,20},... | collective-permute-start | bytes 368648 | tf_op jit(solution)/shard_map/ppermute | solution.py:100
  13.7 0.1 maximum_bitcast_fusion
  13.9 0.1 reshape.26
  14.0 0.1 copy.17
  14.3 0.1 reshape.28
  14.7 1.1 convert_element_type.117.refs_13_
  15.8 1.2 collective-permute-start.18
  17.1 1.2 collective-permute-start.2
  18.3 7.9 %collective-permute-done.1 = bf16[1,10,16,384]{3,2,1,0:T(8,128)(2,1)S(1)} collective-permute-done((bf16[1,10,16,384]{3,2,1,0:T(8,128)(2,1)S(1)}, bf16[1,10,16,384]{3,2,1,0:T(8,128)(2,1)S(1)}, u32[]{:S(2)}, u32[]{:S(2)}) %collective-permute-start.1) | collective-permute-done | bytes 122912 | tf_op jit(solution)/shard_map/ppermute | solution.py:100
  26.2 1.7 %collective-permute-done.18 = bf16[1,10,16,384]{3,2,1,0:T(8,128)(2,1)S(1)} collective-permute-done((bf16[1,10,16,384]{3,2,1,0:T(8,128)(2,1)S(1)}, bf16[1,10,16,384]{3,2,1,0:T(8,128)(2,1)S(1)}, u32[]{:S(2)}, u32[]{:S(2)}) %collective-permute-start.18) | collective-permute-done | bytes 122912 | tf_op jit(solution)/shard_map/ppermute | solution.py:108
  28.0 1.3 %collective-permute-start.19 = (bf16[2,10,16,384]{3,2,1,0:T(8,128)(2,1)S(1)}, bf16[2,10,16,384]{3,2,1,0:T(8,128)(2,1)S(1)}, u32[]{:S(2)}, u32[]{:S(2)}) collective-permute-start(bf16[2,10,16,384]{3,2,1,0:T(8,128)(2,1)S(1)} %constant_dynamic-update-slice_fusion.2.refs_2_), channel_id=1, source_target_pairs={{0,8},{2,6},{8,16},{10,2},{16,24},{18,10},{24,28},{26,18},{28,20},... | collective-permute-start | bytes 737288 | tf_op jit(solution)/shard_map/ppermute | solution.py:111
  29.3 1.3 all-to-all-done.refs_10_
  30.6 1.3 collective-permute-start.10
  31.9 4.3 %collective-permute-start.3 = (bf16[2,10,16,384]{3,2,1,0:T(8,128)(2,1)S(1)}, bf16[2,10,16,384]{3,2,1,0:T(8,128)(2,1)S(1)}, u32[]{:S(2)}, u32[]{:S(2)}) collective-permute-start(bf16[2,10,16,384]{3,2,1,0:T(8,128)(2,1)S(1)} %constant_dynamic-update-slice_fusion.refs_2_), channel_id=1, source_target_pairs={{0,8},{2,6},{8,16},{10,2},{16,24},{18,10},{24,28},{26,18},{28,20},... | collective-permute-start | bytes 737288 | tf_op jit(solution)/shard_map/ppermute | solution.py:111
  36.1 3.0 %collective-permute-done.19.refs_3_ = bf16[2,10,16,384]{3,2,1,0:T(8,128)(2,1)S(1)} collective-permute-done((bf16[2,10,16,384]{3,2,1,0:T(8,128)(2,1)S(1)}, bf16[2,10,16,384]{3,2,1,0:T(8,128)(2,1)S(1)}, u32[]{:S(2)}, u32[]{:S(2)}) %collective-permute-start.19) | collective-permute-done | bytes 245792 | tf_op jit(solution)/shard_map/ppermute | solution.py:111
  39.2 2.6 %collective-permute-done.3.refs_3_ = bf16[2,10,16,384]{3,2,1,0:T(8,128)(2,1)S(1)} collective-permute-done((bf16[2,10,16,384]{3,2,1,0:T(8,128)(2,1)S(1)}, bf16[2,10,16,384]{3,2,1,0:T(8,128)(2,1)S(1)}, u32[]{:S(2)}, u32[]{:S(2)}) %collective-permute-start.3) | collective-permute-done | bytes 245792 | tf_op jit(solution)/shard_map/ppermute | solution.py:111
  41.8 2.7 %collective-permute-start.22 = (bf16[2,10,16,384]{3,2,1,0:T(8,128)(2,1)S(1)}, bf16[2,10,16,384]{3,2,1,0:T(8,128)(2,1)S(1)}, u32[]{:S(2)}, u32[]{:S(2)}) collective-permute-start(bf16[2,10,16,384]{3,2,1,0:T(8,128)(2,1)S(1)} %constant_dynamic-update-slice_fusion.2.refs_2_), channel_id=1, source_target_pairs={{0,2},{2,0},{4,6},{6,4},{8,10},{10,8},{12,14},{14,12},{16,18},{18,... | collective-permute-start | bytes 737288 | tf_op jit(solution)/shard_map/ppermute | solution.py:113
  44.7 2.5 %collective-permute-done.4.refs_4_ = bf16[2,10,16,384]{3,2,1,0:T(8,128)(2,1)S(1)} collective-permute-done((bf16[2,10,16,384]{3,2,1,0:T(8,128)(2,1)S(1)}, bf16[2,10,16,384]{3,2,1,0:T(8,128)(2,1)S(1)}, u32[]{:S(2)}, u32[]{:S(2)}) %collective-permute-start.4) | collective-permute-done | bytes 245792 | tf_op jit(solution)/shard_map/ppermute | solution.py:111
  47.3 1.3 %collective-permute-start.24 = (bf16[2,10,16,384]{3,2,1,0:T(8,128)(2,1)S(1)}, bf16[2,10,16,384]{3,2,1,0:T(8,128)(2,1)}, u32[]{:S(2)}, u32[]{:S(2)}) collective-permute-start(bf16[2,10,16,384]{3,2,1,0:T(8,128)(2,1)S(1)} %collective-permute-done.20.refs_4_), channel_id=1, source_target_pairs={{0,2},{2,0},{4,6},{6,4},{8,10},{10,8},{12,14},{14,12},{16,18},{18,... | collective-permute-start | bytes 737288 | tf_op jit(solution)/shard_map/ppermute | solution.py:113
  48.6 1.8 %collective-permute-start.5 = (bf16[1,10,16,384]{3,2,1,0:T(8,128)(2,1)S(1)}, bf16[1,10,16,384]{3,2,1,0:T(8,128)(2,1)S(1)}, u32[]{:S(2)}, u32[]{:S(2)}) collective-permute-start(bf16[1,10,16,384]{3,2,1,0:T(8,128)(2,1)S(1)} %slice.136), channel_id=1, source_target_pairs={{0,8},{2,6},{8,16},{10,2},{16,24},{18,10},{24,28},{26,18},{28,20},... | collective-permute-start | bytes 368648 | tf_op jit(solution)/shard_map/ppermute | solution.py:111
  50.4 0.5 collective-permute-start.25
  50.9 0.1 concatenate.35.slabs
  51.1 2.0 %collective-permute-done.5.refs_5_ = bf16[1,10,16,384]{3,2,1,0:T(8,128)(2,1)S(1)} collective-permute-done((bf16[1,10,16,384]{3,2,1,0:T(8,128)(2,1)S(1)}, bf16[1,10,16,384]{3,2,1,0:T(8,128)(2,1)S(1)}, u32[]{:S(2)}, u32[]{:S(2)}) %collective-permute-start.5) | collective-permute-done | bytes 122912 | tf_op jit(solution)/shard_map/ppermute | solution.py:111
  53.1 0.5 collective-permute-start.7
  53.6 0.5 collective-permute-start.9
  54.1 12.7 %gradient.3 = (bf16[2,10,16,384]{3,2,1,0:T(8,128)(2,1)S(1)}, bf16[7,10,16,384]{3,2,1,0:T(8,128)(2,1)}, bf16[7,10,16,384]{3,2,1,0:T(8,128)(2,1)}) custom-call(s32[33]{0:T(128)S(1)} %concatenate.35.slabs, bf16[1,10,16,384]{3,2,1,0:T(8,128)(2,1)S(1)} %get-tuple-element.27.refs_0_, bf16[1,10,16,384]{3,2,1,0:T(8,128)(2,1)S(1)} %collective-permute-done.16.refs_1_, ...), custom_call_target="tpu_custom_call" | custom-call | flops 10066329600 | bytes 8388608 | tf_op jit(solution)/shard_map/gradient/pallas_call | solution.py:278
  66.9 0.7 copy-done.11
  67.6 12.8 %gradient.2 = (bf16[2,10,16,384]{3,2,1,0:T(8,128)(2,1)S(1)}, bf16[7,10,16,384]{3,2,1,0:T(8,128)(2,1)}, bf16[7,10,16,384]{3,2,1,0:T(8,128)(2,1)}) custom-call(s32[33]{0:T(128)S(1)} %concatenate.35.slabs, bf16[1,10,16,384]{3,2,1,0:T(8,128)(2,1)S(1)} %get-tuple-element.28.refs_0_, bf16[1,10,16,384]{3,2,1,0:T(8,128)(2,1)S(1)} %collective-permute-done.refs_1_, ...), custom_call_target="tpu_custom_call" | custom-call | flops 10066329600 | bytes 8388608 | tf_op jit(solution)/shard_map/gradient/pallas_call | solution.py:278
  80.4 0.5 collective-permute-start.11
  80.9 1.8 %collective-permute-start.27 = (bf16[1,10,16,384]{3,2,1,0:T(8,128)(2,1)S(1)}, bf16[1,10,16,384]{3,2,1,0:T(8,128)(2,1)S(1)}, u32[]{:S(2)}, u32[]{:S(2)}) collective-permute-start(bf16[1,10,16,384]{3,2,1,0:T(8,128)(2,1)S(1)} %add_convert_fusion.4), channel_id=1, source_target_pairs={{0,8},{2,6},{8,16},{10,2},{16,24},{18,10},{24,28},{26,18},{28,20},... | collective-permute-start | bytes 368648 | tf_op jit(solution)/shard_map/ppermute | solution.py:137
  82.8 0.3 collective-permute-done.11
  83.1 0.9 add_convert_fusion.5
  84.0 1.8 %collective-permute-start.12 = (bf16[1,10,16,384]{3,2,1,0:T(8,128)(2,1)S(1)}, bf16[1,10,16,384]{3,2,1,0:T(8,128)(2,1)S(1)}, u32[]{:S(2)}, u32[]{:S(2)}) collective-permute-start(bf16[1,10,16,384]{3,2,1,0:T(8,128)(2,1)S(1)} %add_convert_fusion.5), channel_id=1, source_target_pairs={{0,8},{2,6},{8,16},{10,2},{16,24},{18,10},{24,28},{26,18},{28,20},... | collective-permute-start | bytes 368648 | tf_op jit(solution)/shard_map/ppermute | solution.py:137
  86.0 1.8 %collective-permute-start.28 = (bf16[2,10,16,384]{3,2,1,0:T(8,128)(2,1)S(1)}, bf16[2,10,16,384]{3,2,1,0:T(8,128)(2,1)S(1)}, u32[]{:S(2)}, u32[]{:S(2)}) collective-permute-start(bf16[2,10,16,384]{3,2,1,0:T(8,128)(2,1)S(1)} %pad_maximum_fusion.2), channel_id=1, source_target_pairs={{0,8},{2,6},{8,16},{10,2},{16,24},{18,10},{24,28},{26,18},{28,20},... | collective-permute-start | bytes 737288 | tf_op jit(solution)/shard_map/ppermute | solution.py:137
  87.8 0.7 collective-permute-done.12
  88.5 1.4 %collective-permute-start.13 = (bf16[2,10,16,384]{3,2,1,0:T(8,128)(2,1)S(1)}, bf16[2,10,16,384]{3,2,1,0:T(8,128)(2,1)S(1)}, u32[]{:S(2)}, u32[]{:S(2)}) collective-permute-start(bf16[2,10,16,384]{3,2,1,0:T(8,128)(2,1)S(1)} %pad_maximum_fusion.1), channel_id=1, source_target_pairs={{0,8},{2,6},{8,16},{10,2},{16,24},{18,10},{24,28},{26,18},{28,20},... | collective-permute-start | bytes 737288 | tf_op jit(solution)/shard_map/ppermute | solution.py:137
  90.0 1.4 %collective-permute-done.28 = bf16[2,10,16,384]{3,2,1,0:T(8,128)(2,1)S(1)} collective-permute-done((bf16[2,10,16,384]{3,2,1,0:T(8,128)(2,1)S(1)}, bf16[2,10,16,384]{3,2,1,0:T(8,128)(2,1)S(1)}, u32[]{:S(2)}, u32[]{:S(2)}) %collective-permute-start.28) | collective-permute-done | bytes 245792 | tf_op jit(solution)/shard_map/ppermute | solution.py:137
  91.5 1.8 %collective-permute-start.29 = (bf16[2,10,16,384]{3,2,1,0:T(8,128)(2,1)S(1)}, bf16[2,10,16,384]{3,2,1,0:T(8,128)(2,1)S(1)}, u32[]{:S(2)}, u32[]{:S(2)}) collective-permute-start(bf16[2,10,16,384]{3,2,1,0:T(8,128)(2,1)S(1)} %add_convert_fusion.1), channel_id=1, source_target_pairs={{0,8},{2,6},{8,16},{10,2},{16,24},{18,10},{24,28},{26,18},{28,20},... | collective-permute-start | bytes 737288 | tf_op jit(solution)/shard_map/ppermute | solution.py:137
  93.3 0.7 collective-permute-done.13
  94.1 1.8 %collective-permute-start.14 = (bf16[2,10,16,384]{3,2,1,0:T(8,128)(2,1)S(1)}, bf16[2,10,16,384]{3,2,1,0:T(8,128)(2,1)S(1)}, u32[]{:S(2)}, u32[]{:S(2)}) collective-permute-start(bf16[2,10,16,384]{3,2,1,0:T(8,128)(2,1)S(1)} %add_convert_fusion.3), channel_id=1, source_target_pairs={{0,8},{2,6},{8,16},{10,2},{16,24},{18,10},{24,28},{26,18},{28,20},... | collective-permute-start | bytes 737288 | tf_op jit(solution)/shard_map/ppermute | solution.py:137
  95.9 1.0 collective-permute-done.29
  97.0 1.8 %collective-permute-start.30 = (bf16[2,10,16,384]{3,2,1,0:T(8,128)(2,1)S(1)}, bf16[2,10,16,384]{3,2,1,0:T(8,128)(2,1)S(1)}, u32[]{:S(2)}, u32[]{:S(2)}) collective-permute-start(bf16[2,10,16,384]{3,2,1,0:T(8,128)(2,1)S(1)} %add_convert_fusion), channel_id=1, source_target_pairs={{0,8},{2,6},{8,16},{10,2},{16,24},{18,10},{24,28},{26,18},{28,20},... | collective-permute-start | bytes 737288 | tf_op jit(solution)/shard_map/ppermute | solution.py:137
  98.8 0.7 collective-permute-done.14
  99.5 0.1 add_convert_fusion.2
  99.6 1.8 %collective-permute-start.15 = (bf16[2,10,16,384]{3,2,1,0:T(8,128)(2,1)S(1)}, bf16[2,10,16,384]{3,2,1,0:T(8,128)(2,1)S(1)}, u32[]{:S(2)}, u32[]{:S(2)}) collective-permute-start(bf16[2,10,16,384]{3,2,1,0:T(8,128)(2,1)S(1)} %add_convert_fusion.2), channel_id=1, source_target_pairs={{0,8},{2,6},{8,16},{10,2},{16,24},{18,10},{24,28},{26,18},{28,20},... | collective-permute-start | bytes 737288 | tf_op jit(solution)/shard_map/ppermute | solution.py:137
  101.4 0.7 collective-permute-done.30
  102.1 2.9 %collective-permute-done.15 = bf16[2,10,16,384]{3,2,1,0:T(8,128)(2,1)S(1)} collective-permute-done((bf16[2,10,16,384]{3,2,1,0:T(8,128)(2,1)S(1)}, bf16[2,10,16,384]{3,2,1,0:T(8,128)(2,1)S(1)}, u32[]{:S(2)}, u32[]{:S(2)}) %collective-permute-start.15) | collective-permute-done | bytes 245792 | tf_op jit(solution)/shard_map/ppermute | solution.py:137
  105.1 3.4 %collective-permute-start.31 = (bf16[2,10,16,384]{3,2,1,0:T(8,128)(2,1)S(1)}, bf16[2,10,16,384]{3,2,1,0:T(8,128)(2,1)S(1)}, u32[]{:S(2)}, u32[]{:S(2)}) collective-permute-start(bf16[2,10,16,384]{3,2,1,0:T(8,128)(2,1)S(1)} %fusion.5), channel_id=1, source_target_pairs={{0,2},{2,0},{4,6},{6,4},{8,10},{10,8},{12,14},{14,12},{16,18},{18,... | collective-permute-start | bytes 737288 | tf_op jit(solution)/shard_map/ppermute | solution.py:535
  108.6 1.1 collective-permute-done.31.received
  109.7 0.7 update.1.refs_0_
  110.4 3.9 %collective-permute-start.32 = (bf16[2,10,2,384]{3,2,1,0:T(2,128)(2,1)S(1)}, bf16[2,10,2,384]{3,2,1,0:T(2,128)(2,1)S(1)}, u32[]{:S(2)}, u32[]{:S(2)}) collective-permute-start(bf16[2,10,2,384]{3,2,1,0:T(2,128)(2,1)S(1)} %get-tuple-element.25), channel_id=1, source_target_pairs={{0,2},{2,4},{4,6},{6,8},{8,10},{10,12},{12,14},{14,16},{16,18},{18... | collective-permute-start | bytes 92168 | tf_op jit(solution)/shard_map/ppermute | solution.py:540
  114.3 2.1 %collective-permute-start.33 = (bf16[2,10,2,384]{3,2,1,0:T(2,128)(2,1)S(1)}, bf16[2,10,2,384]{3,2,1,0:T(2,128)(2,1)S(1)}, u32[]{:S(2)}, u32[]{:S(2)}) collective-permute-start(bf16[2,10,2,384]{3,2,1,0:T(2,128)(2,1)S(1)} %get-tuple-element.26), channel_id=1, source_target_pairs={{2,0},{4,2},{6,4},{8,6},{10,8},{12,10},{14,12},{16,14},{18,16},{20... | collective-permute-start | bytes 92168 | tf_op jit(solution)/shard_map/ppermute | solution.py:540
  116.4 1.3 %collective-permute-start.34 = (bf16[2,10,16,384]{3,2,1,0:T(8,128)(2,1)S(1)}, bf16[2,10,16,384]{3,2,1,0:T(8,128)(2,1)S(1)}, u32[]{:S(2)}, u32[]{:S(2)}) collective-permute-start(bf16[2,10,16,384]{3,2,1,0:T(8,128)(2,1)S(1)} %update.1.refs_0_), channel_id=1, source_target_pairs={{0,1},{1,0},{2,3},{3,2},{4,5},{5,4},{6,7},{7,6},{8,9},{9,8},{10,11... | collective-permute-start | bytes 737288 | tf_op jit(solution)/shard_map/ppermute | solution.py:538
  117.8 0.1 copy.23.refs_5_
  117.9 1.9 %collective-permute-done.33 = bf16[2,10,2,384]{3,2,1,0:T(2,128)(2,1)S(1)} collective-permute-done((bf16[2,10,2,384]{3,2,1,0:T(2,128)(2,1)S(1)}, bf16[2,10,2,384]{3,2,1,0:T(2,128)(2,1)S(1)}, u32[]{:S(2)}, u32[]{:S(2)}) %collective-permute-start.33) | collective-permute-done | bytes 30752 | tf_op jit(solution)/shard_map/ppermute | solution.py:540
  119.9 1.3 %collective-permute-start.35 = (bf16[2,10,4,384]{3,2,1,0:T(4,128)(2,1)S(1)}, bf16[2,10,4,384]{3,2,1,0:T(4,128)(2,1)S(1)}, u32[]{:S(2)}, u32[]{:S(2)}) collective-permute-start(bf16[2,10,4,384]{3,2,1,0:T(4,128)(2,1)S(1)} %pad_maximum_fusion.3.refs_1_), channel_id=1, source_target_pairs={{0,1},{1,0},{2,3},{3,2},{4,5},{5,4},{6,7},{7,6},{8,9},{9,8},{10,11... | collective-permute-start | bytes 184328 | tf_op jit(solution)/shard_map/ppermute | solution.py:542
  121.3 2.5 %collective-permute-done.35.refs_3_ = bf16[2,10,4,384]{3,2,1,0:T(4,128)(2,1)S(1)} collective-permute-done((bf16[2,10,4,384]{3,2,1,0:T(4,128)(2,1)S(1)}, bf16[2,10,4,384]{3,2,1,0:T(4,128)(2,1)S(1)}, u32[]{:S(2)}, u32[]{:S(2)}) %collective-permute-start.35) | collective-permute-done | bytes 61472 | tf_op jit(solution)/shard_map/ppermute | solution.py:542
  123.8 6.9 %convolutions.1 = bf16[1,5,2,2,16,384]{5,4,3,2,1,0:T(8,128)(2,1)} custom-call(s32[2]{0:T(128)S(1)} %add_convert_fusion.6.ends, bf16[2,10,16,384]{3,2,1,0:T(8,128)(2,1)S(1)} %update.1.refs_0_, bf16[2,10,4,384]{3,2,1,0:T(4,128)(2,1)S(1)} %pad_maximum_fusion.3.refs_1_, bf16[2,10,16,384]{3,2,1,0:T(8,128)(2,1)S(1)} %collective-permute-done.34.refs_2_, ...), custom_call_target="tpu_custom_call" | custom-call | flops 1585446912 | bytes 1048576 | tf_op jit(solution)/shard_map/convolutions/pallas_call | solution.py:461
  (92 shorter events, 2.1 us)
Async XLA Ops:
  0.0 3.0 %copy-start.3 = (bf16[128,128]{1,0:T(8,128)(2,1)S(1)}, bf16[128,128]{1,0:T(8,128)(2,1)}, u32[]{:S(2)}) copy-start(bf16[128,128]{1,0:T(8,128)(2,1)} %constant.197.clone.along_z) | copy-start | bytes 98308
  0.0 3.0 %copy-start = (bf16[384,384]{1,0:T(8,128)(2,1)S(1)}, bf16[384,384]{1,0:T(8,128)(2,1)}, u32[]{:S(2)}) copy-start(bf16[384,384]{1,0:T(8,128)(2,1)} %constant.198.clone.along_y) | copy-start | bytes 884740
  0.0 3.0 %copy-start.2 = (bf16[1,5,2,2,16,384]{5,4,3,2,1,0:T(8,128)(2,1)S(1)}, bf16[1,5,2,2,16,384]{5,4,3,2,1,0:T(8,128)(2,1)}, u32[]{:S(2)}) copy-start(bf16[1,5,2,2,16,384]{5,4,3,2,1,0:T(8,128)(2,1)} %image.1) | copy-start | bytes 737284
  3.1 10.5 %copy-start.9 = (bf16[64,10,3,3,3]{0,4,3,2,1:T(4,128)(2,1)S(1)}, bf16[64,10,3,3,3]{0,4,3,2,1:T(4,128)(2,1)}, u32[]{:S(2)}) copy-start(bf16[64,10,3,3,3]{0,4,3,2,1:T(4,128)(2,1)} %param.19) | copy-start | bytes 103684
  3.7 10.4 %copy-start.10 = (bf16[10,64,3,3,3]{1,4,3,2,0:T(4,128)(2,1)S(1)}, bf16[10,64,3,3,3]{1,4,3,2,0:T(4,128)(2,1)}, u32[]{:S(2)}) copy-start(bf16[10,64,3,3,3]{1,4,3,2,0:T(4,128)(2,1)} %param.21) | copy-start | bytes 103684
  3.8 10.8 %copy-start.12 = (f32[64]{0:T(128)S(1)}, f32[64]{0:T(128)}, u32[]{:S(2)}) copy-start(f32[64]{0:T(128)} %param.20) | copy-start | bytes 772
  3.8 10.9 %copy-start.6 = (s32[1,5,384,256]{3,2,1,0:T(8,128)S(1)}, s32[1,5,384,256]{3,2,1,0:T(8,128)}, u32[]{:S(2)}) copy-start(s32[1,5,384,256]{3,2,1,0:T(8,128)} %param.18) | copy-start | bytes 5898244
  3.8 12.0 %collective-permute-start.16 = (bf16[1,10,16,384]{3,2,1,0:T(8,128)(2,1)S(1)}, bf16[1,10,16,384]{3,2,1,0:T(8,128)(2,1)S(1)}, u32[]{:S(2)}, u32[]{:S(2)}) collective-permute-start(bf16[1,10,16,384]{3,2,1,0:T(8,128)(2,1)S(1)} %get-tuple-element.27.refs_0_), channel_id=1, source_target_pairs={{0,2},{2,0},{4,6},{6,4},{8,10},{10,8},{12,14},{14,12},{16,18},{18,... | collective-permute-start | bytes 368648 | tf_op jit(solution)/shard_map/ppermute | solution.py:101
  3.9 13.1 %collective-permute-start.17 = (bf16[1,10,16,384]{3,2,1,0:T(8,128)(2,1)S(1)}, bf16[1,10,16,384]{3,2,1,0:T(8,128)(2,1)S(1)}, u32[]{:S(2)}, u32[]{:S(2)}) collective-permute-start(bf16[1,10,16,384]{3,2,1,0:T(8,128)(2,1)S(1)} %get-tuple-element.27.refs_0_), channel_id=1, source_target_pairs={{0,8},{2,6},{8,16},{10,2},{16,24},{18,10},{24,28},{26,18},{28,20},... | collective-permute-start | bytes 368648 | tf_op jit(solution)/shard_map/ppermute | solution.py:100
  6.6 24.0 %all-to-all-start = ((bf16[16,2,2,16,384]{4,3,2,1,0:T(8,128)(2,1)}), bf16[16,2,2,16,384]{4,3,2,1,0:T(8,128)(2,1)}, u32[]{:S(2)}, u32[]{:S(2)}) async-start(bf16[16,2,2,16,384]{4,3,2,1,0:T(8,128)(2,1)} %prepare_maps.1.earlier), calls=%async_computation | async-start | bytes 1572864 | tf_op jit(solution)/shard_map/all_to_all | solution.py:523
  11.8 5.2 %collective-permute-start = (bf16[1,10,16,384]{3,2,1,0:T(8,128)(2,1)S(1)}, bf16[1,10,16,384]{3,2,1,0:T(8,128)(2,1)S(1)}, u32[]{:S(2)}, u32[]{:S(2)}) collective-permute-start(bf16[1,10,16,384]{3,2,1,0:T(8,128)(2,1)S(1)} %get-tuple-element.28.refs_0_), channel_id=1, source_target_pairs={{0,2},{2,0},{4,6},{6,4},{8,10},{10,8},{12,14},{14,12},{16,18},{18,... | collective-permute-start | bytes 368648 | tf_op jit(solution)/shard_map/ppermute | solution.py:101
  12.0 14.2 %collective-permute-start.1 = (bf16[1,10,16,384]{3,2,1,0:T(8,128)(2,1)S(1)}, bf16[1,10,16,384]{3,2,1,0:T(8,128)(2,1)S(1)}, u32[]{:S(2)}, u32[]{:S(2)}) collective-permute-start(bf16[1,10,16,384]{3,2,1,0:T(8,128)(2,1)S(1)} %get-tuple-element.28.refs_0_), channel_id=1, source_target_pairs={{0,8},{2,6},{8,16},{10,2},{16,24},{18,10},{24,28},{26,18},{28,20},... | collective-permute-start | bytes 368648 | tf_op jit(solution)/shard_map/ppermute | solution.py:100
  15.8 12.1 %collective-permute-start.18 = (bf16[1,10,16,384]{3,2,1,0:T(8,128)(2,1)S(1)}, bf16[1,10,16,384]{3,2,1,0:T(8,128)(2,1)S(1)}, u32[]{:S(2)}, u32[]{:S(2)}) collective-permute-start(bf16[1,10,16,384]{3,2,1,0:T(8,128)(2,1)S(1)} %collective-permute-done.16.refs_1_), channel_id=1, source_target_pairs={{0,8},{2,6},{8,16},{10,2},{16,24},{18,10},{24,28},{26,18},{28,20},... | collective-permute-start | bytes 368648 | tf_op jit(solution)/shard_map/ppermute | solution.py:108
  17.1 14.8 %collective-permute-start.2 = (bf16[1,10,16,384]{3,2,1,0:T(8,128)(2,1)S(1)}, bf16[1,10,16,384]{3,2,1,0:T(8,128)(2,1)S(1)}, u32[]{:S(2)}, u32[]{:S(2)}) collective-permute-start(bf16[1,10,16,384]{3,2,1,0:T(8,128)(2,1)S(1)} %collective-permute-done.refs_1_), channel_id=1, source_target_pairs={{0,8},{2,6},{8,16},{10,2},{16,24},{18,10},{24,28},{26,18},{28,20},... | collective-permute-start | bytes 368648 | tf_op jit(solution)/shard_map/ppermute | solution.py:108
  28.0 11.2 %collective-permute-start.19 = (bf16[2,10,16,384]{3,2,1,0:T(8,128)(2,1)S(1)}, bf16[2,10,16,384]{3,2,1,0:T(8,128)(2,1)S(1)}, u32[]{:S(2)}, u32[]{:S(2)}) collective-permute-start(bf16[2,10,16,384]{3,2,1,0:T(8,128)(2,1)S(1)} %constant_dynamic-update-slice_fusion.2.refs_2_), channel_id=1, source_target_pairs={{0,8},{2,6},{8,16},{10,2},{16,24},{18,10},{24,28},{26,18},{28,20},... | collective-permute-start | bytes 737288 | tf_op jit(solution)/shard_map/ppermute | solution.py:111
  30.6 23.5 %collective-permute-start.10 = (bf16[16,2,2,16,384]{4,3,2,1,0:T(8,128)(2,1)}, bf16[16,2,2,16,384]{4,3,2,1,0:T(8,128)(2,1)}, u32[]{:S(2)}, u32[]{:S(2)}) collective-permute-start(bf16[16,2,2,16,384]{4,3,2,1,0:T(8,128)(2,1)} %all-to-all-done.refs_10_), channel_id=1, source_target_pairs={{0,1},{1,0},{2,3},{3,2},{4,5},{5,4},{6,7},{7,6},{8,9},{9,8},{10,11... | collective-permute-start | bytes 2359304 | tf_op jit(solution)/shard_map/ppermute | solution.py:527
  31.9 9.9 %collective-permute-start.3 = (bf16[2,10,16,384]{3,2,1,0:T(8,128)(2,1)S(1)}, bf16[2,10,16,384]{3,2,1,0:T(8,128)(2,1)S(1)}, u32[]{:S(2)}, u32[]{:S(2)}) collective-permute-start(bf16[2,10,16,384]{3,2,1,0:T(8,128)(2,1)S(1)} %constant_dynamic-update-slice_fusion.refs_2_), channel_id=1, source_target_pairs={{0,8},{2,6},{8,16},{10,2},{16,24},{18,10},{24,28},{26,18},{28,20},... | collective-permute-start | bytes 737288 | tf_op jit(solution)/shard_map/ppermute | solution.py:111
  39.2 5.4 %collective-permute-start.20 = (bf16[2,10,16,384]{3,2,1,0:T(8,128)(2,1)S(1)}, bf16[2,10,16,384]{3,2,1,0:T(8,128)(2,1)S(1)}, u32[]{:S(2)}, u32[]{:S(2)}) collective-permute-start(bf16[2,10,16,384]{3,2,1,0:T(8,128)(2,1)S(1)} %collective-permute-done.19.refs_3_), channel_id=1, source_target_pairs={{0,8},{2,6},{8,16},{10,2},{16,24},{18,10},{24,28},{26,18},{28,20},... | collective-permute-start | bytes 737288 | tf_op jit(solution)/shard_map/ppermute | solution.py:111
  41.8 5.4 %collective-permute-start.4 = (bf16[2,10,16,384]{3,2,1,0:T(8,128)(2,1)S(1)}, bf16[2,10,16,384]{3,2,1,0:T(8,128)(2,1)S(1)}, u32[]{:S(2)}, u32[]{:S(2)}) collective-permute-start(bf16[2,10,16,384]{3,2,1,0:T(8,128)(2,1)S(1)} %collective-permute-done.3.refs_3_), channel_id=1, source_target_pairs={{0,8},{2,6},{8,16},{10,2},{16,24},{18,10},{24,28},{26,18},{28,20},... | collective-permute-start | bytes 737288 | tf_op jit(solution)/shard_map/ppermute | solution.py:111
  41.8 6.8 %collective-permute-start.22 = (bf16[2,10,16,384]{3,2,1,0:T(8,128)(2,1)S(1)}, bf16[2,10,16,384]{3,2,1,0:T(8,128)(2,1)S(1)}, u32[]{:S(2)}, u32[]{:S(2)}) collective-permute-start(bf16[2,10,16,384]{3,2,1,0:T(8,128)(2,1)S(1)} %constant_dynamic-update-slice_fusion.2.refs_2_), channel_id=1, source_target_pairs={{0,2},{2,0},{4,6},{6,4},{8,10},{10,8},{12,14},{14,12},{16,18},{18,... | collective-permute-start | bytes 737288 | tf_op jit(solution)/shard_map/ppermute | solution.py:113
  44.5 6.5 %collective-permute-start.23 = (bf16[2,10,16,384]{3,2,1,0:T(8,128)(2,1)S(1)}, bf16[2,10,16,384]{3,2,1,0:T(8,128)(2,1)S(1)}, u32[]{:S(2)}, u32[]{:S(2)}) collective-permute-start(bf16[2,10,16,384]{3,2,1,0:T(8,128)(2,1)S(1)} %collective-permute-done.19.refs_3_), channel_id=1, source_target_pairs={{0,2},{2,0},{4,6},{6,4},{8,10},{10,8},{12,14},{14,12},{16,18},{18,... | collective-permute-start | bytes 737288 | tf_op jit(solution)/shard_map/ppermute | solution.py:113
  44.6 5.8 %collective-permute-start.21 = (bf16[1,10,16,384]{3,2,1,0:T(8,128)(2,1)S(1)}, bf16[1,10,16,384]{3,2,1,0:T(8,128)(2,1)S(1)}, u32[]{:S(2)}, u32[]{:S(2)}) collective-permute-start(bf16[1,10,16,384]{3,2,1,0:T(8,128)(2,1)S(1)} %slice.144), channel_id=1, source_target_pairs={{0,8},{2,6},{8,16},{10,2},{16,24},{18,10},{24,28},{26,18},{28,20},... | collective-permute-start | bytes 368648 | tf_op jit(solution)/shard_map/ppermute | solution.py:111
  47.3 6.4 %collective-permute-start.24 = (bf16[2,10,16,384]{3,2,1,0:T(8,128)(2,1)S(1)}, bf16[2,10,16,384]{3,2,1,0:T(8,128)(2,1)}, u32[]{:S(2)}, u32[]{:S(2)}) collective-permute-start(bf16[2,10,16,384]{3,2,1,0:T(8,128)(2,1)S(1)} %collective-permute-done.20.refs_4_), channel_id=1, source_target_pairs={{0,2},{2,0},{4,6},{6,4},{8,10},{10,8},{12,14},{14,12},{16,18},{18,... | collective-permute-start | bytes 737288 | tf_op jit(solution)/shard_map/ppermute | solution.py:113
  48.6 4.5 %collective-permute-start.5 = (bf16[1,10,16,384]{3,2,1,0:T(8,128)(2,1)S(1)}, bf16[1,10,16,384]{3,2,1,0:T(8,128)(2,1)S(1)}, u32[]{:S(2)}, u32[]{:S(2)}) collective-permute-start(bf16[1,10,16,384]{3,2,1,0:T(8,128)(2,1)S(1)} %slice.136), channel_id=1, source_target_pairs={{0,8},{2,6},{8,16},{10,2},{16,24},{18,10},{24,28},{26,18},{28,20},... | collective-permute-start | bytes 368648 | tf_op jit(solution)/shard_map/ppermute | solution.py:111
  50.4 3.1 %collective-permute-start.25 = (bf16[1,10,16,384]{3,2,1,0:T(8,128)(2,1)S(1)}, bf16[1,10,16,384]{3,2,1,0:T(8,128)(2,1)S(1)}, u32[]{:S(2)}, u32[]{:S(2)}) collective-permute-start(bf16[1,10,16,384]{3,2,1,0:T(8,128)(2,1)S(1)} %collective-permute-done.21.refs_5_), channel_id=1, source_target_pairs={{0,2},{2,0},{4,6},{6,4},{8,10},{10,8},{12,14},{14,12},{16,18},{18,... | collective-permute-start | bytes 368648 | tf_op jit(solution)/shard_map/ppermute | solution.py:113
  51.1 15.8 %collective-permute-start.6 = (bf16[2,10,16,384]{3,2,1,0:T(8,128)(2,1)S(1)}, bf16[2,10,16,384]{3,2,1,0:T(8,128)(2,1)S(1)}, u32[]{:S(2)}, u32[]{:S(2)}) collective-permute-start(bf16[2,10,16,384]{3,2,1,0:T(8,128)(2,1)S(1)} %constant_dynamic-update-slice_fusion.refs_2_), channel_id=1, source_target_pairs={{0,2},{2,0},{4,6},{6,4},{8,10},{10,8},{12,14},{14,12},{16,18},{18,... | collective-permute-start | bytes 737288 | tf_op jit(solution)/shard_map/ppermute | solution.py:113
  53.1 13.8 %collective-permute-start.7 = (bf16[2,10,16,384]{3,2,1,0:T(8,128)(2,1)S(1)}, bf16[2,10,16,384]{3,2,1,0:T(8,128)(2,1)S(1)}, u32[]{:S(2)}, u32[]{:S(2)}) collective-permute-start(bf16[2,10,16,384]{3,2,1,0:T(8,128)(2,1)S(1)} %collective-permute-done.3.refs_3_), channel_id=1, source_target_pairs={{0,2},{2,0},{4,6},{6,4},{8,10},{10,8},{12,14},{14,12},{16,18},{18,... | collective-permute-start | bytes 737288 | tf_op jit(solution)/shard_map/ppermute | solution.py:113
  53.6 13.3 %collective-permute-start.8 = (bf16[2,10,16,384]{3,2,1,0:T(8,128)(2,1)S(1)}, bf16[2,10,16,384]{3,2,1,0:T(8,128)(2,1)S(1)}, u32[]{:S(2)}, u32[]{:S(2)}) collective-permute-start(bf16[2,10,16,384]{3,2,1,0:T(8,128)(2,1)S(1)} %collective-permute-done.4.refs_4_), channel_id=1, source_target_pairs={{0,2},{2,0},{4,6},{6,4},{8,10},{10,8},{12,14},{14,12},{16,18},{18,... | collective-permute-start | bytes 737288 | tf_op jit(solution)/shard_map/ppermute | solution.py:113
  53.6 13.3 %collective-permute-start.9 = (bf16[1,10,16,384]{3,2,1,0:T(8,128)(2,1)S(1)}, bf16[1,10,16,384]{3,2,1,0:T(8,128)(2,1)S(1)}, u32[]{:S(2)}, u32[]{:S(2)}) collective-permute-start(bf16[1,10,16,384]{3,2,1,0:T(8,128)(2,1)S(1)} %collective-permute-done.5.refs_5_), channel_id=1, source_target_pairs={{0,2},{2,0},{4,6},{6,4},{8,10},{10,8},{12,14},{14,12},{16,18},{18,... | collective-permute-start | bytes 368648 | tf_op jit(solution)/shard_map/ppermute | solution.py:113
  66.8 14.0 %copy-start.7 = (bf16[7,10,16,384]{3,2,1,0:T(8,128)(2,1)S(1)}, bf16[7,10,16,384]{3,2,1,0:T(8,128)(2,1)}, u32[]{:S(2)}) copy-start(bf16[7,10,16,384]{3,2,1,0:T(8,128)(2,1)} %get-tuple-element.23) | copy-start | bytes 2580484
  66.8 14.0 %collective-permute-start.26 = (bf16[7,10,16,384]{3,2,1,0:T(8,128)(2,1)}, bf16[7,10,16,384]{3,2,1,0:T(8,128)(2,1)S(1)}, u32[]{:S(2)}, u32[]{:S(2)}) collective-permute-start(bf16[7,10,16,384]{3,2,1,0:T(8,128)(2,1)} %get-tuple-element.24), channel_id=1, source_target_pairs={{0,2},{2,0},{4,6},{6,4},{8,10},{10,8},{12,14},{14,12},{16,18},{18,... | collective-permute-start | bytes 2580488 | tf_op jit(solution)/shard_map/ppermute | solution.py:122
  66.9 0.7 copy-start.11
  80.4 5.4 %copy-start.8 = (bf16[7,10,16,384]{3,2,1,0:T(8,128)(2,1)S(1)}, bf16[7,10,16,384]{3,2,1,0:T(8,128)(2,1)}, u32[]{:S(2)}) copy-start(bf16[7,10,16,384]{3,2,1,0:T(8,128)(2,1)} %get-tuple-element.18) | copy-start | bytes 2580484
  80.4 2.7 %collective-permute-start.11 = (bf16[7,10,16,384]{3,2,1,0:T(8,128)(2,1)}, bf16[7,10,16,384]{3,2,1,0:T(8,128)(2,1)S(1)}, u32[]{:S(2)}, u32[]{:S(2)}) collective-permute-start(bf16[7,10,16,384]{3,2,1,0:T(8,128)(2,1)} %get-tuple-element.19), channel_id=1, source_target_pairs={{0,2},{2,0},{4,6},{6,4},{8,10},{10,8},{12,14},{14,12},{16,18},{18,... | collective-permute-start | bytes 2580488 | tf_op jit(solution)/shard_map/ppermute | solution.py:122
  80.9 5.0 %collective-permute-start.27 = (bf16[1,10,16,384]{3,2,1,0:T(8,128)(2,1)S(1)}, bf16[1,10,16,384]{3,2,1,0:T(8,128)(2,1)S(1)}, u32[]{:S(2)}, u32[]{:S(2)}) collective-permute-start(bf16[1,10,16,384]{3,2,1,0:T(8,128)(2,1)S(1)} %add_convert_fusion.4), channel_id=1, source_target_pairs={{0,8},{2,6},{8,16},{10,2},{16,24},{18,10},{24,28},{26,18},{28,20},... | collective-permute-start | bytes 368648 | tf_op jit(solution)/shard_map/ppermute | solution.py:137
  84.0 4.5 %collective-permute-start.12 = (bf16[1,10,16,384]{3,2,1,0:T(8,128)(2,1)S(1)}, bf16[1,10,16,384]{3,2,1,0:T(8,128)(2,1)S(1)}, u32[]{:S(2)}, u32[]{:S(2)}) collective-permute-start(bf16[1,10,16,384]{3,2,1,0:T(8,128)(2,1)S(1)} %add_convert_fusion.5), channel_id=1, source_target_pairs={{0,8},{2,6},{8,16},{10,2},{16,24},{18,10},{24,28},{26,18},{28,20},... | collective-permute-start | bytes 368648 | tf_op jit(solution)/shard_map/ppermute | solution.py:137
  86.0 5.4 %collective-permute-start.28 = (bf16[2,10,16,384]{3,2,1,0:T(8,128)(2,1)S(1)}, bf16[2,10,16,384]{3,2,1,0:T(8,128)(2,1)S(1)}, u32[]{:S(2)}, u32[]{:S(2)}) collective-permute-start(bf16[2,10,16,384]{3,2,1,0:T(8,128)(2,1)S(1)} %pad_maximum_fusion.2), channel_id=1, source_target_pairs={{0,8},{2,6},{8,16},{10,2},{16,24},{18,10},{24,28},{26,18},{28,20},... | collective-permute-start | bytes 737288 | tf_op jit(solution)/shard_map/ppermute | solution.py:137
  88.5 5.5 %collective-permute-start.13 = (bf16[2,10,16,384]{3,2,1,0:T(8,128)(2,1)S(1)}, bf16[2,10,16,384]{3,2,1,0:T(8,128)(2,1)S(1)}, u32[]{:S(2)}, u32[]{:S(2)}) collective-permute-start(bf16[2,10,16,384]{3,2,1,0:T(8,128)(2,1)S(1)} %pad_maximum_fusion.1), channel_id=1, source_target_pairs={{0,8},{2,6},{8,16},{10,2},{16,24},{18,10},{24,28},{26,18},{28,20},... | collective-permute-start | bytes 737288 | tf_op jit(solution)/shard_map/ppermute | solution.py:137
  91.5 5.4 %collective-permute-start.29 = (bf16[2,10,16,384]{3,2,1,0:T(8,128)(2,1)S(1)}, bf16[2,10,16,384]{3,2,1,0:T(8,128)(2,1)S(1)}, u32[]{:S(2)}, u32[]{:S(2)}) collective-permute-start(bf16[2,10,16,384]{3,2,1,0:T(8,128)(2,1)S(1)} %add_convert_fusion.1), channel_id=1, source_target_pairs={{0,8},{2,6},{8,16},{10,2},{16,24},{18,10},{24,28},{26,18},{28,20},... | collective-permute-start | bytes 737288 | tf_op jit(solution)/shard_map/ppermute | solution.py:137
  94.1 5.4 %collective-permute-start.14 = (bf16[2,10,16,384]{3,2,1,0:T(8,128)(2,1)S(1)}, bf16[2,10,16,384]{3,2,1,0:T(8,128)(2,1)S(1)}, u32[]{:S(2)}, u32[]{:S(2)}) collective-permute-start(bf16[2,10,16,384]{3,2,1,0:T(8,128)(2,1)S(1)} %add_convert_fusion.3), channel_id=1, source_target_pairs={{0,8},{2,6},{8,16},{10,2},{16,24},{18,10},{24,28},{26,18},{28,20},... | collective-permute-start | bytes 737288 | tf_op jit(solution)/shard_map/ppermute | solution.py:137
  97.0 5.1 %collective-permute-start.30 = (bf16[2,10,16,384]{3,2,1,0:T(8,128)(2,1)S(1)}, bf16[2,10,16,384]{3,2,1,0:T(8,128)(2,1)S(1)}, u32[]{:S(2)}, u32[]{:S(2)}) collective-permute-start(bf16[2,10,16,384]{3,2,1,0:T(8,128)(2,1)S(1)} %add_convert_fusion), channel_id=1, source_target_pairs={{0,8},{2,6},{8,16},{10,2},{16,24},{18,10},{24,28},{26,18},{28,20},... | collective-permute-start | bytes 737288 | tf_op jit(solution)/shard_map/ppermute | solution.py:137
  99.6 5.4 %collective-permute-start.15 = (bf16[2,10,16,384]{3,2,1,0:T(8,128)(2,1)S(1)}, bf16[2,10,16,384]{3,2,1,0:T(8,128)(2,1)S(1)}, u32[]{:S(2)}, u32[]{:S(2)}) collective-permute-start(bf16[2,10,16,384]{3,2,1,0:T(8,128)(2,1)S(1)} %add_convert_fusion.2), channel_id=1, source_target_pairs={{0,8},{2,6},{8,16},{10,2},{16,24},{18,10},{24,28},{26,18},{28,20},... | collective-permute-start | bytes 737288 | tf_op jit(solution)/shard_map/ppermute | solution.py:137
  102.1 7.6 %copy-start.1 = (bf16[384,384]{1,0:T(8,128)(2,1)S(1)}, bf16[384,384]{1,0:T(8,128)(2,1)}, u32[]{:S(2)}) copy-start(bf16[384,384]{1,0:T(8,128)(2,1)} %constant.200.clone.along_y) | copy-start | bytes 884740
  102.1 7.5 %copy-start.4 = (bf16[128,128]{1,0:T(8,128)(2,1)S(1)}, bf16[128,128]{1,0:T(8,128)(2,1)}, u32[]{:S(2)}) copy-start(bf16[128,128]{1,0:T(8,128)(2,1)} %constant.199.clone.along_z) | copy-start | bytes 98308
  105.1 18.7 %copy-start.5 = (f32[10]{0:T(128)S(1)}, f32[10]{0:T(128)}, u32[]{:S(2)}) copy-start(f32[10]{0:T(128)} %refs_7_.1) | copy-start | bytes 124
  105.1 4.5 %collective-permute-start.31 = (bf16[2,10,16,384]{3,2,1,0:T(8,128)(2,1)S(1)}, bf16[2,10,16,384]{3,2,1,0:T(8,128)(2,1)S(1)}, u32[]{:S(2)}, u32[]{:S(2)}) collective-permute-start(bf16[2,10,16,384]{3,2,1,0:T(8,128)(2,1)S(1)} %fusion.5), channel_id=1, source_target_pairs={{0,2},{2,0},{4,6},{6,4},{8,10},{10,8},{12,14},{14,12},{16,18},{18,... | collective-permute-start | bytes 737288 | tf_op jit(solution)/shard_map/ppermute | solution.py:535
  110.4 7.5 %collective-permute-start.32 = (bf16[2,10,2,384]{3,2,1,0:T(2,128)(2,1)S(1)}, bf16[2,10,2,384]{3,2,1,0:T(2,128)(2,1)S(1)}, u32[]{:S(2)}, u32[]{:S(2)}) collective-permute-start(bf16[2,10,2,384]{3,2,1,0:T(2,128)(2,1)S(1)} %get-tuple-element.25), channel_id=1, source_target_pairs={{0,2},{2,4},{4,6},{6,8},{8,10},{10,12},{12,14},{14,16},{16,18},{18... | collective-permute-start | bytes 92168 | tf_op jit(solution)/shard_map/ppermute | solution.py:540
  114.3 5.5 %collective-permute-start.33 = (bf16[2,10,2,384]{3,2,1,0:T(2,128)(2,1)S(1)}, bf16[2,10,2,384]{3,2,1,0:T(2,128)(2,1)S(1)}, u32[]{:S(2)}, u32[]{:S(2)}) collective-permute-start(bf16[2,10,2,384]{3,2,1,0:T(2,128)(2,1)S(1)} %get-tuple-element.26), channel_id=1, source_target_pairs={{2,0},{4,2},{6,4},{8,6},{10,8},{12,10},{14,12},{16,14},{18,16},{20... | collective-permute-start | bytes 92168 | tf_op jit(solution)/shard_map/ppermute | solution.py:540
  116.4 7.4 %collective-permute-start.34 = (bf16[2,10,16,384]{3,2,1,0:T(8,128)(2,1)S(1)}, bf16[2,10,16,384]{3,2,1,0:T(8,128)(2,1)S(1)}, u32[]{:S(2)}, u32[]{:S(2)}) collective-permute-start(bf16[2,10,16,384]{3,2,1,0:T(8,128)(2,1)S(1)} %update.1.refs_0_), channel_id=1, source_target_pairs={{0,1},{1,0},{2,3},{3,2},{4,5},{5,4},{6,7},{7,6},{8,9},{9,8},{10,11... | collective-permute-start | bytes 737288 | tf_op jit(solution)/shard_map/ppermute | solution.py:538
  119.9 3.9 %collective-permute-start.35 = (bf16[2,10,4,384]{3,2,1,0:T(4,128)(2,1)S(1)}, bf16[2,10,4,384]{3,2,1,0:T(4,128)(2,1)S(1)}, u32[]{:S(2)}, u32[]{:S(2)}) collective-permute-start(bf16[2,10,4,384]{3,2,1,0:T(4,128)(2,1)S(1)} %pad_maximum_fusion.3.refs_1_), channel_id=1, source_target_pairs={{0,1},{1,0},{2,3},{3,2},{4,5},{5,4},{6,7},{7,6},{8,9},{9,8},{10,11... | collective-permute-start | bytes 184328 | tf_op jit(solution)/shard_map/ppermute | solution.py:542

commit v7 on v6

--- a/solution.py
+++ b/solution.py
@@ -298,7 +298,7 @@
             ],
         ),
         out_shape=[jax.ShapeDtypeStruct((m, channels, rows, ny), BF16) for m in (2, far, far)],
-        compiler_params=pltpu.CompilerParams(vmem_limit_bytes=52 * 2**20),
+        compiler_params=pltpu.CompilerParams(vmem_limit_bytes=49 * 2**20),
         cost_estimate=pl.CostEstimate(flops=flops, bytes_accessed=8 * 2**20, transcendentals=0),
         name="gradient",
     )(where, *images, *[a for a, _ in maps], measured, sampling, tables)

time: 132 us -> 137 us (1.038)
  local copies, waits for them, and re-layouts: 1.77 us -> 5.37 us
  waiting for transfers between devices: 35.2 us -> 32.9 us
  other arithmetic: 3.48 us -> 5.02 us
    unnamed x28 -> x38, local copies, waits for them, and re-layouts: 0.78 us -> 3.72 us
    ppermute x2, waiting for transfers between devices: 7.92 us -> 6.34 us  [__init__(): self.first = lax.ppermute(mine, SLAB, ring.perm())]
    convert_element_type x1, other arithmetic: 1.14 us -> 2.7 us  [paired(): mask = sampling.astype(BF16)]
  transfers between devices with their start and end apart: 37 -> 37, of which waited for: 19 -> 19; matrix products, arithmetic and copies ran while one was open for 3% -> 5% of each run, Pallas kernels for 19% -> 19%
where the time goes in v7:
time: 137 us; the launch traced here: 135 us
  starting transfers between devices  54.4 us (40%)
  Pallas kernels  36.8 us (27%)
  waiting for transfers between devices  32.9 us (24%)
  local copies, waits for them, and re-layouts  5.37 us (4%)
  other arithmetic  5.02 us (4%)
    pallas_call x2, Pallas kernels, gradient(): pl.pallas_call(functools.partial(gradient_kernel, len(images), n), grid_s...  25.5 us
    ppermute x8, starting transfers between devices, step(): self.held = lax.ppermute(total.astype(BF16), SLAB, self.ring.perm())  14.3 us
    ppermute x6, waiting for transfers between devices, step(): lax.ppermute(after(held, *earlier) if earlier else held, SLAB, self.ring....  10.2 us
    ppermute x8, waiting for transfers between devices, step(): self.held = lax.ppermute(total.astype(BF16), SLAB, self.ring.perm())  7.68 us
    ppermute x6, starting transfers between devices, step(): lax.ppermute(after(held, *earlier) if earlier else held, SLAB, self.ring....  7.6 us
    pallas_call x1, Pallas kernels, convolutions(): pl.pallas_call(convolution_kernel, in_specs=[smem] + [vmem] * (len(parts)...  6.99 us
    ppermute x8, starting transfers between devices, step(): self.other.append(lax.ppermute(self.held, SLAB, self.ring.siblings()))  6.37 us
    ppermute x2, waiting for transfers between devices, __init__(): self.first = lax.ppermute(mine, SLAB, ring.perm())  6.34 us
  transfers between devices with their start and end apart: 37, of which 19 were waited for; matrix products, arithmetic and copies ran while one was open for 5% of the time, Pallas kernels for 19%

profile of v7, /device:TPU:1, one launch (start us, length us, event | category | flops | bytes accessed | tf_op | source)
XLA Modules:
  0.0 135.0 jit_solution(15386354009306717677)
XLA Ops:
  0.0 3.0 %prepare_maps.1.earlier = bf16[16,2,2,16,384]{4,3,2,1,0:T(8,128)(2,1)} custom-call(s32[1]{0:T(128)} %bitcast.2.which, bf16[16,2,2,2,16,384]{5,4,3,2,1,0:T(8,128)(2,1)} %bitcast.69, bf16[128,128]{1,0:T(8,128)(2,1)} %constant.197.clone.along_z, bf16[384,384]{1,0:T(8,128)(2,1)} %constant.198.clone.along_y), custom_call_target="tpu_custom_call" | custom-call | tf_op jit(solution)/shard_map/prepare_maps/pallas_call | solution.py:359
  3.1 0.7 prepare_image.1.image
  3.8 0.1 collective-permute-start.16
  3.9 2.7 %collective-permute-start.17 = (bf16[1,10,16,384]{3,2,1,0:T(8,128)(2,1)S(1)}, bf16[1,10,16,384]{3,2,1,0:T(8,128)(2,1)S(1)}, u32[]{:S(2)}, u32[]{:S(2)}) collective-permute-start(bf16[1,10,16,384]{3,2,1,0:T(8,128)(2,1)S(1)} %get-tuple-element.27.refs_0_), channel_id=1, source_target_pairs={{0,8},{2,6},{8,16},{10,2},{16,24},{18,10},{24,28},{26,18},{28,20},... | collective-permute-start | bytes 368648 | tf_op jit(solution)/shard_map/ppermute | solution.py:100
  6.6 5.2 %all-to-all-start = ((bf16[16,2,2,16,384]{4,3,2,1,0:T(8,128)(2,1)}), bf16[16,2,2,16,384]{4,3,2,1,0:T(8,128)(2,1)S(1)}, u32[]{:S(2)}, u32[]{:S(2)}) async-start(bf16[16,2,2,16,384]{4,3,2,1,0:T(8,128)(2,1)} %prepare_maps.1.earlier), calls=%async_computation | async-start | bytes 1572864 | tf_op jit(solution)/shard_map/all_to_all | solution.py:523
  11.8 0.2 collective-permute-start
  12.0 1.6 %collective-permute-start.1 = (bf16[1,10,16,384]{3,2,1,0:T(8,128)(2,1)S(1)}, bf16[1,10,16,384]{3,2,1,0:T(8,128)(2,1)S(1)}, u32[]{:S(2)}, u32[]{:S(2)}) collective-permute-start(bf16[1,10,16,384]{3,2,1,0:T(8,128)(2,1)S(1)} %get-tuple-element.28.refs_0_), channel_id=1, source_target_pairs={{0,8},{2,6},{8,16},{10,2},{16,24},{18,10},{24,28},{26,18},{28,20},... | collective-permute-start | bytes 368648 | tf_op jit(solution)/shard_map/ppermute | solution.py:100
  14.3 0.1 reshape.28
  14.7 2.7 %convert_element_type.117.refs_13_ = bf16[1,5,384,256]{3,2,1,0:T(8,128)(2,1)} convert(s32[1,5,384,256]{3,2,1,0:T(8,128)} %param.18) | non-fusion elementwise | flops 491520 | bytes 2949120 | tf_op jit(solution)/shard_map/convert_element_type | solution.py:516
  17.4 1.2 collective-permute-start.18
  18.6 1.2 collective-permute-start.2
  19.9 6.3 %collective-permute-done.1 = bf16[1,10,16,384]{3,2,1,0:T(8,128)(2,1)S(1)} collective-permute-done((bf16[1,10,16,384]{3,2,1,0:T(8,128)(2,1)S(1)}, bf16[1,10,16,384]{3,2,1,0:T(8,128)(2,1)S(1)}, u32[]{:S(2)}, u32[]{:S(2)}) %collective-permute-start.1) | collective-permute-done | bytes 122912 | tf_op jit(solution)/shard_map/ppermute | solution.py:100
  26.2 1.6 %collective-permute-done.18 = bf16[1,10,16,384]{3,2,1,0:T(8,128)(2,1)S(1)} collective-permute-done((bf16[1,10,16,384]{3,2,1,0:T(8,128)(2,1)S(1)}, bf16[1,10,16,384]{3,2,1,0:T(8,128)(2,1)S(1)}, u32[]{:S(2)}, u32[]{:S(2)}) %collective-permute-start.18) | collective-permute-done | bytes 122912 | tf_op jit(solution)/shard_map/ppermute | solution.py:108
  27.9 1.4 %collective-permute-start.19 = (bf16[2,10,16,384]{3,2,1,0:T(8,128)(2,1)S(1)}, bf16[2,10,16,384]{3,2,1,0:T(8,128)(2,1)}, u32[]{:S(2)}, u32[]{:S(2)}) collective-permute-start(bf16[2,10,16,384]{3,2,1,0:T(8,128)(2,1)S(1)} %constant_dynamic-update-slice_fusion.2.refs_2_), channel_id=1, source_target_pairs={{0,8},{2,6},{8,16},{10,2},{16,24},{18,10},{24,28},{26,18},{28,20},... | collective-permute-start | bytes 737288 | tf_op jit(solution)/shard_map/ppermute | solution.py:111
  29.3 1.2 all-to-all-done.refs_10_
  30.5 1.2 collective-permute-start.10
  31.7 4.4 %collective-permute-start.3 = (bf16[2,10,16,384]{3,2,1,0:T(8,128)(2,1)S(1)}, bf16[2,10,16,384]{3,2,1,0:T(8,128)(2,1)S(1)}, u32[]{:S(2)}, u32[]{:S(2)}) collective-permute-start(bf16[2,10,16,384]{3,2,1,0:T(8,128)(2,1)S(1)} %constant_dynamic-update-slice_fusion.refs_2_), channel_id=1, source_target_pairs={{0,8},{2,6},{8,16},{10,2},{16,24},{18,10},{24,28},{26,18},{28,20},... | collective-permute-start | bytes 737288 | tf_op jit(solution)/shard_map/ppermute | solution.py:111
  36.1 3.0 %collective-permute-done.19.refs_3_ = bf16[2,10,16,384]{3,2,1,0:T(8,128)(2,1)} collective-permute-done((bf16[2,10,16,384]{3,2,1,0:T(8,128)(2,1)S(1)}, bf16[2,10,16,384]{3,2,1,0:T(8,128)(2,1)}, u32[]{:S(2)}, u32[]{:S(2)}) %collective-permute-start.19) | collective-permute-done | bytes 245792 | tf_op jit(solution)/shard_map/ppermute | solution.py:111
  39.1 2.6 %collective-permute-done.3.refs_3_ = bf16[2,10,16,384]{3,2,1,0:T(8,128)(2,1)S(1)} collective-permute-done((bf16[2,10,16,384]{3,2,1,0:T(8,128)(2,1)S(1)}, bf16[2,10,16,384]{3,2,1,0:T(8,128)(2,1)S(1)}, u32[]{:S(2)}, u32[]{:S(2)}) %collective-permute-start.3) | collective-permute-done | bytes 245792 | tf_op jit(solution)/shard_map/ppermute | solution.py:111
  41.7 2.8 %collective-permute-start.22 = (bf16[2,10,16,384]{3,2,1,0:T(8,128)(2,1)S(1)}, bf16[2,10,16,384]{3,2,1,0:T(8,128)(2,1)S(1)}, u32[]{:S(2)}, u32[]{:S(2)}) collective-permute-start(bf16[2,10,16,384]{3,2,1,0:T(8,128)(2,1)S(1)} %constant_dynamic-update-slice_fusion.2.refs_2_), channel_id=1, source_target_pairs={{0,2},{2,0},{4,6},{6,4},{8,10},{10,8},{12,14},{14,12},{16,18},{18,... | collective-permute-start | bytes 737288 | tf_op jit(solution)/shard_map/ppermute | solution.py:113
  44.7 2.5 %collective-permute-done.4.refs_4_ = bf16[2,10,16,384]{3,2,1,0:T(8,128)(2,1)S(1)} collective-permute-done((bf16[2,10,16,384]{3,2,1,0:T(8,128)(2,1)S(1)}, bf16[2,10,16,384]{3,2,1,0:T(8,128)(2,1)S(1)}, u32[]{:S(2)}, u32[]{:S(2)}) %collective-permute-start.4) | collective-permute-done | bytes 245792 | tf_op jit(solution)/shard_map/ppermute | solution.py:111
  47.3 1.7 %collective-permute-start.24 = (bf16[2,10,16,384]{3,2,1,0:T(8,128)(2,1)S(1)}, bf16[2,10,16,384]{3,2,1,0:T(8,128)(2,1)}, u32[]{:S(2)}, u32[]{:S(2)}) collective-permute-start(bf16[2,10,16,384]{3,2,1,0:T(8,128)(2,1)S(1)} %collective-permute-done.20.refs_4_), channel_id=1, source_target_pairs={{0,2},{2,0},{4,6},{6,4},{8,10},{10,8},{12,14},{14,12},{16,18},{18,... | collective-permute-start | bytes 737288 | tf_op jit(solution)/shard_map/ppermute | solution.py:113
  48.9 0.7 slice.136
  49.6 0.7 copy-done.5
  50.3 1.7 %collective-permute-start.5 = (bf16[1,10,16,384]{3,2,1,0:T(8,128)(2,1)}, bf16[1,10,16,384]{3,2,1,0:T(8,128)(2,1)}, u32[]{:S(2)}, u32[]{:S(2)}) collective-permute-start(bf16[1,10,16,384]{3,2,1,0:T(8,128)(2,1)} %slice.136), channel_id=1, source_target_pairs={{0,8},{2,6},{8,16},{10,2},{16,24},{18,10},{24,28},{26,18},{28,20},... | collective-permute-start | bytes 368648 | tf_op jit(solution)/shard_map/ppermute | solution.py:111
  52.2 0.5 collective-permute-start.6
  52.7 1.9 %collective-permute-done.5.refs_5_ = bf16[1,10,16,384]{3,2,1,0:T(8,128)(2,1)} collective-permute-done((bf16[1,10,16,384]{3,2,1,0:T(8,128)(2,1)}, bf16[1,10,16,384]{3,2,1,0:T(8,128)(2,1)}, u32[]{:S(2)}, u32[]{:S(2)}) %collective-permute-start.5) | collective-permute-done | bytes 122912 | tf_op jit(solution)/shard_map/ppermute | solution.py:111
  54.7 0.8 collective-permute-start.7
  55.5 0.5 collective-permute-start.9
  56.0 0.9 copy-done.6
  57.0 0.9 copy-done.10
  57.9 1.1 copy-done.12
  59.0 12.8 %gradient.3 = (bf16[2,10,16,384]{3,2,1,0:T(8,128)(2,1)S(1)}, bf16[7,10,16,384]{3,2,1,0:T(8,128)(2,1)}, bf16[7,10,16,384]{3,2,1,0:T(8,128)(2,1)}) custom-call(s32[33]{0:T(128)S(1)} %concatenate.35.slabs, bf16[1,10,16,384]{3,2,1,0:T(8,128)(2,1)S(1)} %get-tuple-element.27.refs_0_, bf16[1,10,16,384]{3,2,1,0:T(8,128)(2,1)S(1)} %copy-done.10, ...), custom_call_target="tpu_custom_call" | custom-call | flops 10066329600 | bytes 8388608 | tf_op jit(solution)/shard_map/gradient/pallas_call | solution.py:278
  71.7 0.1 collective-permute-start.26
  71.9 12.7 %gradient.2 = (bf16[2,10,16,384]{3,2,1,0:T(8,128)(2,1)S(1)}, bf16[7,10,16,384]{3,2,1,0:T(8,128)(2,1)}, bf16[7,10,16,384]{3,2,1,0:T(8,128)(2,1)}) custom-call(s32[33]{0:T(128)S(1)} %concatenate.35.slabs, bf16[1,10,16,384]{3,2,1,0:T(8,128)(2,1)S(1)} %get-tuple-element.28.refs_0_, bf16[1,10,16,384]{3,2,1,0:T(8,128)(2,1)S(1)} %copy-done.8, ...), custom_call_target="tpu_custom_call" | custom-call | flops 10066329600 | bytes 8388608 | tf_op jit(solution)/shard_map/gradient/pallas_call | solution.py:278
  84.6 0.4 collective-permute-start.11
  85.0 1.8 %collective-permute-start.27 = (bf16[1,10,16,384]{3,2,1,0:T(8,128)(2,1)S(1)}, bf16[1,10,16,384]{3,2,1,0:T(8,128)(2,1)S(1)}, u32[]{:S(2)}, u32[]{:S(2)}) collective-permute-start(bf16[1,10,16,384]{3,2,1,0:T(8,128)(2,1)S(1)} %add_convert_fusion.4), channel_id=1, source_target_pairs={{0,8},{2,6},{8,16},{10,2},{16,24},{18,10},{24,28},{26,18},{28,20},... | collective-permute-start | bytes 368648 | tf_op jit(solution)/shard_map/ppermute | solution.py:137
  86.9 0.3 collective-permute-done.11
  87.2 0.9 add_convert_fusion.5
  88.2 1.8 %collective-permute-start.12 = (bf16[1,10,16,384]{3,2,1,0:T(8,128)(2,1)S(1)}, bf16[1,10,16,384]{3,2,1,0:T(8,128)(2,1)S(1)}, u32[]{:S(2)}, u32[]{:S(2)}) collective-permute-start(bf16[1,10,16,384]{3,2,1,0:T(8,128)(2,1)S(1)} %add_convert_fusion.5), channel_id=1, source_target_pairs={{0,8},{2,6},{8,16},{10,2},{16,24},{18,10},{24,28},{26,18},{28,20},... | collective-permute-start | bytes 368648 | tf_op jit(solution)/shard_map/ppermute | solution.py:137
  90.1 1.8 %collective-permute-start.28 = (bf16[2,10,16,384]{3,2,1,0:T(8,128)(2,1)S(1)}, bf16[2,10,16,384]{3,2,1,0:T(8,128)(2,1)S(1)}, u32[]{:S(2)}, u32[]{:S(2)}) collective-permute-start(bf16[2,10,16,384]{3,2,1,0:T(8,128)(2,1)S(1)} %pad_maximum_fusion.2), channel_id=1, source_target_pairs={{0,8},{2,6},{8,16},{10,2},{16,24},{18,10},{24,28},{26,18},{28,20},... | collective-permute-start | bytes 737288 | tf_op jit(solution)/shard_map/ppermute | solution.py:137
  91.9 0.4 collective-permute-done.12
  92.4 1.7 %collective-permute-start.13 = (bf16[2,10,16,384]{3,2,1,0:T(8,128)(2,1)S(1)}, bf16[2,10,16,384]{3,2,1,0:T(8,128)(2,1)S(1)}, u32[]{:S(2)}, u32[]{:S(2)}) collective-permute-start(bf16[2,10,16,384]{3,2,1,0:T(8,128)(2,1)S(1)} %pad_maximum_fusion.1), channel_id=1, source_target_pairs={{0,8},{2,6},{8,16},{10,2},{16,24},{18,10},{24,28},{26,18},{28,20},... | collective-permute-start | bytes 737288 | tf_op jit(solution)/shard_map/ppermute | solution.py:137
  94.1 1.4 %collective-permute-done.28 = bf16[2,10,16,384]{3,2,1,0:T(8,128)(2,1)S(1)} collective-permute-done((bf16[2,10,16,384]{3,2,1,0:T(8,128)(2,1)S(1)}, bf16[2,10,16,384]{3,2,1,0:T(8,128)(2,1)S(1)}, u32[]{:S(2)}, u32[]{:S(2)}) %collective-permute-start.28) | collective-permute-done | bytes 245792 | tf_op jit(solution)/shard_map/ppermute | solution.py:137
  95.6 1.8 %collective-permute-start.29 = (bf16[2,10,16,384]{3,2,1,0:T(8,128)(2,1)S(1)}, bf16[2,10,16,384]{3,2,1,0:T(8,128)(2,1)S(1)}, u32[]{:S(2)}, u32[]{:S(2)}) collective-permute-start(bf16[2,10,16,384]{3,2,1,0:T(8,128)(2,1)S(1)} %add_convert_fusion.1), channel_id=1, source_target_pairs={{0,8},{2,6},{8,16},{10,2},{16,24},{18,10},{24,28},{26,18},{28,20},... | collective-permute-start | bytes 737288 | tf_op jit(solution)/shard_map/ppermute | solution.py:137
  97.4 0.7 collective-permute-done.13
  98.2 1.8 %collective-permute-start.14 = (bf16[2,10,16,384]{3,2,1,0:T(8,128)(2,1)S(1)}, bf16[2,10,16,384]{3,2,1,0:T(8,128)(2,1)S(1)}, u32[]{:S(2)}, u32[]{:S(2)}) collective-permute-start(bf16[2,10,16,384]{3,2,1,0:T(8,128)(2,1)S(1)} %add_convert_fusion.3), channel_id=1, source_target_pairs={{0,8},{2,6},{8,16},{10,2},{16,24},{18,10},{24,28},{26,18},{28,20},... | collective-permute-start | bytes 737288 | tf_op jit(solution)/shard_map/ppermute | solution.py:137
  100.0 1.0 collective-permute-done.29
  101.1 1.8 %collective-permute-start.30 = (bf16[2,10,16,384]{3,2,1,0:T(8,128)(2,1)S(1)}, bf16[2,10,16,384]{3,2,1,0:T(8,128)(2,1)S(1)}, u32[]{:S(2)}, u32[]{:S(2)}) collective-permute-start(bf16[2,10,16,384]{3,2,1,0:T(8,128)(2,1)S(1)} %add_convert_fusion), channel_id=1, source_target_pairs={{0,8},{2,6},{8,16},{10,2},{16,24},{18,10},{24,28},{26,18},{28,20},... | collective-permute-start | bytes 737288 | tf_op jit(solution)/shard_map/ppermute | solution.py:137
  102.9 0.7 collective-permute-done.14
  103.7 1.8 %collective-permute-start.15 = (bf16[2,10,16,384]{3,2,1,0:T(8,128)(2,1)S(1)}, bf16[2,10,16,384]{3,2,1,0:T(8,128)(2,1)S(1)}, u32[]{:S(2)}, u32[]{:S(2)}) collective-permute-start(bf16[2,10,16,384]{3,2,1,0:T(8,128)(2,1)S(1)} %add_convert_fusion.2), channel_id=1, source_target_pairs={{0,8},{2,6},{8,16},{10,2},{16,24},{18,10},{24,28},{26,18},{28,20},... | collective-permute-start | bytes 737288 | tf_op jit(solution)/shard_map/ppermute | solution.py:137
  105.5 1.0 collective-permute-done.30
  106.6 2.5 %collective-permute-done.15 = bf16[2,10,16,384]{3,2,1,0:T(8,128)(2,1)S(1)} collective-permute-done((bf16[2,10,16,384]{3,2,1,0:T(8,128)(2,1)S(1)}, bf16[2,10,16,384]{3,2,1,0:T(8,128)(2,1)S(1)}, u32[]{:S(2)}, u32[]{:S(2)}) %collective-permute-start.15) | collective-permute-done | bytes 245792 | tf_op jit(solution)/shard_map/ppermute | solution.py:137
  109.2 3.5 %collective-permute-start.31 = (bf16[2,10,16,384]{3,2,1,0:T(8,128)(2,1)S(1)}, bf16[2,10,16,384]{3,2,1,0:T(8,128)(2,1)S(1)}, u32[]{:S(2)}, u32[]{:S(2)}) collective-permute-start(bf16[2,10,16,384]{3,2,1,0:T(8,128)(2,1)S(1)} %fusion.5), channel_id=1, source_target_pairs={{0,2},{2,0},{4,6},{6,4},{8,10},{10,8},{12,14},{14,12},{16,18},{18,... | collective-permute-start | bytes 737288 | tf_op jit(solution)/shard_map/ppermute | solution.py:535
  112.7 1.1 collective-permute-done.31.received
  113.8 0.7 update.1.refs_0_
  114.6 3.9 %collective-permute-start.32 = (bf16[2,10,2,384]{3,2,1,0:T(2,128)(2,1)S(1)}, bf16[2,10,2,384]{3,2,1,0:T(2,128)(2,1)S(1)}, u32[]{:S(2)}, u32[]{:S(2)}) collective-permute-start(bf16[2,10,2,384]{3,2,1,0:T(2,128)(2,1)S(1)} %get-tuple-element.25), channel_id=1, source_target_pairs={{0,2},{2,4},{4,6},{6,8},{8,10},{10,12},{12,14},{14,16},{16,18},{18... | collective-permute-start | bytes 92168 | tf_op jit(solution)/shard_map/ppermute | solution.py:540
  118.5 2.1 %collective-permute-start.33 = (bf16[2,10,2,384]{3,2,1,0:T(2,128)(2,1)S(1)}, bf16[2,10,2,384]{3,2,1,0:T(2,128)(2,1)S(1)}, u32[]{:S(2)}, u32[]{:S(2)}) collective-permute-start(bf16[2,10,2,384]{3,2,1,0:T(2,128)(2,1)S(1)} %get-tuple-element.26), channel_id=1, source_target_pairs={{2,0},{4,2},{6,4},{8,6},{10,8},{12,10},{14,12},{16,14},{18,16},{20... | collective-permute-start | bytes 92168 | tf_op jit(solution)/shard_map/ppermute | solution.py:540
  120.6 1.3 collective-permute-start.34
  121.9 0.1 copy.23.refs_5_
  122.1 1.9 %collective-permute-done.33 = bf16[2,10,2,384]{3,2,1,0:T(2,128)(2,1)S(1)} collective-permute-done((bf16[2,10,2,384]{3,2,1,0:T(2,128)(2,1)S(1)}, bf16[2,10,2,384]{3,2,1,0:T(2,128)(2,1)S(1)}, u32[]{:S(2)}, u32[]{:S(2)}) %collective-permute-start.33) | collective-permute-done | bytes 30752 | tf_op jit(solution)/shard_map/ppermute | solution.py:540
  124.1 1.3 collective-permute-start.35
  125.4 2.5 %collective-permute-done.35.refs_3_ = bf16[2,10,4,384]{3,2,1,0:T(4,128)(2,1)S(1)} collective-permute-done((bf16[2,10,4,384]{3,2,1,0:T(4,128)(2,1)S(1)}, bf16[2,10,4,384]{3,2,1,0:T(4,128)(2,1)S(1)}, u32[]{:S(2)}, u32[]{:S(2)}) %collective-permute-start.35) | collective-permute-done | bytes 61472 | tf_op jit(solution)/shard_map/ppermute | solution.py:542
  128.0 7.0 %convolutions.1 = bf16[1,5,2,2,16,384]{5,4,3,2,1,0:T(8,128)(2,1)} custom-call(s32[2]{0:T(128)S(1)} %add_convert_fusion.6.ends, bf16[2,10,16,384]{3,2,1,0:T(8,128)(2,1)S(1)} %update.1.refs_0_, bf16[2,10,4,384]{3,2,1,0:T(4,128)(2,1)S(1)} %pad_maximum_fusion.3.refs_1_, bf16[2,10,16,384]{3,2,1,0:T(8,128)(2,1)S(1)} %collective-permute-done.34.refs_2_, ...), custom_call_target="tpu_custom_call" | custom-call | flops 1585446912 | bytes 1048576 | tf_op jit(solution)/shard_map/convolutions/pallas_call | solution.py:461
  (102 shorter events, 2.5 us)
Async XLA Ops:
  0.0 3.1 %copy-start.3 = (bf16[128,128]{1,0:T(8,128)(2,1)S(1)}, bf16[128,128]{1,0:T(8,128)(2,1)}, u32[]{:S(2)}) copy-start(bf16[128,128]{1,0:T(8,128)(2,1)} %constant.197.clone.along_z) | copy-start | bytes 98308
  0.0 3.1 %copy-start = (bf16[384,384]{1,0:T(8,128)(2,1)S(1)}, bf16[384,384]{1,0:T(8,128)(2,1)}, u32[]{:S(2)}) copy-start(bf16[384,384]{1,0:T(8,128)(2,1)} %constant.198.clone.along_y) | copy-start | bytes 884740
  0.0 3.1 %copy-start.2 = (bf16[1,5,2,2,16,384]{5,4,3,2,1,0:T(8,128)(2,1)S(1)}, bf16[1,5,2,2,16,384]{5,4,3,2,1,0:T(8,128)(2,1)}, u32[]{:S(2)}) copy-start(bf16[1,5,2,2,16,384]{5,4,3,2,1,0:T(8,128)(2,1)} %image.1) | copy-start | bytes 737284
  3.1 10.5 %copy-start.15 = (bf16[64,10,3,3,3]{0,4,3,2,1:T(4,128)(2,1)S(1)}, bf16[64,10,3,3,3]{0,4,3,2,1:T(4,128)(2,1)}, u32[]{:S(2)}) copy-start(bf16[64,10,3,3,3]{0,4,3,2,1:T(4,128)(2,1)} %param.19) | copy-start | bytes 103684
  3.7 10.4 %copy-start.16 = (bf16[10,64,3,3,3]{1,4,3,2,0:T(4,128)(2,1)S(1)}, bf16[10,64,3,3,3]{1,4,3,2,0:T(4,128)(2,1)}, u32[]{:S(2)}) copy-start(bf16[10,64,3,3,3]{1,4,3,2,0:T(4,128)(2,1)} %param.21) | copy-start | bytes 103684
  3.8 10.8 %copy-start.17 = (f32[64]{0:T(128)S(1)}, f32[64]{0:T(128)}, u32[]{:S(2)}) copy-start(f32[64]{0:T(128)} %param.20) | copy-start | bytes 772
  3.8 13.6 %collective-permute-start.16 = (bf16[1,10,16,384]{3,2,1,0:T(8,128)(2,1)S(1)}, bf16[1,10,16,384]{3,2,1,0:T(8,128)(2,1)S(1)}, u32[]{:S(2)}, u32[]{:S(2)}) collective-permute-start(bf16[1,10,16,384]{3,2,1,0:T(8,128)(2,1)S(1)} %get-tuple-element.27.refs_0_), channel_id=1, source_target_pairs={{0,2},{2,0},{4,6},{6,4},{8,10},{10,8},{12,14},{14,12},{16,18},{18,... | collective-permute-start | bytes 368648 | tf_op jit(solution)/shard_map/ppermute | solution.py:101
  3.9 14.7 %collective-permute-start.17 = (bf16[1,10,16,384]{3,2,1,0:T(8,128)(2,1)S(1)}, bf16[1,10,16,384]{3,2,1,0:T(8,128)(2,1)S(1)}, u32[]{:S(2)}, u32[]{:S(2)}) collective-permute-start(bf16[1,10,16,384]{3,2,1,0:T(8,128)(2,1)S(1)} %get-tuple-element.27.refs_0_), channel_id=1, source_target_pairs={{0,8},{2,6},{8,16},{10,2},{16,24},{18,10},{24,28},{26,18},{28,20},... | collective-permute-start | bytes 368648 | tf_op jit(solution)/shard_map/ppermute | solution.py:100
  6.6 23.9 %all-to-all-start = ((bf16[16,2,2,16,384]{4,3,2,1,0:T(8,128)(2,1)}), bf16[16,2,2,16,384]{4,3,2,1,0:T(8,128)(2,1)S(1)}, u32[]{:S(2)}, u32[]{:S(2)}) async-start(bf16[16,2,2,16,384]{4,3,2,1,0:T(8,128)(2,1)} %prepare_maps.1.earlier), calls=%async_computation | async-start | bytes 1572864 | tf_op jit(solution)/shard_map/all_to_all | solution.py:523
  11.8 6.8 %collective-permute-start = (bf16[1,10,16,384]{3,2,1,0:T(8,128)(2,1)S(1)}, bf16[1,10,16,384]{3,2,1,0:T(8,128)(2,1)S(1)}, u32[]{:S(2)}, u32[]{:S(2)}) collective-permute-start(bf16[1,10,16,384]{3,2,1,0:T(8,128)(2,1)S(1)} %get-tuple-element.28.refs_0_), channel_id=1, source_target_pairs={{0,2},{2,0},{4,6},{6,4},{8,10},{10,8},{12,14},{14,12},{16,18},{18,... | collective-permute-start | bytes 368648 | tf_op jit(solution)/shard_map/ppermute | solution.py:101
  12.0 14.2 %collective-permute-start.1 = (bf16[1,10,16,384]{3,2,1,0:T(8,128)(2,1)S(1)}, bf16[1,10,16,384]{3,2,1,0:T(8,128)(2,1)S(1)}, u32[]{:S(2)}, u32[]{:S(2)}) collective-permute-start(bf16[1,10,16,384]{3,2,1,0:T(8,128)(2,1)S(1)} %get-tuple-element.28.refs_0_), channel_id=1, source_target_pairs={{0,8},{2,6},{8,16},{10,2},{16,24},{18,10},{24,28},{26,18},{28,20},... | collective-permute-start | bytes 368648 | tf_op jit(solution)/shard_map/ppermute | solution.py:100
  17.4 21.7 %copy-start.9 = (bf16[1,10,16,384]{3,2,1,0:T(8,128)(2,1)}, bf16[1,10,16,384]{3,2,1,0:T(8,128)(2,1)S(1)}, u32[]{:S(2)}) copy-start(bf16[1,10,16,384]{3,2,1,0:T(8,128)(2,1)S(1)} %collective-permute-done.16.refs_1_) | copy-start | bytes 368644
  17.4 10.5 %collective-permute-start.18 = (bf16[1,10,16,384]{3,2,1,0:T(8,128)(2,1)S(1)}, bf16[1,10,16,384]{3,2,1,0:T(8,128)(2,1)S(1)}, u32[]{:S(2)}, u32[]{:S(2)}) collective-permute-start(bf16[1,10,16,384]{3,2,1,0:T(8,128)(2,1)S(1)} %collective-permute-done.16.refs_1_), channel_id=1, source_target_pairs={{0,8},{2,6},{8,16},{10,2},{16,24},{18,10},{24,28},{26,18},{28,20},... | collective-permute-start | bytes 368648 | tf_op jit(solution)/shard_map/ppermute | solution.py:108
  18.6 20.5 %copy-start.7 = (bf16[1,10,16,384]{3,2,1,0:T(8,128)(2,1)}, bf16[1,10,16,384]{3,2,1,0:T(8,128)(2,1)S(1)}, u32[]{:S(2)}) copy-start(bf16[1,10,16,384]{3,2,1,0:T(8,128)(2,1)S(1)} %collective-permute-done.refs_1_) | copy-start | bytes 368644
  18.6 13.1 %collective-permute-start.2 = (bf16[1,10,16,384]{3,2,1,0:T(8,128)(2,1)S(1)}, bf16[1,10,16,384]{3,2,1,0:T(8,128)(2,1)S(1)}, u32[]{:S(2)}, u32[]{:S(2)}) collective-permute-start(bf16[1,10,16,384]{3,2,1,0:T(8,128)(2,1)S(1)} %collective-permute-done.refs_1_), channel_id=1, source_target_pairs={{0,8},{2,6},{8,16},{10,2},{16,24},{18,10},{24,28},{26,18},{28,20},... | collective-permute-start | bytes 368648 | tf_op jit(solution)/shard_map/ppermute | solution.py:108
  27.9 11.2 %collective-permute-start.19 = (bf16[2,10,16,384]{3,2,1,0:T(8,128)(2,1)S(1)}, bf16[2,10,16,384]{3,2,1,0:T(8,128)(2,1)}, u32[]{:S(2)}, u32[]{:S(2)}) collective-permute-start(bf16[2,10,16,384]{3,2,1,0:T(8,128)(2,1)S(1)} %constant_dynamic-update-slice_fusion.2.refs_2_), channel_id=1, source_target_pairs={{0,8},{2,6},{8,16},{10,2},{16,24},{18,10},{24,28},{26,18},{28,20},... | collective-permute-start | bytes 737288 | tf_op jit(solution)/shard_map/ppermute | solution.py:111
  30.5 25.5 %collective-permute-start.10 = (bf16[16,2,2,16,384]{4,3,2,1,0:T(8,128)(2,1)S(1)}, bf16[16,2,2,16,384]{4,3,2,1,0:T(8,128)(2,1)S(1)}, u32[]{:S(2)}, u32[]{:S(2)}) collective-permute-start(bf16[16,2,2,16,384]{4,3,2,1,0:T(8,128)(2,1)S(1)} %all-to-all-done.refs_10_), channel_id=1, source_target_pairs={{0,1},{1,0},{2,3},{3,2},{4,5},{5,4},{6,7},{7,6},{8,9},{9,8},{10,11... | collective-permute-start | bytes 2359304 | tf_op jit(solution)/shard_map/ppermute | solution.py:527
  31.7 10.0 %collective-permute-start.3 = (bf16[2,10,16,384]{3,2,1,0:T(8,128)(2,1)S(1)}, bf16[2,10,16,384]{3,2,1,0:T(8,128)(2,1)S(1)}, u32[]{:S(2)}, u32[]{:S(2)}) collective-permute-start(bf16[2,10,16,384]{3,2,1,0:T(8,128)(2,1)S(1)} %constant_dynamic-update-slice_fusion.refs_2_), channel_id=1, source_target_pairs={{0,8},{2,6},{8,16},{10,2},{16,24},{18,10},{24,28},{26,18},{28,20},... | collective-permute-start | bytes 737288 | tf_op jit(solution)/shard_map/ppermute | solution.py:111
  39.1 5.6 %collective-permute-start.20 = (bf16[2,10,16,384]{3,2,1,0:T(8,128)(2,1)}, bf16[2,10,16,384]{3,2,1,0:T(8,128)(2,1)S(1)}, u32[]{:S(2)}, u32[]{:S(2)}) collective-permute-start(bf16[2,10,16,384]{3,2,1,0:T(8,128)(2,1)} %collective-permute-done.19.refs_3_), channel_id=1, source_target_pairs={{0,8},{2,6},{8,16},{10,2},{16,24},{18,10},{24,28},{26,18},{28,20},... | collective-permute-start | bytes 737288 | tf_op jit(solution)/shard_map/ppermute | solution.py:111
  41.7 5.6 %collective-permute-start.4 = (bf16[2,10,16,384]{3,2,1,0:T(8,128)(2,1)S(1)}, bf16[2,10,16,384]{3,2,1,0:T(8,128)(2,1)S(1)}, u32[]{:S(2)}, u32[]{:S(2)}) collective-permute-start(bf16[2,10,16,384]{3,2,1,0:T(8,128)(2,1)S(1)} %collective-permute-done.3.refs_3_), channel_id=1, source_target_pairs={{0,8},{2,6},{8,16},{10,2},{16,24},{18,10},{24,28},{26,18},{28,20},... | collective-permute-start | bytes 737288 | tf_op jit(solution)/shard_map/ppermute | solution.py:111
  41.7 7.9 %collective-permute-start.22 = (bf16[2,10,16,384]{3,2,1,0:T(8,128)(2,1)S(1)}, bf16[2,10,16,384]{3,2,1,0:T(8,128)(2,1)S(1)}, u32[]{:S(2)}, u32[]{:S(2)}) collective-permute-start(bf16[2,10,16,384]{3,2,1,0:T(8,128)(2,1)S(1)} %constant_dynamic-update-slice_fusion.2.refs_2_), channel_id=1, source_target_pairs={{0,2},{2,0},{4,6},{6,4},{8,10},{10,8},{12,14},{14,12},{16,18},{18,... | collective-permute-start | bytes 737288 | tf_op jit(solution)/shard_map/ppermute | solution.py:113
  44.5 7.7 %collective-permute-start.23 = (bf16[2,10,16,384]{3,2,1,0:T(8,128)(2,1)}, bf16[2,10,16,384]{3,2,1,0:T(8,128)(2,1)}, u32[]{:S(2)}, u32[]{:S(2)}) collective-permute-start(bf16[2,10,16,384]{3,2,1,0:T(8,128)(2,1)} %collective-permute-done.19.refs_3_), channel_id=1, source_target_pairs={{0,2},{2,0},{4,6},{6,4},{8,10},{10,8},{12,14},{14,12},{16,18},{18,... | collective-permute-start | bytes 737288 | tf_op jit(solution)/shard_map/ppermute | solution.py:113
  44.6 7.4 %collective-permute-start.21 = (bf16[1,10,16,384]{3,2,1,0:T(8,128)(2,1)S(1)}, bf16[1,10,16,384]{3,2,1,0:T(8,128)(2,1)}, u32[]{:S(2)}, u32[]{:S(2)}) collective-permute-start(bf16[1,10,16,384]{3,2,1,0:T(8,128)(2,1)S(1)} %slice.144), channel_id=1, source_target_pairs={{0,8},{2,6},{8,16},{10,2},{16,24},{18,10},{24,28},{26,18},{28,20},... | collective-permute-start | bytes 368648 | tf_op jit(solution)/shard_map/ppermute | solution.py:111
  47.3 8.2 %collective-permute-start.24 = (bf16[2,10,16,384]{3,2,1,0:T(8,128)(2,1)S(1)}, bf16[2,10,16,384]{3,2,1,0:T(8,128)(2,1)}, u32[]{:S(2)}, u32[]{:S(2)}) collective-permute-start(bf16[2,10,16,384]{3,2,1,0:T(8,128)(2,1)S(1)} %collective-permute-done.20.refs_4_), channel_id=1, source_target_pairs={{0,2},{2,0},{4,6},{6,4},{8,10},{10,8},{12,14},{14,12},{16,18},{18,... | collective-permute-start | bytes 737288 | tf_op jit(solution)/shard_map/ppermute | solution.py:113
  49.6 0.7 copy-start.5
  50.3 4.4 %collective-permute-start.5 = (bf16[1,10,16,384]{3,2,1,0:T(8,128)(2,1)}, bf16[1,10,16,384]{3,2,1,0:T(8,128)(2,1)}, u32[]{:S(2)}, u32[]{:S(2)}) collective-permute-start(bf16[1,10,16,384]{3,2,1,0:T(8,128)(2,1)} %slice.136), channel_id=1, source_target_pairs={{0,8},{2,6},{8,16},{10,2},{16,24},{18,10},{24,28},{26,18},{28,20},... | collective-permute-start | bytes 368648 | tf_op jit(solution)/shard_map/ppermute | solution.py:111
  52.0 3.5 %collective-permute-start.25 = (bf16[1,10,16,384]{3,2,1,0:T(8,128)(2,1)}, bf16[1,10,16,384]{3,2,1,0:T(8,128)(2,1)}, u32[]{:S(2)}, u32[]{:S(2)}) collective-permute-start(bf16[1,10,16,384]{3,2,1,0:T(8,128)(2,1)} %collective-permute-done.21.refs_5_), channel_id=1, source_target_pairs={{0,2},{2,0},{4,6},{6,4},{8,10},{10,8},{12,14},{14,12},{16,18},{18,... | collective-permute-start | bytes 368648 | tf_op jit(solution)/shard_map/ppermute | solution.py:113
  52.2 19.7 %collective-permute-start.6 = (bf16[2,10,16,384]{3,2,1,0:T(8,128)(2,1)S(1)}, bf16[2,10,16,384]{3,2,1,0:T(8,128)(2,1)S(1)}, u32[]{:S(2)}, u32[]{:S(2)}) collective-permute-start(bf16[2,10,16,384]{3,2,1,0:T(8,128)(2,1)S(1)} %constant_dynamic-update-slice_fusion.refs_2_), channel_id=1, source_target_pairs={{0,2},{2,0},{4,6},{6,4},{8,10},{10,8},{12,14},{14,12},{16,18},{18,... | collective-permute-start | bytes 737288 | tf_op jit(solution)/shard_map/ppermute | solution.py:113
  54.7 17.2 %collective-permute-start.7 = (bf16[2,10,16,384]{3,2,1,0:T(8,128)(2,1)S(1)}, bf16[2,10,16,384]{3,2,1,0:T(8,128)(2,1)S(1)}, u32[]{:S(2)}, u32[]{:S(2)}) collective-permute-start(bf16[2,10,16,384]{3,2,1,0:T(8,128)(2,1)S(1)} %collective-permute-done.3.refs_3_), channel_id=1, source_target_pairs={{0,2},{2,0},{4,6},{6,4},{8,10},{10,8},{12,14},{14,12},{16,18},{18,... | collective-permute-start | bytes 737288 | tf_op jit(solution)/shard_map/ppermute | solution.py:113
  55.5 16.4 %collective-permute-start.8 = (bf16[2,10,16,384]{3,2,1,0:T(8,128)(2,1)S(1)}, bf16[2,10,16,384]{3,2,1,0:T(8,128)(2,1)S(1)}, u32[]{:S(2)}, u32[]{:S(2)}) collective-permute-start(bf16[2,10,16,384]{3,2,1,0:T(8,128)(2,1)S(1)} %collective-permute-done.4.refs_4_), channel_id=1, source_target_pairs={{0,2},{2,0},{4,6},{6,4},{8,10},{10,8},{12,14},{14,12},{16,18},{18,... | collective-permute-start | bytes 737288 | tf_op jit(solution)/shard_map/ppermute | solution.py:113
  55.5 16.4 %collective-permute-start.9 = (bf16[1,10,16,384]{3,2,1,0:T(8,128)(2,1)}, bf16[1,10,16,384]{3,2,1,0:T(8,128)(2,1)S(1)}, u32[]{:S(2)}, u32[]{:S(2)}) collective-permute-start(bf16[1,10,16,384]{3,2,1,0:T(8,128)(2,1)} %collective-permute-done.5.refs_5_), channel_id=1, source_target_pairs={{0,2},{2,0},{4,6},{6,4},{8,10},{10,8},{12,14},{14,12},{16,18},{18,... | collective-permute-start | bytes 368648 | tf_op jit(solution)/shard_map/ppermute | solution.py:113
  56.0 0.9 copy-start.6
  57.0 0.9 copy-start.10
  57.9 1.1 copy-start.12
  59.0 12.9 %copy-start.8 = (bf16[1,10,16,384]{3,2,1,0:T(8,128)(2,1)S(1)}, bf16[1,10,16,384]{3,2,1,0:T(8,128)(2,1)}, u32[]{:S(2)}) copy-start(bf16[1,10,16,384]{3,2,1,0:T(8,128)(2,1)} %copy-done.7) | copy-start | bytes 368644
  71.7 13.3 %copy-start.13 = (bf16[7,10,16,384]{3,2,1,0:T(8,128)(2,1)S(1)}, bf16[7,10,16,384]{3,2,1,0:T(8,128)(2,1)}, u32[]{:S(2)}) copy-start(bf16[7,10,16,384]{3,2,1,0:T(8,128)(2,1)} %get-tuple-element.23) | copy-start | bytes 2580484
  71.7 13.3 %collective-permute-start.26 = (bf16[7,10,16,384]{3,2,1,0:T(8,128)(2,1)}, bf16[7,10,16,384]{3,2,1,0:T(8,128)(2,1)S(1)}, u32[]{:S(2)}, u32[]{:S(2)}) collective-permute-start(bf16[7,10,16,384]{3,2,1,0:T(8,128)(2,1)} %get-tuple-element.24), channel_id=1, source_target_pairs={{0,2},{2,0},{4,6},{6,4},{8,10},{10,8},{12,14},{14,12},{16,18},{18,... | collective-permute-start | bytes 2580488 | tf_op jit(solution)/shard_map/ppermute | solution.py:122
  84.6 5.4 %copy-start.14 = (bf16[7,10,16,384]{3,2,1,0:T(8,128)(2,1)S(1)}, bf16[7,10,16,384]{3,2,1,0:T(8,128)(2,1)}, u32[]{:S(2)}) copy-start(bf16[7,10,16,384]{3,2,1,0:T(8,128)(2,1)} %get-tuple-element.18) | copy-start | bytes 2580484
  84.6 2.6 %collective-permute-start.11 = (bf16[7,10,16,384]{3,2,1,0:T(8,128)(2,1)}, bf16[7,10,16,384]{3,2,1,0:T(8,128)(2,1)S(1)}, u32[]{:S(2)}, u32[]{:S(2)}) collective-permute-start(bf16[7,10,16,384]{3,2,1,0:T(8,128)(2,1)} %get-tuple-element.19), channel_id=1, source_target_pairs={{0,2},{2,0},{4,6},{6,4},{8,10},{10,8},{12,14},{14,12},{16,18},{18,... | collective-permute-start | bytes 2580488 | tf_op jit(solution)/shard_map/ppermute | solution.py:122
  85.0 5.0 %collective-permute-start.27 = (bf16[1,10,16,384]{3,2,1,0:T(8,128)(2,1)S(1)}, bf16[1,10,16,384]{3,2,1,0:T(8,128)(2,1)S(1)}, u32[]{:S(2)}, u32[]{:S(2)}) collective-permute-start(bf16[1,10,16,384]{3,2,1,0:T(8,128)(2,1)S(1)} %add_convert_fusion.4), channel_id=1, source_target_pairs={{0,8},{2,6},{8,16},{10,2},{16,24},{18,10},{24,28},{26,18},{28,20},... | collective-permute-start | bytes 368648 | tf_op jit(solution)/shard_map/ppermute | solution.py:137
  88.2 4.1 %collective-permute-start.12 = (bf16[1,10,16,384]{3,2,1,0:T(8,128)(2,1)S(1)}, bf16[1,10,16,384]{3,2,1,0:T(8,128)(2,1)S(1)}, u32[]{:S(2)}, u32[]{:S(2)}) collective-permute-start(bf16[1,10,16,384]{3,2,1,0:T(8,128)(2,1)S(1)} %add_convert_fusion.5), channel_id=1, source_target_pairs={{0,8},{2,6},{8,16},{10,2},{16,24},{18,10},{24,28},{26,18},{28,20},... | collective-permute-start | bytes 368648 | tf_op jit(solution)/shard_map/ppermute | solution.py:137
  90.1 5.4 %collective-permute-start.28 = (bf16[2,10,16,384]{3,2,1,0:T(8,128)(2,1)S(1)}, bf16[2,10,16,384]{3,2,1,0:T(8,128)(2,1)S(1)}, u32[]{:S(2)}, u32[]{:S(2)}) collective-permute-start(bf16[2,10,16,384]{3,2,1,0:T(8,128)(2,1)S(1)} %pad_maximum_fusion.2), channel_id=1, source_target_pairs={{0,8},{2,6},{8,16},{10,2},{16,24},{18,10},{24,28},{26,18},{28,20},... | collective-permute-start | bytes 737288 | tf_op jit(solution)/shard_map/ppermute | solution.py:137
  92.4 5.8 %collective-permute-start.13 = (bf16[2,10,16,384]{3,2,1,0:T(8,128)(2,1)S(1)}, bf16[2,10,16,384]{3,2,1,0:T(8,128)(2,1)S(1)}, u32[]{:S(2)}, u32[]{:S(2)}) collective-permute-start(bf16[2,10,16,384]{3,2,1,0:T(8,128)(2,1)S(1)} %pad_maximum_fusion.1), channel_id=1, source_target_pairs={{0,8},{2,6},{8,16},{10,2},{16,24},{18,10},{24,28},{26,18},{28,20},... | collective-permute-start | bytes 737288 | tf_op jit(solution)/shard_map/ppermute | solution.py:137
  95.6 5.4 %collective-permute-start.29 = (bf16[2,10,16,384]{3,2,1,0:T(8,128)(2,1)S(1)}, bf16[2,10,16,384]{3,2,1,0:T(8,128)(2,1)S(1)}, u32[]{:S(2)}, u32[]{:S(2)}) collective-permute-start(bf16[2,10,16,384]{3,2,1,0:T(8,128)(2,1)S(1)} %add_convert_fusion.1), channel_id=1, source_target_pairs={{0,8},{2,6},{8,16},{10,2},{16,24},{18,10},{24,28},{26,18},{28,20},... | collective-permute-start | bytes 737288 | tf_op jit(solution)/shard_map/ppermute | solution.py:137
  98.2 5.4 %collective-permute-start.14 = (bf16[2,10,16,384]{3,2,1,0:T(8,128)(2,1)S(1)}, bf16[2,10,16,384]{3,2,1,0:T(8,128)(2,1)S(1)}, u32[]{:S(2)}, u32[]{:S(2)}) collective-permute-start(bf16[2,10,16,384]{3,2,1,0:T(8,128)(2,1)S(1)} %add_convert_fusion.3), channel_id=1, source_target_pairs={{0,8},{2,6},{8,16},{10,2},{16,24},{18,10},{24,28},{26,18},{28,20},... | collective-permute-start | bytes 737288 | tf_op jit(solution)/shard_map/ppermute | solution.py:137
  101.1 5.4 %collective-permute-start.30 = (bf16[2,10,16,384]{3,2,1,0:T(8,128)(2,1)S(1)}, bf16[2,10,16,384]{3,2,1,0:T(8,128)(2,1)S(1)}, u32[]{:S(2)}, u32[]{:S(2)}) collective-permute-start(bf16[2,10,16,384]{3,2,1,0:T(8,128)(2,1)S(1)} %add_convert_fusion), channel_id=1, source_target_pairs={{0,8},{2,6},{8,16},{10,2},{16,24},{18,10},{24,28},{26,18},{28,20},... | collective-permute-start | bytes 737288 | tf_op jit(solution)/shard_map/ppermute | solution.py:137
  103.7 5.4 %collective-permute-start.15 = (bf16[2,10,16,384]{3,2,1,0:T(8,128)(2,1)S(1)}, bf16[2,10,16,384]{3,2,1,0:T(8,128)(2,1)S(1)}, u32[]{:S(2)}, u32[]{:S(2)}) collective-permute-start(bf16[2,10,16,384]{3,2,1,0:T(8,128)(2,1)S(1)} %add_convert_fusion.2), channel_id=1, source_target_pairs={{0,8},{2,6},{8,16},{10,2},{16,24},{18,10},{24,28},{26,18},{28,20},... | collective-permute-start | bytes 737288 | tf_op jit(solution)/shard_map/ppermute | solution.py:137
  106.5 7.3 %copy-start.1 = (bf16[384,384]{1,0:T(8,128)(2,1)S(1)}, bf16[384,384]{1,0:T(8,128)(2,1)}, u32[]{:S(2)}) copy-start(bf16[384,384]{1,0:T(8,128)(2,1)} %constant.200.clone.along_y) | copy-start | bytes 884740
  106.6 7.3 %copy-start.4 = (bf16[128,128]{1,0:T(8,128)(2,1)S(1)}, bf16[128,128]{1,0:T(8,128)(2,1)}, u32[]{:S(2)}) copy-start(bf16[128,128]{1,0:T(8,128)(2,1)} %constant.199.clone.along_z) | copy-start | bytes 98308
  109.2 18.8 %copy-start.11 = (f32[10]{0:T(128)S(1)}, f32[10]{0:T(128)}, u32[]{:S(2)}) copy-start(f32[10]{0:T(128)} %refs_7_.1) | copy-start | bytes 124
  109.2 4.6 %collective-permute-start.31 = (bf16[2,10,16,384]{3,2,1,0:T(8,128)(2,1)S(1)}, bf16[2,10,16,384]{3,2,1,0:T(8,128)(2,1)S(1)}, u32[]{:S(2)}, u32[]{:S(2)}) collective-permute-start(bf16[2,10,16,384]{3,2,1,0:T(8,128)(2,1)S(1)} %fusion.5), channel_id=1, source_target_pairs={{0,2},{2,0},{4,6},{6,4},{8,10},{10,8},{12,14},{14,12},{16,18},{18,... | collective-permute-start | bytes 737288 | tf_op jit(solution)/shard_map/ppermute | solution.py:535
  114.6 7.5 %collective-permute-start.32 = (bf16[2,10,2,384]{3,2,1,0:T(2,128)(2,1)S(1)}, bf16[2,10,2,384]{3,2,1,0:T(2,128)(2,1)S(1)}, u32[]{:S(2)}, u32[]{:S(2)}) collective-permute-start(bf16[2,10,2,384]{3,2,1,0:T(2,128)(2,1)S(1)} %get-tuple-element.25), channel_id=1, source_target_pairs={{0,2},{2,4},{4,6},{6,8},{8,10},{10,12},{12,14},{14,16},{16,18},{18... | collective-permute-start | bytes 92168 | tf_op jit(solution)/shard_map/ppermute | solution.py:540
  118.5 5.5 %collective-permute-start.33 = (bf16[2,10,2,384]{3,2,1,0:T(2,128)(2,1)S(1)}, bf16[2,10,2,384]{3,2,1,0:T(2,128)(2,1)S(1)}, u32[]{:S(2)}, u32[]{:S(2)}) collective-permute-start(bf16[2,10,2,384]{3,2,1,0:T(2,128)(2,1)S(1)} %get-tuple-element.26), channel_id=1, source_target_pairs={{2,0},{4,2},{6,4},{8,6},{10,8},{12,10},{14,12},{16,14},{18,16},{20... | collective-permute-start | bytes 92168 | tf_op jit(solution)/shard_map/ppermute | solution.py:540
  120.6 7.4 %collective-permute-start.34 = (bf16[2,10,16,384]{3,2,1,0:T(8,128)(2,1)S(1)}, bf16[2,10,16,384]{3,2,1,0:T(8,128)(2,1)S(1)}, u32[]{:S(2)}, u32[]{:S(2)}) collective-permute-start(bf16[2,10,16,384]{3,2,1,0:T(8,128)(2,1)S(1)} %update.1.refs_0_), channel_id=1, source_target_pairs={{0,1},{1,0},{2,3},{3,2},{4,5},{5,4},{6,7},{7,6},{8,9},{9,8},{10,11... | collective-permute-start | bytes 737288 | tf_op jit(solution)/shard_map/ppermute | solution.py:538
  124.1 3.9 %collective-permute-start.35 = (bf16[2,10,4,384]{3,2,1,0:T(4,128)(2,1)S(1)}, bf16[2,10,4,384]{3,2,1,0:T(4,128)(2,1)S(1)}, u32[]{:S(2)}, u32[]{:S(2)}) collective-permute-start(bf16[2,10,4,384]{3,2,1,0:T(4,128)(2,1)S(1)} %pad_maximum_fusion.3.refs_1_), channel_id=1, source_target_pairs={{0,1},{1,0},{2,3},{3,2},{4,5},{5,4},{6,7},{7,6},{8,9},{9,8},{10,11... | collective-permute-start | bytes 184328 | tf_op jit(solution)/shard_map/ppermute | solution.py:542
